TPU v7x, 32 devices: a whole 2x2x4 slice. The times are simulated.
32 devices in a mesh: groups: 2 (over y), fsdp: 4 (over z), resp: 2 (over x), tp: 2 (over core).
Axes of the slice: x: 2, y: 2, z: 4, core: 2. Of those that a mesh axis runs over, the one named last changes fastest.
Arguments:
- hidden: bfloat16 [8, 4, 128, 8192], P(('groups', 'fsdp'), 'resp', None, 'tp'), parts along dimension 0, may hold values from -6 to 6
- queries: bfloat16 [8, 4, 128, 4096], P(('groups', 'fsdp'), 'resp', None, 'tp'), parts along dimension 0, may hold values from -140 to 140
- prompt_keys: bfloat16 [8, 1024, 512], P(('groups', 'fsdp'), 'resp', 'tp'), parts along dimension 0, may hold values from -4.5 to 4.5
- prompt_values: bfloat16 [8, 1024, 512], P(('groups', 'fsdp'), 'resp', 'tp'), parts along dimension 0, may hold values from -6 to 6
- key_weight: bfloat16 [8192, 512], P(('fsdp', 'resp'), 'tp'), may hold values from -0.0625 to 0.0625
- value_weight: bfloat16 [8192, 512], P(('fsdp', 'resp'), 'tp'), may hold values from -0.0625 to 0.0625
- counts: int32 [8], P(('groups', 'fsdp')), parts along dimension 0, may hold values from 1 to 4
Outputs:
- attended: bfloat16 [8, 4, 128, 4096], P(('groups', 'fsdp'), 'resp', None, 'tp'), parts along dimension 0
There are 2 independent parts, one for each index of `groups`. A program takes and returns all parts, laid end to end along the dimension named above; an argument that names none is the same for every part. Nothing has to cross between parts.
All inputs are finite; a program needn't handle non-finite values.
Results may differ from a plain program's by a relative error of at most 0.0069.
Values may be sent and summed in bfloat16 or wider, within the bound.
No kernel may reach another device: no remote copies, remote signals or barrier semaphores. Data moves between devices by JAX's collectives and lax.ppermute only.
A program may use at most 128 MiB of HBM per device.

v0:
```python
import functools
import math

import jax
import jax.numpy as jnp
from jax import lax
from jax.sharding import PartitionSpec as P

HD = 128
PLEN = 1024


def rotate(vectors, offset):
    half_size = vectors.shape[-1] // 2
    extent = vectors.shape[-3]
    orders = jnp.arange(half_size, dtype=jnp.float32)
    inverse = jnp.exp(-(2.0 * orders / vectors.shape[-1]) * math.log(500000.0))
    places = (offset + jnp.arange(extent)).astype(jnp.float32)
    angles = places[:, None] * inverse[None, :]
    cosine = jnp.cos(angles)[:, None, :]
    sine_table = jnp.sin(angles)[:, None, :]
    leading = vectors[..., :half_size]
    second = vectors[..., half_size:]
    return jnp.concatenate(
        [leading * cosine - second * sine_table, second * cosine + leading * sine_table], axis=-1
    )


def absorb(queried, cache_keys, cache_values, allowed, carry_state):
    row_top, row_total, mixed_sum = carry_state
    scores = jnp.einsum("rkgd,lkd->rkgl", queried, cache_keys, preferred_element_type=jnp.float32)
    scores = scores * queried.shape[-1] ** (-0.5)
    if allowed is not None:
        scores = jnp.where(allowed, scores, -1e30)
    new_top = jnp.maximum(row_top, jnp.max(scores, axis=-1))
    weights = jnp.exp(scores - new_top[..., None])
    shrink = jnp.exp(row_top - new_top)
    row_total = row_total * shrink + jnp.sum(weights, axis=-1)
    mixed_sum = mixed_sum * shrink[..., None] + jnp.einsum(
        "rkgl,lkd->rkgd",
        weights.astype(jnp.bfloat16),
        cache_values,
        preferred_element_type=jnp.float32,
    )
    return (new_top, row_total, mixed_sum)


def visit_slot(carry_state, queried, cache_keys, cache_values, allowed):
    update = functools.partial(absorb, queried, cache_keys, cache_values, allowed)
    return update(carry_state)


def on_device(hidden, queries, prompt_keys, prompt_values, key_weight, value_weight, counts):
    slot_count = hidden.shape[1]
    resp_len = hidden.shape[2]
    columns = key_weight.shape[1]
    kv_heads = columns // HD
    group_size = queries.shape[3] // columns
    row_count = slot_count * resp_len
    gathered = lax.all_gather(hidden, "tp", axis=3, tiled=True)
    feature_width = gathered.shape[3]
    token_rows = gathered.reshape(row_count, feature_width)
    pieces = (
        lax.all_gather(key_weight, ("fsdp", "resp"), axis=0, tiled=True),
        lax.all_gather(value_weight, ("fsdp", "resp"), axis=0, tiled=True),
    )
    key_sums = jnp.dot(token_rows, pieces[0], preferred_element_type=jnp.float32)
    value_sums = jnp.dot(token_rows, pieces[1], preferred_element_type=jnp.float32)
    own_keys = rotate(key_sums.reshape(slot_count, resp_len, kv_heads, HD), PLEN).astype(
        jnp.bfloat16
    )
    own_values = value_sums.astype(jnp.bfloat16).reshape(slot_count, resp_len, kv_heads, HD)
    queried = queries.reshape(slot_count, resp_len, kv_heads, group_size, HD)
    first_slot = lax.axis_index("resp") * slot_count
    live_flags = [first_slot + number < counts[0] for number in range(slot_count)]

    def fold_prompt(carry_state, pieces):
        tile_keys = pieces[0].reshape(-1, kv_heads, HD)
        tile_values = pieces[1].reshape(-1, kv_heads, HD)
        return tuple(
            (
                visit_slot(carry_state[number], queried[number], tile_keys, tile_values, None)
                for number in range(slot_count)
            )
        )

    top_start = jnp.full((resp_len, kv_heads, group_size), -1e30, jnp.float32)
    total_start = jnp.zeros((resp_len, kv_heads, group_size), jnp.float32)
    mixed_start = jnp.zeros((resp_len, kv_heads, group_size, HD), jnp.float32)
    initial = tuple(((top_start, total_start, mixed_start) for number in range(slot_count)))
    states = fold_prompt(
        initial,
        (
            lax.all_gather(prompt_keys, "resp", axis=1, tiled=True),
            lax.all_gather(prompt_values, "resp", axis=1, tiled=True),
        ),
    )
    causal = (jnp.arange(resp_len)[:, None] >= jnp.arange(resp_len)[None, :])[:, None, None, :]
    results = []
    for number in range(slot_count):
        row_top, row_total, mixed_sum = visit_slot(
            states[number], queried[number], own_keys[number], own_values[number], causal
        )
        safe_total = jnp.where(live_flags[number], row_total, 1.0)
        result = jnp.where(live_flags[number], mixed_sum / safe_total[..., None], 0.0)
        results.append(result.reshape(resp_len, kv_heads * group_size * HD).astype(jnp.bfloat16))
    return jnp.stack(results)[None]


def solution(mesh):
    placed = (
        P(("groups", "fsdp"), "resp", None, "tp"),
        P(("groups", "fsdp"), "resp", None, "tp"),
        P(("groups", "fsdp"), "resp", "tp"),
        P(("groups", "fsdp"), "resp", "tp"),
        P(("fsdp", "resp"), "tp"),
        P(("fsdp", "resp"), "tp"),
        P(("groups", "fsdp")),
    )
    return jax.shard_map(
        on_device,
        mesh=mesh,
        in_specs=placed,
        out_specs=P(("groups", "fsdp"), "resp", None, "tp"),
        check_vma=False,
    )
```

profile of v0, /device:TPU:0, one launch (start us, length us, event | category | flops | bytes accessed | tf_op | source)
XLA Modules:
  0.0 206.8 jit_solution(12124071699441862929)
XLA Ops:
  6.5 0.7 all-gather.6.cloned.1.call-update
  7.3 0.7 all-gather.4.cloned.1.call-update
  8.1 0.7 all-gather.8.cloned.1.call-update
  9.4 1.1 copy.18
  10.5 10.2 %all_gather.16 = bf16[1,1024,256]{2,1,0:T(8,128)(2,1)S(1)} all-gather(bf16[1,512,256]{2,1,0:T(8,128)(2,1)} %param.10), channel_id=1, replica_groups=mesh['groups'=2,'fsdp'=4,'resp'=2,'tp'=2] {'resp'}, dimensions={1}, use_global_device_ids=true | all-gather | bytes 786432 | tf_op jit(solution)/shard_map/all_gather | solution.py:95
  20.9 1.3 fusion.66
  22.8 11.4 %all_gather.15 = bf16[1,1024,256]{1,2,0:T(8,128)(2,1)S(1)} all-gather(bf16[1,512,256]{1,2,0:T(8,128)(2,1)S(1)} %copy.18), channel_id=1, replica_groups=mesh['groups'=2,'fsdp'=4,'resp'=2,'tp'=2] {'resp'}, dimensions={1}, use_global_device_ids=true | all-gather | bytes 786432 | tf_op jit(solution)/shard_map/all_gather | solution.py:94
  34.4 4.5 %bitcast_reduce_fusion.1 = (f32[128,2,8]{0,2,1:T(8,128)S(1)}, f32[2,1024,128,8]{2,1,3,0:T(8,128)}) fusion(bf16[1024,2,128,1]{0,2,3,1:T(8,128)(2,1)S(1)} %bitcast.152, bf16[128,2,8,128]{0,3,2,1:T(8,128)(2,1)S(1)} %bitcast.146), kind=kOutput, calls=%fused_computation.4 | convolution fusion | flops 541063168 | bytes 9445376 | tf_op jit(solution)/shard_map/rkgd,lkd->rkgl/dot_general | solution.py:31
  39.0 4.5 %bitcast_reduce_fusion = (f32[128,2,8]{0,2,1:T(8,128)S(1)}, f32[2,1024,128,8]{2,1,3,0:T(8,128)}) fusion(bf16[1024,2,128,1]{0,2,3,1:T(8,128)(2,1)S(1)} %bitcast.153, bf16[128,2,8,128]{0,3,2,1:T(8,128)(2,1)S(1)} %bitcast.148), kind=kOutput, calls=%fused_computation.1 | convolution fusion | flops 541063168 | bytes 9445376 | tf_op jit(solution)/shard_map/rkgd,lkd->rkgl/dot_general | solution.py:31
  43.5 42.1 %all-gather.6.cloned.1.call-done = bf16[8192,256]{1,0:T(8,128)(2,1)} async-done(((bf16[1024,256]{1,0:T(8,128)(2,1)}), bf16[8192,256]{1,0:T(8,128)(2,1)}) %all-gather.6.cloned.1.call-update) | async-done | bytes 4194320 | tf_op jit(solution)/shard_map/all_gather | solution.py:64
  85.6 6.4 %copy.24 = bf16[256,8192]{1,0:T(8,128)(2,1)} copy(bf16[256,8192]{0,1:T(8,128)(2,1)} %bitcast.155) | data formatting | bytes 8388608 | tf_op jit(solution)/shard_map/dot_general | solution.py:67
  92.0 7.1 %all-gather.4.cloned.1.call-done = bf16[1,2,128,8192]{3,2,1,0:T(8,128)(2,1)} async-done(((bf16[1,2,128,4096]{3,2,1,0:T(8,128)(2,1)}), bf16[1,2,128,8192]{3,2,1,0:T(8,128)(2,1)}) %all-gather.4.cloned.1.call-update) | async-done | bytes 4194320 | tf_op jit(solution)/shard_map/all_gather | solution.py:60
  99.1 4.7 %fusion.10 = f32[2,128,2,128]{1,3,2,0:T(8,128)S(1)} fusion(bf16[2,128,8192,1]{2,1,0,3:T(8,128)(2,1)} %bitcast.156, bf16[1,2,128,8192]{3,2,1,0:T(8,128)(2,1)} %all-gather.4.cloned.1.call-done), kind=kOutput, calls=%fused_computation.12 | convolution fusion | flops 1073741824 | bytes 8650752 | tf_op jit(solution)/shard_map/dot_general | solution.py:67
  103.9 0.4 fusion.68
  104.3 1.3 fusion.69
  105.6 70.2 %all-gather.8.cloned.1.call-done = bf16[8192,256]{1,0:T(8,128)(2,1)} async-done(((bf16[1024,256]{1,0:T(8,128)(2,1)}), bf16[8192,256]{1,0:T(8,128)(2,1)}) %all-gather.8.cloned.1.call-update) | async-done | bytes 4194320 | tf_op jit(solution)/shard_map/all_gather | solution.py:65
  175.9 5.3 %convolution_convert_fusion = bf16[256,256]{0,1:T(8,128)(2,1)S(1)} fusion(bf16[256,8192]{1,0:T(8,128)(2,1)} %bitcast.154, bf16[8192,256]{1,0:T(8,128)(2,1)} %all-gather.8.cloned.1.call-done), kind=kOutput, calls=%fused_computation.40 | convolution fusion | flops 1073807360 | bytes 8519680 | tf_op jit(solution)/shard_map/dot_general | solution.py:68
  181.4 4.9 %fusion.2 = f32[128,2,8]{0,2,1:T(8,128)S(1)} fusion(f32[2,1024,128,8]{2,1,3,0:T(8,128)} %get-tuple-element.28, f32[128,2,8]{0,2,1:T(8,128)S(1)} %get-tuple-element.17), kind=kLoop, calls=%fused_computation.6 | loop fusion | flops 6289408 | bytes 8404992 | tf_op jit(solution)/shard_map/reduce_sum | solution.py:38
  186.4 1.7 fusion.38
  188.1 0.3 fusion.45
  188.8 4.8 %fusion.4 = f32[128,2,8]{0,2,1:T(8,128)S(1)} fusion(f32[2,1024,128,8]{2,1,3,0:T(8,128)} %get-tuple-element.24, f32[128,2,8]{0,2,1:T(8,128)S(1)} %get-tuple-element.20), kind=kLoop, calls=%fused_computation.8 | loop fusion | flops 6289408 | bytes 8404992 | tf_op jit(solution)/shard_map/reduce_sum | solution.py:38
  193.6 5.0 %fusion.41 = f32[128,2,8,128]{0,3,2,1:T(8,128)S(1)} fusion(bf16[1024,2,128,1]{0,2,3,1:T(8,128)(2,1)S(1)} %bitcast.151, f32[2,1024,128,8]{2,1,3,0:T(8,128)} %get-tuple-element.24, f32[128,2,8]{0,2,1:T(8,128)S(1)} %get-tuple-element.20, f32[128,2,8]{0,2,1:T(8,128)S(1)} %get-tuple-element.8, f32[128,2,8]{0,2,1:T(8,128)S(1)} %get-tuple-element.18), kind=kOutput, calls=%fused_computation.37 | convolution fusion | flops 543686656 | bytes 9986048 | tf_op jit(solution)/shard_map/rkgl,lkd->rkgd/dot_general | solution.py:39
  198.6 0.3 fusion.44
  199.2 1.1 maximum_bitcast_fusion
  (27 shorter events, 1.9 us)
Async XLA Ops:
  6.5 79.1 %all-gather.6.cloned.1.call-start = ((), (), s32[]{:S(2)}) async-start(), calls=%async_computation.1 | async-start | bytes 4718592 | tf_op jit(solution)/shard_map/all_gather | solution.py:64
  7.3 91.9 %all-gather.4.cloned.1.call-start = ((), (), s32[]{:S(2)}) async-start(), calls=%async_computation | async-start | bytes 6291456 | tf_op jit(solution)/shard_map/all_gather | solution.py:60
  8.0 167.8 %all-gather.8.cloned.1.call-start = ((), (), s32[]{:S(2)}) async-start(), calls=%async_computation.2 | async-start | bytes 4718592 | tf_op jit(solution)/shard_map/all_gather | solution.py:65
  105.6 75.6 %copy-start = (f32[128,2,8,128]{0,3,2,1:T(8,128)S(1)}, f32[128,2,8,128]{0,3,2,1:T(8,128)}, u32[]{:S(2)}) copy-start(f32[128,2,8,128]{0,3,2,1:T(8,128)} %get-tuple-element.30) | copy-start | bytes 3145732
  175.9 10.5 %slice-start = ((s8[8388608]{0:T(1024)(128)(4,1)}), s8[4194304]{0:T(1024)(128)(4,1)S(1)}, s32[]{:S(2)}) async-start(s8[8388608]{0:T(1024)(128)(4,1)} %bitcast.144), calls=%async_computation.3 | async-start | bytes 8388608
  181.2 5.1 %slice-start.1 = ((s8[8388608]{0:T(1024)(128)(4,1)}), s8[4194304]{0:T(1024)(128)(4,1)S(1)}, s32[]{:S(2)}) async-start(s8[8388608]{0:T(1024)(128)(4,1)} %bitcast.144), calls=%async_computation.4 | async-start | bytes 8388608
Sparse Core Ops, SparseCore 0:
  9.5 76.0 all-gather.5
  87.2 11.9 all-gather.3
  101.3 74.5 all-gather.7
where the time goes:
time: 207 us
  waiting for transfers between devices  122 us (59%)
  matrix products  28.2 us (14%)
  blocking collectives  21.6 us (10%)
  between operations  14 us (7%)
  other arithmetic  11.4 us (6%)
  local copies, waits for them, and re-layouts  10.1 us (5%)
    all_gather x1, waiting for transfers between devices, on_device(): lax.all_gather(value_weight, ('fsdp', 'resp'), axis=0, tiled=True)  70.2 us
    all_gather x1, waiting for transfers between devices, on_device(): lax.all_gather(key_weight, ('fsdp', 'resp'), axis=0, tiled=True)  42.1 us
    all_gather x1, blocking collectives, on_device(): lax.all_gather(prompt_keys, 'resp', axis=1, tiled=True)  11.4 us
    dot_general x4, matrix products, absorb(): jnp.einsum('rkgd,lkd->rkgl', queried, cache_keys, preferred_element_type=...  10.7 us
    all_gather x1, blocking collectives, on_device(): lax.all_gather(prompt_values, 'resp', axis=1, tiled=True)  10.2 us
    reduce_sum x4, other arithmetic, absorb(): row_total = row_total * shrink + jnp.sum(weights, axis=-1)  9.98 us
    dot_general x4, matrix products, absorb(): jnp.einsum('rkgl,lkd->rkgd', weights.astype(jnp.bfloat16), cache_values,...  7.38 us
    all_gather x1, waiting for transfers between devices, on_device(): gathered = lax.all_gather(hidden, 'tp', axis=3, tiled=True)  7.09 us
  transfers between devices with their start and end apart: 3, of which 3 were waited for; matrix products, arithmetic and copies ran while one was open for 12% of the time, Pallas kernels for 0%

commit v1 on v0

v1 whole, which is shorter than its diff:
```python
import functools
import math

import jax
import jax.numpy as jnp
from jax import lax
from jax.experimental import pallas as pl
from jax.experimental.pallas import tpu as pltpu
from jax.sharding import PartitionSpec as P

HD = 128
PLEN = 1024
LOG2E = 1.4426950408889634
MIB = 1 << 20


def dot_nt(a, b):
    return lax.dot_general(a, b, (((1,), (1,)), ((), ())), preferred_element_type=jnp.float32)


def dot_nn(a, b):
    return lax.dot_general(a, b, (((1,), (0,)), ((), ())), preferred_element_type=jnp.float32)


def stacked_heads(ref, first, count):
    return jnp.concatenate(
        [ref[:, (first + n) * HD : (first + n + 1) * HD] for n in range(count)], axis=0
    )


def prompt_kernel(sources, group_size, factor, q_ref, *refs):
    keys = refs[:sources]
    values = refs[sources : 2 * sources]
    acc_ref, stat_ref = refs[2 * sources :]
    tokens = q_ref.shape[0]
    wide = [
        jnp.concatenate([v[...], jnp.ones(v.shape, v.dtype)], axis=1) for v in values
    ]
    lane = lax.broadcasted_iota(jnp.int32, (tokens, HD), 1)
    stats = jnp.zeros((tokens, HD), jnp.float32)
    pair = 2 if group_size % 2 == 0 else 1
    for first in range(0, group_size, pair):
        q = stacked_heads(q_ref, first, pair)
        scores = [dot_nt(q, k[...]) for k in keys]
        top = functools.reduce(
            jnp.maximum, [jnp.max(s, axis=1, keepdims=True) for s in scores]
        )
        out = None
        for s, v in zip(scores, wide):
            probs = jnp.exp2((s - top) * factor).astype(jnp.bfloat16)
            part = dot_nn(probs, v)
            out = part if out is None else out + part
        for n in range(pair):
            rows = slice(n * tokens, (n + 1) * tokens)
            head = first + n
            acc_ref[:, head * HD : (head + 1) * HD] = out[rows, :HD]
            stats = jnp.where(lane == head, top[rows], stats)
            stats = jnp.where(lane == group_size + head, out[rows, HD:], stats)
    stat_ref[...] = stats


def prompt_attention(slot, head, tokens, group_size, queries, keys, values):
    width = group_size * HD
    count = len(keys)
    length = keys[0].shape[0]
    spec_q = pl.BlockSpec((tokens, width), lambda _: (slot, head))
    spec_c = pl.BlockSpec((length, HD), lambda _: (0, head))
    work = tokens * group_size * length * count
    return pl.pallas_call(
        functools.partial(prompt_kernel, count, group_size, HD**-0.5 * LOG2E),
        grid=(1,),
        in_specs=[spec_q] + [spec_c] * (2 * count),
        out_specs=[
            pl.BlockSpec((tokens, width), lambda _: (0, 0)),
            pl.BlockSpec((tokens, HD), lambda _: (0, 0)),
        ],
        out_shape=[
            jax.ShapeDtypeStruct((tokens, width), jnp.float32),
            jax.ShapeDtypeStruct((tokens, HD), jnp.float32),
        ],
        compiler_params=pltpu.CompilerParams(vmem_limit_bytes=24 * MIB),
        cost_estimate=pl.CostEstimate(
            flops=6 * work * HD, bytes_accessed=2 * MIB, transcendentals=work
        ),
        name="prompt_attention",
    )(queries, *keys, *values)


def project(meta, near, far, pieces, start, dtype):
    rows = near.shape[1]
    columns = pieces[0][0].shape[1]
    vmem = pl.BlockSpec(memory_space=pltpu.VMEM)
    operands = [near, far]
    for parts in pieces:
        operands.extend(parts)
    if start is not None:
        operands.append(start)
    halves = [len(parts) == 2 for parts in pieces]

    def body(meta_ref, near_ref, far_ref, *refs):
        project_kernel_body(halves, start is not None, meta_ref, near_ref, far_ref, refs)

    return pl.pallas_call(
        body,
        in_specs=[pl.BlockSpec(memory_space=pltpu.SMEM)] + [vmem] * len(operands),
        out_specs=vmem,
        out_shape=jax.ShapeDtypeStruct((rows, columns), dtype),
        compiler_params=pltpu.CompilerParams(vmem_limit_bytes=24 * MIB),
        cost_estimate=pl.CostEstimate(
            flops=2 * rows * columns * near.shape[2] * len(pieces),
            bytes_accessed=2 * MIB,
            transcendentals=0,
        ),
        name="project",
    )(meta, *operands)


def project_kernel_body(halves, started, meta_ref, near_ref, far_ref, refs):
    refs = list(refs)
    out_ref = refs.pop()
    total = refs.pop()[...] if started else None
    group = meta_ref[0]
    for n, split in enumerate(halves):
        place = meta_ref[1 + 2 * n]
        near = meta_ref[2 + 2 * n] == 1
        features = jnp.where(near, near_ref[place], far_ref[place])
        if split:
            mine, other = refs.pop(0)[...], refs.pop(0)[...]
            weight = jnp.concatenate(
                [jnp.where(group == 0, mine, other), jnp.where(group == 0, other, mine)], axis=0
            )
        else:
            weight = refs.pop(0)[...]
        part = dot_nn(features, weight)
        total = part if total is None else total + part
    out_ref[...] = total.astype(out_ref.dtype)


def own_kernel(received, kv_heads, group_size, factor, meta_ref, *refs):
    refs = list(refs)
    q_ref, cos_ref, sin_ref = refs[:3]
    key_refs = refs[3 : 4 + received]
    value_refs = refs[4 + received : 5 + 2 * received]
    state = refs[5 + 2 * received : -1]
    out_ref = refs[-1]
    tokens = cos_ref.shape[0]
    slots = q_ref.shape[0] // tokens
    row = lax.broadcasted_iota(jnp.int32, (tokens, tokens), 0)
    column = lax.broadcasted_iota(jnp.int32, (tokens, tokens), 1)
    causal = row >= column
    pair = 2 if group_size % 2 == 0 else 1
    causal_rows = jnp.concatenate([causal] * pair, axis=0) if pair > 1 else causal
    for slot in range(slots):
        live = slot < meta_ref[0]
        rows_of = slice(slot * tokens, (slot + 1) * tokens)
        for head in range(kv_heads):
            lanes = slice(head * HD, (head + 1) * HD)
            key = key_refs[0][rows_of, lanes].astype(jnp.float32)
            for ref in key_refs[1:]:
                key = key + ref[rows_of, lanes].astype(jnp.float32)
            key = key * cos_ref[...] + pltpu.roll(key, HD // 2, 1) * sin_ref[...]
            key = key.astype(jnp.bfloat16)
            value = value_refs[0][rows_of, lanes].astype(jnp.float32)
            for ref in value_refs[1:]:
                value = value + ref[rows_of, lanes].astype(jnp.float32)
            value = value.astype(jnp.bfloat16)
            wide = jnp.concatenate([value, jnp.ones(value.shape, value.dtype)], axis=1)
            acc_ref, stat_ref = state[2 * (slot * kv_heads + head) :][:2]
            for first in range(0, group_size, pair):
                base = head * group_size + first
                q = jnp.concatenate(
                    [q_ref[rows_of, (base + n) * HD : (base + n + 1) * HD] for n in range(pair)],
                    axis=0,
                )
                scores = jnp.where(causal_rows, dot_nt(q, key), -1e30)
                old_top = jnp.concatenate(
                    [stat_ref[:, first + n : first + n + 1] for n in range(pair)], axis=0
                )
                old_total = jnp.concatenate(
                    [
                        stat_ref[:, group_size + first + n : group_size + first + n + 1]
                        for n in range(pair)
                    ],
                    axis=0,
                )
                top = jnp.maximum(old_top, jnp.max(scores, axis=1, keepdims=True))
                probs = jnp.exp2((scores - top) * factor).astype(jnp.bfloat16)
                shrink = jnp.exp2((old_top - top) * factor)
                out = dot_nn(probs, wide)
                old = stacked_heads(acc_ref, first, pair)
                mixed = old * shrink + out[:, :HD]
                total = old_total * shrink + out[:, HD:]
                result = jnp.where(live, mixed / total, 0.0).astype(out_ref.dtype)
                for n in range(pair):
                    out_ref[rows_of, (base + n) * HD : (base + n + 1) * HD] = result[
                        n * tokens : (n + 1) * tokens
                    ]


def own_attention(meta, queries, cosine, sine, key_parts, value_parts, states, group_size):
    kv_heads = key_parts[0].shape[1] // HD
    vmem = pl.BlockSpec(memory_space=pltpu.VMEM)
    operands = [queries, cosine, sine, *key_parts, *value_parts]
    for acc, stats in states:
        operands.extend((acc, stats))

    def body(meta_ref, *refs):
        own_kernel(
            len(key_parts) - 1, kv_heads, group_size, HD**-0.5 * LOG2E, meta_ref, *refs
        )

    work = queries.shape[0] * queries.shape[1]
    return pl.pallas_call(
        body,
        in_specs=[pl.BlockSpec(memory_space=pltpu.SMEM)] + [vmem] * len(operands),
        out_specs=vmem,
        out_shape=jax.ShapeDtypeStruct(queries.shape, queries.dtype),
        compiler_params=pltpu.CompilerParams(vmem_limit_bytes=24 * MIB),
        cost_estimate=pl.CostEstimate(
            flops=6 * work * HD, bytes_accessed=5 * MIB, transcendentals=work
        ),
        name="own_attention",
    )(meta, *operands)


def rotation_tables(extent, offset):
    half = HD // 2
    orders = jnp.arange(half, dtype=jnp.float32)
    inverse = jnp.exp(-(2.0 * orders / HD) * math.log(500000.0))
    places = (offset + jnp.arange(extent)).astype(jnp.float32)
    angles = places[:, None] * inverse[None, :]
    cosine, sine = jnp.cos(angles), jnp.sin(angles)
    return jnp.concatenate([cosine, cosine], axis=1), jnp.concatenate([-sine, sine], axis=1)


def pick(index, choices):
    chosen = choices[0]
    for n in range(1, len(choices)):
        chosen = jnp.where(index == n, choices[n], chosen)
    return chosen


def line_ring(size):
    return list(range(0, size, 2)) + list(range(1, size, 2))[::-1]


def on_device(sizes, hidden, queries, prompt_keys, prompt_values, key_weight, value_weight, counts):
    n_groups, n_fsdp, n_resp, n_tp = sizes
    _, slots, tokens, part_width = hidden.shape
    block, columns = key_weight.shape
    kv_heads = columns // HD
    group_size = queries.shape[3] // columns
    rows = slots * tokens
    per_core = n_fsdp // n_tp
    group = lax.axis_index("groups")
    fsdp = lax.axis_index("fsdp")
    resp = lax.axis_index("resp")
    core = lax.axis_index("tp")

    ring = line_ring(n_fsdp)
    hops = [(ring[n], ring[(n + 1) % n_fsdp]) for n in range(n_fsdp)]
    twins = [(n, n_groups - 1 - n) for n in range(n_groups)]
    cores = [(n, (n + 1) % n_tp) for n in range(n_tp)]
    half = block // n_groups

    def share(weight):
        return pick(group, [weight[n * half : (n + 1) * half] for n in range(n_groups)])

    def shift(number):
        return [(n, (n + number) % n_resp) for n in range(n_resp)]

    caches = [(prompt_keys[0], prompt_values[0])]
    for number in range(1, n_resp):
        caches.append(
            (
                lax.ppermute(prompt_keys[0], "resp", shift(number)),
                lax.ppermute(prompt_values[0], "resp", shift(number)),
            )
        )

    moving = [share(key_weight), share(value_weight)]
    pieces = [[(key_weight,)], [(value_weight,)]]
    for _ in range(n_fsdp - 1):
        for chunk in range(2):
            moving[chunk] = lax.ppermute(moving[chunk], "fsdp", hops)
            pieces[chunk].append((moving[chunk], lax.ppermute(moving[chunk], "groups", twins)))

    flat = hidden.reshape(rows, part_width)

    def features_of(target):
        return jnp.stack(
            [
                pick(
                    target,
                    [
                        flat[:, (n * n_resp + r) * block : (n * n_resp + r + 1) * block]
                        for r in range(n_resp)
                    ],
                )
                for n in range(per_core)
            ]
        )

    near = [features_of(resp)]
    for number in range(1, n_resp):
        near.append(
            lax.ppermute(features_of((resp + number) % n_resp), "resp", shift(number))
        )
    far = [lax.ppermute(x, "tp", cores) for x in near]

    ring_table = jnp.array(ring, jnp.int32)
    place_table = jnp.array([ring.index(n) for n in range(n_fsdp)], jnp.int32)
    place = place_table[fsdp]
    owners = [ring_table[(place + n_fsdp - n) % n_fsdp] for n in range(n_fsdp)]

    def meta_of(chosen):
        fields = [group.astype(jnp.int32)]
        for n in chosen:
            fields.append(owners[n] % per_core)
            fields.append((owners[n] // per_core == core).astype(jnp.int32))
        return jnp.stack(fields)

    early = list(range(n_fsdp - 1))
    late = [n_fsdp - 1]
    meta_early, meta_late = meta_of(early), meta_of(late)

    flat_queries = queries.reshape(rows, queries.shape[3])
    states = []
    for slot in range(slots):
        for head in range(kv_heads):
            states.append(
                prompt_attention(
                    slot,
                    head,
                    tokens,
                    group_size,
                    flat_queries,
                    [c[0] for c in caches],
                    [c[1] for c in caches],
                )
            )

    sums = []
    for chunk in range(2):
        started = [
            project(
                meta_early, near[n], far[n], [pieces[chunk][p] for p in early], None, jnp.float32
            )
            for n in range(n_resp)
        ]
        parts = []
        for number in range(1, n_resp):
            sent = project(
                meta_late,
                near[number],
                far[number],
                [pieces[chunk][p] for p in late],
                started[number],
                jnp.bfloat16,
            )
            parts.append(lax.ppermute(sent, "resp", shift(n_resp - number)))
        kept = project(
            meta_late,
            near[0],
            far[0],
            [pieces[chunk][p] for p in late],
            started[0],
            jnp.float32,
        )
        sums.append([kept, *parts])

    cosine, sine = rotation_tables(tokens, PLEN)
    live = (counts[0] - resp * slots).astype(jnp.int32)[None]
    out = own_attention(
        live, flat_queries, cosine, sine, sums[0], sums[1], states, group_size
    )
    return out.reshape(queries.shape)


def solution(mesh):
    placed = (
        P(("groups", "fsdp"), "resp", None, "tp"),
        P(("groups", "fsdp"), "resp", None, "tp"),
        P(("groups", "fsdp"), "resp", "tp"),
        P(("groups", "fsdp"), "resp", "tp"),
        P(("fsdp", "resp"), "tp"),
        P(("fsdp", "resp"), "tp"),
        P(("groups", "fsdp")),
    )
    sizes = tuple(mesh.shape[name] for name in ("groups", "fsdp", "resp", "tp"))
    return jax.shard_map(
        functools.partial(on_device, sizes),
        mesh=mesh,
        in_specs=placed,
        out_specs=P(("groups", "fsdp"), "resp", None, "tp"),
        check_vma=False,
    )
```

time: 207 us -> 110 us (0.53)
  waiting for transfers between devices: 122 us -> 22.3 us
  Pallas kernels: 0 us -> 30.5 us
  starting transfers between devices: 0.08 us -> 30.4 us
  matrix products: 28.2 us -> 0 us
  blocking collectives: 21.6 us -> 0 us
  other arithmetic: 11.4 us -> 6.12 us
  local copies, waits for them, and re-layouts: 10.1 us -> 6.64 us
    all_gather x3 -> x0, waiting for transfers between devices: 119 us -> none  [the longest x1 70.2 us: on_device(): lax.all_gather(value_weight, ('fsdp', 'resp'), axis=0, tiled=True)]
    pallas_call x0 -> x13, Pallas kernels: none -> 30.5 us  [the longest x8 13 us: project(): pl.pallas_call(body, in_specs=[pl.BlockSpec(memory_space=pltpu.SMEM)] + [...]
    ppermute x0 -> x19, starting transfers between devices: none -> 30.4 us  [the longest x6 15.3 us: on_device(): moving[chunk] = lax.ppermute(moving[chunk], 'fsdp', hops)]
    dot_general x10 -> x0, matrix products: 28.2 us -> none  [the longest x4 10.7 us: absorb(): jnp.einsum('rkgd,lkd->rkgl', queried, cache_keys, preferred_element_type=...]
    ppermute x0 -> x19, waiting for transfers between devices: none -> 22.3 us  [the longest x1 18.8 us: on_device(): lax.ppermute(features_of((resp + number) % n_resp), 'resp', shift(number))]
    all_gather x2 -> x0, blocking collectives: 21.6 us -> none  [the longest x1 11.4 us: on_device(): lax.all_gather(prompt_keys, 'resp', axis=1, tiled=True)]
    reduce_sum x4 -> x0, other arithmetic: 9.98 us -> none  [absorb(): row_total = row_total * shrink + jnp.sum(weights, axis=-1)]
    dot_general x1 -> x0, local copies, waits for them, and re-layouts: 6.42 us -> none  [on_device(): jnp.dot(token_rows, pieces[0], preferred_element_type=jnp.float32)]
  transfers between devices with their start and end apart: 3 -> 19, of which waited for: 3 -> 3; matrix products, arithmetic and copies ran while one was open for 12% -> 4% of each run, Pallas kernels for 0% -> 22%
where the time goes in v1:
time: 110 us; the launch traced here: 109 us
  Pallas kernels  30.5 us (28%)
  starting transfers between devices  30.4 us (28%)
  waiting for transfers between devices  22.3 us (20%)
  between operations  13.3 us (12%)
  local copies, waits for them, and re-layouts  6.64 us (6%)
  other arithmetic  6.12 us (6%)
    ppermute x1, waiting for transfers between devices, on_device(): lax.ppermute(features_of((resp + number) % n_resp), 'resp', shift(number))  18.8 us
    ppermute x6, starting transfers between devices, on_device(): moving[chunk] = lax.ppermute(moving[chunk], 'fsdp', hops)  15.3 us
    pallas_call x8, Pallas kernels, project(): pl.pallas_call(body, in_specs=[pl.BlockSpec(memory_space=pltpu.SMEM)] + [...  13 us
    pallas_call x4, Pallas kernels, prompt_attention(): pl.pallas_call(functools.partial(prompt_kernel, count, group_size, HD **...  10.9 us
    ppermute x6, starting transfers between devices, on_device(): lax.ppermute(moving[chunk], 'groups', twins)  7.24 us
    pallas_call x1, Pallas kernels, own_attention(): pl.pallas_call(body, in_specs=[pl.BlockSpec(memory_space=pltpu.SMEM)] + [...  6.55 us
    unnamed x36, local copies, waits for them, and re-layouts  5.3 us
    another operation x3, other arithmetic, features_of(): jnp.stack([pick(target, [flat[:, (n * n_resp + r) * block:(n * n_resp + r...  4.02 us
  transfers between devices with their start and end apart: 19, of which 3 were waited for; matrix products, arithmetic and copies ran while one was open for 4% of the time, Pallas kernels for 22%

profile of v1, /device:TPU:0, one launch (start us, length us, event | category | flops | bytes accessed | tf_op | source)
XLA Modules:
  0.0 109.3 jit_solution(17863631187642993954)
XLA Ops:
  0.0 2.6 %select_bitcast_fusion.1 = (bf16[1,256,1024]{2,1,0:T(8,128)(2,1)S(1)}, bf16[1,256,1024]{2,1,0:T(8,128)(2,1)}, bf16[1,256,1024]{2,1,0:T(8,128)(2,1)}, bf16[1,256,1024]{2,1,0:T(8,128)(2,1)S(1)}) fusion(pred[]{:T(512)S(6)} %eq.40, bf16[256,4096]{1,0:T(8,128)(2,1)} %bitcast.38, pred[]{:T(512)S(6)} %eq.35), kind=kLoop, calls=%fused_computation.3 | loop fusion | flops 1048576 | bytes 4194306 | tf_op jit(solution)/shard_map/stack | solution.py:291
  2.8 3.0 %collective-permute-start.7 = (bf16[2,256,1024]{2,1,0:T(8,128)(2,1)S(1)}, bf16[2,256,1024]{2,1,0:T(8,128)(2,1)S(1)}, u32[]{:S(2)}, u32[]{:S(2)}) collective-permute-start(bf16[2,256,1024]{2,1,0:T(8,128)(2,1)S(1)} %pad_maximum_fusion.1), channel_id=1, source_target_pairs={{0,2},{2,0},{1,3},{3,1},{4,6},{6,4},{5,7},{7,5},{8,10},{10,8},{9,1... | collective-permute-start | bytes 3145736 | tf_op jit(solution)/shard_map/ppermute | solution.py:307
  5.8 2.6 %collective-permute-start.10 = (bf16[512,256]{1,0:T(8,128)(2,1)S(1)}, bf16[512,256]{1,0:T(8,128)(2,1)S(1)}, u32[]{:S(2)}, u32[]{:S(2)}) collective-permute-start(bf16[512,256]{1,0:T(8,128)(2,1)S(1)} %slice_select_fusion), channel_id=1, source_target_pairs={{0,8},{8,12},{12,4},{4,0},{1,9},{9,13},{13,5},{5,1},{2,10},{10,14}... | collective-permute-start | bytes 786440 | tf_op jit(solution)/shard_map/ppermute | solution.py:285
  8.5 1.6 %collective-permute-start.1 = (bf16[512,256]{1,0:T(8,128)(2,1)S(1)}, bf16[512,256]{1,0:T(8,128)(2,1)S(1)}, u32[]{:S(2)}, u32[]{:S(2)}) collective-permute-start(bf16[512,256]{1,0:T(8,128)(2,1)S(1)} %slice_select_fusion.1), channel_id=1, source_target_pairs={{0,8},{8,12},{12,4},{4,0},{1,9},{9,13},{13,5},{5,1},{2,10},{10,14}... | collective-permute-start | bytes 786440 | tf_op jit(solution)/shard_map/ppermute | solution.py:285
  11.0 18.8 %collective-permute-done.7.near_ref = bf16[2,256,1024]{2,1,0:T(8,128)(2,1)S(1)} collective-permute-done((bf16[2,256,1024]{2,1,0:T(8,128)(2,1)S(1)}, bf16[2,256,1024]{2,1,0:T(8,128)(2,1)S(1)}, u32[]{:S(2)}, u32[]{:S(2)}) %collective-permute-start.7) | collective-permute-done | bytes 1048608 | tf_op jit(solution)/shard_map/ppermute | solution.py:307
  29.8 2.1 %collective-permute-start.18 = (bf16[512,256]{1,0:T(8,128)(2,1)}, bf16[512,256]{1,0:T(8,128)(2,1)S(1)}, u32[]{:S(2)}, u32[]{:S(2)}) collective-permute-start(bf16[512,256]{1,0:T(8,128)(2,1)} %bitcast.26.refs_2_), channel_id=1, source_target_pairs={{0,2},{2,0},{1,3},{3,1},{4,6},{6,4},{5,7},{7,5},{8,10},{10,8},{9,1... | collective-permute-start | bytes 786440 | tf_op jit(solution)/shard_map/ppermute | solution.py:277
  31.8 2.6 %collective-permute-start.11 = (bf16[512,256]{1,0:T(8,128)(2,1)S(1)}, bf16[512,256]{1,0:T(8,128)(2,1)}, u32[]{:S(2)}, u32[]{:S(2)}) collective-permute-start(bf16[512,256]{1,0:T(8,128)(2,1)S(1)} %collective-permute-done.10.refs_1_), channel_id=1, source_target_pairs={{0,8},{8,12},{12,4},{4,0},{1,9},{9,13},{13,5},{5,1},{2,10},{10,14}... | collective-permute-start | bytes 786440 | tf_op jit(solution)/shard_map/ppermute | solution.py:285
  36.6 2.6 %collective-permute-start.2 = (bf16[512,256]{1,0:T(8,128)(2,1)S(1)}, bf16[512,256]{1,0:T(8,128)(2,1)}, u32[]{:S(2)}, u32[]{:S(2)}) collective-permute-start(bf16[512,256]{1,0:T(8,128)(2,1)S(1)} %collective-permute-done.1.refs_1_), channel_id=1, source_target_pairs={{0,8},{8,12},{12,4},{4,0},{1,9},{9,13},{13,5},{5,1},{2,10},{10,14}... | collective-permute-start | bytes 786440 | tf_op jit(solution)/shard_map/ppermute | solution.py:285
  43.6 3.2 %collective-permute-start.12 = (bf16[512,256]{1,0:T(8,128)(2,1)}, bf16[512,256]{1,0:T(8,128)(2,1)}, u32[]{:S(2)}, u32[]{:S(2)}) collective-permute-start(bf16[512,256]{1,0:T(8,128)(2,1)} %collective-permute-done.11.refs_3_), channel_id=1, source_target_pairs={{0,8},{8,12},{12,4},{4,0},{1,9},{9,13},{13,5},{5,1},{2,10},{10,14}... | collective-permute-start | bytes 786440 | tf_op jit(solution)/shard_map/ppermute | solution.py:285
  46.8 2.7 %collective-permute-start.3 = (bf16[512,256]{1,0:T(8,128)(2,1)}, bf16[512,256]{1,0:T(8,128)(2,1)}, u32[]{:S(2)}, u32[]{:S(2)}) collective-permute-start(bf16[512,256]{1,0:T(8,128)(2,1)} %collective-permute-done.2.refs_3_), channel_id=1, source_target_pairs={{0,8},{8,12},{12,4},{4,0},{1,9},{9,13},{13,5},{5,1},{2,10},{10,14}... | collective-permute-start | bytes 786440 | tf_op jit(solution)/shard_map/ppermute | solution.py:285
  65.9 1.9 %collective-permute-start.5 = (bf16[512,256]{1,0:T(8,128)(2,1)S(1)}, bf16[512,256]{1,0:T(8,128)(2,1)S(1)}, u32[]{:S(2)}, u32[]{:S(2)}) collective-permute-start(bf16[512,256]{1,0:T(8,128)(2,1)S(1)} %collective-permute-done.1.refs_1_), channel_id=1, source_target_pairs={{0,16},{16,0},{1,17},{17,1},{2,18},{18,2},{3,19},{19,3},{4,20},{20... | collective-permute-start | bytes 786440 | tf_op jit(solution)/shard_map/ppermute | solution.py:286
  68.0 1.9 %collective-permute-start.13 = (bf16[512,256]{1,0:T(8,128)(2,1)}, bf16[512,256]{1,0:T(8,128)(2,1)S(1)}, u32[]{:S(2)}, u32[]{:S(2)}) collective-permute-start(bf16[512,256]{1,0:T(8,128)(2,1)} %collective-permute-done.12.refs_0_), channel_id=1, source_target_pairs={{0,16},{16,0},{1,17},{17,1},{2,18},{18,2},{3,19},{19,3},{4,20},{20... | collective-permute-start | bytes 786440 | tf_op jit(solution)/shard_map/ppermute | solution.py:286
  73.2 2.7 %prompt_attention.4 = (f32[128,1024]{1,0:T(8,128)S(1)}, f32[128,128]{1,0:T(8,128)S(1)}) custom-call(bf16[256,2048]{1,0:T(8,128)(2,1)S(1)} %bitcast.33, bf16[512,256]{1,0:T(8,128)(2,1)} %bitcast.25.refs_0_, bf16[512,256]{1,0:T(8,128)(2,1)S(1)} %copy-done.11, bf16[512,256]{1,0:T(8,128)(2,1)} %bitcast.26.refs_2_, bf16[512,256]{1,0:T(8,128)(2,1)S(1)} %copy-done.14), custom_call_target="tpu_custom_call" | custom-call | flops 805306368 | bytes 2097152 | tf_op jit(solution)/shard_map/prompt_attention/pallas_call | solution.py:69
  75.9 2.7 %prompt_attention.5 = (f32[128,1024]{1,0:T(8,128)S(1)}, f32[128,128]{1,0:T(8,128)S(1)}) custom-call(bf16[256,2048]{1,0:T(8,128)(2,1)S(1)} %bitcast.34, bf16[512,256]{1,0:T(8,128)(2,1)} %bitcast.25.refs_0_, bf16[512,256]{1,0:T(8,128)(2,1)S(1)} %copy-done.12, bf16[512,256]{1,0:T(8,128)(2,1)} %bitcast.26.refs_2_, bf16[512,256]{1,0:T(8,128)(2,1)S(1)} %copy-done.15), custom_call_target="tpu_custom_call" | custom-call | flops 805306368 | bytes 2097152 | tf_op jit(solution)/shard_map/prompt_attention/pallas_call | solution.py:69
  78.7 2.8 %prompt_attention.6 = (f32[128,1024]{1,0:T(8,128)S(1)}, f32[128,128]{1,0:T(8,128)S(1)}) custom-call(bf16[256,2048]{1,0:T(8,128)(2,1)S(1)} %bitcast.35, bf16[512,256]{1,0:T(8,128)(2,1)} %bitcast.25.refs_0_, bf16[512,256]{1,0:T(8,128)(2,1)S(1)} %copy-done.12, bf16[512,256]{1,0:T(8,128)(2,1)} %bitcast.26.refs_2_, bf16[512,256]{1,0:T(8,128)(2,1)S(1)} %copy-done.15), custom_call_target="tpu_custom_call" | custom-call | flops 805306368 | bytes 2097152 | tf_op jit(solution)/shard_map/prompt_attention/pallas_call | solution.py:69
  81.5 1.7 %project.14.refs_2_ = f32[256,256]{1,0:T(8,128)S(1)} custom-call(s32[7]{0:T(128)S(1)} %stack.81.meta_ref, bf16[2,256,1024]{2,1,0:T(8,128)(2,1)S(1)} %collective-permute-done.7.near_ref, bf16[2,256,1024]{2,1,0:T(8,128)(2,1)S(1)} %collective-permute-done.8.far_ref, bf16[1024,256]{1,0:T(8,128)(2,1)S(1)} %copy-done.1, bf16[512,256]{1,0:T(8,128)(2,1)S(1)} %copy-done.5, ...), custom_call_target="tpu_custom_call" | custom-call | flops 402653184 | bytes 2097152 | tf_op jit(solution)/shard_map/project/pallas_call | solution.py:103
  83.2 3.3 %collective-permute-done.13.refs_1_ = bf16[512,256]{1,0:T(8,128)(2,1)S(1)} collective-permute-done((bf16[512,256]{1,0:T(8,128)(2,1)}, bf16[512,256]{1,0:T(8,128)(2,1)S(1)}, u32[]{:S(2)}, u32[]{:S(2)}) %collective-permute-start.13) | collective-permute-done | bytes 262176 | tf_op jit(solution)/shard_map/ppermute | solution.py:286
  88.3 1.6 %project.10.refs_2_ = f32[256,256]{1,0:T(8,128)S(1)} custom-call(s32[7]{0:T(128)S(1)} %stack.81.meta_ref, bf16[2,256,1024]{2,1,0:T(8,128)(2,1)S(1)} %collective-permute-done.7.near_ref, bf16[2,256,1024]{2,1,0:T(8,128)(2,1)S(1)} %collective-permute-done.8.far_ref, bf16[1024,256]{1,0:T(8,128)(2,1)S(1)} %copy-done.3, ...), custom_call_target="tpu_custom_call" | custom-call | flops 402653184 | bytes 2097152 | tf_op jit(solution)/shard_map/project/pallas_call | solution.py:103
  92.9 2.7 %prompt_attention.7 = (f32[128,1024]{1,0:T(8,128)S(1)}, f32[128,128]{1,0:T(8,128)S(1)}) custom-call(bf16[256,2048]{1,0:T(8,128)(2,1)S(1)} %bitcast.36, bf16[512,256]{1,0:T(8,128)(2,1)} %bitcast.25.refs_0_, bf16[512,256]{1,0:T(8,128)(2,1)S(1)} %copy-done.12, bf16[512,256]{1,0:T(8,128)(2,1)} %bitcast.26.refs_2_, bf16[512,256]{1,0:T(8,128)(2,1)S(1)} %copy-done.15), custom_call_target="tpu_custom_call" | custom-call | flops 805306368 | bytes 2097152 | tf_op jit(solution)/shard_map/prompt_attention/pallas_call | solution.py:69
  95.6 2.0 %project.12.refs_2_ = f32[256,256]{1,0:T(8,128)S(1)} custom-call(s32[7]{0:T(128)S(1)} %stack.81.meta_ref, bf16[2,256,1024]{2,1,0:T(8,128)(2,1)S(1)} %pad_maximum_fusion.near_ref, bf16[2,256,1024]{2,1,0:T(8,128)(2,1)} %collective-permute-done.far_ref, bf16[1024,256]{1,0:T(8,128)(2,1)S(1)} %copy-done.1, bf16[512,256]{1,0:T(8,128)(2,1)S(1)} %copy-done.5, ...), custom_call_target="tpu_custom_call" | custom-call | flops 402653184 | bytes 2097152 | tf_op jit(solution)/shard_map/project/pallas_call | solution.py:103
  97.6 1.6 %project.13.refs_5_ = f32[256,256]{1,0:T(8,128)S(1)} custom-call(s32[3]{0:T(128)S(1)} %pad_add_fusion.meta_ref, bf16[2,256,1024]{2,1,0:T(8,128)(2,1)S(1)} %pad_maximum_fusion.near_ref, bf16[2,256,1024]{2,1,0:T(8,128)(2,1)} %collective-permute-done.far_ref, bf16[512,256]{1,0:T(8,128)(2,1)} %collective-permute-done.12.refs_0_, ...), custom_call_target="tpu_custom_call" | custom-call | flops 134217728 | bytes 2097152 | tf_op jit(solution)/shard_map/project/pallas_call | solution.py:103
  99.2 1.9 %project.8.refs_2_ = f32[256,256]{1,0:T(8,128)S(1)} custom-call(s32[7]{0:T(128)S(1)} %stack.81.meta_ref, bf16[2,256,1024]{2,1,0:T(8,128)(2,1)S(1)} %pad_maximum_fusion.near_ref, bf16[2,256,1024]{2,1,0:T(8,128)(2,1)} %collective-permute-done.far_ref, bf16[1024,256]{1,0:T(8,128)(2,1)S(1)} %copy-done.3, bf16[512,256]{1,0:T(8,128)(2,1)S(1)} %collective-permute-done.1.refs_1_, ...), custom_call_target="tpu_custom_call" | custom-call | flops 402653184 | bytes 2097152 | tf_op jit(solution)/shard_map/project/pallas_call | solution.py:103
  101.2 1.6 %project.9.refs_3_ = f32[256,256]{1,0:T(8,128)S(1)} custom-call(s32[3]{0:T(128)S(1)} %pad_add_fusion.meta_ref, bf16[2,256,1024]{2,1,0:T(8,128)(2,1)S(1)} %pad_maximum_fusion.near_ref, bf16[2,256,1024]{2,1,0:T(8,128)(2,1)} %collective-permute-done.far_ref, bf16[512,256]{1,0:T(8,128)(2,1)} %collective-permute-done.3.refs_0_, ...), custom_call_target="tpu_custom_call" | custom-call | flops 134217728 | bytes 2097152 | tf_op jit(solution)/shard_map/project/pallas_call | solution.py:103
  102.8 6.5 %own_attention.1 = bf16[256,2048]{1,0:T(8,128)(2,1)} custom-call(s32[1]{0:T(128)} %bitcast.1.meta_ref, bf16[256,2048]{1,0:T(8,128)(2,1)S(1)} %bitcast.37, f32[128,128]{1,0:T(8,128)S(1)} %get-tuple-element.32.refs_1_, f32[128,128]{1,0:T(8,128)S(1)} %get-tuple-element.33.refs_2_, f32[256,256]{1,0:T(8,128)S(1)} %project.9.refs_3_, ...), custom_call_target="tpu_custom_call" | custom-call | flops 402653184 | bytes 5242880 | tf_op jit(solution)/shard_map/own_attention/pallas_call | solution.py:213
  (76 shorter events, 19.3 us)
Async XLA Ops:
  2.6 5.8 %copy-start.2 = (bf16[1024,256]{1,0:T(8,128)(2,1)S(1)}, bf16[1024,256]{1,0:T(8,128)(2,1)}, u32[]{:S(2)}) copy-start(bf16[1024,256]{1,0:T(8,128)(2,1)} %refs_0_.5) | copy-start | bytes 1572868
  2.7 47.7 %copy-start.17 = (s32[4]{0:T(128)S(1)}, s32[4]{0:T(128)}, u32[]{:S(2)}) copy-start(s32[4]{0:T(128)} %constant.129.clone) | copy-start | bytes 52
  2.7 50.9 %copy-start.16 = (s32[4]{0:T(128)S(1)}, s32[4]{0:T(128)}, u32[]{:S(2)}) copy-start(s32[4]{0:T(128)} %constant.128.clone) | copy-start | bytes 52
  2.8 27.0 %collective-permute-start.7 = (bf16[2,256,1024]{2,1,0:T(8,128)(2,1)S(1)}, bf16[2,256,1024]{2,1,0:T(8,128)(2,1)S(1)}, u32[]{:S(2)}, u32[]{:S(2)}) collective-permute-start(bf16[2,256,1024]{2,1,0:T(8,128)(2,1)S(1)} %pad_maximum_fusion.1), channel_id=1, source_target_pairs={{0,2},{2,0},{1,3},{3,1},{4,6},{6,4},{5,7},{7,5},{8,10},{10,8},{9,1... | collective-permute-start | bytes 3145736 | tf_op jit(solution)/shard_map/ppermute | solution.py:307
  5.8 26.0 %collective-permute-start.10 = (bf16[512,256]{1,0:T(8,128)(2,1)S(1)}, bf16[512,256]{1,0:T(8,128)(2,1)S(1)}, u32[]{:S(2)}, u32[]{:S(2)}) collective-permute-start(bf16[512,256]{1,0:T(8,128)(2,1)S(1)} %slice_select_fusion), channel_id=1, source_target_pairs={{0,8},{8,12},{12,4},{4,0},{1,9},{9,13},{13,5},{5,1},{2,10},{10,14}... | collective-permute-start | bytes 786440 | tf_op jit(solution)/shard_map/ppermute | solution.py:285
  8.5 25.9 %collective-permute-start.1 = (bf16[512,256]{1,0:T(8,128)(2,1)S(1)}, bf16[512,256]{1,0:T(8,128)(2,1)S(1)}, u32[]{:S(2)}, u32[]{:S(2)}) collective-permute-start(bf16[512,256]{1,0:T(8,128)(2,1)S(1)} %slice_select_fusion.1), channel_id=1, source_target_pairs={{0,8},{8,12},{12,4},{4,0},{1,9},{9,13},{13,5},{5,1},{2,10},{10,14}... | collective-permute-start | bytes 786440 | tf_op jit(solution)/shard_map/ppermute | solution.py:285
  10.1 25.8 %collective-permute-start.17 = (bf16[512,256]{1,0:T(8,128)(2,1)}, bf16[512,256]{1,0:T(8,128)(2,1)S(1)}, u32[]{:S(2)}, u32[]{:S(2)}) collective-permute-start(bf16[512,256]{1,0:T(8,128)(2,1)} %bitcast.25.refs_0_), channel_id=1, source_target_pairs={{0,2},{2,0},{1,3},{3,1},{4,6},{6,4},{5,7},{7,5},{8,10},{10,8},{9,1... | collective-permute-start | bytes 786440 | tf_op jit(solution)/shard_map/ppermute | solution.py:276
  29.8 40.1 %collective-permute-start.8 = (bf16[2,256,1024]{2,1,0:T(8,128)(2,1)S(1)}, bf16[2,256,1024]{2,1,0:T(8,128)(2,1)S(1)}, u32[]{:S(2)}, u32[]{:S(2)}) collective-permute-start(bf16[2,256,1024]{2,1,0:T(8,128)(2,1)S(1)} %collective-permute-done.7.near_ref), channel_id=1, source_target_pairs={{0,1},{1,0},{2,3},{3,2},{4,5},{5,4},{6,7},{7,6},{8,9},{9,8},{10,11... | collective-permute-start | bytes 3145736 | tf_op jit(solution)/shard_map/ppermute | solution.py:309
  29.8 10.8 %collective-permute-start.18 = (bf16[512,256]{1,0:T(8,128)(2,1)}, bf16[512,256]{1,0:T(8,128)(2,1)S(1)}, u32[]{:S(2)}, u32[]{:S(2)}) collective-permute-start(bf16[512,256]{1,0:T(8,128)(2,1)} %bitcast.26.refs_2_), channel_id=1, source_target_pairs={{0,2},{2,0},{1,3},{3,1},{4,6},{6,4},{5,7},{7,5},{8,10},{10,8},{9,1... | collective-permute-start | bytes 786440 | tf_op jit(solution)/shard_map/ppermute | solution.py:277
  31.8 15.0 %copy-start.4 = (bf16[512,256]{1,0:T(8,128)(2,1)}, bf16[512,256]{1,0:T(8,128)(2,1)S(1)}, u32[]{:S(2)}) copy-start(bf16[512,256]{1,0:T(8,128)(2,1)S(1)} %collective-permute-done.10.refs_1_) | copy-start | bytes 786436
  31.8 9.5 %collective-permute-start.11 = (bf16[512,256]{1,0:T(8,128)(2,1)S(1)}, bf16[512,256]{1,0:T(8,128)(2,1)}, u32[]{:S(2)}, u32[]{:S(2)}) collective-permute-start(bf16[512,256]{1,0:T(8,128)(2,1)S(1)} %collective-permute-done.10.refs_1_), channel_id=1, source_target_pairs={{0,8},{8,12},{12,4},{4,0},{1,9},{9,13},{13,5},{5,1},{2,10},{10,14}... | collective-permute-start | bytes 786440 | tf_op jit(solution)/shard_map/ppermute | solution.py:285
  34.4 8.5 %collective-permute-start.14 = (bf16[512,256]{1,0:T(8,128)(2,1)S(1)}, bf16[512,256]{1,0:T(8,128)(2,1)S(1)}, u32[]{:S(2)}, u32[]{:S(2)}) collective-permute-start(bf16[512,256]{1,0:T(8,128)(2,1)S(1)} %collective-permute-done.10.refs_1_), channel_id=1, source_target_pairs={{0,16},{16,0},{1,17},{17,1},{2,18},{18,2},{3,19},{19,3},{4,20},{20... | collective-permute-start | bytes 786440 | tf_op jit(solution)/shard_map/ppermute | solution.py:286
  36.6 10.1 %collective-permute-start.2 = (bf16[512,256]{1,0:T(8,128)(2,1)S(1)}, bf16[512,256]{1,0:T(8,128)(2,1)}, u32[]{:S(2)}, u32[]{:S(2)}) collective-permute-start(bf16[512,256]{1,0:T(8,128)(2,1)S(1)} %collective-permute-done.1.refs_1_), channel_id=1, source_target_pairs={{0,8},{8,12},{12,4},{4,0},{1,9},{9,13},{13,5},{5,1},{2,10},{10,14}... | collective-permute-start | bytes 786440 | tf_op jit(solution)/shard_map/ppermute | solution.py:285
  41.3 54.4 %collective-permute-start = (bf16[2,256,1024]{2,1,0:T(8,128)(2,1)S(1)}, bf16[2,256,1024]{2,1,0:T(8,128)(2,1)}, u32[]{:S(2)}, u32[]{:S(2)}) collective-permute-start(bf16[2,256,1024]{2,1,0:T(8,128)(2,1)S(1)} %pad_maximum_fusion.near_ref), channel_id=1, source_target_pairs={{0,1},{1,0},{2,3},{3,2},{4,5},{5,4},{6,7},{7,6},{8,9},{9,8},{10,11... | collective-permute-start | bytes 3145736 | tf_op jit(solution)/shard_map/ppermute | solution.py:309
  41.3 24.6 %collective-permute-start.15 = (bf16[512,256]{1,0:T(8,128)(2,1)}, bf16[512,256]{1,0:T(8,128)(2,1)}, u32[]{:S(2)}, u32[]{:S(2)}) collective-permute-start(bf16[512,256]{1,0:T(8,128)(2,1)} %collective-permute-done.11.refs_3_), channel_id=1, source_target_pairs={{0,16},{16,0},{1,17},{17,1},{2,18},{18,2},{3,19},{19,3},{4,20},{20... | collective-permute-start | bytes 786440 | tf_op jit(solution)/shard_map/ppermute | solution.py:286
  43.6 24.3 %collective-permute-start.12 = (bf16[512,256]{1,0:T(8,128)(2,1)}, bf16[512,256]{1,0:T(8,128)(2,1)}, u32[]{:S(2)}, u32[]{:S(2)}) collective-permute-start(bf16[512,256]{1,0:T(8,128)(2,1)} %collective-permute-done.11.refs_3_), channel_id=1, source_target_pairs={{0,8},{8,12},{12,4},{4,0},{1,9},{9,13},{13,5},{5,1},{2,10},{10,14}... | collective-permute-start | bytes 786440 | tf_op jit(solution)/shard_map/ppermute | solution.py:285
  46.8 21.2 %collective-permute-start.3 = (bf16[512,256]{1,0:T(8,128)(2,1)}, bf16[512,256]{1,0:T(8,128)(2,1)}, u32[]{:S(2)}, u32[]{:S(2)}) collective-permute-start(bf16[512,256]{1,0:T(8,128)(2,1)} %collective-permute-done.2.refs_3_), channel_id=1, source_target_pairs={{0,8},{8,12},{12,4},{4,0},{1,9},{9,13},{13,5},{5,1},{2,10},{10,14}... | collective-permute-start | bytes 786440 | tf_op jit(solution)/shard_map/ppermute | solution.py:285
  64.8 11.1 %copy-start.12 = (bf16[512,256]{1,0:T(8,128)(2,1)S(1)}, bf16[512,256]{1,0:T(8,128)(2,1)}, u32[]{:S(2)}) copy-start(bf16[512,256]{1,0:T(8,128)(2,1)} %copy-done.10) | copy-start | bytes 786436
  65.9 22.4 %collective-permute-start.5 = (bf16[512,256]{1,0:T(8,128)(2,1)S(1)}, bf16[512,256]{1,0:T(8,128)(2,1)S(1)}, u32[]{:S(2)}, u32[]{:S(2)}) collective-permute-start(bf16[512,256]{1,0:T(8,128)(2,1)S(1)} %collective-permute-done.1.refs_1_), channel_id=1, source_target_pairs={{0,16},{16,0},{1,17},{17,1},{2,18},{18,2},{3,19},{19,3},{4,20},{20... | collective-permute-start | bytes 786440 | tf_op jit(solution)/shard_map/ppermute | solution.py:286
  67.8 20.5 %collective-permute-start.6 = (bf16[512,256]{1,0:T(8,128)(2,1)}, bf16[512,256]{1,0:T(8,128)(2,1)S(1)}, u32[]{:S(2)}, u32[]{:S(2)}) collective-permute-start(bf16[512,256]{1,0:T(8,128)(2,1)} %collective-permute-done.2.refs_3_), channel_id=1, source_target_pairs={{0,16},{16,0},{1,17},{17,1},{2,18},{18,2},{3,19},{19,3},{4,20},{20... | collective-permute-start | bytes 786440 | tf_op jit(solution)/shard_map/ppermute | solution.py:286
  68.0 18.4 %collective-permute-start.13 = (bf16[512,256]{1,0:T(8,128)(2,1)}, bf16[512,256]{1,0:T(8,128)(2,1)S(1)}, u32[]{:S(2)}, u32[]{:S(2)}) collective-permute-start(bf16[512,256]{1,0:T(8,128)(2,1)} %collective-permute-done.12.refs_0_), channel_id=1, source_target_pairs={{0,16},{16,0},{1,17},{17,1},{2,18},{18,2},{3,19},{19,3},{4,20},{20... | collective-permute-start | bytes 786440 | tf_op jit(solution)/shard_map/ppermute | solution.py:286
  69.9 20.3 %collective-permute-start.4 = (bf16[512,256]{1,0:T(8,128)(2,1)}, bf16[512,256]{1,0:T(8,128)(2,1)S(1)}, u32[]{:S(2)}, u32[]{:S(2)}) collective-permute-start(bf16[512,256]{1,0:T(8,128)(2,1)} %collective-permute-done.3.refs_0_), channel_id=1, source_target_pairs={{0,16},{16,0},{1,17},{17,1},{2,18},{18,2},{3,19},{19,3},{4,20},{20... | collective-permute-start | bytes 786440 | tf_op jit(solution)/shard_map/ppermute | solution.py:286
  87.7 15.0 %collective-permute-start.16 = (bf16[256,256]{1,0:T(8,128)(2,1)S(1)}, bf16[256,256]{1,0:T(8,128)(2,1)S(1)}, u32[]{:S(2)}, u32[]{:S(2)}) collective-permute-start(bf16[256,256]{1,0:T(8,128)(2,1)S(1)} %project.15), channel_id=1, source_target_pairs={{0,2},{2,0},{1,3},{3,1},{4,6},{6,4},{5,7},{7,5},{8,10},{10,8},{9,1... | collective-permute-start | bytes 393224 | tf_op jit(solution)/shard_map/ppermute | solution.py:361
  91.5 11.2 %collective-permute-start.9 = (bf16[256,256]{1,0:T(8,128)(2,1)S(1)}, bf16[256,256]{1,0:T(8,128)(2,1)S(1)}, u32[]{:S(2)}, u32[]{:S(2)}) collective-permute-start(bf16[256,256]{1,0:T(8,128)(2,1)S(1)} %project.11), channel_id=1, source_target_pairs={{0,2},{2,0},{1,3},{3,1},{4,6},{6,4},{5,7},{7,5},{8,10},{10,8},{9,1... | collective-permute-start | bytes 393224 | tf_op jit(solution)/shard_map/ppermute | solution.py:361
  (13 other events, 27.7 us)

commit v2 on v0

v2 whole, which is shorter than its diff:
```python
import functools
import math

import jax
import jax.numpy as jnp
from jax import lax
from jax.experimental import pallas as pl
from jax.experimental.pallas import tpu as pltpu
from jax.sharding import PartitionSpec as P

HD = 128
PLEN = 1024
LOG2E = 1.4426950408889634
FACTOR = HD**-0.5 * LOG2E
MIB = 1 << 20
VMEM = pl.BlockSpec(memory_space=pltpu.VMEM)
SMEM = pl.BlockSpec(memory_space=pltpu.SMEM)
ANYWHERE = pl.BlockSpec(memory_space=pl.ANY)
HBM = pl.BlockSpec(memory_space=pltpu.HBM)


def dot_nt(a, b):
    return lax.dot_general(a, b, (((1,), (1,)), ((), ())), preferred_element_type=jnp.float32)


def dot_nn(a, b):
    return lax.dot_general(a, b, (((1,), (0,)), ((), ())), preferred_element_type=jnp.float32)


def take_heads(ref, first, count):
    return jnp.concatenate(
        [ref[:, (first + n) * HD : (first + n + 1) * HD] for n in range(count)], axis=0
    )


def put_heads(ref, first, count, stacked):
    tokens = ref.shape[0]
    for n in range(count):
        ref[:, (first + n) * HD : (first + n + 1) * HD] = stacked[
            n * tokens : (n + 1) * tokens
        ].astype(ref.dtype)


def take_column(ref, first, count):
    return jnp.concatenate([ref[:, first + n : first + n + 1] for n in range(count)], axis=0)


def put_column(stats, lane, first, count, stacked):
    tokens = stats.shape[0]
    for n in range(count):
        stats = jnp.where(lane == first + n, stacked[n * tokens : (n + 1) * tokens], stats)
    return stats


def with_ones(values):
    return jnp.concatenate([values, jnp.ones(values.shape, values.dtype)], axis=1)


def pack(sizes, hidden, key_weight, value_weight, prompt_keys, prompt_values):
    n_groups, n_fsdp, n_resp, n_tp = sizes
    rows = hidden.shape[0]
    block, columns = key_weight.shape
    per_core = n_fsdp // n_tp
    half = block // n_groups
    length = prompt_keys.shape[0]
    sets = [(a, b) for a in range(n_groups) for b in range(n_resp)]

    if half % HD:

        def cut(target_group, target_resp):
            parts = []
            for n in range(per_core):
                start = (n * n_resp + target_resp) * block + target_group * half
                parts.append(lax.dynamic_slice_in_dim(hidden, start, half, axis=1))
            return jnp.concatenate(parts, axis=1)

        group, resp = lax.axis_index("groups"), lax.axis_index("resp")
        features = [cut((group + a) % n_groups, (resp + b) % n_resp) for a, b in sets]
        shares = [
            lax.dynamic_slice_in_dim(w, group * half, half, axis=0)
            for w in (key_weight, value_weight)
        ]
        return features, shares, jnp.concatenate([prompt_keys, prompt_values], axis=0)

    def body(hidden_ref, kw_ref, vw_ref, pk_ref, pv_ref, *refs):
        outs, sems = refs[:-1], refs[-1]
        group, resp = lax.axis_index("groups"), lax.axis_index("resp")
        moves = []
        rows_of = pl.ds(pl.multiple_of(group * half, half), half)
        moves.append((kw_ref.at[rows_of, :], outs[len(sets)]))
        moves.append((vw_ref.at[rows_of, :], outs[len(sets) + 1]))
        for (a, b), out in zip(sets, outs):
            target_group, target_resp = (group + a) % n_groups, (resp + b) % n_resp
            for n in range(per_core):
                start = (n * n_resp + target_resp) * block + target_group * half
                moves.append(
                    (
                        hidden_ref.at[:, pl.ds(pl.multiple_of(start, HD), half)],
                        out.at[:, pl.ds(n * half, half)],
                    )
                )
        moves.append((pk_ref, outs[-1].at[pl.ds(0, length), :]))
        moves.append((pv_ref, outs[-1].at[pl.ds(length, length), :]))
        copies = [
            pltpu.make_async_copy(source, target, sems.at[n])
            for n, (source, target) in enumerate(moves)
        ]
        for copy in copies:
            copy.start()
        for copy in copies:
            copy.wait()

    kind = hidden.dtype
    shapes = [jax.ShapeDtypeStruct((rows, per_core * half), kind)] * len(sets)
    shapes += [jax.ShapeDtypeStruct((half, columns), kind)] * 2
    shapes += [jax.ShapeDtypeStruct((2 * length, columns), kind)]
    outs = pl.pallas_call(
        body,
        in_specs=[HBM] * 5,
        out_specs=[ANYWHERE] * len(shapes),
        out_shape=shapes,
        scratch_shapes=[pltpu.SemaphoreType.DMA((4 + per_core * len(sets),))],
        cost_estimate=pl.CostEstimate(flops=0, bytes_accessed=6 * MIB, transcendentals=0),
        name="pack",
    )(hidden, key_weight, value_weight, prompt_keys, prompt_values)
    return outs[: len(sets)], list(outs[len(sets) : len(sets) + 2]), outs[-1]


def project(sets, weight, dtype):
    rows, depth = sets[0][0].shape
    columns = weight.shape[1]
    count = len(sets)

    def body(weight_ref, *refs):
        core = lax.axis_index("tp")
        first = pl.ds(pl.multiple_of(core * depth, depth), depth)
        second = pl.ds(pl.multiple_of((1 - core) * depth, depth), depth)
        near_weight, far_weight = weight_ref[first, :], weight_ref[second, :]
        for n in range(count):
            near_ref, far_ref = refs[2 * n], refs[2 * n + 1]
            out_ref = refs[2 * count + n]
            total = dot_nn(near_ref[...], near_weight) + dot_nn(far_ref[...], far_weight)
            out_ref[...] = total.astype(out_ref.dtype)

    return pl.pallas_call(
        body,
        in_specs=[VMEM] * (1 + 2 * count),
        out_specs=[VMEM] * count,
        out_shape=[jax.ShapeDtypeStruct((rows, columns), dtype)] * count,
        compiler_params=pltpu.CompilerParams(vmem_limit_bytes=24 * MIB),
        cost_estimate=pl.CostEstimate(
            flops=4 * rows * columns * depth * count, bytes_accessed=3 * MIB, transcendentals=0
        ),
        name="project",
    )(weight, *[x for pair in sets for x in pair])


def attend(slot, head, tokens, group_size, queries, keys, values, own=None, state=None):
    width = group_size * HD
    pair = 2 if group_size % 2 == 0 else 1
    count = len(keys)
    own_parts, tables = own if own is not None else ([], [])
    extra = len(own_parts)

    def body(q_ref, *refs):
        refs = list(refs)
        key_refs = [refs.pop(0) for _ in range(count)]
        value_refs = [refs.pop(0) for _ in range(count)]
        own_refs = [refs.pop(0) for _ in range(extra)]
        if extra:
            cos_ref, sin_ref = refs.pop(0), refs.pop(0)
        if state is not None:
            old_acc_ref, old_stat_ref = refs.pop(0), refs.pop(0)
        acc_ref, stat_ref = refs[:2]
        wide = [with_ones(v[...]) for v in value_refs]
        lane = lax.broadcasted_iota(jnp.int32, (tokens, HD), 1)
        stats = jnp.zeros((tokens, HD), jnp.float32)
        if extra:
            key = own_refs[0][...].astype(jnp.float32)
            for ref in own_refs[1:]:
                key = key + ref[...].astype(jnp.float32)
            key = key * cos_ref[...] + pltpu.roll(key, HD // 2, 1) * sin_ref[...]
            own_key = key.astype(jnp.bfloat16)
            ones = jnp.ones((tokens, HD), jnp.bfloat16)
            causal = lax.broadcasted_iota(jnp.int32, (tokens, tokens), 0) >= (
                lax.broadcasted_iota(jnp.int32, (tokens, tokens), 1)
            )
            causal = jnp.concatenate([causal] * pair, axis=0)
        for first in range(0, group_size, pair):
            q = take_heads(q_ref, first, pair)
            scores = [dot_nt(q, k[...]) for k in key_refs]
            if extra:
                scores.append(jnp.where(causal, dot_nt(q, own_key), -1e30))
            tops = [jnp.max(s, axis=1, keepdims=True) for s in scores]
            if state is not None:
                old_top = take_column(old_stat_ref, first, pair)
                tops.append(old_top)
            top = functools.reduce(jnp.maximum, tops)
            probs = [jnp.exp2((s - top) * FACTOR).astype(jnp.bfloat16) for s in scores]
            out = functools.reduce(jnp.add, [dot_nn(p, v) for p, v in zip(probs, wide)])
            mixed, total = out[:, :HD], out[:, HD:]
            if extra:
                total = total + dot_nn(probs[-1], ones)
                put_heads(refs[2], first, pair, probs[-1])
            if state is not None:
                shrink = jnp.exp2((old_top - top) * FACTOR)
                mixed = mixed + take_heads(old_acc_ref, first, pair) * shrink
                total = total + take_column(old_stat_ref, group_size + first, pair) * shrink
            if extra:
                inverse = 1.0 / total
                put_heads(acc_ref, first, pair, mixed * inverse)
                stats = put_column(stats, lane, first, pair, inverse)
            else:
                put_heads(acc_ref, first, pair, mixed)
                stats = put_column(stats, lane, first, pair, top)
                stats = put_column(stats, lane, group_size + first, pair, total)
        stat_ref[...] = stats

    length = keys[0].shape[0]
    spec_q = pl.BlockSpec((tokens, width), lambda _: (slot, head))
    spec_c = pl.BlockSpec((length, HD), lambda _: (0, head))
    spec_own = pl.BlockSpec((tokens, HD), lambda _: (slot, head))
    spec_table = pl.BlockSpec((tokens, HD), lambda _: (0, 0))
    spec_wide = pl.BlockSpec((tokens, width), lambda _: (0, 0))
    operands = [queries, *keys, *values, *own_parts, *tables]
    specs = [spec_q] + [spec_c] * (2 * count) + [spec_own] * extra + [spec_table] * len(tables)
    if state is not None:
        operands.extend(state)
        specs.extend([spec_wide, spec_table])
    out_specs = [spec_wide, spec_table]
    shapes = [
        jax.ShapeDtypeStruct((tokens, width), jnp.float32),
        jax.ShapeDtypeStruct((tokens, HD), jnp.float32),
    ]
    if extra:
        out_specs.append(spec_wide)
        shapes.append(jax.ShapeDtypeStruct((tokens, width), jnp.bfloat16))
    work = tokens * group_size * (length * count + (tokens if extra else 0))
    return pl.pallas_call(
        body,
        grid=(1,),
        in_specs=specs,
        out_specs=out_specs,
        out_shape=shapes,
        compiler_params=pltpu.CompilerParams(vmem_limit_bytes=24 * MIB),
        cost_estimate=pl.CostEstimate(
            flops=6 * work * HD, bytes_accessed=2 * MIB, transcendentals=work
        ),
        name="attend_rest" if extra else "attend_local",
    )(*operands)


def finish(live, value_parts, states, slots, group_size, shape, dtype):
    count = len(value_parts)
    rows, columns = value_parts[0].shape
    tokens = rows // slots
    kv_heads = columns // HD

    def body(live_ref, *refs):
        out_ref = refs[-1]
        total = value_refs_sum(refs[:count])
        values = total.astype(jnp.bfloat16)
        for slot in range(slots):
            alive = slot < live_ref[0]
            for head in range(kv_heads):
                acc_ref, stat_ref, probs_ref = refs[count + 3 * (slot * kv_heads + head) :][:3]
                value = values[slot * tokens : (slot + 1) * tokens, head * HD : (head + 1) * HD]
                for n in range(group_size):
                    lanes = slice(n * HD, (n + 1) * HD)
                    part = dot_nn(probs_ref[:, lanes], value) * stat_ref[:, n : n + 1]
                    result = jnp.where(alive, acc_ref[:, lanes] + part, 0.0)
                    start = (head * group_size + n) * HD
                    out_ref[slot * tokens : (slot + 1) * tokens, start : start + HD] = (
                        result.astype(out_ref.dtype)
                    )

    def value_refs_sum(refs):
        total = refs[0][...].astype(jnp.float32)
        for ref in refs[1:]:
            total = total + ref[...].astype(jnp.float32)
        return total

    operands = [*value_parts, *[x for state in states for x in state]]
    return pl.pallas_call(
        body,
        in_specs=[SMEM] + [VMEM] * len(operands),
        out_specs=VMEM,
        out_shape=jax.ShapeDtypeStruct(shape, dtype),
        compiler_params=pltpu.CompilerParams(vmem_limit_bytes=24 * MIB),
        cost_estimate=pl.CostEstimate(
            flops=2 * shape[0] * shape[1] * tokens, bytes_accessed=5 * MIB, transcendentals=0
        ),
        name="finish",
    )(live, *operands)


def rotation_tables(extent, offset):
    half = HD // 2
    orders = jnp.arange(half, dtype=jnp.float32)
    inverse = jnp.exp(-(2.0 * orders / HD) * math.log(500000.0))
    places = (offset + jnp.arange(extent)).astype(jnp.float32)
    angles = places[:, None] * inverse[None, :]
    cosine, sine = jnp.cos(angles), jnp.sin(angles)
    return jnp.concatenate([cosine, cosine], axis=1), jnp.concatenate([-sine, sine], axis=1)


def on_device(sizes, hidden, queries, prompt_keys, prompt_values, key_weight, value_weight, counts):
    n_groups, n_fsdp, n_resp, n_tp = sizes
    _, slots, tokens, part_width = hidden.shape
    columns = key_weight.shape[1]
    kv_heads = columns // HD
    group_size = queries.shape[3] // columns
    rows = slots * tokens
    length = prompt_keys.shape[1]
    sets = [(a, b) for a in range(n_groups) for b in range(n_resp)]
    plane = ("groups", "resp")
    cores = [(n, (n + 1) % n_tp) for n in range(n_tp)]

    def shift(a, b):
        return [
            (g * n_resp + r, (g + a) % n_groups * n_resp + (r + b) % n_resp)
            for g in range(n_groups)
            for r in range(n_resp)
        ]

    features, shares, cache = pack(
        sizes,
        hidden.reshape(rows, part_width),
        key_weight,
        value_weight,
        prompt_keys[0],
        prompt_values[0],
    )
    flat_queries = queries.reshape(rows, queries.shape[3])
    places = [(slot, head) for slot in range(slots) for head in range(kv_heads)]
    started = [
        attend(
            slot,
            head,
            tokens,
            group_size,
            flat_queries,
            [prompt_keys[0]],
            [prompt_values[0]],
        )
        for slot, head in places
    ]

    def after(value, *earlier):
        return lax.optimization_barrier((value, *earlier))[0]

    near = [features[0]]
    for (a, b), sent in zip(sets[1:], features[1:]):
        moved = lax.ppermute(sent, plane, shift(a, b))
        near.append(after(moved, started[-1][1]))
    far = [lax.ppermute(x, "tp", cores) for x in near]

    shares[1] = after(shares[1], started[0][1])
    gathered = [lax.all_gather(share, "fsdp", axis=0, tiled=True) for share in shares]

    held = after(cache, *near)
    others = [
        lax.ppermute(held, "resp", [(n, (n + b) % n_resp) for n in range(n_resp)])
        for b in range(1, n_resp)
    ]

    sums = []
    for weight in gathered:
        sent = project(list(zip(near[1:], far[1:])), weight, jnp.bfloat16)
        parts = [
            lax.ppermute(x, plane, shift(n_groups - a, n_resp - b))
            for (a, b), x in zip(sets[1:], sent)
        ]
        kept = project([(near[0], far[0])], weight, jnp.float32)
        sums.append([*kept, *parts])

    tables = rotation_tables(tokens, PLEN)
    states = [
        attend(
            slot,
            head,
            tokens,
            group_size,
            flat_queries,
            [x[:length] for x in others],
            [x[length:] for x in others],
            (sums[0], tables),
            state,
        )
        for (slot, head), state in zip(places, started)
    ]
    live = (counts[0] - lax.axis_index("resp") * slots).astype(jnp.int32)[None]
    out = finish(live, sums[1], states, slots, group_size, flat_queries.shape, queries.dtype)
    return out.reshape(queries.shape)


def solution(mesh):
    placed = (
        P(("groups", "fsdp"), "resp", None, "tp"),
        P(("groups", "fsdp"), "resp", None, "tp"),
        P(("groups", "fsdp"), "resp", "tp"),
        P(("groups", "fsdp"), "resp", "tp"),
        P(("fsdp", "resp"), "tp"),
        P(("fsdp", "resp"), "tp"),
        P(("groups", "fsdp")),
    )
    sizes = tuple(mesh.shape[name] for name in ("groups", "fsdp", "resp", "tp"))
    return jax.shard_map(
        functools.partial(on_device, sizes),
        mesh=mesh,
        in_specs=placed,
        out_specs=P(("groups", "fsdp"), "resp", None, "tp"),
        check_vma=False,
    )
```

time: 207 us -> 190 us (0.918)
  Pallas kernels: 0 us -> 119 us
  waiting for transfers between devices: 122 us -> 35.7 us
  matrix products: 28.2 us -> 0 us
  blocking collectives: 21.6 us -> 0 us
  starting transfers between devices: 0.08 us -> 13.1 us
  other arithmetic: 11.4 us -> 2.62 us
  local copies, waits for them, and re-layouts: 10.1 us -> 5.2 us
    pallas_call x0 -> x14, Pallas kernels: none -> 119 us  [the longest x1 96.5 us: pack(): pl.pallas_call(body, in_specs=[HBM] * 5, out_specs=[ANYWHERE] * len(shape...]
    all_gather x3 -> x2, waiting for transfers between devices: 119 us -> 13.3 us  [on_device(): lax.all_gather(share, 'fsdp', axis=0, tiled=True)]
    dot_general x10 -> x0, matrix products: 28.2 us -> none  [the longest x4 10.7 us: absorb(): jnp.einsum('rkgd,lkd->rkgl', queried, cache_keys, preferred_element_type=...]
    ppermute x0 -> x14, waiting for transfers between devices: none -> 22.4 us  [the longest x3 22.3 us: on_device(): moved = lax.ppermute(sent, plane, shift(a, b))]
    all_gather x2 -> x0, blocking collectives: 21.6 us -> none  [the longest x1 11.4 us: on_device(): lax.all_gather(prompt_keys, 'resp', axis=1, tiled=True)]
    ppermute x0 -> x14, starting transfers between devices: none -> 13 us  [the longest x6 7.24 us: on_device(): lax.ppermute(x, plane, shift(n_groups - a, n_resp - b))]
    reduce_sum x4 -> x0, other arithmetic: 9.98 us -> none  [absorb(): row_total = row_total * shrink + jnp.sum(weights, axis=-1)]
    dot_general x1 -> x0, local copies, waits for them, and re-layouts: 6.42 us -> none  [on_device(): jnp.dot(token_rows, pieces[0], preferred_element_type=jnp.float32)]
  transfers between devices with their start and end apart: 3 -> 16, of which waited for: 3 -> 3; matrix products, arithmetic and copies ran while one was open for 12% -> 2% of each run, Pallas kernels for 0% -> 11%
where the time goes in v2:
time: 190 us
  Pallas kernels  119 us (63%)
  waiting for transfers between devices  35.7 us (19%)
  between operations  14.5 us (8%)
  starting transfers between devices  13.1 us (7%)
  local copies, waits for them, and re-layouts  5.2 us (3%)
  other arithmetic  2.62 us (1%)
    pallas_call x1, Pallas kernels, pack(): pl.pallas_call(body, in_specs=[HBM] * 5, out_specs=[ANYWHERE] * len(shape...  96.5 us
    ppermute x3, waiting for transfers between devices, on_device(): moved = lax.ppermute(sent, plane, shift(a, b))  22.3 us
    pallas_call x8, Pallas kernels, attend(): pl.pallas_call(body, grid=(1,), in_specs=specs, out_specs=out_specs, out_...  13.7 us
    all_gather x2, waiting for transfers between devices, on_device(): lax.all_gather(share, 'fsdp', axis=0, tiled=True)  13.3 us
    ppermute x6, starting transfers between devices, on_device(): lax.ppermute(x, plane, shift(n_groups - a, n_resp - b))  7.24 us
    pallas_call x4, Pallas kernels, project(): pl.pallas_call(body, in_specs=[VMEM] * (1 + 2 * count), out_specs=[VMEM]...  7.06 us
    ppermute x3, starting transfers between devices, on_device(): moved = lax.ppermute(sent, plane, shift(a, b))  4.55 us
    unnamed x52, local copies, waits for them, and re-layouts  4.13 us
  transfers between devices with their start and end apart: 16, of which 3 were waited for; matrix products, arithmetic and copies ran while one was open for 2% of the time, Pallas kernels for 11%

profile of v2, /device:TPU:0, one launch (start us, length us, event | category | flops | bytes accessed | tf_op | source)
XLA Modules:
  0.0 190.0 jit_solution(11339977998591565287)
XLA Ops:
  6.5 96.5 %pack.1 = (bf16[256,1024]{1,0:T(8,128)(2,1)}, bf16[256,1024]{1,0:T(8,128)(2,1)}, bf16[256,1024]{1,0:T(8,128)(2,1)}, bf16[256,1024]{1,0:T(8,128)(2,1)}, bf16[512,...) custom-call(bf16[256,4096]{1,0:T(8,128)(2,1)} %bitcast.26, bf16[1024,256]{1,0:T(8,128)(2,1)} %kw_ref.1, ...), custom_call_target="tpu_custom_call" | custom-call | bytes 6291456 | tf_op jit(solution)/shard_map/pack/pallas_call | solution.py:117
  103.2 1.0 attend_local.4
  105.0 3.0 %collective-permute-start.1 = (bf16[256,1024]{1,0:T(8,128)(2,1)}, bf16[256,1024]{1,0:T(8,128)(2,1)S(1)}, u32[]{:S(2)}, u32[]{:S(2)}) collective-permute-start(bf16[256,1024]{1,0:T(8,128)(2,1)} %get-tuple-element.47), channel_id=1, source_target_pairs={{0,2},{2,0},{16,18},{18,16},{1,3},{3,1},{17,19},{19,17},{4,6},{6,4... | collective-permute-start | bytes 1572872 | tf_op jit(solution)/shard_map/ppermute | solution.py:354
  108.0 1.5 collective-permute-start.3
  109.6 1.0 attend_local.5
  110.6 10.4 %collective-permute-done.1.refs_0_ = bf16[256,1024]{1,0:T(8,128)(2,1)S(1)} collective-permute-done((bf16[256,1024]{1,0:T(8,128)(2,1)}, bf16[256,1024]{1,0:T(8,128)(2,1)S(1)}, u32[]{:S(2)}, u32[]{:S(2)}) %collective-permute-start.1) | collective-permute-done | bytes 524320 | tf_op jit(solution)/shard_map/ppermute | solution.py:354
  121.0 12.0 %collective-permute-done.3.refs_2_ = bf16[256,1024]{1,0:T(8,128)(2,1)} collective-permute-done((bf16[256,1024]{1,0:T(8,128)(2,1)}, bf16[256,1024]{1,0:T(8,128)(2,1)}, u32[]{:S(2)}, u32[]{:S(2)}) %collective-permute-start.3) | collective-permute-done | bytes 524320 | tf_op jit(solution)/shard_map/ppermute | solution.py:354
  136.1 1.0 attend_local.7
  138.6 1.7 pad_maximum_fusion
  140.4 1.2 copy-done.3
  141.6 3.4 %project.7 = (bf16[256,256]{1,0:T(8,128)(2,1)}, bf16[256,256]{1,0:T(8,128)(2,1)}, bf16[256,256]{1,0:T(8,128)(2,1)}) custom-call(bf16[2048,256]{1,0:T(8,128)(2,1)S(1)} %copy-done.3, bf16[256,1024]{1,0:T(8,128)(2,1)S(1)} %collective-permute-done.1.refs_0_, bf16[256,1024]{1,0:T(8,128)(2,1)} %collective-permute-done.2.refs_1_, ...), custom_call_target="tpu_custom_call" | custom-call | flops 805306368 | bytes 3145728 | tf_op jit(solution)/shard_map/project/pallas_call | solution.py:145
  145.0 1.4 collective-permute-start.11
  146.4 1.5 collective-permute-start.12
  148.6 1.1 fusion.1
  149.7 13.2 %all-gather.3.cloned.1.call-done.weight_ref = bf16[2048,256]{1,0:T(8,128)(2,1)} async-done(((bf16[512,256]{1,0:T(8,128)(2,1)}), bf16[2048,256]{1,0:T(8,128)(2,1)}) %all-gather.3.cloned.1.call-update) | async-done | bytes 1048592 | tf_op jit(solution)/shard_map/all_gather | solution.py:359
  162.9 1.2 copy-done.5
  164.1 2.7 %project.5 = (bf16[256,256]{1,0:T(8,128)(2,1)S(1)}, bf16[256,256]{1,0:T(8,128)(2,1)S(1)}, bf16[256,256]{1,0:T(8,128)(2,1)S(1)}) custom-call(bf16[2048,256]{1,0:T(8,128)(2,1)S(1)} %copy-done.5, bf16[256,1024]{1,0:T(8,128)(2,1)S(1)} %collective-permute-done.1.refs_0_, bf16[256,1024]{1,0:T(8,128)(2,1)} %collective-permute-done.2.refs_1_, ...), custom_call_target="tpu_custom_call" | custom-call | flops 805306368 | bytes 3145728 | tf_op jit(solution)/shard_map/project/pallas_call | solution.py:145
  166.9 1.5 collective-permute-start.7
  168.5 1.5 collective-permute-start.8
  171.6 2.4 %attend_rest.4 = (f32[128,1024]{1,0:T(8,128)S(1)}, f32[128,128]{1,0:T(8,128)S(1)}, bf16[128,1024]{1,0:T(8,128)(2,1)S(1)}) custom-call(bf16[256,2048]{1,0:T(8,128)(2,1)S(1)} %bitcast.12, bf16[512,256]{1,0:T(8,128)(2,1)S(1)} %get-tuple-element.82.refs_0_, bf16[512,256]{1,0:T(8,128)(2,1)S(1)} %get-tuple-element.81.refs_1_, f32[256,256]{1,0:T(8,128)S(1)} %project.6.refs_2_, ...), custom_call_target="tpu_custom_call" | custom-call | flops 503316480 | bytes 2097152 | tf_op jit(solution)/shard_map/attend_rest/pallas_call | solution.py:239
  174.0 2.4 %attend_rest.7 = (f32[128,1024]{1,0:T(8,128)S(1)}, f32[128,128]{1,0:T(8,128)S(1)}, bf16[128,1024]{1,0:T(8,128)(2,1)S(1)}) custom-call(bf16[256,2048]{1,0:T(8,128)(2,1)S(1)} %bitcast.13, bf16[512,256]{1,0:T(8,128)(2,1)S(1)} %get-tuple-element.82.refs_0_, bf16[512,256]{1,0:T(8,128)(2,1)S(1)} %get-tuple-element.81.refs_1_, f32[256,256]{1,0:T(8,128)S(1)} %project.6.refs_2_, ...), custom_call_target="tpu_custom_call" | custom-call | flops 503316480 | bytes 2097152 | tf_op jit(solution)/shard_map/attend_rest/pallas_call | solution.py:239
  176.4 2.6 %attend_rest.5 = (f32[128,1024]{1,0:T(8,128)S(1)}, f32[128,128]{1,0:T(8,128)S(1)}, bf16[128,1024]{1,0:T(8,128)(2,1)S(1)}) custom-call(bf16[256,2048]{1,0:T(8,128)(2,1)S(1)} %bitcast.14, bf16[512,256]{1,0:T(8,128)(2,1)S(1)} %get-tuple-element.82.refs_0_, bf16[512,256]{1,0:T(8,128)(2,1)S(1)} %get-tuple-element.81.refs_1_, f32[256,256]{1,0:T(8,128)S(1)} %project.6.refs_2_, ...), custom_call_target="tpu_custom_call" | custom-call | flops 503316480 | bytes 2097152 | tf_op jit(solution)/shard_map/attend_rest/pallas_call | solution.py:239
  179.0 2.4 %attend_rest.6 = (f32[128,1024]{1,0:T(8,128)S(1)}, f32[128,128]{1,0:T(8,128)S(1)}, bf16[128,1024]{1,0:T(8,128)(2,1)S(1)}) custom-call(bf16[256,2048]{1,0:T(8,128)(2,1)S(1)} %bitcast.15, bf16[512,256]{1,0:T(8,128)(2,1)S(1)} %get-tuple-element.82.refs_0_, bf16[512,256]{1,0:T(8,128)(2,1)S(1)} %get-tuple-element.81.refs_1_, f32[256,256]{1,0:T(8,128)S(1)} %project.6.refs_2_, ...), custom_call_target="tpu_custom_call" | custom-call | flops 503316480 | bytes 2097152 | tf_op jit(solution)/shard_map/attend_rest/pallas_call | solution.py:239
  181.4 1.7 finish.1
  (81 shorter events, 7.2 us)
Async XLA Ops:
  6.5 96.6 %copy-start.1 = (bf16[1,512,256]{2,1,0:T(8,128)(2,1)S(1)}, bf16[1,512,256]{2,1,0:T(8,128)(2,1)}, u32[]{:S(2)}) copy-start(bf16[1,512,256]{2,1,0:T(8,128)(2,1)} %param.9) | copy-start | bytes 786436
  6.5 96.6 %copy-start.2 = (bf16[1,512,256]{2,1,0:T(8,128)(2,1)S(1)}, bf16[1,512,256]{2,1,0:T(8,128)(2,1)}, u32[]{:S(2)}) copy-start(bf16[1,512,256]{2,1,0:T(8,128)(2,1)} %param.10) | copy-start | bytes 786436
  6.5 96.6 %copy-start = (bf16[1,2,128,2048]{3,2,1,0:T(8,128)(2,1)S(1)}, bf16[1,2,128,2048]{3,2,1,0:T(8,128)(2,1)}, u32[]{:S(2)}) copy-start(bf16[1,2,128,2048]{3,2,1,0:T(8,128)(2,1)} %param.8) | copy-start | bytes 3145732
  6.5 133.8 %all-gather.5.cloned.1.call-start = ((), (), s32[]{:S(2)}) async-start(), calls=%async_computation.1 | async-start | bytes 1310720 | tf_op jit(solution)/shard_map/all_gather | solution.py:359
  103.1 59.8 %all-gather.3.cloned.1.call-start = ((), (), s32[]{:S(2)}) async-start(), calls=%async_computation | async-start | bytes 1310720 | tf_op jit(solution)/shard_map/all_gather | solution.py:359
  105.0 32.2 %copy-start.18 = (f32[128,128]{1,0:T(8,128)}, f32[128,128]{1,0:T(8,128)S(1)}, u32[]{:S(2)}) copy-start(f32[128,128]{1,0:T(8,128)S(1)} %get-tuple-element.44.refs_9_) | copy-start | bytes 196612
  105.0 16.0 %collective-permute-start.1 = (bf16[256,1024]{1,0:T(8,128)(2,1)}, bf16[256,1024]{1,0:T(8,128)(2,1)S(1)}, u32[]{:S(2)}, u32[]{:S(2)}) collective-permute-start(bf16[256,1024]{1,0:T(8,128)(2,1)} %get-tuple-element.47), channel_id=1, source_target_pairs={{0,2},{2,0},{16,18},{18,16},{1,3},{3,1},{17,19},{19,17},{4,6},{6,4... | collective-permute-start | bytes 1572872 | tf_op jit(solution)/shard_map/ppermute | solution.py:354
  108.0 24.9 %collective-permute-start.3 = (bf16[256,1024]{1,0:T(8,128)(2,1)}, bf16[256,1024]{1,0:T(8,128)(2,1)}, u32[]{:S(2)}, u32[]{:S(2)}) collective-permute-start(bf16[256,1024]{1,0:T(8,128)(2,1)} %get-tuple-element.50), channel_id=1, source_target_pairs={{0,16},{2,18},{16,0},{18,2},{1,17},{3,19},{17,1},{19,3},{4,20},{6,... | collective-permute-start | bytes 1572872 | tf_op jit(solution)/shard_map/ppermute | solution.py:354
  109.5 23.4 %collective-permute-start.5 = (bf16[256,1024]{1,0:T(8,128)(2,1)}, bf16[256,1024]{1,0:T(8,128)(2,1)}, u32[]{:S(2)}, u32[]{:S(2)}) collective-permute-start(bf16[256,1024]{1,0:T(8,128)(2,1)} %get-tuple-element.52), channel_id=1, source_target_pairs={{0,18},{2,16},{16,2},{18,0},{1,19},{3,17},{17,3},{19,1},{4,22},{6,... | collective-permute-start | bytes 1572872 | tf_op jit(solution)/shard_map/ppermute | solution.py:354
  109.6 58.9 %collective-permute-start = (bf16[256,1024]{1,0:T(8,128)(2,1)S(1)}, bf16[256,1024]{1,0:T(8,128)(2,1)S(1)}, u32[]{:S(2)}, u32[]{:S(2)}) collective-permute-start(bf16[256,1024]{1,0:T(8,128)(2,1)S(1)} %copy-done.7), channel_id=1, source_target_pairs={{0,1},{1,0},{2,3},{3,2},{4,5},{5,4},{6,7},{7,6},{8,9},{9,8},{10,11... | collective-permute-start | bytes 1572872 | tf_op jit(solution)/shard_map/ppermute | solution.py:356
  110.6 26.6 %copy-start.12 = (f32[128,1024]{1,0:T(8,128)}, f32[128,1024]{1,0:T(8,128)S(1)}, u32[]{:S(2)}) copy-start(f32[128,1024]{1,0:T(8,128)S(1)} %get-tuple-element.77.refs_8_) | copy-start | bytes 1572868
  110.6 34.5 %copy-start.20 = (f32[128,128]{1,0:T(8,128)}, f32[128,128]{1,0:T(8,128)S(1)}, u32[]{:S(2)}) copy-start(f32[128,128]{1,0:T(8,128)S(1)} %get-tuple-element.48.refs_9_) | copy-start | bytes 196612
  121.0 19.3 %collective-permute-start.2 = (bf16[256,1024]{1,0:T(8,128)(2,1)S(1)}, bf16[256,1024]{1,0:T(8,128)(2,1)}, u32[]{:S(2)}, u32[]{:S(2)}) collective-permute-start(bf16[256,1024]{1,0:T(8,128)(2,1)S(1)} %collective-permute-done.1.refs_0_), channel_id=1, source_target_pairs={{0,1},{1,0},{2,3},{3,2},{4,5},{5,4},{6,7},{7,6},{8,9},{9,8},{10,11... | collective-permute-start | bytes 1572872 | tf_op jit(solution)/shard_map/ppermute | solution.py:356
  132.9 7.4 %collective-permute-start.4 = (bf16[256,1024]{1,0:T(8,128)(2,1)}, bf16[256,1024]{1,0:T(8,128)(2,1)}, u32[]{:S(2)}, u32[]{:S(2)}) collective-permute-start(bf16[256,1024]{1,0:T(8,128)(2,1)} %collective-permute-done.3.refs_2_), channel_id=1, source_target_pairs={{0,1},{1,0},{2,3},{3,2},{4,5},{5,4},{6,7},{7,6},{8,9},{9,8},{10,11... | collective-permute-start | bytes 1572872 | tf_op jit(solution)/shard_map/ppermute | solution.py:356
  133.0 7.4 %collective-permute-start.6 = (bf16[256,1024]{1,0:T(8,128)(2,1)}, bf16[256,1024]{1,0:T(8,128)(2,1)}, u32[]{:S(2)}, u32[]{:S(2)}) collective-permute-start(bf16[256,1024]{1,0:T(8,128)(2,1)} %collective-permute-done.5.refs_4_), channel_id=1, source_target_pairs={{0,1},{1,0},{2,3},{3,2},{4,5},{5,4},{6,7},{7,6},{8,9},{9,8},{10,11... | collective-permute-start | bytes 1572872 | tf_op jit(solution)/shard_map/ppermute | solution.py:356
  133.5 15.1 %collective-permute-start.10 = (bf16[1024,256]{1,0:T(8,128)(2,1)}, bf16[1024,256]{1,0:T(8,128)(2,1)}, u32[]{:S(2)}, u32[]{:S(2)}) collective-permute-start(bf16[1024,256]{1,0:T(8,128)(2,1)} %get-tuple-element.58), channel_id=1, source_target_pairs={{0,2},{2,0},{1,3},{3,1},{4,6},{6,4},{5,7},{7,5},{8,10},{10,8},{9,1... | collective-permute-start | bytes 1572872 | tf_op jit(solution)/shard_map/ppermute | solution.py:363
  135.2 9.8 %copy-start.22 = (f32[128,128]{1,0:T(8,128)}, f32[128,128]{1,0:T(8,128)S(1)}, u32[]{:S(2)}) copy-start(f32[128,128]{1,0:T(8,128)S(1)} %get-tuple-element.68.refs_9_) | copy-start | bytes 196612
  138.0 7.1 %copy-start.24 = (f32[128,128]{1,0:T(8,128)}, f32[128,128]{1,0:T(8,128)S(1)}, u32[]{:S(2)}) copy-start(f32[128,128]{1,0:T(8,128)S(1)} %get-tuple-element.73.refs_9_) | copy-start | bytes 196612
  145.0 25.9 %collective-permute-start.11 = (bf16[256,256]{1,0:T(8,128)(2,1)}, bf16[256,256]{1,0:T(8,128)(2,1)S(1)}, u32[]{:S(2)}, u32[]{:S(2)}) collective-permute-start(bf16[256,256]{1,0:T(8,128)(2,1)} %get-tuple-element.60), channel_id=1, source_target_pairs={{0,2},{2,0},{16,18},{18,16},{1,3},{3,1},{17,19},{19,17},{4,6},{6,4... | collective-permute-start | bytes 393224 | tf_op jit(solution)/shard_map/ppermute | solution.py:371
  146.4 25.1 %collective-permute-start.12 = (bf16[256,256]{1,0:T(8,128)(2,1)}, bf16[256,256]{1,0:T(8,128)(2,1)S(1)}, u32[]{:S(2)}, u32[]{:S(2)}) collective-permute-start(bf16[256,256]{1,0:T(8,128)(2,1)} %get-tuple-element.61), channel_id=1, source_target_pairs={{0,16},{2,18},{16,0},{18,2},{1,17},{3,19},{17,1},{19,3},{4,20},{6,... | collective-permute-start | bytes 393224 | tf_op jit(solution)/shard_map/ppermute | solution.py:371
  147.9 23.6 %collective-permute-start.13 = (bf16[256,256]{1,0:T(8,128)(2,1)}, bf16[256,256]{1,0:T(8,128)(2,1)S(1)}, u32[]{:S(2)}, u32[]{:S(2)}) collective-permute-start(bf16[256,256]{1,0:T(8,128)(2,1)} %get-tuple-element.62), channel_id=1, source_target_pairs={{0,18},{2,16},{16,2},{18,0},{1,19},{3,17},{17,3},{19,1},{4,22},{6,... | collective-permute-start | bytes 393224 | tf_op jit(solution)/shard_map/ppermute | solution.py:371
  166.9 14.5 %collective-permute-start.7 = (bf16[256,256]{1,0:T(8,128)(2,1)S(1)}, bf16[256,256]{1,0:T(8,128)(2,1)S(1)}, u32[]{:S(2)}, u32[]{:S(2)}) collective-permute-start(bf16[256,256]{1,0:T(8,128)(2,1)S(1)} %get-tuple-element.54), channel_id=1, source_target_pairs={{0,2},{2,0},{16,18},{18,16},{1,3},{3,1},{17,19},{19,17},{4,6},{6,4... | collective-permute-start | bytes 393224 | tf_op jit(solution)/shard_map/ppermute | solution.py:371
  168.5 12.9 %collective-permute-start.8 = (bf16[256,256]{1,0:T(8,128)(2,1)S(1)}, bf16[256,256]{1,0:T(8,128)(2,1)S(1)}, u32[]{:S(2)}, u32[]{:S(2)}) collective-permute-start(bf16[256,256]{1,0:T(8,128)(2,1)S(1)} %get-tuple-element.55), channel_id=1, source_target_pairs={{0,16},{2,18},{16,0},{18,2},{1,17},{3,19},{17,1},{19,3},{4,20},{6,... | collective-permute-start | bytes 393224 | tf_op jit(solution)/shard_map/ppermute | solution.py:371
  170.9 10.5 %collective-permute-start.9 = (bf16[256,256]{1,0:T(8,128)(2,1)S(1)}, bf16[256,256]{1,0:T(8,128)(2,1)S(1)}, u32[]{:S(2)}, u32[]{:S(2)}) collective-permute-start(bf16[256,256]{1,0:T(8,128)(2,1)S(1)} %get-tuple-element.56), channel_id=1, source_target_pairs={{0,18},{2,16},{16,2},{18,0},{1,19},{3,17},{17,3},{19,1},{4,22},{6,... | collective-permute-start | bytes 393224 | tf_op jit(solution)/shard_map/ppermute | solution.py:371
  (18 other events, 52.4 us)
Sparse Core Ops, SparseCore 0:
  103.2 30.6 all-gather.4
  135.4 27.4 all-gather.2

commit v3 on v0

v3 whole, which is shorter than its diff:
```python
import functools
import math

import jax
import jax.numpy as jnp
import numpy as np
from jax import lax
from jax.experimental import pallas as pl
from jax.experimental.pallas import tpu as pltpu
from jax.sharding import PartitionSpec as P

HD = 128
PLEN = 1024
FACTOR = HD**-0.5 * math.log2(math.e)
MIB = 1 << 20
VMEM = pl.BlockSpec(memory_space=pltpu.VMEM)
SMEM = pl.BlockSpec(memory_space=pltpu.SMEM)
ANYWHERE = pl.BlockSpec(memory_space=pl.ANY)


def dot_nt(a, b):
    return lax.dot_general(a, b, (((1,), (1,)), ((), ())), preferred_element_type=jnp.float32)


def dot_nn(a, b):
    return lax.dot_general(a, b, (((1,), (0,)), ((), ())), preferred_element_type=jnp.float32)


def call(name, body, operands, shapes, flops, transcendentals=0, scratch=(), first_scalar=False):
    specs = [VMEM] * len(operands)
    if first_scalar:
        specs[0] = SMEM
    return pl.pallas_call(
        body,
        in_specs=specs,
        out_specs=[VMEM] * len(shapes),
        out_shape=shapes,
        scratch_shapes=list(scratch),
        compiler_params=pltpu.CompilerParams(vmem_limit_bytes=16 * MIB),
        cost_estimate=pl.CostEstimate(
            flops=0, bytes_accessed=0, transcendentals=0
        ),
        name=name,
    )(*operands)


def after(value, *earlier):
    return pl.pallas_call(
        lambda *refs: None,
        in_specs=[ANYWHERE] * (1 + len(earlier)),
        out_specs=ANYWHERE,
        out_shape=jax.ShapeDtypeStruct(value.shape, value.dtype),
        input_output_aliases={0: 0},
        cost_estimate=pl.CostEstimate(flops=0, bytes_accessed=0, transcendentals=0),
        name="after",
    )(value, *earlier)


def pack_weights(n_groups, key_weight, value_weight):
    block, columns = key_weight.shape
    half = block // n_groups

    def body(key_ref, value_ref, out_ref):
        first = pl.multiple_of(lax.axis_index("groups") * half, half)
        out_ref[0] = key_ref[pl.ds(first, half), :]
        out_ref[1] = value_ref[pl.ds(first, half), :]

    shape = jax.ShapeDtypeStruct((2, half, columns), key_weight.dtype)
    return call("pack_weights", body, [key_weight, value_weight], [shape], 0)[0]


def pack_features(sizes, block, hidden):
    n_groups, n_fsdp, n_resp, n_tp = sizes
    rows = hidden.shape[0]
    per_core = n_fsdp // n_tp
    half = block // n_groups
    starts = [
        [(n * n_resp + resp) * block + group * half for n in range(per_core)]
        for group in range(n_groups)
        for resp in range(n_resp)
    ]

    def body(hidden_ref, out_ref):
        for n, parts in enumerate(starts):
            for k, start in enumerate(parts):
                out_ref[n, :, k * half : (k + 1) * half] = hidden_ref[:, start : start + half]

    shape = jax.ShapeDtypeStruct((len(starts), rows, per_core * half), hidden.dtype)
    return call("pack_features", body, [hidden], [shape], 0)[0]


def line_ring(size):
    return list(range(0, size, 2)) + list(range(1, size, 2))[::-1]


def project(n_fsdp, chunk, near, far, pieces):
    count, rows, depth = near.shape
    half, columns = pieces[0][0].shape[-2:]
    total = len(pieces)

    def body(*refs):
        piece_refs = refs[:total]
        near_ref, far_ref, out_ref, weight_ref = refs[total:]
        fsdp, core = lax.axis_index("fsdp"), lax.axis_index("tp")
        place = jnp.where(fsdp % 2 == 0, fsdp // 2, n_fsdp - (fsdp + 1) // 2)
        for ref, (_, distance) in zip(piece_refs, pieces):
            at = (place - distance + n_fsdp) % n_fsdp
            owner = jnp.where(at < n_fsdp // 2, 2 * at, 2 * n_fsdp - 1 - 2 * at)
            value = ref[chunk] if len(ref.shape) == 3 else ref[...]
            weight_ref[pl.ds(pl.multiple_of(owner * half, half), half), :] = value
        first = pl.ds(pl.multiple_of(core * depth, depth), depth)
        second = pl.ds(pl.multiple_of((1 - core) * depth, depth), depth)
        for n in range(count):
            out = dot_nn(near_ref[n], weight_ref[first, :])
            out = out + dot_nn(far_ref[n], weight_ref[second, :])
            out_ref[n] = out.astype(out_ref.dtype)

    return call(
        "project",
        body,
        [x for x, _ in pieces] + [near, far],
        [jax.ShapeDtypeStruct((count, rows, columns), near.dtype)],
        4 * rows * columns * depth * count,
        scratch=[pltpu.VMEM((n_fsdp * half, columns), pieces[0][0].dtype)],
    )[0]


class Place:
    def __init__(self, slot, head, tokens, group_size):
        self.rows = slice(slot * tokens, (slot + 1) * tokens)
        self.lanes = slice(head * HD, (head + 1) * HD)
        self.tokens = tokens
        self.group_size = group_size
        self.first = head * group_size
        self.pair = 2 if group_size % 2 == 0 else 1
        self.starts = range(0, group_size, self.pair)
        self.wide = jax.ShapeDtypeStruct((tokens, group_size * HD), jnp.float32)

    def queries(self, ref, first):
        heads = [self.first + first + n for n in range(self.pair)]
        return jnp.concatenate([ref[self.rows, h * HD : (h + 1) * HD] for h in heads], axis=0)

    def take(self, ref, first):
        heads = [first + n for n in range(self.pair)]
        return jnp.concatenate([ref[:, h * HD : (h + 1) * HD] for h in heads], axis=0)

    def put(self, ref, first, value):
        value = jnp.broadcast_to(value, (self.pair * self.tokens, HD)).astype(ref.dtype)
        for n in range(self.pair):
            lanes = slice((first + n) * HD, (first + n + 1) * HD)
            ref[:, lanes] = value[n * self.tokens : (n + 1) * self.tokens]


def attend_cache(name, place, queries, caches, length, state=None):
    def body(q_ref, *refs):
        acc_ref, top_ref, total_ref = refs[-3:]
        sources = []
        for n, cache in enumerate(caches):
            if len(cache) == 2:
                keys, values = refs[0][:, place.lanes], refs[1][:, place.lanes]
            else:
                keys = refs[0][:length, place.lanes]
                values = refs[0][length:, place.lanes]
            refs = refs[len(cache) :]
            wide = jnp.concatenate([values, jnp.ones(values.shape, values.dtype)], axis=1)
            sources.append((keys, wide))
        for first in place.starts:
            q = place.queries(q_ref, first)
            scores = [dot_nt(q, keys) for keys, _ in sources]
            tops = [jnp.max(s, axis=1, keepdims=True) for s in scores]
            top = functools.reduce(jnp.maximum, tops)
            if state is not None:
                old_top = place.take(refs[1], first)
                spread = jnp.maximum(old_top, top)
                shrink = jnp.exp2((old_top - spread) * FACTOR)
                top = jnp.max(spread, axis=1, keepdims=True)
            out = None
            for s, (_, wide) in zip(scores, sources):
                probs = jnp.exp2((s - top) * FACTOR).astype(jnp.bfloat16)
                part = dot_nn(probs, wide)
                out = part if out is None else out + part
            mixed, total = out[:, :HD], out[:, HD:]
            if state is not None:
                mixed = mixed + place.take(refs[0], first) * shrink
                total = total + place.take(refs[2], first) * shrink
            place.put(acc_ref, first, mixed)
            place.put(top_ref, first, top)
            place.put(total_ref, first, total)

    operands = [queries, *[x for cache in caches for x in cache]]
    if state is not None:
        operands.extend(state)
    work = place.tokens * place.group_size * length * len(caches)
    return call(name, body, operands, [place.wide] * 3, 6 * work * HD, work)


def sum_parts(ref, rows, lanes):
    total = ref[0, rows, lanes].astype(jnp.float32)
    for n in range(1, ref.shape[0]):
        total = total + ref[n, rows, lanes].astype(jnp.float32)
    return total


def attend_own(place, queries, key_parts, tables, state):
    tokens = place.tokens

    def body(q_ref, key_ref, cos_ref, sin_ref, old_acc, old_tops, old_total, *outs):
        acc_ref, inverse_ref, probs_ref = outs
        key = sum_parts(key_ref, place.rows, place.lanes)
        key = key * cos_ref[...] + pltpu.roll(key, HD // 2, 1) * sin_ref[...]
        key = key.astype(jnp.bfloat16)
        ones = jnp.ones((tokens, HD), jnp.bfloat16)
        row = lax.broadcasted_iota(jnp.int32, (tokens, tokens), 0)
        causal = row >= lax.broadcasted_iota(jnp.int32, (tokens, tokens), 1)
        causal = jnp.concatenate([causal] * place.pair, axis=0)
        for first in place.starts:
            scores = jnp.where(causal, dot_nt(place.queries(q_ref, first), key), -1e30)
            old_top = place.take(old_tops, first)
            top = jnp.maximum(old_top, jnp.max(scores, axis=1, keepdims=True))
            probs = jnp.exp2((scores - top) * FACTOR).astype(jnp.bfloat16)
            shrink = jnp.exp2((old_top - top) * FACTOR)
            total = place.take(old_total, first) * shrink + dot_nn(probs, ones)
            inverse = 1.0 / total
            place.put(acc_ref, first, place.take(old_acc, first) * shrink * inverse)
            place.put(inverse_ref, first, inverse)
            place.put(probs_ref, first, probs)

    work = tokens * tokens * place.group_size
    probs = jax.ShapeDtypeStruct(place.wide.shape, jnp.bfloat16)
    return call(
        "attend_own",
        body,
        [queries, key_parts, *tables, *state],
        [place.wide, place.wide, probs],
        4 * work * HD,
        work,
    )


def finish(live, value_parts, states, places, shape, dtype):
    def body(live_ref, value_ref, *refs):
        out_ref = refs[-1]
        for n, place in enumerate(places):
            alive = place.rows.start // place.tokens < live_ref[0]
            acc_ref, inverse_ref, probs_ref = refs[3 * n : 3 * n + 3]
            value = sum_parts(value_ref, place.rows, place.lanes).astype(jnp.bfloat16)
            for first in place.starts:
                part = dot_nn(place.take(probs_ref, first), value)
                result = place.take(acc_ref, first) + part * place.take(inverse_ref, first)
                result = jnp.where(alive, result, 0.0).astype(dtype)
                for k in range(place.pair):
                    head = place.first + first + k
                    out_ref[place.rows, head * HD : (head + 1) * HD] = result[
                        k * place.tokens : (k + 1) * place.tokens
                    ]

    return call(
        "finish",
        body,
        [live, value_parts, *[x for state in states for x in state]],
        [jax.ShapeDtypeStruct(shape, dtype)],
        2 * shape[0] * shape[1] * places[0].tokens,
        first_scalar=True,
    )[0]


def rotation_tables(extent, offset):
    orders = np.arange(HD // 2, dtype=np.float64)
    inverse = np.exp(-(2.0 * orders / HD) * math.log(500000.0))
    angles = (offset + np.arange(extent))[:, None] * inverse[None, :]
    cosine, sine = np.cos(angles), np.sin(angles)
    return (
        jnp.asarray(np.concatenate([cosine, cosine], axis=1), jnp.float32),
        jnp.asarray(np.concatenate([-sine, sine], axis=1), jnp.float32),
    )


def on_device(sizes, hidden, queries, prompt_keys, prompt_values, key_weight, value_weight, counts):
    n_groups, n_fsdp, n_resp, n_tp = sizes
    _, slots, tokens, part_width = hidden.shape
    block, columns = key_weight.shape
    kv_heads = columns // HD
    group_size = queries.shape[3] // columns
    rows = slots * tokens
    length = prompt_keys.shape[1]
    plane = ("groups", "resp")
    cores = [(n, (n + 1) % n_tp) for n in range(n_tp)]
    ring = line_ring(n_fsdp)
    rightward = [(ring[n], ring[(n + 1) % n_fsdp]) for n in range(n_fsdp)]
    leftward = [(b, a) for a, b in rightward]

    def exchange(parts):
        return lax.all_to_all(parts, plane, split_axis=0, concat_axis=0, tiled=True)

    share = pack_weights(n_groups, key_weight, value_weight)
    pieces = [(share, 0)]
    hops = {1: lax.ppermute(share, "fsdp", rightward), -1: lax.ppermute(share, "fsdp", leftward)}

    near = exchange(pack_features(sizes, block, hidden.reshape(rows, part_width)))
    cache = jnp.concatenate([prompt_keys[0], prompt_values[0]], axis=0)
    others = [
        lax.ppermute(cache, "resp", [(n, (n + b) % n_resp) for n in range(n_resp)])
        for b in range(1, n_resp)
    ]

    flat_queries = queries.reshape(rows, queries.shape[3])
    places = [
        Place(slot, head, tokens, group_size) for slot in range(slots) for head in range(kv_heads)
    ]
    states = [
        attend_cache(
            "attend_local", p, flat_queries, [(prompt_keys[0], prompt_values[0])], length
        )
        for p in places
    ]
    marks = [state[1] for state in states]

    held = after(hops[1], *marks)
    pieces.append((held, 1))
    for hop in range(2, n_fsdp // 2):
        held = lax.ppermute(held, "fsdp", rightward)
        pieces.append((held, hop))
    last = [lax.ppermute(held[chunk], "fsdp", rightward) for chunk in range(2)]
    held = hops[-1]
    pieces.append((held, -1))
    for hop in range(2, n_fsdp - n_fsdp // 2):
        held = lax.ppermute(held, "fsdp", leftward)
        pieces.append((held, -hop))

    near = after(near, *marks)
    far = lax.ppermute(near, "tp", cores)

    states = [
        attend_cache("attend_remote", p, flat_queries, [(x,) for x in others], length, state)
        for p, state in zip(places, states)
    ]

    sums = [exchange(project(n_fsdp, chunk, near, far, [*pieces, (last[chunk], n_fsdp // 2)])) for chunk in range(2)]
    tables = rotation_tables(tokens, PLEN)
    states = [
        attend_own(p, flat_queries, sums[0], tables, state) for p, state in zip(places, states)
    ]
    live = (counts[0] - lax.axis_index("resp") * slots).astype(jnp.int32)[None]
    out = finish(live, sums[1], states, places, flat_queries.shape, queries.dtype)
    return out.reshape(queries.shape)


def solution(mesh):
    placed = (
        P(("groups", "fsdp"), "resp", None, "tp"),
        P(("groups", "fsdp"), "resp", None, "tp"),
        P(("groups", "fsdp"), "resp", "tp"),
        P(("groups", "fsdp"), "resp", "tp"),
        P(("fsdp", "resp"), "tp"),
        P(("fsdp", "resp"), "tp"),
        P(("groups", "fsdp")),
    )
    sizes = tuple(mesh.shape[name] for name in ("groups", "fsdp", "resp", "tp"))
    return jax.shard_map(
        functools.partial(on_device, sizes),
        mesh=mesh,
        in_specs=placed,
        out_specs=P(("groups", "fsdp"), "resp", None, "tp"),
        check_vma=False,
    )
```

time: 207 us -> 137 us (0.66)
  waiting for transfers between devices: 122 us -> 42.4 us
  Pallas kernels: 0 us -> 30.1 us
  matrix products: 28.2 us -> 0 us
  local copies, waits for them, and re-layouts: 10.1 us -> 37.3 us
  starting transfers between devices: 0.08 us -> 23.1 us
  blocking collectives: 21.6 us -> 0 us
  between operations: 14 us -> 1.07 us
  other arithmetic: 11.4 us -> 1.77 us
    all_gather x3 -> x0, waiting for transfers between devices: 119 us -> none  [the longest x1 70.2 us: on_device(): lax.all_gather(value_weight, ('fsdp', 'resp'), axis=0, tiled=True)]
    unnamed x9 -> x106, local copies, waits for them, and re-layouts: 1.65 us -> 35.5 us
    ppermute x0 -> x6, waiting for transfers between devices: none -> 32.1 us  [the longest x1 12.6 us: on_device(): lax.ppermute(share, 'fsdp', rightward)]
    pallas_call x0 -> x19, Pallas kernels: none -> 30.1 us  [the longest x17 30.1 us: call(): pl.pallas_call(body, in_specs=specs, out_specs=[VMEM] * len(shapes), out_...]
    dot_general x10 -> x0, matrix products: 28.2 us -> none  [the longest x4 10.7 us: absorb(): jnp.einsum('rkgd,lkd->rkgl', queried, cache_keys, preferred_element_type=...]
    all_gather x2 -> x0, blocking collectives: 21.6 us -> none  [the longest x1 11.4 us: on_device(): lax.all_gather(prompt_keys, 'resp', axis=1, tiled=True)]
    all_to_all x0 -> x3, starting transfers between devices: none -> 13.4 us  [exchange(): return lax.all_to_all(parts, plane, split_axis=0, concat_axis=0, tiled=True)]
    all_to_all x0 -> x3, waiting for transfers between devices: none -> 10.3 us  [exchange(): return lax.all_to_all(parts, plane, split_axis=0, concat_axis=0, tiled=True)]
  transfers between devices with their start and end apart: 3 -> 9, of which waited for: 3 -> 6; matrix products, arithmetic and copies ran while one was open for 12% -> 3% of each run, Pallas kernels for 0% -> 18%
where the time goes in v3:
time: 137 us; the launch traced here: 136 us
  waiting for transfers between devices  42.4 us (31%)
  local copies, waits for them, and re-layouts  37.3 us (27%)
  Pallas kernels  30.1 us (22%)
  starting transfers between devices  23.1 us (17%)
  other arithmetic  1.77 us (1%)
    unnamed x106, local copies, waits for them, and re-layouts  35.5 us
    pallas_call x17, Pallas kernels, call(): pl.pallas_call(body, in_specs=specs, out_specs=[VMEM] * len(shapes), out_...  30.1 us
    all_to_all x3, starting transfers between devices, exchange(): return lax.all_to_all(parts, plane, split_axis=0, concat_axis=0, tiled=True)  13.4 us
    ppermute x1, waiting for transfers between devices, on_device(): lax.ppermute(share, 'fsdp', rightward)  12.6 us
    all_to_all x3, waiting for transfers between devices, exchange(): return lax.all_to_all(parts, plane, split_axis=0, concat_axis=0, tiled=True)  10.3 us
    ppermute x2, waiting for transfers between devices, on_device(): last = [lax.ppermute(held[chunk], 'fsdp', rightward) for chunk in range(2)]  8.21 us
    ppermute x1, waiting for transfers between devices, on_device(): lax.ppermute(share, 'fsdp', leftward)  7.88 us
    ppermute x2, starting transfers between devices, on_device(): last = [lax.ppermute(held[chunk], 'fsdp', rightward) for chunk in range(2)]  5.05 us
  transfers between devices with their start and end apart: 9, of which 6 were waited for; matrix products, arithmetic and copies ran while one was open for 3% of the time, Pallas kernels for 18%

profile of v3, /device:TPU:0, one launch (start us, length us, event | category | flops | bytes accessed | tf_op | source)
XLA Modules:
  0.0 135.7 jit_solution(5916707577719538175)
XLA Ops:
  3.1 5.3 %all-to-all-start = ((bf16[4,256,1024]{2,1,0:T(8,128)(2,1)}), bf16[4,256,1024]{2,1,0:T(8,128)(2,1)S(1)}, u32[]{:S(2)}, u32[]{:S(2)}) async-start(bf16[4,256,1024]{2,1,0:T(8,128)(2,1)} %copy-done.3), calls=%async_computation | async-start | bytes 4194304 | tf_op jit(solution)/shard_map/all_to_all | solution.py:293
  23.0 10.3 %all-to-all-done.refs_0_ = bf16[4,256,1024]{2,1,0:T(8,128)(2,1)S(1)} async-done(((bf16[4,256,1024]{2,1,0:T(8,128)(2,1)}), bf16[4,256,1024]{2,1,0:T(8,128)(2,1)S(1)}, u32[]{:S(2)}, u32[]{:S(2)}) %all-to-all-start) | async-done | bytes 2097184 | tf_op jit(solution)/shard_map/all_to_all | solution.py:293
  37.5 2.7 %collective-permute-start = (bf16[2,512,256]{2,1,0:T(8,128)(2,1)}, bf16[2,512,256]{2,1,0:T(8,128)(2,1)}, u32[]{:S(2)}, u32[]{:S(2)}) collective-permute-start(bf16[2,512,256]{2,1,0:T(8,128)(2,1)} %pack_weights.1.refs_0_), channel_id=1, source_target_pairs={{0,8},{8,12},{12,4},{4,0},{1,9},{9,13},{13,5},{5,1},{2,10},{10,14}... | collective-permute-start | bytes 1572872 | tf_op jit(solution)/shard_map/ppermute | solution.py:297
  40.3 12.6 %collective-permute-done.refs_0_ = bf16[2,512,256]{2,1,0:T(8,128)(2,1)} collective-permute-done((bf16[2,512,256]{2,1,0:T(8,128)(2,1)}, bf16[2,512,256]{2,1,0:T(8,128)(2,1)}, u32[]{:S(2)}, u32[]{:S(2)}) %collective-permute-start) | collective-permute-done | bytes 524320 | tf_op jit(solution)/shard_map/ppermute | solution.py:297
  52.9 1.8 %slice_bitcast_fusion = (bf16[512,256]{1,0:T(8,128)(2,1)S(1)}, bf16[512,256]{1,0:T(8,128)(2,1)}) fusion(bf16[2,512,256]{2,1,0:T(8,128)(2,1)} %after.2.refs_1_), kind=kLoop, calls=%fused_computation.1 | loop fusion | bytes 1048576 | tf_op jit(solution)/shard_map/squeeze | solution.py:323
  54.6 3.4 %collective-permute-start.4 = (bf16[512,256]{1,0:T(8,128)(2,1)S(1)}, bf16[512,256]{1,0:T(8,128)(2,1)S(1)}, u32[]{:S(2)}, u32[]{:S(2)}) collective-permute-start(bf16[512,256]{1,0:T(8,128)(2,1)S(1)} %get-tuple-element.77), channel_id=1, source_target_pairs={{0,8},{8,12},{12,4},{4,0},{1,9},{9,13},{13,5},{5,1},{2,10},{10,14}... | collective-permute-start | bytes 786440 | tf_op jit(solution)/shard_map/ppermute | solution.py:323
  58.0 7.9 %collective-permute-done.1.refs_2_ = bf16[2,512,256]{2,1,0:T(8,128)(2,1)} collective-permute-done((bf16[2,512,256]{2,1,0:T(8,128)(2,1)}, bf16[2,512,256]{2,1,0:T(8,128)(2,1)}, u32[]{:S(2)}, u32[]{:S(2)}) %collective-permute-start.1) | collective-permute-done | bytes 524320 | tf_op jit(solution)/shard_map/ppermute | solution.py:297
  65.9 5.1 %collective-permute-done.4.refs_3_ = bf16[512,256]{1,0:T(8,128)(2,1)S(1)} collective-permute-done((bf16[512,256]{1,0:T(8,128)(2,1)S(1)}, bf16[512,256]{1,0:T(8,128)(2,1)S(1)}, u32[]{:S(2)}, u32[]{:S(2)}) %collective-permute-start.4) | collective-permute-done | bytes 262176 | tf_op jit(solution)/shard_map/ppermute | solution.py:323
  71.0 3.4 %project.3 = bf16[4,256,256]{2,1,0:T(8,128)(2,1)S(1)} custom-call(bf16[2,512,256]{2,1,0:T(8,128)(2,1)} %pack_weights.1.refs_0_, bf16[2,512,256]{2,1,0:T(8,128)(2,1)} %after.2.refs_1_, bf16[2,512,256]{2,1,0:T(8,128)(2,1)} %collective-permute-done.1.refs_2_, bf16[512,256]{1,0:T(8,128)(2,1)S(1)} %collective-permute-done.4.refs_3_, ...), custom_call_target="tpu_custom_call" | custom-call | tf_op jit(solution)/shard_map/project/pallas_call | solution.py:33
  75.2 4.1 %all-to-all-start.2 = ((bf16[4,256,256]{2,1,0:T(8,128)(2,1)}), bf16[4,256,256]{2,1,0:T(8,128)(2,1)}, u32[]{:S(2)}, u32[]{:S(2)}) async-start(bf16[4,256,256]{2,1,0:T(8,128)(2,1)} %copy-done.15), calls=%async_computation.2 | async-start | bytes 1048576 | tf_op jit(solution)/shard_map/all_to_all | solution.py:293
  81.0 1.8 %pad_maximum_fusion = bf16[1024,256]{1,0:T(8,128)(2,1)} fusion(bf16[512,256]{1,0:T(8,128)(2,1)} %bitcast.29, bf16[512,256]{1,0:T(8,128)(2,1)S(1)} %bitcast.28), kind=kLoop, calls=%fused_computation | loop fusion | flops 1048576 | bytes 1048576 | tf_op jit(solution)/shard_map/concatenate | solution.py:300
  82.8 1.9 %collective-permute-start.5 = (bf16[1024,256]{1,0:T(8,128)(2,1)}, bf16[1024,256]{1,0:T(8,128)(2,1)}, u32[]{:S(2)}, u32[]{:S(2)}) collective-permute-start(bf16[1024,256]{1,0:T(8,128)(2,1)} %pad_maximum_fusion), channel_id=1, source_target_pairs={{0,2},{2,0},{1,3},{3,1},{4,6},{6,4},{5,7},{7,5},{8,10},{10,8},{9,1... | collective-permute-start | bytes 1572872 | tf_op jit(solution)/shard_map/ppermute | solution.py:302
  84.7 3.1 %collective-permute-done.2.refs_3_ = bf16[512,256]{1,0:T(8,128)(2,1)S(1)} collective-permute-done((bf16[512,256]{1,0:T(8,128)(2,1)}, bf16[512,256]{1,0:T(8,128)(2,1)S(1)}, u32[]{:S(2)}, u32[]{:S(2)}) %collective-permute-start.2) | collective-permute-done | bytes 262176 | tf_op jit(solution)/shard_map/ppermute | solution.py:323
  87.8 3.4 %project.2 = bf16[4,256,256]{2,1,0:T(8,128)(2,1)S(1)} custom-call(bf16[2,512,256]{2,1,0:T(8,128)(2,1)} %pack_weights.1.refs_0_, bf16[2,512,256]{2,1,0:T(8,128)(2,1)} %after.2.refs_1_, bf16[2,512,256]{2,1,0:T(8,128)(2,1)} %collective-permute-done.1.refs_2_, bf16[512,256]{1,0:T(8,128)(2,1)S(1)} %collective-permute-done.2.refs_3_, ...), custom_call_target="tpu_custom_call" | custom-call | tf_op jit(solution)/shard_map/project/pallas_call | solution.py:33
  92.1 4.0 %all-to-all-start.1 = ((bf16[4,256,256]{2,1,0:T(8,128)(2,1)}), bf16[4,256,256]{2,1,0:T(8,128)(2,1)S(1)}, u32[]{:S(2)}, u32[]{:S(2)}) async-start(bf16[4,256,256]{2,1,0:T(8,128)(2,1)} %copy-done.14), calls=%async_computation.1 | async-start | bytes 1048576 | tf_op jit(solution)/shard_map/all_to_all | solution.py:293
  96.7 3.4 %collective-permute-done.5.refs_0_ = bf16[1024,256]{1,0:T(8,128)(2,1)} collective-permute-done((bf16[1024,256]{1,0:T(8,128)(2,1)}, bf16[1024,256]{1,0:T(8,128)(2,1)}, u32[]{:S(2)}, u32[]{:S(2)}) %collective-permute-start.5) | collective-permute-done | bytes 524320 | tf_op jit(solution)/shard_map/ppermute | solution.py:302
  103.2 2.3 %attend_remote.4 = (f32[128,1024]{1,0:T(8,128)S(1)}, f32[128,1024]{1,0:T(8,128)S(1)}, f32[128,1024]{1,0:T(8,128)S(1)}) custom-call(bf16[256,2048]{1,0:T(8,128)(2,1)S(1)} %bitcast.16, bf16[1024,256]{1,0:T(8,128)(2,1)} %collective-permute-done.5.refs_0_, f32[128,1024]{1,0:T(8,128)S(1)} %copy-done.34, f32[128,1024]{1,0:T(8,128)S(1)} %copy-done.13, ...), custom_call_target="tpu_custom_call" | custom-call | tf_op jit(solution)/shard_map/attend_remote/pallas_call | solution.py:33
  106.7 2.3 %attend_remote.5 = (f32[128,1024]{1,0:T(8,128)S(1)}, f32[128,1024]{1,0:T(8,128)S(1)}, f32[128,1024]{1,0:T(8,128)S(1)}) custom-call(bf16[256,2048]{1,0:T(8,128)(2,1)S(1)} %bitcast.17, bf16[1024,256]{1,0:T(8,128)(2,1)} %collective-permute-done.5.refs_0_, f32[128,1024]{1,0:T(8,128)S(1)} %copy-done.30, f32[128,1024]{1,0:T(8,128)S(1)} %copy-done.11, ...), custom_call_target="tpu_custom_call" | custom-call | tf_op jit(solution)/shard_map/attend_remote/pallas_call | solution.py:33
  109.0 2.4 %attend_remote.6 = (f32[128,1024]{1,0:T(8,128)S(1)}, f32[128,1024]{1,0:T(8,128)S(1)}, f32[128,1024]{1,0:T(8,128)S(1)}) custom-call(bf16[256,2048]{1,0:T(8,128)(2,1)S(1)} %bitcast.18, bf16[1024,256]{1,0:T(8,128)(2,1)} %collective-permute-done.5.refs_0_, f32[128,1024]{1,0:T(8,128)S(1)} %copy-done.26, f32[128,1024]{1,0:T(8,128)S(1)} %copy-done.9, ...), custom_call_target="tpu_custom_call" | custom-call | tf_op jit(solution)/shard_map/attend_remote/pallas_call | solution.py:33
  111.5 2.3 %attend_remote.7 = (f32[128,1024]{1,0:T(8,128)S(1)}, f32[128,1024]{1,0:T(8,128)S(1)}, f32[128,1024]{1,0:T(8,128)S(1)}) custom-call(bf16[256,2048]{1,0:T(8,128)(2,1)S(1)} %bitcast.19, bf16[1024,256]{1,0:T(8,128)(2,1)} %collective-permute-done.5.refs_0_, f32[128,1024]{1,0:T(8,128)S(1)} %copy-done.22, f32[128,1024]{1,0:T(8,128)S(1)} %copy-done.7, ...), custom_call_target="tpu_custom_call" | custom-call | tf_op jit(solution)/shard_map/attend_remote/pallas_call | solution.py:33
  113.8 1.8 %attend_own.4 = (f32[128,1024]{1,0:T(8,128)S(1)}, f32[128,1024]{1,0:T(8,128)S(1)}, bf16[128,1024]{1,0:T(8,128)(2,1)S(1)}) custom-call(bf16[256,2048]{1,0:T(8,128)(2,1)S(1)} %bitcast.20, bf16[4,256,256]{2,1,0:T(8,128)(2,1)} %all-to-all-done.2.key_ref, f32[128,128]{1,0:T(8,128)S(1)} %copy-done.17, f32[128,128]{1,0:T(8,128)S(1)} %copy-done.18, ...), custom_call_target="tpu_custom_call" | custom-call | tf_op jit(solution)/shard_map/attend_own/pallas_call | solution.py:33
  115.6 1.9 %attend_own.5 = (f32[128,1024]{1,0:T(8,128)S(1)}, f32[128,1024]{1,0:T(8,128)S(1)}, bf16[128,1024]{1,0:T(8,128)(2,1)S(1)}) custom-call(bf16[256,2048]{1,0:T(8,128)(2,1)S(1)} %bitcast.21, bf16[4,256,256]{2,1,0:T(8,128)(2,1)} %all-to-all-done.2.key_ref, f32[128,128]{1,0:T(8,128)S(1)} %copy-done.17, f32[128,128]{1,0:T(8,128)S(1)} %copy-done.18, ...), custom_call_target="tpu_custom_call" | custom-call | tf_op jit(solution)/shard_map/attend_own/pallas_call | solution.py:33
  117.5 2.1 %attend_own.6 = (f32[128,1024]{1,0:T(8,128)S(1)}, f32[128,1024]{1,0:T(8,128)S(1)}, bf16[128,1024]{1,0:T(8,128)(2,1)S(1)}) custom-call(bf16[256,2048]{1,0:T(8,128)(2,1)S(1)} %bitcast.22, bf16[4,256,256]{2,1,0:T(8,128)(2,1)} %all-to-all-done.2.key_ref, f32[128,128]{1,0:T(8,128)S(1)} %copy-done.17, f32[128,128]{1,0:T(8,128)S(1)} %copy-done.18, ...), custom_call_target="tpu_custom_call" | custom-call | tf_op jit(solution)/shard_map/attend_own/pallas_call | solution.py:33
  122.0 1.9 %attend_own.7 = (f32[128,1024]{1,0:T(8,128)S(1)}, f32[128,1024]{1,0:T(8,128)S(1)}, bf16[128,1024]{1,0:T(8,128)(2,1)S(1)}) custom-call(bf16[256,2048]{1,0:T(8,128)(2,1)S(1)} %bitcast.23, bf16[4,256,256]{2,1,0:T(8,128)(2,1)} %all-to-all-done.2.key_ref, f32[128,128]{1,0:T(8,128)S(1)} %copy-done.17, f32[128,128]{1,0:T(8,128)S(1)} %copy-done.18, ...), custom_call_target="tpu_custom_call" | custom-call | tf_op jit(solution)/shard_map/attend_own/pallas_call | solution.py:33
  (121 shorter events, 43.6 us)
Async XLA Ops:
  3.1 5.3 %copy-start = (bf16[1,2,128,2048]{3,2,1,0:T(8,128)(2,1)S(1)}, bf16[1,2,128,2048]{3,2,1,0:T(8,128)(2,1)}, u32[]{:S(2)}) copy-start(bf16[1,2,128,2048]{3,2,1,0:T(8,128)(2,1)} %param.10) | copy-start | bytes 3145732
  3.1 5.3 %copy-start.4 = (bf16[1,512,256]{2,1,0:T(8,128)(2,1)S(1)}, bf16[1,512,256]{2,1,0:T(8,128)(2,1)}, u32[]{:S(2)}) copy-start(bf16[1,512,256]{2,1,0:T(8,128)(2,1)} %param.11) | copy-start | bytes 786436
  3.1 30.2 %all-to-all-start = ((bf16[4,256,1024]{2,1,0:T(8,128)(2,1)}), bf16[4,256,1024]{2,1,0:T(8,128)(2,1)S(1)}, u32[]{:S(2)}, u32[]{:S(2)}) async-start(bf16[4,256,1024]{2,1,0:T(8,128)(2,1)} %copy-done.3), calls=%async_computation | async-start | bytes 4194304 | tf_op jit(solution)/shard_map/all_to_all | solution.py:293
  34.6 36.4 %collective-permute-start.3 = (bf16[4,256,1024]{2,1,0:T(8,128)(2,1)}, bf16[4,256,1024]{2,1,0:T(8,128)(2,1)}, u32[]{:S(2)}, u32[]{:S(2)}) collective-permute-start(bf16[4,256,1024]{2,1,0:T(8,128)(2,1)} %after.3.refs_4_), channel_id=1, source_target_pairs={{0,1},{1,0},{2,3},{3,2},{4,5},{5,4},{6,7},{7,6},{8,9},{9,8},{10,11... | collective-permute-start | bytes 6291464 | tf_op jit(solution)/shard_map/ppermute | solution.py:331
  37.5 33.5 %copy-start.2 = (bf16[4,256,1024]{2,1,0:T(8,128)(2,1)S(1)}, bf16[4,256,1024]{2,1,0:T(8,128)(2,1)}, u32[]{:S(2)}) copy-start(bf16[4,256,1024]{2,1,0:T(8,128)(2,1)} %after.3.refs_4_) | copy-start | bytes 6291460
  37.5 15.3 %collective-permute-start = (bf16[2,512,256]{2,1,0:T(8,128)(2,1)}, bf16[2,512,256]{2,1,0:T(8,128)(2,1)}, u32[]{:S(2)}, u32[]{:S(2)}) collective-permute-start(bf16[2,512,256]{2,1,0:T(8,128)(2,1)} %pack_weights.1.refs_0_), channel_id=1, source_target_pairs={{0,8},{8,12},{12,4},{4,0},{1,9},{9,13},{13,5},{5,1},{2,10},{10,14}... | collective-permute-start | bytes 1572872 | tf_op jit(solution)/shard_map/ppermute | solution.py:297
  40.3 25.6 %collective-permute-start.1 = (bf16[2,512,256]{2,1,0:T(8,128)(2,1)}, bf16[2,512,256]{2,1,0:T(8,128)(2,1)}, u32[]{:S(2)}, u32[]{:S(2)}) collective-permute-start(bf16[2,512,256]{2,1,0:T(8,128)(2,1)} %pack_weights.1.refs_0_), channel_id=1, source_target_pairs={{8,0},{12,8},{4,12},{0,4},{9,1},{13,9},{5,13},{1,5},{10,2},{14,10}... | collective-permute-start | bytes 1572872 | tf_op jit(solution)/shard_map/ppermute | solution.py:297
  54.6 16.4 %collective-permute-start.4 = (bf16[512,256]{1,0:T(8,128)(2,1)S(1)}, bf16[512,256]{1,0:T(8,128)(2,1)S(1)}, u32[]{:S(2)}, u32[]{:S(2)}) collective-permute-start(bf16[512,256]{1,0:T(8,128)(2,1)S(1)} %get-tuple-element.77), channel_id=1, source_target_pairs={{0,8},{8,12},{12,4},{4,0},{1,9},{9,13},{13,5},{5,1},{2,10},{10,14}... | collective-permute-start | bytes 786440 | tf_op jit(solution)/shard_map/ppermute | solution.py:323
  75.2 16.9 %all-to-all-start.2 = ((bf16[4,256,256]{2,1,0:T(8,128)(2,1)}), bf16[4,256,256]{2,1,0:T(8,128)(2,1)}, u32[]{:S(2)}, u32[]{:S(2)}) async-start(bf16[4,256,256]{2,1,0:T(8,128)(2,1)} %copy-done.15), calls=%async_computation.2 | async-start | bytes 1048576 | tf_op jit(solution)/shard_map/all_to_all | solution.py:293
  79.4 8.5 %collective-permute-start.2 = (bf16[512,256]{1,0:T(8,128)(2,1)}, bf16[512,256]{1,0:T(8,128)(2,1)S(1)}, u32[]{:S(2)}, u32[]{:S(2)}) collective-permute-start(bf16[512,256]{1,0:T(8,128)(2,1)} %get-tuple-element.78), channel_id=1, source_target_pairs={{0,8},{8,12},{12,4},{4,0},{1,9},{9,13},{13,5},{5,1},{2,10},{10,14}... | collective-permute-start | bytes 786440 | tf_op jit(solution)/shard_map/ppermute | solution.py:323
  82.8 17.3 %collective-permute-start.5 = (bf16[1024,256]{1,0:T(8,128)(2,1)}, bf16[1024,256]{1,0:T(8,128)(2,1)}, u32[]{:S(2)}, u32[]{:S(2)}) collective-permute-start(bf16[1024,256]{1,0:T(8,128)(2,1)} %pad_maximum_fusion), channel_id=1, source_target_pairs={{0,2},{2,0},{1,3},{3,1},{4,6},{6,4},{5,7},{7,5},{8,10},{10,8},{9,1... | collective-permute-start | bytes 1572872 | tf_op jit(solution)/shard_map/ppermute | solution.py:302
  92.1 13.4 %copy-start.11 = (f32[128,1024]{1,0:T(8,128)S(1)}, f32[128,1024]{1,0:T(8,128)}, u32[]{:S(2)}) copy-start(f32[128,1024]{1,0:T(8,128)} %copy-done.10) | copy-start | bytes 1572868
  92.1 13.4 %copy-start.30 = (f32[128,1024]{1,0:T(8,128)S(1)}, f32[128,1024]{1,0:T(8,128)}, u32[]{:S(2)}) copy-start(f32[128,1024]{1,0:T(8,128)} %copy-done.29) | copy-start | bytes 1572868
  92.1 34.1 %all-to-all-start.1 = ((bf16[4,256,256]{2,1,0:T(8,128)(2,1)}), bf16[4,256,256]{2,1,0:T(8,128)(2,1)S(1)}, u32[]{:S(2)}, u32[]{:S(2)}) async-start(bf16[4,256,256]{2,1,0:T(8,128)(2,1)} %copy-done.14), calls=%async_computation.1 | async-start | bytes 1048576 | tf_op jit(solution)/shard_map/all_to_all | solution.py:293
  105.5 3.5 %copy-start.9 = (f32[128,1024]{1,0:T(8,128)S(1)}, f32[128,1024]{1,0:T(8,128)}, u32[]{:S(2)}) copy-start(f32[128,1024]{1,0:T(8,128)} %copy-done.8) | copy-start | bytes 1572868
  105.5 3.5 %copy-start.26 = (f32[128,1024]{1,0:T(8,128)S(1)}, f32[128,1024]{1,0:T(8,128)}, u32[]{:S(2)}) copy-start(f32[128,1024]{1,0:T(8,128)} %copy-done.25) | copy-start | bytes 1572868
  105.5 3.5 %copy-start.28 = (f32[128,1024]{1,0:T(8,128)S(1)}, f32[128,1024]{1,0:T(8,128)}, u32[]{:S(2)}) copy-start(f32[128,1024]{1,0:T(8,128)} %copy-done.27) | copy-start | bytes 1572868
  109.0 2.5 %copy-start.7 = (f32[128,1024]{1,0:T(8,128)S(1)}, f32[128,1024]{1,0:T(8,128)}, u32[]{:S(2)}) copy-start(f32[128,1024]{1,0:T(8,128)} %copy-done.6) | copy-start | bytes 1572868
  109.0 2.5 %copy-start.22 = (f32[128,1024]{1,0:T(8,128)S(1)}, f32[128,1024]{1,0:T(8,128)}, u32[]{:S(2)}) copy-start(f32[128,1024]{1,0:T(8,128)} %copy-done.21) | copy-start | bytes 1572868
  109.0 2.5 %copy-start.24 = (f32[128,1024]{1,0:T(8,128)S(1)}, f32[128,1024]{1,0:T(8,128)}, u32[]{:S(2)}) copy-start(f32[128,1024]{1,0:T(8,128)} %copy-done.23) | copy-start | bytes 1572868
  111.4 2.4 %copy-start.17 = (f32[128,128]{1,0:T(8,128)S(1)}, f32[128,128]{1,0:T(8,128)}, u32[]{:S(2)}) copy-start(f32[128,128]{1,0:T(8,128)} %constant.10.clone.cos_ref) | copy-start | bytes 196612
  111.4 2.4 %copy-start.18 = (f32[128,128]{1,0:T(8,128)S(1)}, f32[128,128]{1,0:T(8,128)}, u32[]{:S(2)}) copy-start(f32[128,128]{1,0:T(8,128)} %constant.11.clone.sin_ref) | copy-start | bytes 196612
  117.5 4.5 %copy-start.37 = (f32[128,1024]{1,0:T(8,128)}, f32[128,1024]{1,0:T(8,128)S(1)}, u32[]{:S(2)}) copy-start(f32[128,1024]{1,0:T(8,128)S(1)} %get-tuple-element.59.refs_4_) | copy-start | bytes 1572868
  117.5 4.5 %copy-start.47 = (bf16[128,1024]{1,0:T(8,128)(2,1)}, bf16[128,1024]{1,0:T(8,128)(2,1)S(1)}, u32[]{:S(2)}) copy-start(bf16[128,1024]{1,0:T(8,128)(2,1)S(1)} %get-tuple-element.60.refs_5_) | copy-start | bytes 786436
  (38 other events, 35.5 us)

commit v4 on v3

v4 whole, which is shorter than its diff:
```python
import functools
import math

import jax
import jax.numpy as jnp
import numpy as np
from jax import lax
from jax.experimental import pallas as pl
from jax.experimental.pallas import tpu as pltpu
from jax.sharding import PartitionSpec as P

HD = 128
PLEN = 1024
FACTOR = HD**-0.5 * math.log2(math.e)
MIB = 1 << 20
VMEM = pl.BlockSpec(memory_space=pltpu.VMEM)
SMEM = pl.BlockSpec(memory_space=pltpu.SMEM)
ANYWHERE = pl.BlockSpec(memory_space=pl.ANY)


def dot_nt(a, b):
    return lax.dot_general(a, b, (((1,), (1,)), ((), ())), preferred_element_type=jnp.float32)


def dot_nn(a, b):
    return lax.dot_general(a, b, (((1,), (0,)), ((), ())), preferred_element_type=jnp.float32)


def call(name, body, operands, shapes, scratch=(), first=VMEM, waits=(), limit=8):
    count = len(operands)
    specs = [first] + [VMEM] * (count - 1) + [ANYWHERE] * len(waits)
    kernel = body
    if waits:

        def kernel(*refs):
            body(*refs[:count], *refs[count + len(waits) :])

    return pl.pallas_call(
        kernel,
        in_specs=specs,
        out_specs=[VMEM] * len(shapes),
        out_shape=shapes,
        scratch_shapes=list(scratch),
        compiler_params=pltpu.CompilerParams(vmem_limit_bytes=limit * MIB),
        cost_estimate=pl.CostEstimate(
            flops=0, bytes_accessed=0, transcendentals=0
        ),
        name=name,
    )(*operands, *waits)


def after(value, *earlier):
    return pl.pallas_call(
        lambda *refs: None,
        in_specs=[ANYWHERE] * (1 + len(earlier)),
        out_specs=ANYWHERE,
        out_shape=jax.ShapeDtypeStruct(value.shape, value.dtype),
        input_output_aliases={0: 0},
        compiler_params=pltpu.CompilerParams(vmem_limit_bytes=MIB),
        cost_estimate=pl.CostEstimate(flops=0, bytes_accessed=0, transcendentals=0),
        name="after",
    )(value, *earlier)


def pack_weights(n_groups, key_weight, value_weight):
    block, columns = key_weight.shape
    half = block // n_groups

    def body(key_ref, value_ref, out_ref):
        first = pl.multiple_of(lax.axis_index("groups") * half, half)
        out_ref[0] = key_ref[pl.ds(first, half), :]
        out_ref[1] = value_ref[pl.ds(first, half), :]

    shape = jax.ShapeDtypeStruct((2, half, columns), key_weight.dtype)
    return call("pack_weights", body, [key_weight, value_weight], [shape])[0]


def pack_features(sizes, block, hidden):
    n_groups, n_fsdp, n_resp, n_tp = sizes
    rows = hidden.shape[0]
    per_run = n_fsdp // n_tp // 2
    half = block // n_groups
    targets = [(group, resp) for group in range(n_groups) for resp in range(n_resp)]

    def body(hidden_ref, *outs):
        for run, out_ref in enumerate(outs):
            for n, (group, resp) in enumerate(targets):
                for k in range(per_run):
                    start = ((run * per_run + k) * n_resp + resp) * block + group * half
                    out_ref[n, :, k * half : (k + 1) * half] = hidden_ref[:, start : start + half]

    shape = jax.ShapeDtypeStruct((len(targets), rows, per_run * half), hidden.dtype)
    return call("pack_features", body, [hidden], [shape] * 2, limit=16)


def line_ring(size):
    return list(range(0, size, 2)) + list(range(1, size, 2))[::-1]


def rows_of(core, run, depth, runs):
    start = (core * runs + run) * depth
    return pl.ds(pl.multiple_of(start, depth), depth)


def project_early(n_fsdp, chunk, features, pieces):
    count, rows, depth = features[0][0].shape
    half, columns = pieces[0][0].shape[-2:]
    total = len(pieces)

    def body(*refs):
        piece_refs, feature_refs = refs[:total], refs[total:-2]
        weight_ref, out_ref = refs[-2:]
        fsdp, core = lax.axis_index("fsdp"), lax.axis_index("tp")
        place = jnp.where(fsdp % 2 == 0, fsdp // 2, n_fsdp - (fsdp + 1) // 2)
        for ref, (_, distance) in zip(piece_refs, pieces):
            at = (place - distance + n_fsdp) % n_fsdp
            owner = jnp.where(at < n_fsdp // 2, 2 * at, 2 * n_fsdp - 1 - 2 * at)
            value = ref[chunk] if len(ref.shape) == 3 else ref[...]
            weight_ref[pl.ds(pl.multiple_of(owner * half, half), half), :] = value
        for n in range(count):
            out = None
            for ref, (_, other, run) in zip(feature_refs, features):
                whose = 1 - core if other else core
                part = dot_nn(ref[n], weight_ref[rows_of(whose, run, depth, 2), :])
                out = part if out is None else out + part
            out_ref[n] = out

    return call(
        "project_early",
        body,
        [x for x, _ in pieces] + [x for x, _, _ in features],
        [
            jax.ShapeDtypeStruct((n_fsdp * half, columns), pieces[0][0].dtype),
            jax.ShapeDtypeStruct((count, rows, columns), jnp.float32),
        ],
    )


def project_late(feature, weight, started):
    array, other, run = feature
    count, rows, depth = array.shape
    columns = weight.shape[1]

    def body(array_ref, weight_ref, started_ref, out_ref):
        core = lax.axis_index("tp")
        whose = 1 - core if other else core
        for n in range(count):
            out = dot_nn(array_ref[n], weight_ref[rows_of(whose, run, depth, 2), :])
            out_ref[n] = (out + started_ref[n]).astype(out_ref.dtype)

    shape = jax.ShapeDtypeStruct((count, rows, columns), weight.dtype)
    return call("project_late", body, [array, weight, started], [shape])[0]


class Place:
    def __init__(self, slot, head, tokens, group_size):
        self.slot = slot
        self.rows = slice(slot * tokens, (slot + 1) * tokens)
        self.lanes = slice(head * HD, (head + 1) * HD)
        self.tokens = tokens
        self.group_size = group_size
        self.first = head * group_size
        self.wide = jax.ShapeDtypeStruct((tokens, group_size * HD), jnp.float32)

    def queries(self, ref, first, count):
        heads = [self.first + first + n for n in range(count)]
        return jnp.concatenate([ref[self.rows, h * HD : (h + 1) * HD] for h in heads], axis=0)

    def take(self, ref, first, count):
        heads = [first + n for n in range(count)]
        return jnp.concatenate([ref[:, h * HD : (h + 1) * HD] for h in heads], axis=0)

    def put(self, ref, first, count, value):
        value = jnp.broadcast_to(value, (count * self.tokens, HD)).astype(ref.dtype)
        for n in range(count):
            lanes = slice((first + n) * HD, (first + n + 1) * HD)
            ref[:, lanes] = value[n * self.tokens : (n + 1) * self.tokens]


def widest(group_size, most):
    return max(n for n in range(1, most + 1) if group_size % n == 0)


def attend_cache(place, queries, caches, waits):
    count = len(caches)
    step = widest(place.group_size, 2)

    def body(q_ref, *refs):
        acc_ref, top_ref, total_ref = refs[-3:]
        keys = [ref[:, place.lanes] for ref in refs[:count]]
        values = [ref[:, place.lanes] for ref in refs[count : 2 * count]]
        wide = [jnp.concatenate([v, jnp.ones(v.shape, v.dtype)], axis=1) for v in values]

        def scores_of(first):
            q = place.queries(q_ref, first, step)
            return [dot_nt(q, k) for k in keys]

        coming = scores_of(0)
        for first in range(0, place.group_size, step):
            scores = coming
            if first + step < place.group_size:
                coming = scores_of(first + step)
            tops = [s[:, n * HD : (n + 1) * HD] for s in scores for n in range(s.shape[1] // HD)]
            top = jnp.max(functools.reduce(jnp.maximum, tops), axis=1, keepdims=True)
            out = None
            for s, v in zip(scores, wide):
                probs = jnp.exp2((s - top) * FACTOR).astype(jnp.bfloat16)
                part = dot_nn(probs, v)
                out = part if out is None else out + part
            place.put(acc_ref, first, step, out[:, :HD])
            place.put(top_ref, first, step, top)
            place.put(total_ref, first, step, out[:, HD:])

    operands = [queries, *[k for k, _ in caches], *[v for _, v in caches]]
    return call("attend_cache", body, operands, [place.wide] * 3, waits=waits, limit=16)


def sum_parts(ref, rows, lanes):
    total = ref[0, rows, lanes].astype(jnp.float32)
    for n in range(1, ref.shape[0]):
        total = total + ref[n, rows, lanes].astype(jnp.float32)
    return total


def attend_own(place, queries, key_parts, tables, state):
    tokens = place.tokens
    count = place.group_size

    def body(q_ref, key_ref, cos_ref, sin_ref, old_acc, old_tops, old_total, *outs):
        acc_ref, inverse_ref, probs_ref = outs
        key = sum_parts(key_ref, place.rows, place.lanes)
        key = key * cos_ref[...] + pltpu.roll(key, HD // 2, 1) * sin_ref[...]
        key = key.astype(jnp.bfloat16)
        ones = jnp.ones((tokens, HD), jnp.bfloat16)
        row = lax.broadcasted_iota(jnp.int32, (tokens, tokens), 0)
        causal = row >= lax.broadcasted_iota(jnp.int32, (tokens, tokens), 1)
        causal = jnp.concatenate([causal] * count, axis=0)
        scores = jnp.where(causal, dot_nt(place.queries(q_ref, 0, count), key), -1e30)
        old_top = place.take(old_tops, 0, count)
        top = jnp.max(jnp.maximum(old_top, scores), axis=1, keepdims=True)
        probs = jnp.exp2((scores - top) * FACTOR).astype(jnp.bfloat16)
        shrink = jnp.exp2((old_top - top) * FACTOR)
        total = place.take(old_total, 0, count) * shrink + dot_nn(probs, ones)
        inverse = 1.0 / total
        place.put(acc_ref, 0, count, place.take(old_acc, 0, count) * (shrink * inverse))
        place.put(inverse_ref, 0, count, inverse)
        place.put(probs_ref, 0, count, probs)

    probs = jax.ShapeDtypeStruct(place.wide.shape, jnp.bfloat16)
    operands = [queries, key_parts, *tables, *state]
    return call("attend_own", body, operands, [place.wide, place.wide, probs], limit=16)


def finish(live, value_parts, states, places, shape, dtype):
    def body(live_ref, value_ref, *refs):
        out_ref = refs[-1]
        for n, place in enumerate(places):
            alive = place.slot < live_ref[0]
            acc_ref, inverse_ref, probs_ref = refs[3 * n : 3 * n + 3]
            value = sum_parts(value_ref, place.rows, place.lanes).astype(jnp.bfloat16)
            count = place.group_size
            part = dot_nn(place.take(probs_ref, 0, count), value)
            result = place.take(acc_ref, 0, count) + part * place.take(inverse_ref, 0, count)
            result = jnp.where(alive, result, 0.0).astype(dtype)
            for k in range(count):
                lanes = slice((place.first + k) * HD, (place.first + k + 1) * HD)
                out_ref[place.rows, lanes] = result[k * place.tokens : (k + 1) * place.tokens]

    operands = [live, value_parts, *[x for state in states for x in state]]
    shapes = [jax.ShapeDtypeStruct(shape, dtype)]
    return call("finish", body, operands, shapes, first=SMEM, limit=16)[0]


def rotation_tables(extent, offset):
    orders = np.arange(HD // 2, dtype=np.float64)
    inverse = np.exp(-(2.0 * orders / HD) * math.log(500000.0))
    angles = (offset + np.arange(extent))[:, None] * inverse[None, :]
    cosine, sine = np.cos(angles), np.sin(angles)
    return (
        jnp.asarray(np.concatenate([cosine, cosine], axis=1), jnp.float32),
        jnp.asarray(np.concatenate([-sine, sine], axis=1), jnp.float32),
    )


def on_device(sizes, hidden, queries, prompt_keys, prompt_values, key_weight, value_weight, counts):
    n_groups, n_fsdp, n_resp, n_tp = sizes
    _, slots, tokens, part_width = hidden.shape
    block, columns = key_weight.shape
    kv_heads = columns // HD
    group_size = queries.shape[3] // columns
    rows = slots * tokens
    plane = ("groups", "resp")
    cores = [(n, (n + 1) % n_tp) for n in range(n_tp)]
    ring = line_ring(n_fsdp)
    rightward = [(ring[n], ring[(n + 1) % n_fsdp]) for n in range(n_fsdp)]
    leftward = [(b, a) for a, b in rightward]

    def exchange(parts):
        return lax.all_to_all(parts, plane, split_axis=0, concat_axis=0, tiled=True)

    caches = [(prompt_keys[0], prompt_values[0])]
    for b in range(1, n_resp):
        around = [(n, (n + b) % n_resp) for n in range(n_resp)]
        caches.append(tuple(lax.ppermute(x, "resp", around) for x in caches[0]))

    share = pack_weights(n_groups, key_weight, value_weight)
    hops = {1: lax.ppermute(share, "fsdp", rightward), -1: lax.ppermute(share, "fsdp", leftward)}

    near = [exchange(x) for x in pack_features(sizes, block, hidden.reshape(rows, part_width))]

    pieces = [(share, 0)]
    held = hops[1]
    pieces.append((held, 1))
    for hop in range(2, n_fsdp // 2):
        held = lax.ppermute(held, "fsdp", rightward)
        pieces.append((held, hop))
    last = [lax.ppermute(held[chunk], "fsdp", rightward) for chunk in range(2)]
    held = hops[-1]
    pieces.append((held, -1))
    for hop in range(2, n_fsdp - n_fsdp // 2):
        held = lax.ppermute(held, "fsdp", leftward)
        pieces.append((held, -hop))

    flat_queries = queries.reshape(rows, queries.shape[3])
    places = [
        Place(slot, head, tokens, group_size) for slot in range(slots) for head in range(kv_heads)
    ]
    states = [attend_cache(p, flat_queries, caches, [hops[1]]) for p in places]
    near[0] = after(near[0], *[state[1] for state in states])
    far = [lax.ppermute(x, "tp", cores) for x in near]

    sums = []
    for chunk in range(2):
        features = [(near[0], False, 0), (far[0], True, 0), (near[1], False, 1)]
        whole = [*pieces, (last[chunk], n_fsdp // 2)]
        weight, started = project_early(n_fsdp, chunk, features, whole)
        sums.append(exchange(project_late((far[1], True, 1), weight, started)))

    tables = rotation_tables(tokens, PLEN)
    states = [
        attend_own(p, flat_queries, sums[0], tables, state) for p, state in zip(places, states)
    ]
    live = (counts[0] - lax.axis_index("resp") * slots).astype(jnp.int32)[None]
    out = finish(live, sums[1], states, places, flat_queries.shape, queries.dtype)
    return out.reshape(queries.shape)


def solution(mesh):
    placed = (
        P(("groups", "fsdp"), "resp", None, "tp"),
        P(("groups", "fsdp"), "resp", None, "tp"),
        P(("groups", "fsdp"), "resp", "tp"),
        P(("groups", "fsdp"), "resp", "tp"),
        P(("fsdp", "resp"), "tp"),
        P(("fsdp", "resp"), "tp"),
        P(("groups", "fsdp")),
    )
    sizes = tuple(mesh.shape[name] for name in ("groups", "fsdp", "resp", "tp"))
    return jax.shard_map(
        functools.partial(on_device, sizes),
        mesh=mesh,
        in_specs=placed,
        out_specs=P(("groups", "fsdp"), "resp", None, "tp"),
        check_vma=False,
    )
```

time: 137 us -> 140 us (1.022)
  blocking collectives: 0 us -> 19.2 us
  Pallas kernels: 30.1 us -> 19.5 us
  local copies, waits for them, and re-layouts: 37.3 us -> 35.5 us
  other arithmetic: 1.77 us -> 0 us
    all_to_all x0 -> x1, blocking collectives: none -> 19.2 us  [exchange(): return lax.all_to_all(parts, plane, split_axis=0, concat_axis=0, tiled=True)]
    ppermute x2 -> x4, waiting for transfers between devices: 3.39 us -> 17.8 us  [the longest x2 17.8 us: on_device(): caches.append(tuple((lax.ppermute(x, 'resp', around) for x in caches[0])))]
    ppermute x1, waiting for transfers between devices: 12.6 us -> 0.01 us  [on_device(): lax.ppermute(share, 'fsdp', rightward)]
    pallas_call x17 -> x15, Pallas kernels: 30.1 us -> 19.5 us  [call(): pl.pallas_call(kernel, in_specs=specs, out_specs=[VMEM] * len(shapes), ou...]
    all_to_all x3, waiting for transfers between devices: 10.3 us -> 0.01 us  [exchange(): return lax.all_to_all(parts, plane, split_axis=0, concat_axis=0, tiled=True)]
    ppermute x1, waiting for transfers between devices: 7.88 us -> 11.8 us  [on_device(): lax.ppermute(share, 'fsdp', leftward)]
    ppermute x2, waiting for transfers between devices: 8.21 us -> 12.1 us  [on_device(): last = [lax.ppermute(held[chunk], 'fsdp', rightward) for chunk in range(2)]]
    ppermute x2, starting transfers between devices: 5.05 us -> 3.13 us  [on_device(): last = [lax.ppermute(held[chunk], 'fsdp', rightward) for chunk in range(2)]]
  transfers between devices with their start and end apart: 9 -> 11, of which waited for: 6 -> 5; matrix products, arithmetic and copies ran while one was open for 3% -> 0% of each run, Pallas kernels for 18% -> 11%
where the time goes in v4:
time: 140 us; the launch traced here: 139 us
  waiting for transfers between devices  41.7 us (30%)
  local copies, waits for them, and re-layouts  35.5 us (25%)
  starting transfers between devices  22.1 us (16%)
  Pallas kernels  19.5 us (14%)
  blocking collectives  19.2 us (14%)
    unnamed x122, local copies, waits for them, and re-layouts  35.4 us
    pallas_call x15, Pallas kernels, call(): pl.pallas_call(kernel, in_specs=specs, out_specs=[VMEM] * len(shapes), ou...  19.5 us
    all_to_all x1, blocking collectives, exchange(): return lax.all_to_all(parts, plane, split_axis=0, concat_axis=0, tiled=True)  19.2 us
    ppermute x2, waiting for transfers between devices, on_device(): caches.append(tuple((lax.ppermute(x, 'resp', around) for x in caches[0])))  17.8 us
    all_to_all x3, starting transfers between devices, exchange(): return lax.all_to_all(parts, plane, split_axis=0, concat_axis=0, tiled=True)  12.2 us
    ppermute x2, waiting for transfers between devices, on_device(): last = [lax.ppermute(held[chunk], 'fsdp', rightward) for chunk in range(2)]  12.1 us
    ppermute x1, waiting for transfers between devices, on_device(): lax.ppermute(share, 'fsdp', leftward)  11.8 us
    ppermute x2, starting transfers between devices, on_device(): last = [lax.ppermute(held[chunk], 'fsdp', rightward) for chunk in range(2)]  3.13 us
  transfers between devices with their start and end apart: 11, of which 5 were waited for; matrix products, arithmetic and copies ran while one was open for 0% of the time, Pallas kernels for 11%

profile of v4, /device:TPU:0, one launch (start us, length us, event | category | flops | bytes accessed | tf_op | source)
XLA Modules:
  0.0 139.1 jit_solution(13448383807411902252)
XLA Ops:
  0.0 1.6 %copy-done.10 = bf16[1,2,128,4096]{3,2,1,0:T(8,128)(2,1)S(1)} copy-done((bf16[1,2,128,4096]{3,2,1,0:T(8,128)(2,1)S(1)}, bf16[1,2,128,4096]{3,2,1,0:T(8,128)(2,1)}, u32[]{:S(2)}) %copy-start.10) | copy-done | bytes 2097176
  1.6 1.1 pack_features.1
  2.7 19.2 %all_to_all.20.refs_0_ = bf16[4,256,512]{2,1,0:T(8,128)(2,1)S(1)} all-to-all(bf16[4,256,512]{2,1,0:T(8,128)(2,1)S(1)} %get-tuple-element.36), channel_id=1, replica_groups=mesh['groups'=2,'fsdp'=4,'resp'=2,'tp'=2] {'groups','resp'}, dimensions={0} | all-to-all | bytes 2097152 | tf_op jit(solution)/shard_map/all_to_all | solution.py:299
  22.0 4.4 %all-to-all-start = ((bf16[4,256,512]{2,1,0:T(8,128)(2,1)}), bf16[4,256,512]{2,1,0:T(8,128)(2,1)}, u32[]{:S(2)}, u32[]{:S(2)}) async-start(bf16[4,256,512]{2,1,0:T(8,128)(2,1)} %get-tuple-element.35), calls=%async_computation | async-start | bytes 2097152 | tf_op jit(solution)/shard_map/all_to_all | solution.py:299
  27.4 2.6 %collective-permute-start.1 = (bf16[2,512,256]{2,1,0:T(8,128)(2,1)S(1)}, bf16[2,512,256]{2,1,0:T(8,128)(2,1)S(1)}, u32[]{:S(2)}, u32[]{:S(2)}) collective-permute-start(bf16[2,512,256]{2,1,0:T(8,128)(2,1)S(1)} %pack_weights.1.refs_0_), channel_id=1, source_target_pairs={{0,8},{8,12},{12,4},{4,0},{1,9},{9,13},{13,5},{5,1},{2,10},{10,14}... | collective-permute-start | bytes 1572872 | tf_op jit(solution)/shard_map/ppermute | solution.py:307
  30.1 2.0 %collective-permute-start.4 = (bf16[512,256]{1,0:T(8,128)(2,1)S(1)}, bf16[512,256]{1,0:T(8,128)(2,1)S(1)}, u32[]{:S(2)}, u32[]{:S(2)}) collective-permute-start(bf16[512,256]{1,0:T(8,128)(2,1)S(1)} %bitcast.20), channel_id=1, source_target_pairs={{0,2},{2,0},{1,3},{3,1},{4,6},{6,4},{5,7},{7,5},{8,10},{10,8},{9,1... | collective-permute-start | bytes 786440 | tf_op jit(solution)/shard_map/ppermute | solution.py:304
  32.1 14.9 %collective-permute-done.4.refs_2_ = bf16[512,256]{1,0:T(8,128)(2,1)S(1)} collective-permute-done((bf16[512,256]{1,0:T(8,128)(2,1)S(1)}, bf16[512,256]{1,0:T(8,128)(2,1)S(1)}, u32[]{:S(2)}, u32[]{:S(2)}) %collective-permute-start.4) | collective-permute-done | bytes 262176 | tf_op jit(solution)/shard_map/ppermute | solution.py:304
  47.0 2.9 %collective-permute-done.5.refs_4_ = bf16[512,256]{1,0:T(8,128)(2,1)S(1)} collective-permute-done((bf16[512,256]{1,0:T(8,128)(2,1)}, bf16[512,256]{1,0:T(8,128)(2,1)S(1)}, u32[]{:S(2)}, u32[]{:S(2)}) %collective-permute-start.5) | collective-permute-done | bytes 262176 | tf_op jit(solution)/shard_map/ppermute | solution.py:304
  50.9 1.6 %attend_cache.4 = (f32[128,1024]{1,0:T(8,128)S(1)}, f32[128,1024]{1,0:T(8,128)S(1)}, f32[128,1024]{1,0:T(8,128)S(1)}) custom-call(bf16[256,2048]{1,0:T(8,128)(2,1)S(1)} %bitcast.12, bf16[512,256]{1,0:T(8,128)(2,1)S(1)} %bitcast.21, bf16[512,256]{1,0:T(8,128)(2,1)S(1)} %collective-permute-done.4.refs_2_, bf16[512,256]{1,0:T(8,128)(2,1)S(1)} %bitcast.26, ...), custom_call_target="tpu_custom_call" | custom-call | tf_op jit(solution)/shard_map/attend_cache/pallas_call | solution.py:38
  53.2 1.6 %attend_cache.5 = (f32[128,1024]{1,0:T(8,128)S(1)}, f32[128,1024]{1,0:T(8,128)S(1)}, f32[128,1024]{1,0:T(8,128)S(1)}) custom-call(bf16[256,2048]{1,0:T(8,128)(2,1)S(1)} %bitcast.13, bf16[512,256]{1,0:T(8,128)(2,1)S(1)} %bitcast.22, bf16[512,256]{1,0:T(8,128)(2,1)S(1)} %collective-permute-done.4.refs_2_, bf16[512,256]{1,0:T(8,128)(2,1)S(1)} %bitcast.27, ...), custom_call_target="tpu_custom_call" | custom-call | tf_op jit(solution)/shard_map/attend_cache/pallas_call | solution.py:38
  56.4 1.6 %attend_cache.6 = (f32[128,1024]{1,0:T(8,128)S(1)}, f32[128,1024]{1,0:T(8,128)S(1)}, f32[128,1024]{1,0:T(8,128)S(1)}) custom-call(bf16[256,2048]{1,0:T(8,128)(2,1)S(1)} %bitcast.14, bf16[512,256]{1,0:T(8,128)(2,1)S(1)} %bitcast.23, bf16[512,256]{1,0:T(8,128)(2,1)S(1)} %collective-permute-done.4.refs_2_, bf16[512,256]{1,0:T(8,128)(2,1)S(1)} %bitcast.28, ...), custom_call_target="tpu_custom_call" | custom-call | tf_op jit(solution)/shard_map/attend_cache/pallas_call | solution.py:38
  59.6 1.6 %attend_cache.7 = (f32[128,1024]{1,0:T(8,128)S(1)}, f32[128,1024]{1,0:T(8,128)S(1)}, f32[128,1024]{1,0:T(8,128)S(1)}) custom-call(bf16[256,2048]{1,0:T(8,128)(2,1)S(1)} %bitcast.15, bf16[512,256]{1,0:T(8,128)(2,1)S(1)} %bitcast.24, bf16[512,256]{1,0:T(8,128)(2,1)S(1)} %collective-permute-done.4.refs_2_, bf16[512,256]{1,0:T(8,128)(2,1)S(1)} %bitcast.29, ...), custom_call_target="tpu_custom_call" | custom-call | tf_op jit(solution)/shard_map/attend_cache/pallas_call | solution.py:38
  62.9 1.6 %collective-permute-start.2 = (bf16[2,512,256]{2,1,0:T(8,128)(2,1)S(1)}, bf16[2,512,256]{2,1,0:T(8,128)(2,1)S(1)}, u32[]{:S(2)}, u32[]{:S(2)}) collective-permute-start(bf16[2,512,256]{2,1,0:T(8,128)(2,1)S(1)} %pack_weights.1.refs_0_), channel_id=1, source_target_pairs={{8,0},{12,8},{4,12},{0,4},{9,1},{13,9},{5,13},{1,5},{10,2},{14,10}... | collective-permute-start | bytes 1572872 | tf_op jit(solution)/shard_map/ppermute | solution.py:307
  64.5 1.4 %collective-permute-start.7 = (bf16[512,256]{1,0:T(8,128)(2,1)S(1)}, bf16[512,256]{1,0:T(8,128)(2,1)S(1)}, u32[]{:S(2)}, u32[]{:S(2)}) collective-permute-start(bf16[512,256]{1,0:T(8,128)(2,1)S(1)} %get-tuple-element.65), channel_id=1, source_target_pairs={{0,8},{8,12},{12,4},{4,0},{1,9},{9,13},{13,5},{5,1},{2,10},{10,14}... | collective-permute-start | bytes 786440 | tf_op jit(solution)/shard_map/ppermute | solution.py:317
  65.9 11.8 %collective-permute-done.2.refs_2_ = bf16[2,512,256]{2,1,0:T(8,128)(2,1)S(1)} collective-permute-done((bf16[2,512,256]{2,1,0:T(8,128)(2,1)S(1)}, bf16[2,512,256]{2,1,0:T(8,128)(2,1)S(1)}, u32[]{:S(2)}, u32[]{:S(2)}) %collective-permute-start.2) | collective-permute-done | bytes 524320 | tf_op jit(solution)/shard_map/ppermute | solution.py:307
  77.7 5.5 %collective-permute-done.7.refs_3_ = bf16[512,256]{1,0:T(8,128)(2,1)S(1)} collective-permute-done((bf16[512,256]{1,0:T(8,128)(2,1)S(1)}, bf16[512,256]{1,0:T(8,128)(2,1)S(1)}, u32[]{:S(2)}, u32[]{:S(2)}) %collective-permute-start.7) | collective-permute-done | bytes 262176 | tf_op jit(solution)/shard_map/ppermute | solution.py:317
  83.2 2.6 %project_early.3 = (bf16[2048,256]{1,0:T(8,128)(2,1)S(1)}, f32[4,256,256]{2,1,0:T(8,128)S(1)}) custom-call(bf16[2,512,256]{2,1,0:T(8,128)(2,1)S(1)} %pack_weights.1.refs_0_, bf16[2,512,256]{2,1,0:T(8,128)(2,1)S(1)} %collective-permute-done.1.refs_5_.refs_1_, bf16[2,512,256]{2,1,0:T(8,128)(2,1)S(1)} %collective-permute-done.2.refs_2_, ...), custom_call_target="tpu_custom_call" | custom-call | tf_op jit(solution)/shard_map/project_early/pallas_call | solution.py:38
  88.1 3.5 %all-to-all-start.3 = ((bf16[4,256,256]{2,1,0:T(8,128)(2,1)}), bf16[4,256,256]{2,1,0:T(8,128)(2,1)S(1)}, u32[]{:S(2)}, u32[]{:S(2)}) async-start(bf16[4,256,256]{2,1,0:T(8,128)(2,1)} %copy-done.9), calls=%async_computation.3 | async-start | bytes 1048576 | tf_op jit(solution)/shard_map/all_to_all | solution.py:299
  91.6 1.7 %collective-permute-start.3 = (bf16[512,256]{1,0:T(8,128)(2,1)S(1)}, bf16[512,256]{1,0:T(8,128)(2,1)S(1)}, u32[]{:S(2)}, u32[]{:S(2)}) collective-permute-start(bf16[512,256]{1,0:T(8,128)(2,1)S(1)} %get-tuple-element.66), channel_id=1, source_target_pairs={{0,8},{8,12},{12,4},{4,0},{1,9},{9,13},{13,5},{5,1},{2,10},{10,14}... | collective-permute-start | bytes 786440 | tf_op jit(solution)/shard_map/ppermute | solution.py:317
  93.3 6.5 %collective-permute-done.3.refs_3_ = bf16[512,256]{1,0:T(8,128)(2,1)S(1)} collective-permute-done((bf16[512,256]{1,0:T(8,128)(2,1)S(1)}, bf16[512,256]{1,0:T(8,128)(2,1)S(1)}, u32[]{:S(2)}, u32[]{:S(2)}) %collective-permute-start.3) | collective-permute-done | bytes 262176 | tf_op jit(solution)/shard_map/ppermute | solution.py:317
  102.0 2.7 %project_early.2 = (bf16[2048,256]{1,0:T(8,128)(2,1)S(1)}, f32[4,256,256]{2,1,0:T(8,128)S(1)}) custom-call(bf16[2,512,256]{2,1,0:T(8,128)(2,1)S(1)} %copy-done.2, bf16[2,512,256]{2,1,0:T(8,128)(2,1)S(1)} %collective-permute-done.1.refs_5_.refs_1_, bf16[2,512,256]{2,1,0:T(8,128)(2,1)S(1)} %copy-done.8, bf16[512,256]{1,0:T(8,128)(2,1)S(1)} %collective-permute-done.3.refs_3_, ...), custom_call_target="tpu_custom_call" | custom-call | tf_op jit(solution)/shard_map/project_early/pallas_call | solution.py:38
  104.7 1.2 project_late.2
  106.0 4.3 %all-to-all-start.2 = ((bf16[4,256,256]{2,1,0:T(8,128)(2,1)}), bf16[4,256,256]{2,1,0:T(8,128)(2,1)}, u32[]{:S(2)}, u32[]{:S(2)}) async-start(bf16[4,256,256]{2,1,0:T(8,128)(2,1)} %project_late.2), calls=%async_computation.2 | async-start | bytes 1048576 | tf_op jit(solution)/shard_map/all_to_all | solution.py:299
  136.4 2.7 %finish.1 = bf16[256,2048]{1,0:T(8,128)(2,1)} custom-call(s32[1]{0:T(128)} %bitcast.1.live_ref, bf16[4,256,256]{2,1,0:T(8,128)(2,1)} %all-to-all-done.2.value_ref, f32[128,1024]{1,0:T(8,128)S(1)} %copy-done.52, f32[128,1024]{1,0:T(8,128)S(1)} %copy-done.54, bf16[128,1024]{1,0:T(8,128)(2,1)S(1)} %copy-done.60, f32[128,1024]{1,0:T(8,128)S(1)} %copy-done.48, ...), custom_call_target="tpu_custom_call" | custom-call | tf_op jit(solution)/shard_map/finish/pallas_call | solution.py:38
  (138 shorter events, 37.4 us)
Async XLA Ops:
  2.7 23.6 %copy-start.21 = (bf16[1024,256]{1,0:T(8,128)(2,1)S(1)}, bf16[1024,256]{1,0:T(8,128)(2,1)}, u32[]{:S(2)}) copy-start(bf16[1024,256]{1,0:T(8,128)(2,1)} %key_ref.1) | copy-start | bytes 1572868
  21.9 8.1 %copy-start.5 = (bf16[1,512,256]{2,1,0:T(8,128)(2,1)S(1)}, bf16[1,512,256]{2,1,0:T(8,128)(2,1)}, u32[]{:S(2)}) copy-start(bf16[1,512,256]{2,1,0:T(8,128)(2,1)} %param.11) | copy-start | bytes 786436
  21.9 28.0 %copy-start = (bf16[1,2,128,2048]{3,2,1,0:T(8,128)(2,1)S(1)}, bf16[1,2,128,2048]{3,2,1,0:T(8,128)(2,1)}, u32[]{:S(2)}) copy-start(bf16[1,2,128,2048]{3,2,1,0:T(8,128)(2,1)} %param.10) | copy-start | bytes 3145732
  22.0 40.4 %all-to-all-start = ((bf16[4,256,512]{2,1,0:T(8,128)(2,1)}), bf16[4,256,512]{2,1,0:T(8,128)(2,1)}, u32[]{:S(2)}, u32[]{:S(2)}) async-start(bf16[4,256,512]{2,1,0:T(8,128)(2,1)} %get-tuple-element.35), calls=%async_computation | async-start | bytes 2097152 | tf_op jit(solution)/shard_map/all_to_all | solution.py:299
  27.4 55.8 %copy-start.1 = (bf16[2,512,256]{2,1,0:T(8,128)(2,1)}, bf16[2,512,256]{2,1,0:T(8,128)(2,1)S(1)}, u32[]{:S(2)}) copy-start(bf16[2,512,256]{2,1,0:T(8,128)(2,1)S(1)} %pack_weights.1.refs_0_) | copy-start | bytes 1572868
  27.4 22.5 %collective-permute-start.1 = (bf16[2,512,256]{2,1,0:T(8,128)(2,1)S(1)}, bf16[2,512,256]{2,1,0:T(8,128)(2,1)S(1)}, u32[]{:S(2)}, u32[]{:S(2)}) collective-permute-start(bf16[2,512,256]{2,1,0:T(8,128)(2,1)S(1)} %pack_weights.1.refs_0_), channel_id=1, source_target_pairs={{0,8},{8,12},{12,4},{4,0},{1,9},{9,13},{13,5},{5,1},{2,10},{10,14}... | collective-permute-start | bytes 1572872 | tf_op jit(solution)/shard_map/ppermute | solution.py:307
  30.1 16.9 %collective-permute-start.4 = (bf16[512,256]{1,0:T(8,128)(2,1)S(1)}, bf16[512,256]{1,0:T(8,128)(2,1)S(1)}, u32[]{:S(2)}, u32[]{:S(2)}) collective-permute-start(bf16[512,256]{1,0:T(8,128)(2,1)S(1)} %bitcast.20), channel_id=1, source_target_pairs={{0,2},{2,0},{1,3},{3,1},{4,6},{6,4},{5,7},{7,5},{8,10},{10,8},{9,1... | collective-permute-start | bytes 786440 | tf_op jit(solution)/shard_map/ppermute | solution.py:304
  32.0 17.8 %collective-permute-start.5 = (bf16[512,256]{1,0:T(8,128)(2,1)}, bf16[512,256]{1,0:T(8,128)(2,1)S(1)}, u32[]{:S(2)}, u32[]{:S(2)}) collective-permute-start(bf16[512,256]{1,0:T(8,128)(2,1)} %bitcast.25), channel_id=1, source_target_pairs={{0,2},{2,0},{1,3},{3,1},{4,6},{6,4},{5,7},{7,5},{8,10},{10,8},{9,1... | collective-permute-start | bytes 786440 | tf_op jit(solution)/shard_map/ppermute | solution.py:304
  53.2 8.0 %copy-start.11 = (f32[128,1024]{1,0:T(8,128)}, f32[128,1024]{1,0:T(8,128)S(1)}, u32[]{:S(2)}) copy-start(f32[128,1024]{1,0:T(8,128)S(1)} %get-tuple-element.37.refs_1_.old_tops) | copy-start | bytes 1572868
  56.4 4.8 %copy-start.13 = (f32[128,1024]{1,0:T(8,128)}, f32[128,1024]{1,0:T(8,128)S(1)}, u32[]{:S(2)}) copy-start(f32[128,1024]{1,0:T(8,128)S(1)} %get-tuple-element.38.refs_2_.old_tops) | copy-start | bytes 1572868
  62.3 20.9 %collective-permute-start.6 = (bf16[4,256,512]{2,1,0:T(8,128)(2,1)S(1)}, bf16[4,256,512]{2,1,0:T(8,128)(2,1)}, u32[]{:S(2)}, u32[]{:S(2)}) collective-permute-start(bf16[4,256,512]{2,1,0:T(8,128)(2,1)S(1)} %after.1.refs_4_), channel_id=1, source_target_pairs={{0,1},{1,0},{2,3},{3,2},{4,5},{5,4},{6,7},{7,6},{8,9},{9,8},{10,11... | collective-permute-start | bytes 3145736 | tf_op jit(solution)/shard_map/ppermute | solution.py:330
  62.4 23.5 %collective-permute-start = (bf16[4,256,512]{2,1,0:T(8,128)(2,1)}, bf16[4,256,512]{2,1,0:T(8,128)(2,1)S(1)}, u32[]{:S(2)}, u32[]{:S(2)}) collective-permute-start(bf16[4,256,512]{2,1,0:T(8,128)(2,1)} %all-to-all-done.refs_6_), channel_id=1, source_target_pairs={{0,1},{1,0},{2,3},{3,2},{4,5},{5,4},{6,7},{7,6},{8,9},{9,8},{10,11... | collective-permute-start | bytes 3145736 | tf_op jit(solution)/shard_map/ppermute | solution.py:330
  62.9 14.8 %collective-permute-start.2 = (bf16[2,512,256]{2,1,0:T(8,128)(2,1)S(1)}, bf16[2,512,256]{2,1,0:T(8,128)(2,1)S(1)}, u32[]{:S(2)}, u32[]{:S(2)}) collective-permute-start(bf16[2,512,256]{2,1,0:T(8,128)(2,1)S(1)} %pack_weights.1.refs_0_), channel_id=1, source_target_pairs={{8,0},{12,8},{4,12},{0,4},{9,1},{13,9},{5,13},{1,5},{10,2},{14,10}... | collective-permute-start | bytes 1572872 | tf_op jit(solution)/shard_map/ppermute | solution.py:307
  64.5 18.7 %collective-permute-start.7 = (bf16[512,256]{1,0:T(8,128)(2,1)S(1)}, bf16[512,256]{1,0:T(8,128)(2,1)S(1)}, u32[]{:S(2)}, u32[]{:S(2)}) collective-permute-start(bf16[512,256]{1,0:T(8,128)(2,1)S(1)} %get-tuple-element.65), channel_id=1, source_target_pairs={{0,8},{8,12},{12,4},{4,0},{1,9},{9,13},{13,5},{5,1},{2,10},{10,14}... | collective-permute-start | bytes 786440 | tf_op jit(solution)/shard_map/ppermute | solution.py:317
  77.7 8.1 %copy-start.7 = (bf16[2,512,256]{2,1,0:T(8,128)(2,1)}, bf16[2,512,256]{2,1,0:T(8,128)(2,1)S(1)}, u32[]{:S(2)}) copy-start(bf16[2,512,256]{2,1,0:T(8,128)(2,1)S(1)} %collective-permute-done.2.refs_2_) | copy-start | bytes 1572868
  88.1 17.8 %all-to-all-start.3 = ((bf16[4,256,256]{2,1,0:T(8,128)(2,1)}), bf16[4,256,256]{2,1,0:T(8,128)(2,1)S(1)}, u32[]{:S(2)}, u32[]{:S(2)}) async-start(bf16[4,256,256]{2,1,0:T(8,128)(2,1)} %copy-done.9), calls=%async_computation.3 | async-start | bytes 1048576 | tf_op jit(solution)/shard_map/all_to_all | solution.py:299
  91.6 8.3 %collective-permute-start.3 = (bf16[512,256]{1,0:T(8,128)(2,1)S(1)}, bf16[512,256]{1,0:T(8,128)(2,1)S(1)}, u32[]{:S(2)}, u32[]{:S(2)}) collective-permute-start(bf16[512,256]{1,0:T(8,128)(2,1)S(1)} %get-tuple-element.66), channel_id=1, source_target_pairs={{0,8},{8,12},{12,4},{4,0},{1,9},{9,13},{13,5},{5,1},{2,10},{10,14}... | collective-permute-start | bytes 786440 | tf_op jit(solution)/shard_map/ppermute | solution.py:317
  104.7 6.3 %copy-start.19 = (f32[128,128]{1,0:T(8,128)S(1)}, f32[128,128]{1,0:T(8,128)}, u32[]{:S(2)}) copy-start(f32[128,128]{1,0:T(8,128)} %constant.10.clone.cos_ref) | copy-start | bytes 196612
  104.7 6.3 %copy-start.20 = (f32[128,128]{1,0:T(8,128)S(1)}, f32[128,128]{1,0:T(8,128)}, u32[]{:S(2)}) copy-start(f32[128,128]{1,0:T(8,128)} %constant.11.clone.sin_ref) | copy-start | bytes 196612
  104.7 6.3 %copy-start.36 = (f32[128,1024]{1,0:T(8,128)S(1)}, f32[128,1024]{1,0:T(8,128)}, u32[]{:S(2)}) copy-start(f32[128,1024]{1,0:T(8,128)} %copy-done.35) | copy-start | bytes 1572868
  106.0 21.3 %all-to-all-start.2 = ((bf16[4,256,256]{2,1,0:T(8,128)(2,1)}), bf16[4,256,256]{2,1,0:T(8,128)(2,1)}, u32[]{:S(2)}, u32[]{:S(2)}) async-start(bf16[4,256,256]{2,1,0:T(8,128)(2,1)} %project_late.2), calls=%async_computation.2 | async-start | bytes 1048576 | tf_op jit(solution)/shard_map/all_to_all | solution.py:299
  113.1 8.3 %copy-start.28 = (f32[128,1024]{1,0:T(8,128)S(1)}, f32[128,1024]{1,0:T(8,128)}, u32[]{:S(2)}) copy-start(f32[128,1024]{1,0:T(8,128)} %copy-done.27) | copy-start | bytes 1572868
  113.1 8.3 %copy-start.30 = (f32[128,1024]{1,0:T(8,128)S(1)}, f32[128,1024]{1,0:T(8,128)}, u32[]{:S(2)}) copy-start(f32[128,1024]{1,0:T(8,128)} %copy-done.29) | copy-start | bytes 1572868
  115.3 6.1 %copy-start.14 = (f32[128,1024]{1,0:T(8,128)S(1)}, f32[128,1024]{1,0:T(8,128)}, u32[]{:S(2)}) copy-start(f32[128,1024]{1,0:T(8,128)} %copy-done.13) | copy-start | bytes 1572868
  (48 other events, 58.0 us)

commit v5 on v0

v5 whole, which is shorter than its diff:
```python
import functools
import math

import jax
import jax.numpy as jnp
import numpy as np
from jax import lax
from jax.experimental import pallas as pl
from jax.experimental.pallas import tpu as pltpu
from jax.sharding import PartitionSpec as P

HD = 128
PLEN = 1024
FACTOR = HD**-0.5 * math.log2(math.e)
MIB = 1 << 20
ANYWHERE = pl.BlockSpec(memory_space=pl.ANY)


def dot_nt(a, b):
    return lax.dot_general(a, b, (((1,), (1,)), ((), ())), preferred_element_type=jnp.float32)


def dot_nn(a, b):
    return lax.dot_general(a, b, (((1,), (0,)), ((), ())), preferred_element_type=jnp.float32)


def settings(limit):
    return {
        "compiler_params": pltpu.CompilerParams(vmem_limit_bytes=limit * MIB),
        "cost_estimate": pl.CostEstimate(flops=0, bytes_accessed=0, transcendentals=0),
    }


def after(value, *earlier):
    return pl.pallas_call(
        lambda *refs: None,
        in_specs=[ANYWHERE] * (1 + len(earlier)),
        out_specs=ANYWHERE,
        out_shape=jax.ShapeDtypeStruct(value.shape, value.dtype),
        input_output_aliases={0: 0},
        name="after",
        **settings(1),
    )(value, *earlier)


def run_copies(copies):
    for copy in copies:
        copy.start()
    for copy in copies:
        copy.wait()


def pack_rows(n_groups, key_weight, value_weight, prompt_keys, prompt_values):
    block, columns = key_weight.shape
    half = block // n_groups

    def body(kw_ref, vw_ref, pk_ref, pv_ref, share_ref, cache_ref, sems):
        rows = pl.ds(pl.multiple_of(lax.axis_index("groups") * half, half), half)
        run_copies(
            [
                pltpu.make_async_copy(pk_ref, cache_ref.at[0], sems.at[0]),
                pltpu.make_async_copy(pv_ref, cache_ref.at[1], sems.at[1]),
                pltpu.make_async_copy(kw_ref.at[rows, :], share_ref.at[0], sems.at[2]),
                pltpu.make_async_copy(vw_ref.at[rows, :], share_ref.at[1], sems.at[3]),
            ]
        )

    return pl.pallas_call(
        body,
        in_specs=[ANYWHERE] * 4,
        out_specs=[ANYWHERE] * 2,
        out_shape=[
            jax.ShapeDtypeStruct((2, half, columns), key_weight.dtype),
            jax.ShapeDtypeStruct((2, *prompt_keys.shape), prompt_keys.dtype),
        ],
        scratch_shapes=[pltpu.SemaphoreType.DMA((4,))],
        name="pack_rows",
        **settings(1),
    )(key_weight, value_weight, prompt_keys, prompt_values)


def split_pair(pair):
    def body(pair_ref, first_ref, second_ref, sems):
        run_copies(
            [
                pltpu.make_async_copy(pair_ref.at[0], first_ref, sems.at[0]),
                pltpu.make_async_copy(pair_ref.at[1], second_ref, sems.at[1]),
            ]
        )

    return pl.pallas_call(
        body,
        in_specs=[ANYWHERE],
        out_specs=[ANYWHERE] * 2,
        out_shape=[jax.ShapeDtypeStruct(pair.shape[1:], pair.dtype)] * 2,
        scratch_shapes=[pltpu.SemaphoreType.DMA((2,))],
        name="split_pair",
        **settings(1),
    )(pair)


def pack_features(sizes, block, sets, hidden):
    n_groups, n_fsdp, n_resp, n_tp = sizes
    rows, width = hidden.shape
    per_core = n_fsdp // n_tp
    half = block // n_groups

    def start_of(place, n):
        group = (lax.axis_index("groups") + place[0]) % n_groups
        resp = (lax.axis_index("resp") + place[1]) % n_resp
        return (n * n_resp + resp) * block + group * half

    if half % HD:
        return [
            jnp.concatenate(
                [
                    lax.dynamic_slice_in_dim(hidden, start_of(place, n), half, axis=1)
                    for n in range(per_core)
                ],
                axis=1,
            )
            for place in sets
        ]

    def body(hidden_ref, *outs):
        for place, out in zip(sets, outs):
            for n in range(per_core):
                first = pl.multiple_of(start_of(place, n), HD)
                out[:, n * half : (n + 1) * half] = hidden_ref[:, pl.ds(first, half)]

    step = rows // 4
    return pl.pallas_call(
        body,
        grid=(rows // step,),
        in_specs=[pl.BlockSpec((step, width), lambda n: (n, 0))],
        out_specs=[pl.BlockSpec((step, per_core * half), lambda n: (n, 0))] * len(sets),
        out_shape=[jax.ShapeDtypeStruct((rows, per_core * half), hidden.dtype)] * len(sets),
        name="pack_features",
        **settings(8),
    )(hidden)


def line_ring(size):
    return list(range(0, size, 2)) + list(range(1, size, 2))[::-1]


def project(n_fsdp, pieces, jobs, waits=()):
    kinds = [kind for kind in range(len(pieces)) if any(job[0] == kind for job in jobs)]
    piece_list = [(kind, piece) for kind in kinds for piece in pieces[kind]]
    rows, depth = jobs[0][1].shape
    half, columns = pieces[0][0][0].shape[-2:]
    dtype = jobs[0][1].dtype
    total, count = len(piece_list), len(jobs)
    arrays = []
    for job in jobs:
        for x in job[1:3]:
            if not any(x is y for y in arrays):
                arrays.append(x)
    slots = [[next(i for i, y in enumerate(arrays) if x is y) for x in job[1:3]] for job in jobs]

    def body(*refs):
        piece_refs, refs = refs[:total], refs[total:]
        array_refs, refs = refs[: len(arrays)], refs[len(arrays) + len(waits) :]
        out_refs, (weights, features, piece_sems, array_sems) = refs[:count], refs[count:]
        fsdp, core = lax.axis_index("fsdp"), lax.axis_index("tp")
        place = jnp.where(fsdp % 2 == 0, fsdp // 2, n_fsdp - (fsdp + 1) // 2)
        piece_copies, array_copies = [], []
        for n, (ref, (kind, (_, index, hops))) in enumerate(zip(piece_refs, piece_list)):
            at = (place - hops + n_fsdp) % n_fsdp
            owner = jnp.where(at < n_fsdp // 2, 2 * at, 2 * n_fsdp - 1 - 2 * at)
            source = ref if index is None else ref.at[index]
            target = weights.at[kinds.index(kind), pl.ds(pl.multiple_of(owner * half, half), half), :]
            piece_copies.append(pltpu.make_async_copy(source, target, piece_sems.at[n]))
        for n, ref in enumerate(array_refs):
            array_copies.append(pltpu.make_async_copy(ref, features.at[n], array_sems.at[n]))
        for copy in piece_copies + array_copies:
            copy.start()
        for copy in piece_copies:
            copy.wait()
        first = pl.ds(pl.multiple_of(core * depth, depth), depth)
        second = pl.ds(pl.multiple_of((1 - core) * depth, depth), depth)
        waited = set()
        for (kind, _, _, _), (near, far), out in zip(jobs, slots, out_refs):
            for slot in (near, far):
                if slot not in waited:
                    waited.add(slot)
                    array_copies[slot].wait()
            which = kinds.index(kind)
            sums = dot_nn(features[near], weights[which, first, :])
            sums = sums + dot_nn(features[far], weights[which, second, :])
            out[...] = sums.astype(out.dtype)

    return pl.pallas_call(
        body,
        grid=(1,),
        in_specs=[ANYWHERE] * (total + len(arrays) + len(waits)),
        out_specs=[pl.BlockSpec((rows, columns), lambda _: (0, 0))] * count,
        out_shape=[jax.ShapeDtypeStruct((rows, columns), job[3]) for job in jobs],
        scratch_shapes=[
            pltpu.VMEM((len(kinds), n_fsdp * half, columns), dtype),
            pltpu.VMEM((len(arrays), rows, depth), dtype),
            pltpu.SemaphoreType.DMA((total,)),
            pltpu.SemaphoreType.DMA((len(arrays),)),
        ],
        name="project",
        **settings(20),
    )(*[piece[0] for _, piece in piece_list], *arrays, *waits)


def take(ref, first, count):
    return jnp.concatenate(
        [ref[:, (first + n) * HD : (first + n + 1) * HD] for n in range(count)], axis=0
    )


def put(ref, first, count, value):
    tokens = ref.shape[0]
    value = jnp.broadcast_to(value, (count * tokens, HD)).astype(ref.dtype)
    for n in range(count):
        ref[:, (first + n) * HD : (first + n + 1) * HD] = value[n * tokens : (n + 1) * tokens]


def attend_cache(slot, tokens, group_size, queries, caches, waits):
    count = len(caches)
    heads = queries.shape[1] // (group_size * HD)
    length = caches[0].shape[1]
    step = 2 if group_size % 2 == 0 else 1

    def body(q_ref, *refs):
        mixed_ref, level_ref = refs[-2:]
        keys = [ref[0] for ref in refs[:count]]
        values = [ref[1] for ref in refs[:count]]
        wide = [jnp.concatenate([v, jnp.ones(v.shape, v.dtype)], axis=1) for v in values]

        def scores_of(first):
            q = take(q_ref, first, step)
            return [dot_nt(q, k) for k in keys]

        coming = scores_of(0)
        for first in range(0, group_size, step):
            scores = coming
            if first + step < group_size:
                coming = scores_of(first + step)
            tops = [s[:, n * HD : (n + 1) * HD] for s in scores for n in range(length // HD)]
            top = jnp.max(functools.reduce(jnp.maximum, tops), axis=1, keepdims=True)
            out = None
            for s, v in zip(scores, wide):
                probs = jnp.exp2((s - top) * FACTOR).astype(jnp.bfloat16)
                part = dot_nn(probs, v)
                out = part if out is None else out + part
            total = out[:, HD:]
            put(mixed_ref, first, step, out[:, :HD] / total)
            put(level_ref, first, step, top * FACTOR + jnp.log2(total))

    width = group_size * HD
    spec_q = pl.BlockSpec((tokens, width), lambda head: (slot, head))
    spec_c = pl.BlockSpec((2, length, HD), lambda head: (0, 0, head))
    spec_out = pl.BlockSpec((tokens, width), lambda head: (0, head))
    return pl.pallas_call(
        body,
        grid=(heads,),
        in_specs=[spec_q] + [spec_c] * count + [ANYWHERE] * len(waits),
        out_specs=[spec_out] * 2,
        out_shape=[jax.ShapeDtypeStruct((tokens, heads * width), jnp.float32)] * 2,
        name="attend_cache",
        **settings(20),
    )(queries, *caches, *waits)


def sum_refs(refs):
    return functools.reduce(jnp.add, [ref[...].astype(jnp.float32) for ref in refs])


def attend_own(slot, tokens, group_size, queries, key_parts, tables, state):
    parts = len(key_parts)
    heads = queries.shape[1] // (group_size * HD)

    def body(q_ref, *refs):
        cos_ref, sin_ref, old_mixed, old_level, mixed_ref, probs_ref = refs[parts:]
        key = sum_refs(refs[:parts])
        key = key * cos_ref[...] + pltpu.roll(key, HD // 2, 1) * sin_ref[...]
        key = key.astype(jnp.bfloat16)
        ones = jnp.ones((tokens, HD), jnp.bfloat16)
        row = lax.broadcasted_iota(jnp.int32, (tokens, tokens), 0)
        causal = row >= lax.broadcasted_iota(jnp.int32, (tokens, tokens), 1)
        causal = jnp.concatenate([causal] * group_size, axis=0)
        scores = dot_nt(take(q_ref, 0, group_size), key) * FACTOR
        scores = jnp.where(causal, scores, -1e30)
        level = take(old_level, 0, group_size)
        top = jnp.max(jnp.maximum(level, scores), axis=1, keepdims=True)
        probs = jnp.exp2(scores - top)
        kept = jnp.exp2(level - top)
        inverse = 1.0 / (kept + dot_nn(probs.astype(jnp.bfloat16), ones))
        put(mixed_ref, 0, group_size, take(old_mixed, 0, group_size) * (kept * inverse))
        put(probs_ref, 0, group_size, probs * inverse)

    width = group_size * HD
    spec_q = pl.BlockSpec((tokens, width), lambda head: (slot, head))
    spec_key = pl.BlockSpec((tokens, HD), lambda head: (slot, head))
    spec_table = pl.BlockSpec((tokens, HD), lambda head: (0, 0))
    spec_wide = pl.BlockSpec((tokens, width), lambda head: (0, head))
    shape = (tokens, heads * width)
    return pl.pallas_call(
        body,
        grid=(heads,),
        in_specs=[spec_q] + [spec_key] * parts + [spec_table] * 2 + [spec_wide] * 2,
        out_specs=[spec_wide] * 2,
        out_shape=[
            jax.ShapeDtypeStruct(shape, jnp.float32),
            jax.ShapeDtypeStruct(shape, jnp.bfloat16),
        ],
        name="attend_own",
        **settings(20),
    )(queries, *key_parts, *tables, *state)


def finish(live, value_parts, states, tokens, group_size, dtype):
    parts, slots = len(value_parts), len(states)
    width = group_size * HD
    heads = states[0][0].shape[1] // width

    def body(live_ref, *refs):
        out_ref = refs[-1]
        for slot in range(slots):
            mixed_ref, probs_ref = refs[parts + 2 * slot : parts + 2 * slot + 2]
            rows = slice(slot * tokens, (slot + 1) * tokens)
            value = sum_refs([ref.at[rows, :] for ref in refs[:parts]]).astype(jnp.bfloat16)
            out = take(mixed_ref, 0, group_size) + dot_nn(take(probs_ref, 0, group_size), value)
            out = jnp.where(slot < live_ref[0], out, 0.0)
            put(out_ref.at[rows, :], 0, group_size, out)

    spec_value = pl.BlockSpec((slots * tokens, HD), lambda head: (0, head))
    spec_wide = pl.BlockSpec((tokens, width), lambda head: (0, head))
    return pl.pallas_call(
        body,
        grid=(heads,),
        in_specs=[pl.BlockSpec(memory_space=pltpu.SMEM)]
        + [spec_value] * parts
        + [spec_wide] * (2 * slots),
        out_specs=pl.BlockSpec((slots * tokens, width), lambda head: (0, head)),
        out_shape=jax.ShapeDtypeStruct((slots * tokens, heads * width), dtype),
        name="finish",
        **settings(20),
    )(live, *value_parts, *[x for state in states for x in state])


def rotation_tables(extent, offset):
    orders = np.arange(HD // 2, dtype=np.float64)
    inverse = np.exp(-(2.0 * orders / HD) * math.log(500000.0))
    angles = (offset + np.arange(extent))[:, None] * inverse[None, :]
    cosine, sine = np.cos(angles), np.sin(angles)
    return (
        jnp.asarray(np.concatenate([cosine, cosine], axis=1), jnp.float32),
        jnp.asarray(np.concatenate([-sine, sine], axis=1), jnp.float32),
    )


def on_device(sizes, hidden, queries, prompt_keys, prompt_values, key_weight, value_weight, counts):
    n_groups, n_fsdp, n_resp, n_tp = sizes
    _, slots, tokens, part_width = hidden.shape
    block, columns = key_weight.shape
    group_size = queries.shape[3] // columns
    rows = slots * tokens
    plane = ("groups", "resp")
    cores = [(n, (n + 1) % n_tp) for n in range(n_tp)]
    ring = line_ring(n_fsdp)
    rightward = [(ring[n], ring[(n + 1) % n_fsdp]) for n in range(n_fsdp)]
    leftward = [(b, a) for a, b in rightward]
    along = [(0, b) for b in range(1, n_resp)]
    across = [(a, b) for a in range(1, n_groups) for b in range(1, n_resp)]
    twins = [(a, 0) for a in range(1, n_groups)]
    sets = [(0, 0), *along, *across, *twins]

    def shift(a, b):
        return [
            (g * n_resp + r, (g + a) % n_groups * n_resp + (r + b) % n_resp)
            for g in range(n_groups)
            for r in range(n_resp)
        ]

    share, cache = pack_rows(n_groups, key_weight, value_weight, prompt_keys[0], prompt_values[0])

    caches = [cache]
    for b in range(1, n_resp):
        around = [(n, (n + b) % n_resp) for n in range(n_resp)]
        caches.append(lax.ppermute(cache, "resp", around))

    pieces = [[(share, kind, 0)] for kind in range(2)]
    held = lax.ppermute(share, "fsdp", rightward)
    left = lax.ppermute(share, "fsdp", leftward)
    for hop in range(1, n_fsdp // 2):
        if hop > 1:
            held = lax.ppermute(held, "fsdp", rightward)
        for kind in range(2):
            pieces[kind].append((held, kind, hop))
    ends = split_pair(held)
    for kind in range(2):
        pieces[kind].append((lax.ppermute(ends[kind], "fsdp", rightward), None, n_fsdp // 2))
    for hop in range(1, n_fsdp - n_fsdp // 2):
        if hop > 1:
            left = lax.ppermute(left, "fsdp", leftward)
        for kind in range(2):
            pieces[kind].append((left, kind, -hop))

    near = dict(zip(sets, pack_features(sizes, block, sets, hidden.reshape(rows, part_width))))
    for place in sets[1:]:
        near[place] = lax.ppermute(near[place], plane, shift(*place))

    flat_queries = queries.reshape(rows, queries.shape[3])
    states = [
        attend_cache(slot, tokens, group_size, flat_queries, caches, [ends[0]])
        for slot in range(slots)
    ]
    for place in sets[1:]:
        near[place] = after(near[place], *[state[1] for state in states])
    far = {place: lax.ppermute(near[place], "tp", cores) for place in sets}

    def send(place, sums):
        return lax.ppermute(sums, plane, shift(n_groups - place[0], n_resp - place[1]))

    narrow, wide = jnp.bfloat16, jnp.float32
    parts = [[], []]
    for kind in range(2):
        jobs = [(kind, near[p], far[p], narrow) for p in [*along, *twins]]
        sums = project(n_fsdp, pieces, [*jobs, (kind, near[sets[0]], far[sets[0]], wide)])
        parts[kind].append(sums[-1])
        parts[kind].extend(send(p, x) for p, x in zip([*along, *twins], sums))
    jobs = [(kind, near[p], far[p], narrow) for kind in range(2) for p in across]
    sums = list(project(n_fsdp, pieces, jobs))
    for kind in range(2):
        for p in across:
            parts[kind].append(send(p, sums.pop(0)))

    tables = rotation_tables(tokens, PLEN)
    states = [
        attend_own(slot, tokens, group_size, flat_queries, parts[0], tables, state)
        for slot, state in enumerate(states)
    ]
    live = (counts[0] - lax.axis_index("resp") * slots).astype(jnp.int32)[None]
    out = finish(live, parts[1], states, tokens, group_size, queries.dtype)
    return out.reshape(queries.shape)


def solution(mesh):
    placed = (
        P(("groups", "fsdp"), "resp", None, "tp"),
        P(("groups", "fsdp"), "resp", None, "tp"),
        P(("groups", "fsdp"), "resp", "tp"),
        P(("groups", "fsdp"), "resp", "tp"),
        P(("fsdp", "resp"), "tp"),
        P(("fsdp", "resp"), "tp"),
        P(("groups", "fsdp")),
    )
    sizes = tuple(mesh.shape[name] for name in ("groups", "fsdp", "resp", "tp"))
    return jax.shard_map(
        functools.partial(on_device, sizes),
        mesh=mesh,
        in_specs=placed,
        out_specs=P(("groups", "fsdp"), "resp", None, "tp"),
        check_vma=False,
    )
```

time: 207 us -> 78.5 us (0.38)
  waiting for transfers between devices: 122 us -> 24.1 us
  matrix products: 28.2 us -> 0 us
  starting transfers between devices: 0.08 us -> 22.4 us
  blocking collectives: 21.6 us -> 0 us
  Pallas kernels: 0 us -> 20.4 us
  between operations: 14 us -> 0.85 us
  other arithmetic: 11.4 us -> 0 us
    all_gather x3 -> x0, waiting for transfers between devices: 119 us -> none  [the longest x1 70.2 us: on_device(): lax.all_gather(value_weight, ('fsdp', 'resp'), axis=0, tiled=True)]
    dot_general x10 -> x0, matrix products: 28.2 us -> none  [the longest x4 10.7 us: absorb(): jnp.einsum('rkgd,lkd->rkgl', queried, cache_keys, preferred_element_type=...]
    ppermute x0 -> x18, waiting for transfers between devices: none -> 24.1 us  [the longest x3 11.4 us: on_device(): near[place] = lax.ppermute(near[place], plane, shift(*place))]
    ppermute x0 -> x18, starting transfers between devices: none -> 22.4 us  [the longest x6 7.11 us: send(): lax.ppermute(sums, plane, shift(n_groups - place[0], n_resp - place[1]))]
    all_gather x2 -> x0, blocking collectives: 21.6 us -> none  [the longest x1 11.4 us: on_device(): lax.all_gather(prompt_keys, 'resp', axis=1, tiled=True)]
    pallas_call x0 -> x14, Pallas kernels: none -> 20.4 us  [the longest x2 7.05 us: attend_cache(): pl.pallas_call(body, grid=(heads,), in_specs=[spec_q] + [spec_c] * count...]
    reduce_sum x4 -> x0, other arithmetic: 9.98 us -> none  [absorb(): row_total = row_total * shrink + jnp.sum(weights, axis=-1)]
    unnamed x9 -> x28, local copies, waits for them, and re-layouts: 1.65 us -> 10.2 us
  transfers between devices with their start and end apart: 3 -> 18, of which waited for: 3 -> 5; matrix products, arithmetic and copies ran while one was open for 12% -> 0% of each run, Pallas kernels for 0% -> 23%
where the time goes in v5:
time: 78.5 us; the launch traced here: 77.9 us
  waiting for transfers between devices  24.1 us (31%)
  starting transfers between devices  22.4 us (29%)
  Pallas kernels  20.4 us (26%)
  local copies, waits for them, and re-layouts  10.2 us (13%)
  between operations  0.85 us (1%)
    ppermute x3, waiting for transfers between devices, on_device(): near[place] = lax.ppermute(near[place], plane, shift(*place))  11.4 us
    unnamed x28, local copies, waits for them, and re-layouts  10.2 us
    ppermute x6, starting transfers between devices, send(): lax.ppermute(sums, plane, shift(n_groups - place[0], n_resp - place[1]))  7.11 us
    ppermute x2, waiting for transfers between devices, on_device(): lax.ppermute(ends[kind], 'fsdp', rightward)  7.07 us
    pallas_call x2, Pallas kernels, attend_cache(): pl.pallas_call(body, grid=(heads,), in_specs=[spec_q] + [spec_c] * count...  7.05 us
    pallas_call x3, Pallas kernels, project(): pl.pallas_call(body, grid=(1,), in_specs=[ANYWHERE] * (total + len(arrays...  6.19 us
    pallas_call x2, Pallas kernels, attend_own(): pl.pallas_call(body, grid=(heads,), in_specs=[spec_q] + [spec_key] * part...  4.35 us
    ppermute x1, waiting for transfers between devices, on_device(): held = lax.ppermute(share, 'fsdp', rightward)  4.3 us
  transfers between devices with their start and end apart: 18, of which 5 were waited for; matrix products, arithmetic and copies ran while one was open for 0% of the time, Pallas kernels for 23%

profile of v5, /device:TPU:0, one launch (start us, length us, event | category | flops | bytes accessed | tf_op | source)
XLA Modules:
  0.0 77.9 jit_solution(10517924323897472716)
XLA Ops:
  4.1 4.1 %collective-permute-start = (bf16[2,512,256]{2,1,0:T(8,128)(2,1)S(1)}, bf16[2,512,256]{2,1,0:T(8,128)(2,1)S(1)}, u32[]{:S(2)}, u32[]{:S(2)}) collective-permute-start(bf16[2,512,256]{2,1,0:T(8,128)(2,1)S(1)} %get-tuple-element.29.refs_0_.refs_4_), channel_id=1, source_target_pairs={{0,8},{8,12},{12,4},{4,0},{1,9},{9,13},{13,5},{5,1},{2,10},{10,14}... | collective-permute-start | bytes 1572872 | tf_op jit(solution)/shard_map/ppermute | solution.py:389
  8.2 1.5 %collective-permute-start.4 = (bf16[2,512,256]{2,1,0:T(8,128)(2,1)S(1)}, bf16[2,512,256]{2,1,0:T(8,128)(2,1)S(1)}, u32[]{:S(2)}, u32[]{:S(2)}) collective-permute-start(bf16[2,512,256]{2,1,0:T(8,128)(2,1)S(1)} %get-tuple-element.32.refs_0_), channel_id=1, source_target_pairs={{0,2},{2,0},{1,3},{3,1},{4,6},{6,4},{5,7},{7,5},{8,10},{10,8},{9,1... | collective-permute-start | bytes 1572872 | tf_op jit(solution)/shard_map/ppermute | solution.py:386
  9.7 1.6 %copy-done.1 = bf16[1,2,128,4096]{3,2,1,0:T(8,128)(2,1)S(1)} copy-done((bf16[1,2,128,4096]{3,2,1,0:T(8,128)(2,1)S(1)}, bf16[1,2,128,4096]{3,2,1,0:T(8,128)(2,1)}, u32[]{:S(2)}) %copy-start.1) | copy-done | bytes 2097176
  11.5 1.6 %collective-permute-start.12 = (bf16[256,1024]{1,0:T(8,128)(2,1)S(1)}, bf16[256,1024]{1,0:T(8,128)(2,1)S(1)}, u32[]{:S(2)}, u32[]{:S(2)}) collective-permute-start(bf16[256,1024]{1,0:T(8,128)(2,1)S(1)} %get-tuple-element.41), channel_id=1, source_target_pairs={{0,18},{2,16},{16,2},{18,0},{1,19},{3,17},{17,3},{19,1},{4,22},{6,... | collective-permute-start | bytes 1572872 | tf_op jit(solution)/shard_map/ppermute | solution.py:407
  13.1 1.5 %collective-permute-start.3 = (bf16[256,1024]{1,0:T(8,128)(2,1)S(1)}, bf16[256,1024]{1,0:T(8,128)(2,1)S(1)}, u32[]{:S(2)}, u32[]{:S(2)}) collective-permute-start(bf16[256,1024]{1,0:T(8,128)(2,1)S(1)} %get-tuple-element.31), channel_id=1, source_target_pairs={{0,2},{2,0},{16,18},{18,16},{1,3},{3,1},{17,19},{19,17},{4,6},{6,4... | collective-permute-start | bytes 1572872 | tf_op jit(solution)/shard_map/ppermute | solution.py:407
  15.1 4.3 %collective-permute-done.pair_ref.refs_1_.refs_5_ = bf16[2,512,256]{2,1,0:T(8,128)(2,1)S(1)} collective-permute-done((bf16[2,512,256]{2,1,0:T(8,128)(2,1)S(1)}, bf16[2,512,256]{2,1,0:T(8,128)(2,1)S(1)}, u32[]{:S(2)}, u32[]{:S(2)}) %collective-permute-start) | collective-permute-done | bytes 524320 | tf_op jit(solution)/shard_map/ppermute | solution.py:389
  19.4 2.4 %collective-permute-start.2 = (bf16[2,512,256]{2,1,0:T(8,128)(2,1)S(1)}, bf16[2,512,256]{2,1,0:T(8,128)(2,1)S(1)}, u32[]{:S(2)}, u32[]{:S(2)}) collective-permute-start(bf16[2,512,256]{2,1,0:T(8,128)(2,1)S(1)} %get-tuple-element.29.refs_0_.refs_4_), channel_id=1, source_target_pairs={{8,0},{12,8},{4,12},{0,4},{9,1},{13,9},{5,13},{1,5},{10,2},{14,10}... | collective-permute-start | bytes 1572872 | tf_op jit(solution)/shard_map/ppermute | solution.py:390
  21.8 1.2 %collective-permute-done.4.refs_1_ = bf16[2,512,256]{2,1,0:T(8,128)(2,1)S(1)} collective-permute-done((bf16[2,512,256]{2,1,0:T(8,128)(2,1)S(1)}, bf16[2,512,256]{2,1,0:T(8,128)(2,1)S(1)}, u32[]{:S(2)}, u32[]{:S(2)}) %collective-permute-start.4) | collective-permute-done | bytes 524320 | tf_op jit(solution)/shard_map/ppermute | solution.py:386
  23.0 1.6 %collective-permute-start.1 = (bf16[512,256]{1,0:T(8,128)(2,1)S(1)}, bf16[512,256]{1,0:T(8,128)(2,1)S(1)}, u32[]{:S(2)}, u32[]{:S(2)}) collective-permute-start(bf16[512,256]{1,0:T(8,128)(2,1)S(1)} %get-tuple-element.30), channel_id=1, source_target_pairs={{0,8},{8,12},{12,4},{4,0},{1,9},{9,13},{13,5},{5,1},{2,10},{10,14}... | collective-permute-start | bytes 786440 | tf_op jit(solution)/shard_map/ppermute | solution.py:398
  24.6 3.5 %attend_cache.3 = (f32[128,2048]{1,0:T(8,128)S(1)}, f32[128,2048]{1,0:T(8,128)S(1)}) custom-call(bf16[256,2048]{1,0:T(8,128)(2,1)S(1)} %bitcast.8, bf16[2,512,256]{2,1,0:T(8,128)(2,1)S(1)} %get-tuple-element.32.refs_0_, bf16[2,512,256]{2,1,0:T(8,128)(2,1)S(1)} %collective-permute-done.4.refs_1_, bf16[512,256]{1,0:T(8,128)(2,1)S(1)} %get-tuple-element.33.refs_2_), custom_call_target="tpu_custom_call" | custom-call | tf_op jit(solution)/shard_map/attend_cache/pallas_call | solution.py:259
  29.2 3.5 %attend_cache.2 = (f32[128,2048]{1,0:T(8,128)S(1)}, f32[128,2048]{1,0:T(8,128)S(1)}) custom-call(bf16[256,2048]{1,0:T(8,128)(2,1)S(1)} %bitcast.9, bf16[2,512,256]{2,1,0:T(8,128)(2,1)S(1)} %get-tuple-element.32.refs_0_, bf16[2,512,256]{2,1,0:T(8,128)(2,1)S(1)} %collective-permute-done.4.refs_1_, bf16[512,256]{1,0:T(8,128)(2,1)S(1)} %get-tuple-element.33.refs_2_), custom_call_target="tpu_custom_call" | custom-call | tf_op jit(solution)/shard_map/attend_cache/pallas_call | solution.py:259
  32.7 2.6 %collective-permute-done.12.refs_0_ = bf16[256,1024]{1,0:T(8,128)(2,1)S(1)} collective-permute-done((bf16[256,1024]{1,0:T(8,128)(2,1)S(1)}, bf16[256,1024]{1,0:T(8,128)(2,1)S(1)}, u32[]{:S(2)}, u32[]{:S(2)}) %collective-permute-start.12) | collective-permute-done | bytes 524320 | tf_op jit(solution)/shard_map/ppermute | solution.py:407
  35.3 8.8 %collective-permute-done.3.refs_0_ = bf16[256,1024]{1,0:T(8,128)(2,1)S(1)} collective-permute-done((bf16[256,1024]{1,0:T(8,128)(2,1)S(1)}, bf16[256,1024]{1,0:T(8,128)(2,1)S(1)}, u32[]{:S(2)}, u32[]{:S(2)}) %collective-permute-start.3) | collective-permute-done | bytes 524320 | tf_op jit(solution)/shard_map/ppermute | solution.py:407
  44.7 1.6 %collective-permute-start.11 = (bf16[512,256]{1,0:T(8,128)(2,1)S(1)}, bf16[512,256]{1,0:T(8,128)(2,1)S(1)}, u32[]{:S(2)}, u32[]{:S(2)}) collective-permute-start(bf16[512,256]{1,0:T(8,128)(2,1)S(1)} %get-tuple-element.33.refs_2_), channel_id=1, source_target_pairs={{0,8},{8,12},{12,4},{4,0},{1,9},{9,13},{13,5},{5,1},{2,10},{10,14}... | collective-permute-start | bytes 786440 | tf_op jit(solution)/shard_map/ppermute | solution.py:398
  46.3 7.1 %collective-permute-done.11.refs_2_ = bf16[512,256]{1,0:T(8,128)(2,1)S(1)} collective-permute-done((bf16[512,256]{1,0:T(8,128)(2,1)S(1)}, bf16[512,256]{1,0:T(8,128)(2,1)S(1)}, u32[]{:S(2)}, u32[]{:S(2)}) %collective-permute-start.11) | collective-permute-done | bytes 262176 | tf_op jit(solution)/shard_map/ppermute | solution.py:398
  53.4 1.7 %project.4 = (bf16[256,256]{1,0:T(8,128)(2,1)S(1)}, bf16[256,256]{1,0:T(8,128)(2,1)}) custom-call(bf16[2,512,256]{2,1,0:T(8,128)(2,1)S(1)} %get-tuple-element.29.refs_0_.refs_4_, bf16[2,512,256]{2,1,0:T(8,128)(2,1)S(1)} %collective-permute-done.pair_ref.refs_1_.refs_5_, bf16[512,256]{1,0:T(8,128)(2,1)S(1)} %collective-permute-done.11.refs_2_, ...), custom_call_target="tpu_custom_call" | custom-call | tf_op jit(solution)/shard_map/project/pallas_call | solution.py:193
  55.0 2.5 %collective-permute-start.17 = (bf16[256,256]{1,0:T(8,128)(2,1)S(1)}, bf16[256,256]{1,0:T(8,128)(2,1)S(1)}, u32[]{:S(2)}, u32[]{:S(2)}) collective-permute-start(bf16[256,256]{1,0:T(8,128)(2,1)S(1)} %get-tuple-element.46), channel_id=1, source_target_pairs={{0,18},{2,16},{16,2},{18,0},{1,19},{3,17},{17,3},{19,1},{4,22},{6,... | collective-permute-start | bytes 393224 | tf_op jit(solution)/shard_map/ppermute | solution.py:419
  57.6 2.3 %project.5 = (bf16[256,256]{1,0:T(8,128)(2,1)}, bf16[256,256]{1,0:T(8,128)(2,1)}, f32[256,256]{1,0:T(8,128)S(1)}) custom-call(bf16[2,512,256]{2,1,0:T(8,128)(2,1)S(1)} %get-tuple-element.29.refs_0_.refs_4_, bf16[2,512,256]{2,1,0:T(8,128)(2,1)S(1)} %collective-permute-done.pair_ref.refs_1_.refs_5_, bf16[512,256]{1,0:T(8,128)(2,1)S(1)} %collective-permute-done.11.refs_2_, ...), custom_call_target="tpu_custom_call" | custom-call | tf_op jit(solution)/shard_map/project/pallas_call | solution.py:193
  61.0 2.4 %collective-permute-start.14 = (bf16[256,256]{1,0:T(8,128)(2,1)}, bf16[256,256]{1,0:T(8,128)(2,1)}, u32[]{:S(2)}, u32[]{:S(2)}) collective-permute-start(bf16[256,256]{1,0:T(8,128)(2,1)} %get-tuple-element.42), channel_id=1, source_target_pairs={{0,18},{2,16},{16,2},{18,0},{1,19},{3,17},{17,3},{19,1},{4,22},{6,... | collective-permute-start | bytes 393224 | tf_op jit(solution)/shard_map/ppermute | solution.py:419
  63.4 2.2 %project.3 = (bf16[256,256]{1,0:T(8,128)(2,1)}, bf16[256,256]{1,0:T(8,128)(2,1)}, f32[256,256]{1,0:T(8,128)S(1)}) custom-call(bf16[2,512,256]{2,1,0:T(8,128)(2,1)S(1)} %get-tuple-element.29.refs_0_.refs_4_, bf16[2,512,256]{2,1,0:T(8,128)(2,1)S(1)} %collective-permute-done.pair_ref.refs_1_.refs_5_, ...), custom_call_target="tpu_custom_call" | custom-call | tf_op jit(solution)/shard_map/project/pallas_call | solution.py:193
  68.1 1.3 %copy-done.5 = f32[128,2048]{1,0:T(8,128)S(1)} copy-done((f32[128,2048]{1,0:T(8,128)S(1)}, f32[128,2048]{1,0:T(8,128)}, u32[]{:S(2)}) %copy-start.5) | copy-done | bytes 1048600
  71.1 2.1 %attend_own.3 = (f32[128,2048]{1,0:T(8,128)S(1)}, bf16[128,2048]{1,0:T(8,128)(2,1)S(1)}) custom-call(bf16[256,2048]{1,0:T(8,128)(2,1)S(1)} %bitcast.10, f32[256,256]{1,0:T(8,128)S(1)} %get-tuple-element.43.refs_0_, bf16[256,256]{1,0:T(8,128)(2,1)} %collective-permute-done.15.refs_1_, bf16[256,256]{1,0:T(8,128)(2,1)} %collective-permute-done.16.refs_2_, ...), custom_call_target="tpu_custom_call" | custom-call | tf_op jit(solution)/shard_map/attend_own/pallas_call | solution.py:303
  73.3 2.2 %attend_own.2 = (f32[128,2048]{1,0:T(8,128)S(1)}, bf16[128,2048]{1,0:T(8,128)(2,1)S(1)}) custom-call(bf16[256,2048]{1,0:T(8,128)(2,1)S(1)} %bitcast.11, f32[256,256]{1,0:T(8,128)S(1)} %get-tuple-element.43.refs_0_, bf16[256,256]{1,0:T(8,128)(2,1)} %collective-permute-done.15.refs_1_, bf16[256,256]{1,0:T(8,128)(2,1)} %collective-permute-done.16.refs_2_, ...), custom_call_target="tpu_custom_call" | custom-call | tf_op jit(solution)/shard_map/attend_own/pallas_call | solution.py:303
  75.5 2.4 %finish.1 = bf16[256,2048]{1,0:T(8,128)(2,1)} custom-call(s32[1]{0:T(128)} %bitcast.1.live_ref, f32[256,256]{1,0:T(8,128)S(1)} %copy-done.11, bf16[256,256]{1,0:T(8,128)(2,1)} %collective-permute-done.9.refs_1_, bf16[256,256]{1,0:T(8,128)(2,1)} %collective-permute-done.10.refs_2_, bf16[256,256]{1,0:T(8,128)(2,1)} %collective-permute-done.14.refs_3_, ...), custom_call_target="tpu_custom_call" | custom-call | tf_op jit(solution)/shard_map/finish/pallas_call | solution.py:334
  (54 shorter events, 11.1 us)
Async XLA Ops:
  4.0 20.6 %copy-start = (bf16[1,2,128,2048]{3,2,1,0:T(8,128)(2,1)S(1)}, bf16[1,2,128,2048]{3,2,1,0:T(8,128)(2,1)}, u32[]{:S(2)}) copy-start(bf16[1,2,128,2048]{3,2,1,0:T(8,128)(2,1)} %param.10) | copy-start | bytes 3145732
  4.1 15.3 %collective-permute-start = (bf16[2,512,256]{2,1,0:T(8,128)(2,1)S(1)}, bf16[2,512,256]{2,1,0:T(8,128)(2,1)S(1)}, u32[]{:S(2)}, u32[]{:S(2)}) collective-permute-start(bf16[2,512,256]{2,1,0:T(8,128)(2,1)S(1)} %get-tuple-element.29.refs_0_.refs_4_), channel_id=1, source_target_pairs={{0,8},{8,12},{12,4},{4,0},{1,9},{9,13},{13,5},{5,1},{2,10},{10,14}... | collective-permute-start | bytes 1572872 | tf_op jit(solution)/shard_map/ppermute | solution.py:389
  8.2 14.8 %collective-permute-start.4 = (bf16[2,512,256]{2,1,0:T(8,128)(2,1)S(1)}, bf16[2,512,256]{2,1,0:T(8,128)(2,1)S(1)}, u32[]{:S(2)}, u32[]{:S(2)}) collective-permute-start(bf16[2,512,256]{2,1,0:T(8,128)(2,1)S(1)} %get-tuple-element.32.refs_0_), channel_id=1, source_target_pairs={{0,2},{2,0},{1,3},{3,1},{4,6},{6,4},{5,7},{7,5},{8,10},{10,8},{9,1... | collective-permute-start | bytes 1572872 | tf_op jit(solution)/shard_map/ppermute | solution.py:386
  9.7 1.6 %copy-start.1 = (bf16[1,2,128,4096]{3,2,1,0:T(8,128)(2,1)S(1)}, bf16[1,2,128,4096]{3,2,1,0:T(8,128)(2,1)}, u32[]{:S(2)}) copy-start(bf16[1,2,128,4096]{3,2,1,0:T(8,128)(2,1)} %param.9) | copy-start | bytes 6291460
  11.5 23.8 %collective-permute-start.12 = (bf16[256,1024]{1,0:T(8,128)(2,1)S(1)}, bf16[256,1024]{1,0:T(8,128)(2,1)S(1)}, u32[]{:S(2)}, u32[]{:S(2)}) collective-permute-start(bf16[256,1024]{1,0:T(8,128)(2,1)S(1)} %get-tuple-element.41), channel_id=1, source_target_pairs={{0,18},{2,16},{16,2},{18,0},{1,19},{3,17},{17,3},{19,1},{4,22},{6,... | collective-permute-start | bytes 1572872 | tf_op jit(solution)/shard_map/ppermute | solution.py:407
  13.1 31.0 %collective-permute-start.3 = (bf16[256,1024]{1,0:T(8,128)(2,1)S(1)}, bf16[256,1024]{1,0:T(8,128)(2,1)S(1)}, u32[]{:S(2)}, u32[]{:S(2)}) collective-permute-start(bf16[256,1024]{1,0:T(8,128)(2,1)S(1)} %get-tuple-element.31), channel_id=1, source_target_pairs={{0,2},{2,0},{16,18},{18,16},{1,3},{3,1},{17,19},{19,17},{4,6},{6,4... | collective-permute-start | bytes 1572872 | tf_op jit(solution)/shard_map/ppermute | solution.py:407
  14.6 29.5 %collective-permute-start.6 = (bf16[256,1024]{1,0:T(8,128)(2,1)S(1)}, bf16[256,1024]{1,0:T(8,128)(2,1)S(1)}, u32[]{:S(2)}, u32[]{:S(2)}) collective-permute-start(bf16[256,1024]{1,0:T(8,128)(2,1)S(1)} %get-tuple-element.36), channel_id=1, source_target_pairs={{0,16},{2,18},{16,0},{18,2},{1,17},{3,19},{17,1},{19,3},{4,20},{6,... | collective-permute-start | bytes 1572872 | tf_op jit(solution)/shard_map/ppermute | solution.py:407
  19.4 25.2 %collective-permute-start.2 = (bf16[2,512,256]{2,1,0:T(8,128)(2,1)S(1)}, bf16[2,512,256]{2,1,0:T(8,128)(2,1)S(1)}, u32[]{:S(2)}, u32[]{:S(2)}) collective-permute-start(bf16[2,512,256]{2,1,0:T(8,128)(2,1)S(1)} %get-tuple-element.29.refs_0_.refs_4_), channel_id=1, source_target_pairs={{8,0},{12,8},{4,12},{0,4},{9,1},{13,9},{5,13},{1,5},{10,2},{14,10}... | collective-permute-start | bytes 1572872 | tf_op jit(solution)/shard_map/ppermute | solution.py:390
  23.0 21.7 %collective-permute-start.1 = (bf16[512,256]{1,0:T(8,128)(2,1)S(1)}, bf16[512,256]{1,0:T(8,128)(2,1)S(1)}, u32[]{:S(2)}, u32[]{:S(2)}) collective-permute-start(bf16[512,256]{1,0:T(8,128)(2,1)S(1)} %get-tuple-element.30), channel_id=1, source_target_pairs={{0,8},{8,12},{12,4},{4,0},{1,9},{9,13},{13,5},{5,1},{2,10},{10,14}... | collective-permute-start | bytes 786440 | tf_op jit(solution)/shard_map/ppermute | solution.py:398
  32.7 11.4 %copy-start.2 = (f32[128,2048]{1,0:T(8,128)}, f32[128,2048]{1,0:T(8,128)S(1)}, u32[]{:S(2)}) copy-start(f32[128,2048]{1,0:T(8,128)S(1)} %get-tuple-element.47.refs_6_) | copy-start | bytes 3145732
  35.3 18.1 %collective-permute-start.13 = (bf16[256,1024]{1,0:T(8,128)(2,1)S(1)}, bf16[256,1024]{1,0:T(8,128)(2,1)S(1)}, u32[]{:S(2)}, u32[]{:S(2)}) collective-permute-start(bf16[256,1024]{1,0:T(8,128)(2,1)S(1)} %after.5.refs_8_), channel_id=1, source_target_pairs={{0,1},{1,0},{2,3},{3,2},{4,5},{5,4},{6,7},{7,6},{8,9},{9,8},{10,11... | collective-permute-start | bytes 1572872 | tf_op jit(solution)/shard_map/ppermute | solution.py:416
  44.1 13.5 %collective-permute-start.8 = (bf16[256,1024]{1,0:T(8,128)(2,1)S(1)}, bf16[256,1024]{1,0:T(8,128)(2,1)S(1)}, u32[]{:S(2)}, u32[]{:S(2)}) collective-permute-start(bf16[256,1024]{1,0:T(8,128)(2,1)S(1)} %get-tuple-element.37.refs_8_), channel_id=1, source_target_pairs={{0,1},{1,0},{2,3},{3,2},{4,5},{5,4},{6,7},{7,6},{8,9},{9,8},{10,11... | collective-permute-start | bytes 1572872 | tf_op jit(solution)/shard_map/ppermute | solution.py:416
  44.1 13.5 %collective-permute-start.5 = (bf16[256,1024]{1,0:T(8,128)(2,1)S(1)}, bf16[256,1024]{1,0:T(8,128)(2,1)S(1)}, u32[]{:S(2)}, u32[]{:S(2)}) collective-permute-start(bf16[256,1024]{1,0:T(8,128)(2,1)S(1)} %after.3.refs_4_), channel_id=1, source_target_pairs={{0,1},{1,0},{2,3},{3,2},{4,5},{5,4},{6,7},{7,6},{8,9},{9,8},{10,11... | collective-permute-start | bytes 1572872 | tf_op jit(solution)/shard_map/ppermute | solution.py:416
  44.6 12.9 %collective-permute-start.7 = (bf16[256,1024]{1,0:T(8,128)(2,1)S(1)}, bf16[256,1024]{1,0:T(8,128)(2,1)S(1)}, u32[]{:S(2)}, u32[]{:S(2)}) collective-permute-start(bf16[256,1024]{1,0:T(8,128)(2,1)S(1)} %after.4.refs_6_), channel_id=1, source_target_pairs={{0,1},{1,0},{2,3},{3,2},{4,5},{5,4},{6,7},{7,6},{8,9},{9,8},{10,11... | collective-permute-start | bytes 1572872 | tf_op jit(solution)/shard_map/ppermute | solution.py:416
  44.7 8.6 %collective-permute-start.11 = (bf16[512,256]{1,0:T(8,128)(2,1)S(1)}, bf16[512,256]{1,0:T(8,128)(2,1)S(1)}, u32[]{:S(2)}, u32[]{:S(2)}) collective-permute-start(bf16[512,256]{1,0:T(8,128)(2,1)S(1)} %get-tuple-element.33.refs_2_), channel_id=1, source_target_pairs={{0,8},{8,12},{12,4},{4,0},{1,9},{9,13},{13,5},{5,1},{2,10},{10,14}... | collective-permute-start | bytes 786440 | tf_op jit(solution)/shard_map/ppermute | solution.py:398
  55.0 11.8 %collective-permute-start.17 = (bf16[256,256]{1,0:T(8,128)(2,1)S(1)}, bf16[256,256]{1,0:T(8,128)(2,1)S(1)}, u32[]{:S(2)}, u32[]{:S(2)}) collective-permute-start(bf16[256,256]{1,0:T(8,128)(2,1)S(1)} %get-tuple-element.46), channel_id=1, source_target_pairs={{0,18},{2,16},{16,2},{18,0},{1,19},{3,17},{17,3},{19,1},{4,22},{6,... | collective-permute-start | bytes 393224 | tf_op jit(solution)/shard_map/ppermute | solution.py:419
  59.9 8.2 %collective-permute-start.15 = (bf16[256,256]{1,0:T(8,128)(2,1)}, bf16[256,256]{1,0:T(8,128)(2,1)}, u32[]{:S(2)}, u32[]{:S(2)}) collective-permute-start(bf16[256,256]{1,0:T(8,128)(2,1)} %get-tuple-element.44), channel_id=1, source_target_pairs={{0,2},{2,0},{16,18},{18,16},{1,3},{3,1},{17,19},{19,17},{4,6},{6,4... | collective-permute-start | bytes 393224 | tf_op jit(solution)/shard_map/ppermute | solution.py:419
  60.5 7.6 %collective-permute-start.16 = (bf16[256,256]{1,0:T(8,128)(2,1)}, bf16[256,256]{1,0:T(8,128)(2,1)}, u32[]{:S(2)}, u32[]{:S(2)}) collective-permute-start(bf16[256,256]{1,0:T(8,128)(2,1)} %get-tuple-element.45), channel_id=1, source_target_pairs={{0,16},{2,18},{16,0},{18,2},{1,17},{3,19},{17,1},{19,3},{4,20},{6,... | collective-permute-start | bytes 393224 | tf_op jit(solution)/shard_map/ppermute | solution.py:419
  61.0 14.5 %collective-permute-start.14 = (bf16[256,256]{1,0:T(8,128)(2,1)}, bf16[256,256]{1,0:T(8,128)(2,1)}, u32[]{:S(2)}, u32[]{:S(2)}) collective-permute-start(bf16[256,256]{1,0:T(8,128)(2,1)} %get-tuple-element.42), channel_id=1, source_target_pairs={{0,18},{2,16},{16,2},{18,0},{1,19},{3,17},{17,3},{19,1},{4,22},{6,... | collective-permute-start | bytes 393224 | tf_op jit(solution)/shard_map/ppermute | solution.py:419
  66.3 9.1 %collective-permute-start.9 = (bf16[256,256]{1,0:T(8,128)(2,1)}, bf16[256,256]{1,0:T(8,128)(2,1)}, u32[]{:S(2)}, u32[]{:S(2)}) collective-permute-start(bf16[256,256]{1,0:T(8,128)(2,1)} %get-tuple-element.39), channel_id=1, source_target_pairs={{0,2},{2,0},{16,18},{18,16},{1,3},{3,1},{17,19},{19,17},{4,6},{6,4... | collective-permute-start | bytes 393224 | tf_op jit(solution)/shard_map/ppermute | solution.py:419
  66.9 8.6 %collective-permute-start.10 = (bf16[256,256]{1,0:T(8,128)(2,1)}, bf16[256,256]{1,0:T(8,128)(2,1)}, u32[]{:S(2)}, u32[]{:S(2)}) collective-permute-start(bf16[256,256]{1,0:T(8,128)(2,1)} %get-tuple-element.40), channel_id=1, source_target_pairs={{0,16},{2,18},{16,0},{18,2},{1,17},{3,19},{17,1},{19,3},{4,20},{6,... | collective-permute-start | bytes 393224 | tf_op jit(solution)/shard_map/ppermute | solution.py:419
  68.0 5.2 %copy-start.3 = (f32[128,2048]{1,0:T(8,128)S(1)}, f32[128,2048]{1,0:T(8,128)}, u32[]{:S(2)}) copy-start(f32[128,2048]{1,0:T(8,128)} %copy-done.2) | copy-start | bytes 3145732
  68.1 1.3 %copy-start.5 = (f32[128,2048]{1,0:T(8,128)S(1)}, f32[128,2048]{1,0:T(8,128)}, u32[]{:S(2)}) copy-start(f32[128,2048]{1,0:T(8,128)} %copy-done.4) | copy-start | bytes 3145732
  73.2 2.3 %copy-start.11 = (f32[256,256]{1,0:T(8,128)S(1)}, f32[256,256]{1,0:T(8,128)}, u32[]{:S(2)}) copy-start(f32[256,256]{1,0:T(8,128)} %copy-done.10) | copy-start | bytes 786436
  (8 other events, 7.3 us)

commit v6 on v5

v6 whole, which is shorter than its diff:
```python
import functools
import math

import jax
import jax.numpy as jnp
import numpy as np
from jax import lax
from jax.experimental import pallas as pl
from jax.experimental.pallas import tpu as pltpu
from jax.sharding import PartitionSpec as P

HD = 128
PLEN = 1024
FACTOR = HD**-0.5 * math.log2(math.e)
MIB = 1 << 20
ANYWHERE = pl.BlockSpec(memory_space=pl.ANY)
HBM = pl.BlockSpec(memory_space=pltpu.HBM)


def dot_nt(a, b):
    return lax.dot_general(a, b, (((1,), (1,)), ((), ())), preferred_element_type=jnp.float32)


def dot_nn(a, b):
    return lax.dot_general(a, b, (((1,), (0,)), ((), ())), preferred_element_type=jnp.float32)


def settings(limit):
    return {
        "compiler_params": pltpu.CompilerParams(vmem_limit_bytes=limit * MIB),
        "cost_estimate": pl.CostEstimate(flops=0, bytes_accessed=0, transcendentals=0),
    }


def after(value, *earlier):
    return pl.pallas_call(
        lambda *refs: None,
        in_specs=[ANYWHERE] * (1 + len(earlier)),
        out_specs=ANYWHERE,
        out_shape=jax.ShapeDtypeStruct(value.shape, value.dtype),
        input_output_aliases={0: 0},
        name="after",
        **settings(1),
    )(value, *earlier)


def run_copies(copies):
    for copy in copies:
        copy.start()
    for copy in copies:
        copy.wait()


def pack_rows(n_groups, key_weight, value_weight, prompt_keys, prompt_values):
    block, columns = key_weight.shape
    half = block // n_groups

    arguments = [
        pltpu.with_memory_space_constraint(x, pltpu.HBM)
        for x in (key_weight, value_weight, prompt_keys, prompt_values)
    ]

    def body(kw_ref, vw_ref, pk_ref, pv_ref, share_ref, cache_ref, ks_ref, vs_ref, sems):
        rows = pl.ds(pl.multiple_of(lax.axis_index("groups") * half, half), half)
        run_copies(
            [
                pltpu.make_async_copy(pk_ref, cache_ref.at[0], sems.at[0]),
                pltpu.make_async_copy(pv_ref, cache_ref.at[1], sems.at[1]),
                pltpu.make_async_copy(kw_ref.at[rows, :], share_ref.at[0], sems.at[2]),
                pltpu.make_async_copy(vw_ref.at[rows, :], share_ref.at[1], sems.at[3]),
                pltpu.make_async_copy(kw_ref.at[rows, :], ks_ref, sems.at[4]),
                pltpu.make_async_copy(vw_ref.at[rows, :], vs_ref, sems.at[5]),
            ]
        )

    return pl.pallas_call(
        body,
        in_specs=[HBM] * 4,
        out_specs=[ANYWHERE] * 4,
        out_shape=[
            jax.ShapeDtypeStruct((2, half, columns), key_weight.dtype),
            jax.ShapeDtypeStruct((2, *prompt_keys.shape), prompt_keys.dtype),
            jax.ShapeDtypeStruct((half, columns), key_weight.dtype),
            jax.ShapeDtypeStruct((half, columns), key_weight.dtype),
        ],
        scratch_shapes=[pltpu.SemaphoreType.DMA((6,))],
        name="pack_rows",
        **settings(1),
    )(*arguments)


def pack_features(sizes, block, sets, hidden):
    n_groups, n_fsdp, n_resp, n_tp = sizes
    rows, width = hidden.shape
    per_core = n_fsdp // n_tp
    half = block // n_groups

    def start_of(place, n):
        group = (lax.axis_index("groups") + place[0]) % n_groups
        resp = (lax.axis_index("resp") + place[1]) % n_resp
        return (n * n_resp + resp) * block + group * half

    if half % HD:
        return [
            jnp.concatenate(
                [
                    lax.dynamic_slice_in_dim(hidden, start_of(place, n), half, axis=1)
                    for n in range(per_core)
                ],
                axis=1,
            )
            for place in sets
        ]

    step = rows // 4

    def body(hidden_ref, *refs):
        outs, (held, sems) = refs[: len(sets)], refs[len(sets) :]
        copies = []
        for n in range(rows // step):
            part = pl.ds(n * step, step)
            copies.append(
                pltpu.make_async_copy(hidden_ref.at[part, :], held.at[part, :], sems.at[n])
            )
        for copy in copies:
            copy.start()
        for n, copy in enumerate(copies):
            copy.wait()
            part = slice(n * step, (n + 1) * step)
            for place, out in zip(sets, outs):
                for k in range(per_core):
                    first = pl.multiple_of(start_of(place, k), HD)
                    out[part, k * half : (k + 1) * half] = held[part, pl.ds(first, half)]

    shape = (rows, per_core * half)
    return pl.pallas_call(
        body,
        grid=(1,),
        in_specs=[HBM],
        out_specs=[pl.BlockSpec(shape, lambda _: (0, 0))] * len(sets),
        out_shape=[jax.ShapeDtypeStruct(shape, hidden.dtype)] * len(sets),
        scratch_shapes=[pltpu.VMEM((rows, width), hidden.dtype), pltpu.SemaphoreType.DMA((4,))],
        name="pack_features",
        **settings(12),
    )(pltpu.with_memory_space_constraint(hidden, pltpu.HBM))


def line_ring(size):
    return list(range(0, size, 2)) + list(range(1, size, 2))[::-1]


def owner_of(n_fsdp, hops):
    fsdp = lax.axis_index("fsdp")
    place = jnp.where(fsdp % 2 == 0, fsdp // 2, n_fsdp - (fsdp + 1) // 2)
    at = (place - hops + n_fsdp) % n_fsdp
    return jnp.where(at < n_fsdp // 2, 2 * at, 2 * n_fsdp - 1 - 2 * at)


def project(n_fsdp, pieces, kinds, pairs, types, waits=()):
    half, columns = pieces[0][0][0].shape[-2:]
    rows, depth = pairs[0][0].shape
    dtype = pairs[0][0].dtype
    listed = [piece for kind in kinds for piece in pieces[kind]]
    total, count = len(listed), len(pairs)
    each = total // len(kinds)

    def body(*refs):
        piece_refs, refs = refs[:total], refs[total:]
        pair_refs, refs = refs[: 2 * count], refs[2 * count + len(waits) :]
        outs, weights = refs[:-1], refs[-1]
        core = lax.axis_index("tp")
        owners = [owner_of(n_fsdp, hops) for _, _, hops in listed[:each]]
        for k in range(len(kinds)):
            for ref, owner in zip(piece_refs[k * each : (k + 1) * each], owners):
                rows_here = pl.ds(pl.multiple_of(owner * half, half), half)
                weights[k, rows_here, :] = ref[0] if len(ref.shape) == 3 else ref[...]
        first = pl.ds(pl.multiple_of(core * depth, depth), depth)
        second = pl.ds(pl.multiple_of((1 - core) * depth, depth), depth)
        for n in range(count):
            near_ref, far_ref = pair_refs[2 * n : 2 * n + 2]
            for k in range(len(kinds)):
                sums = dot_nn(near_ref[...], weights[k, first, :])
                sums = sums + dot_nn(far_ref[...], weights[k, second, :])
                out = outs[n * len(kinds) + k]
                out[...] = sums.astype(out.dtype)

    def whole(shape):
        return pl.BlockSpec(shape, lambda _: (0,) * len(shape))

    def piece_spec(index):
        if index is None:
            return whole((half, columns))
        return pl.BlockSpec((1, half, columns), lambda _: (index, 0, 0))

    types = [t for t in types for _ in kinds]
    return pl.pallas_call(
        body,
        grid=(1,),
        in_specs=[piece_spec(index) for _, index, _ in listed]
        + [whole((rows, depth))] * (2 * count)
        + [ANYWHERE] * len(waits),
        out_specs=[whole((rows, columns))] * len(types),
        out_shape=[jax.ShapeDtypeStruct((rows, columns), t) for t in types],
        scratch_shapes=[pltpu.VMEM((len(kinds), n_fsdp * half, columns), dtype)],
        name="project",
        **settings(24),
    )(*[x for x, _, _ in listed], *[x for pair in pairs for x in pair], *waits)


def take(ref, first, count):
    return jnp.concatenate(
        [ref[:, (first + n) * HD : (first + n + 1) * HD] for n in range(count)], axis=0
    )


def put(ref, first, count, value):
    tokens = ref.shape[0]
    value = jnp.broadcast_to(value, (count * tokens, HD)).astype(ref.dtype)
    for n in range(count):
        ref[:, (first + n) * HD : (first + n + 1) * HD] = value[n * tokens : (n + 1) * tokens]


def attend_cache(slot, tokens, group_size, queries, caches, waits):
    count = len(caches)
    heads = queries.shape[1] // (group_size * HD)
    length = caches[0].shape[1]
    step = 2 if group_size % 2 == 0 else 1

    def body(q_ref, *refs):
        mixed_ref, level_ref, mark_ref = refs[-3:]
        mark_ref[...] = jnp.zeros(mark_ref.shape, mark_ref.dtype)
        keys = [ref[0] for ref in refs[:count]]
        values = [ref[1] for ref in refs[:count]]
        wide = [jnp.concatenate([v, jnp.ones(v.shape, v.dtype)], axis=1) for v in values]

        def scores_of(first):
            q = take(q_ref, first, step)
            return [dot_nt(q, k) for k in keys]

        coming = scores_of(0)
        for first in range(0, group_size, step):
            scores = coming
            if first + step < group_size:
                coming = scores_of(first + step)
            tops = [s[:, n * HD : (n + 1) * HD] for s in scores for n in range(length // HD)]
            top = jnp.max(functools.reduce(jnp.maximum, tops), axis=1, keepdims=True)
            out = None
            for s, v in zip(scores, wide):
                probs = jnp.exp2((s - top) * FACTOR).astype(jnp.bfloat16)
                part = dot_nn(probs, v)
                out = part if out is None else out + part
            total = out[:, HD:]
            put(mixed_ref, first, step, out[:, :HD] / total)
            put(level_ref, first, step, top * FACTOR + jnp.log2(total))

    width = group_size * HD
    spec_q = pl.BlockSpec((tokens, width), lambda head: (slot, head))
    spec_c = pl.BlockSpec((2, length, HD), lambda head: (0, 0, head))
    spec_out = pl.BlockSpec((tokens, width), lambda head: (0, head))
    return pl.pallas_call(
        body,
        grid=(heads,),
        in_specs=[spec_q] + [spec_c] * count + [ANYWHERE] * len(waits),
        out_specs=[spec_out] * 2 + [pl.BlockSpec((8, HD), lambda head: (0, 0))],
        out_shape=[jax.ShapeDtypeStruct((tokens, heads * width), jnp.float32)] * 2
        + [jax.ShapeDtypeStruct((8, HD), jnp.float32)],
        name="attend_cache",
        **settings(20),
    )(queries, *caches, *waits)


def sum_refs(refs, rows=slice(None)):
    views = [ref[0, rows] if len(ref.shape) == 3 else ref[rows] for ref in refs]
    return functools.reduce(jnp.add, [view.astype(jnp.float32) for view in views])


def part_spec(part, kind, rows, index):
    if len(part.shape) == 3:
        return pl.BlockSpec((1, rows, HD), lambda head: (kind, index, head))
    return pl.BlockSpec((rows, HD), lambda head: (index, head))


def attend_own(slot, tokens, group_size, queries, key_parts, table, state):
    parts = len(key_parts)
    heads = queries.shape[1] // (group_size * HD)

    def body(q_ref, *refs):
        table_ref, old_mixed, old_level, mixed_ref, probs_ref, table, sem = refs[parts:]

        @pl.when(pl.program_id(0) == 0)
        def _():
            copy = pltpu.make_async_copy(table_ref, table, sem)
            copy.start()
            copy.wait()

        key = sum_refs(refs[:parts])
        key = key * table[0] + pltpu.roll(key, HD // 2, 1) * table[1]
        key = key.astype(jnp.bfloat16)
        ones = jnp.ones((tokens, HD), jnp.bfloat16)
        row = lax.broadcasted_iota(jnp.int32, (tokens, tokens), 0)
        causal = row >= lax.broadcasted_iota(jnp.int32, (tokens, tokens), 1)
        causal = jnp.concatenate([causal] * group_size, axis=0)
        scores = dot_nt(take(q_ref, 0, group_size), key) * FACTOR
        scores = jnp.where(causal, scores, -1e30)
        level = take(old_level, 0, group_size)
        top = jnp.max(jnp.maximum(level, scores), axis=1, keepdims=True)
        probs = jnp.exp2(scores - top)
        kept = jnp.exp2(level - top)
        inverse = 1.0 / (kept + dot_nn(probs.astype(jnp.bfloat16), ones))
        put(mixed_ref, 0, group_size, take(old_mixed, 0, group_size) * (kept * inverse))
        put(probs_ref, 0, group_size, probs * inverse)

    width = group_size * HD
    spec_q = pl.BlockSpec((tokens, width), lambda head: (slot, head))
    spec_keys = [part_spec(part, 0, tokens, slot) for part in key_parts]
    spec_wide = pl.BlockSpec((tokens, width), lambda head: (0, head))
    shape = (tokens, heads * width)
    return pl.pallas_call(
        body,
        grid=(heads,),
        in_specs=[spec_q] + spec_keys + [HBM] + [spec_wide] * 2,
        out_specs=[spec_wide] * 2,
        out_shape=[
            jax.ShapeDtypeStruct(shape, jnp.float32),
            jax.ShapeDtypeStruct(shape, jnp.bfloat16),
        ],
        scratch_shapes=[pltpu.VMEM(table.shape, table.dtype), pltpu.SemaphoreType.DMA],
        name="attend_own",
        **settings(20),
    )(queries, *key_parts, pltpu.with_memory_space_constraint(table, pltpu.HBM), *state)


def finish(live, value_parts, states, tokens, group_size, dtype):
    parts, slots = len(value_parts), len(states)
    width = group_size * HD
    heads = states[0][0].shape[1] // width

    def body(live_ref, *refs):
        out_ref = refs[-1]
        for slot in range(slots):
            mixed_ref, probs_ref = refs[parts + 2 * slot : parts + 2 * slot + 2]
            rows = slice(slot * tokens, (slot + 1) * tokens)
            value = sum_refs(refs[:parts], rows).astype(jnp.bfloat16)
            out = take(mixed_ref, 0, group_size) + dot_nn(take(probs_ref, 0, group_size), value)
            out = jnp.where(slot < live_ref[0], out, 0.0)
            put(out_ref.at[rows, :], 0, group_size, out)

    spec_values = [part_spec(part, 1, slots * tokens, 0) for part in value_parts]
    spec_wide = pl.BlockSpec((tokens, width), lambda head: (0, head))
    return pl.pallas_call(
        body,
        grid=(heads,),
        in_specs=[pl.BlockSpec(memory_space=pltpu.SMEM)]
        + spec_values
        + [spec_wide] * (2 * slots),
        out_specs=pl.BlockSpec((slots * tokens, width), lambda head: (0, head)),
        out_shape=jax.ShapeDtypeStruct((slots * tokens, heads * width), dtype),
        name="finish",
        **settings(20),
    )(live, *value_parts, *[x for state in states for x in state])


def rotation_tables(extent, offset):
    orders = np.arange(HD // 2, dtype=np.float64)
    inverse = np.exp(-(2.0 * orders / HD) * math.log(500000.0))
    angles = (offset + np.arange(extent))[:, None] * inverse[None, :]
    cosine, sine = np.cos(angles), np.sin(angles)
    halves = [np.concatenate([cosine, cosine], axis=1), np.concatenate([-sine, sine], axis=1)]
    return jnp.asarray(np.stack(halves), jnp.float32)


def on_device(sizes, hidden, queries, prompt_keys, prompt_values, key_weight, value_weight, counts):
    n_groups, n_fsdp, n_resp, n_tp = sizes
    _, slots, tokens, part_width = hidden.shape
    block, columns = key_weight.shape
    group_size = queries.shape[3] // columns
    rows = slots * tokens
    plane = ("groups", "resp")
    cores = [(n, (n + 1) % n_tp) for n in range(n_tp)]
    ring = line_ring(n_fsdp)
    rightward = [(ring[n], ring[(n + 1) % n_fsdp]) for n in range(n_fsdp)]
    leftward = [(b, a) for a, b in rightward]
    along = [(0, b) for b in range(1, n_resp)]
    across = [(a, b) for a in range(1, n_groups) for b in range(1, n_resp)]
    twins = [(a, 0) for a in range(1, n_groups)]
    sets = [(0, 0), *across, *along, *twins]

    def shift(a, b):
        return [
            (g * n_resp + r, (g + a) % n_groups * n_resp + (r + b) % n_resp)
            for g in range(n_groups)
            for r in range(n_resp)
        ]

    share, cache, key_share, value_share = pack_rows(n_groups, key_weight, value_weight, prompt_keys[0], prompt_values[0])

    caches = [cache]
    for b in range(1, n_resp):
        around = [(n, (n + b) % n_resp) for n in range(n_resp)]
        caches.append(lax.ppermute(cache, "resp", around))

    pieces = [[(share, kind, 0)] for kind in range(2)]
    held = share
    for hop in range(1, n_fsdp // 2 + 1):
        held = lax.ppermute(held, "fsdp", rightward)
        for kind in range(2):
            pieces[kind].append((held, kind, hop))
    first_hop, far_hop = pieces[0][1][0], held
    held = share
    for hop in range(1, n_fsdp - n_fsdp // 2 - 1):
        held = lax.ppermute(held, "fsdp", leftward)
        for kind in range(2):
            pieces[kind].append((held, kind, -hop))
    ends = (key_share, value_share) if held is share else (held[0], held[1])
    ends = [lax.ppermute(x, "fsdp", leftward) for x in ends]
    for kind in range(2):
        pieces[kind].append((ends[kind], None, 1 + n_fsdp // 2 - n_fsdp))

    flat_queries = queries.reshape(rows, queries.shape[3])
    states, marks = [], []
    for slot in range(slots):
        *state, mark = attend_cache(slot, tokens, group_size, flat_queries, caches, [first_hop])
        states.append(state)
        marks.append(mark)

    near = dict(zip(sets, pack_features(sizes, block, sets, hidden.reshape(rows, part_width))))
    for place in twins:
        near[place] = after(near[place], first_hop)
    for place in sets[1:]:
        waits = [ends[1]] if place in along else [far_hop, ends[0]]
        moved = lax.ppermute(near[place], plane, shift(*place))
        near[place] = after(moved, *marks, *waits)
    far = {place: lax.ppermute(near[place], "tp", cores) for place in sets}

    def send(place, sums):
        return lax.ppermute(sums, plane, shift(n_groups - place[0], n_resp - place[1]))

    narrow, wide = jnp.bfloat16, jnp.float32
    soon = [sets[0], *across, *twins]
    types = [wide] + [narrow] * (len(soon) - 1)
    pairs = [(near[p], far[p]) for p in soon]
    parts = [[], []]
    for kind in range(2):
        waits = [near[p] for p in along] if kind else []
        sums = project(n_fsdp, pieces, [kind], pairs, types, waits)
        parts[kind].append(sums[0])
        parts[kind].extend(send(p, x) for p, x in zip(soon[1:], sums[1:]))
    pairs = [(near[p], far[p]) for p in along]
    sums = project(n_fsdp, pieces, [0, 1], pairs, [narrow] * len(along))
    for n, p in enumerate(along):
        for kind in range(2):
            parts[kind].append(send(p, sums[2 * n + kind]))

    table = rotation_tables(tokens, PLEN)
    states = [
        attend_own(slot, tokens, group_size, flat_queries, parts[0], table, state)
        for slot, state in enumerate(states)
    ]
    live = (counts[0] - lax.axis_index("resp") * slots).astype(jnp.int32)[None]
    out = finish(live, parts[1], states, tokens, group_size, queries.dtype)
    return out.reshape(queries.shape)


def solution(mesh):
    placed = (
        P(("groups", "fsdp"), "resp", None, "tp"),
        P(("groups", "fsdp"), "resp", None, "tp"),
        P(("groups", "fsdp"), "resp", "tp"),
        P(("groups", "fsdp"), "resp", "tp"),
        P(("fsdp", "resp"), "tp"),
        P(("fsdp", "resp"), "tp"),
        P(("groups", "fsdp")),
    )
    sizes = tuple(mesh.shape[name] for name in ("groups", "fsdp", "resp", "tp"))
    return jax.shard_map(
        functools.partial(on_device, sizes),
        mesh=mesh,
        in_specs=placed,
        out_specs=P(("groups", "fsdp"), "resp", None, "tp"),
        check_vma=False,
    )
```

time: 78.5 us -> 76.9 us (0.980)
  local copies, waits for them, and re-layouts: 10.2 us -> 3.17 us
  Pallas kernels: 20.4 us -> 23.8 us
  waiting for transfers between devices: 24.1 us -> 27.4 us
  starting transfers between devices: 22.4 us -> 21.3 us
    unnamed x28 -> x14, local copies, waits for them, and re-layouts: 10.2 us -> 3.17 us
    pallas_call x8 -> x7, Pallas kernels: 10.9 us -> 14.4 us  [the longest x2 6.19 us: attend_own(): pl.pallas_call(body, grid=(heads,), in_specs=[spec_q] + spec_keys + [HBM]...]
    ppermute x7, waiting for transfers between devices: 22.8 us -> 25.8 us  [the longest x2 10.3 us: on_device(): ends = [lax.ppermute(x, 'fsdp', leftward) for x in ends]]
    ppermute x6, waiting for transfers between devices: 0.04 us -> 1.54 us  [send(): lax.ppermute(sums, plane, shift(n_groups - place[0], n_resp - place[1]))]
    ppermute x1, waiting for transfers between devices: 1.23 us -> 0.01 us  [on_device(): caches.append(lax.ppermute(cache, 'resp', around))]
  transfers between devices with their start and end apart: 18 -> 18, of which waited for: 5 -> 6; matrix products, arithmetic and copies ran while one was open for 0% -> 0% of each run, Pallas kernels for 23% -> 26%
where the time goes in v6:
time: 76.9 us; the launch traced here: 76.5 us
  waiting for transfers between devices  27.4 us (36%)
  Pallas kernels  23.8 us (31%)
  starting transfers between devices  21.3 us (28%)
  local copies, waits for them, and re-layouts  3.17 us (4%)
  between operations  0.83 us (1%)
    ppermute x2, waiting for transfers between devices, on_device(): ends = [lax.ppermute(x, 'fsdp', leftward) for x in ends]  10.3 us
    ppermute x3, waiting for transfers between devices, on_device(): moved = lax.ppermute(near[place], plane, shift(*place))  9.24 us
    ppermute x2, starting transfers between devices, on_device(): held = lax.ppermute(held, 'fsdp', rightward)  7.47 us
    pallas_call x2, Pallas kernels, attend_cache(): pl.pallas_call(body, grid=(heads,), in_specs=[spec_q] + [spec_c] * count...  7.07 us
    ppermute x6, starting transfers between devices, send(): lax.ppermute(sums, plane, shift(n_groups - place[0], n_resp - place[1]))  6.98 us
    ppermute x2, waiting for transfers between devices, on_device(): held = lax.ppermute(held, 'fsdp', rightward)  6.24 us
    pallas_call x2, Pallas kernels, attend_own(): pl.pallas_call(body, grid=(heads,), in_specs=[spec_q] + spec_keys + [HBM]...  6.19 us
    pallas_call x3, Pallas kernels, project(): pl.pallas_call(body, grid=(1,), in_specs=[piece_spec(index) for _, index,...  5.18 us
  transfers between devices with their start and end apart: 18, of which 6 were waited for; matrix products, arithmetic and copies ran while one was open for 0% of the time, Pallas kernels for 26%

profile of v6, /device:TPU:0, one launch (start us, length us, event | category | flops | bytes accessed | tf_op | source)
XLA Modules:
  0.0 76.5 jit_solution(1315602539455601027)
XLA Ops:
  0.0 1.4 %pack_rows.1 = (bf16[2,512,256]{2,1,0:T(8,128)(2,1)S(1)}, bf16[2,512,256]{2,1,0:T(8,128)(2,1)S(1)}, bf16[512,256]{1,0:T(8,128)(2,1)S(1)}, bf16[512,256]{1,0:T(8,128)(2,1)S(1)}) custom-call(bf16[1024,256]{1,0:T(8,128)(2,1)} %kw_ref.1, bf16[1024,256]{1,0:T(8,128)(2,1)} %vw_ref.1, bf16[512,256]{1,0:T(8,128)(2,1)} %bitcast.13, bf16[512,256]{1,0:T(8,128)(2,1)} %bitcast.14), custom_call_target="tpu_custom_call" | custom-call | tf_op jit(solution)/shard_map/pack_rows/pallas_call | solution.py:76
  1.4 4.1 %collective-permute-start = (bf16[2,512,256]{2,1,0:T(8,128)(2,1)S(1)}, bf16[2,512,256]{2,1,0:T(8,128)(2,1)S(1)}, u32[]{:S(2)}, u32[]{:S(2)}) collective-permute-start(bf16[2,512,256]{2,1,0:T(8,128)(2,1)S(1)} %get-tuple-element.31.refs_0_.refs_4_), channel_id=1, source_target_pairs={{0,8},{8,12},{12,4},{4,0},{1,9},{9,13},{13,5},{5,1},{2,10},{10,14}... | collective-permute-start | bytes 1572872 | tf_op jit(solution)/shard_map/ppermute | solution.py:405
  5.5 1.5 %collective-permute-start.5 = (bf16[2,512,256]{2,1,0:T(8,128)(2,1)S(1)}, bf16[2,512,256]{2,1,0:T(8,128)(2,1)S(1)}, u32[]{:S(2)}, u32[]{:S(2)}) collective-permute-start(bf16[2,512,256]{2,1,0:T(8,128)(2,1)S(1)} %get-tuple-element.35.refs_0_), channel_id=1, source_target_pairs={{0,2},{2,0},{1,3},{3,1},{4,6},{6,4},{5,7},{7,5},{8,10},{10,8},{9,1... | collective-permute-start | bytes 1572872 | tf_op jit(solution)/shard_map/ppermute | solution.py:400
  7.0 1.6 %pack_features.1 = (bf16[256,1024]{1,0:T(8,128)(2,1)S(1)}, bf16[256,1024]{1,0:T(8,128)(2,1)S(1)}, bf16[256,1024]{1,0:T(8,128)(2,1)S(1)}, bf16[256,1024]{1,0:T(8,128)(2,1)S(1)}) custom-call(bf16[256,4096]{1,0:T(8,128)(2,1)} %bitcast.12), custom_call_target="tpu_custom_call" | custom-call | tf_op jit(solution)/shard_map/pack_features/pallas_call | solution.py:136
  9.2 2.4 %collective-permute-start.4 = (bf16[256,1024]{1,0:T(8,128)(2,1)S(1)}, bf16[256,1024]{1,0:T(8,128)(2,1)S(1)}, u32[]{:S(2)}, u32[]{:S(2)}) collective-permute-start(bf16[256,1024]{1,0:T(8,128)(2,1)S(1)} %get-tuple-element.34), channel_id=1, source_target_pairs={{0,18},{2,16},{16,2},{18,0},{1,19},{3,17},{17,3},{19,1},{4,22},{6,... | collective-permute-start | bytes 1572872 | tf_op jit(solution)/shard_map/ppermute | solution.py:431
  11.6 6.2 %collective-permute-done.refs_2_.refs_1_.refs_5_ = bf16[2,512,256]{2,1,0:T(8,128)(2,1)S(1)} collective-permute-done((bf16[2,512,256]{2,1,0:T(8,128)(2,1)S(1)}, bf16[2,512,256]{2,1,0:T(8,128)(2,1)S(1)}, u32[]{:S(2)}, u32[]{:S(2)}) %collective-permute-start) | collective-permute-done | bytes 524320 | tf_op jit(solution)/shard_map/ppermute | solution.py:405
  17.9 3.4 %collective-permute-start.1 = (bf16[2,512,256]{2,1,0:T(8,128)(2,1)S(1)}, bf16[2,512,256]{2,1,0:T(8,128)(2,1)S(1)}, u32[]{:S(2)}, u32[]{:S(2)}) collective-permute-start(bf16[2,512,256]{2,1,0:T(8,128)(2,1)S(1)} %collective-permute-done.refs_2_.refs_1_.refs_5_), channel_id=1, source_target_pairs={{0,8},{8,12},{12,4},{4,0},{1,9},{9,13},{13,5},{5,1},{2,10},{10,14}... | collective-permute-start | bytes 1572872 | tf_op jit(solution)/shard_map/ppermute | solution.py:405
  21.3 4.0 %collective-permute-done.2.refs_3_.refs_7_ = bf16[512,256]{1,0:T(8,128)(2,1)S(1)} collective-permute-done((bf16[512,256]{1,0:T(8,128)(2,1)S(1)}, bf16[512,256]{1,0:T(8,128)(2,1)S(1)}, u32[]{:S(2)}, u32[]{:S(2)}) %collective-permute-start.2) | collective-permute-done | bytes 262176 | tf_op jit(solution)/shard_map/ppermute | solution.py:415
  25.3 1.5 %collective-permute-start.8 = (bf16[256,1024]{1,0:T(8,128)(2,1)S(1)}, bf16[256,1024]{1,0:T(8,128)(2,1)S(1)}, u32[]{:S(2)}, u32[]{:S(2)}) collective-permute-start(bf16[256,1024]{1,0:T(8,128)(2,1)S(1)} %after.5), channel_id=1, source_target_pairs={{0,16},{2,18},{16,0},{18,2},{1,17},{3,19},{17,1},{19,3},{4,20},{6,... | collective-permute-start | bytes 1572872 | tf_op jit(solution)/shard_map/ppermute | solution.py:431
  27.5 3.5 %attend_cache.3 = (f32[128,2048]{1,0:T(8,128)S(1)}, f32[128,2048]{1,0:T(8,128)S(1)}, f32[8,128]{1,0:T(8,128)S(1)}) custom-call(bf16[256,2048]{1,0:T(8,128)(2,1)S(1)} %bitcast.8, bf16[2,512,256]{2,1,0:T(8,128)(2,1)S(1)} %get-tuple-element.35.refs_0_, bf16[2,512,256]{2,1,0:T(8,128)(2,1)S(1)} %collective-permute-done.5.refs_1_, ...), custom_call_target="tpu_custom_call" | custom-call | tf_op jit(solution)/shard_map/attend_cache/pallas_call | solution.py:260
  31.1 3.5 %attend_cache.2 = (f32[128,2048]{1,0:T(8,128)S(1)}, f32[128,2048]{1,0:T(8,128)S(1)}, f32[8,128]{1,0:T(8,128)S(1)}) custom-call(bf16[256,2048]{1,0:T(8,128)(2,1)S(1)} %bitcast.9, bf16[2,512,256]{2,1,0:T(8,128)(2,1)S(1)} %get-tuple-element.35.refs_0_, bf16[2,512,256]{2,1,0:T(8,128)(2,1)S(1)} %collective-permute-done.5.refs_1_, ...), custom_call_target="tpu_custom_call" | custom-call | tf_op jit(solution)/shard_map/attend_cache/pallas_call | solution.py:260
  34.7 6.3 %collective-permute-done.6.refs_4_.refs_3_ = bf16[512,256]{1,0:T(8,128)(2,1)S(1)} collective-permute-done((bf16[512,256]{1,0:T(8,128)(2,1)S(1)}, bf16[512,256]{1,0:T(8,128)(2,1)S(1)}, u32[]{:S(2)}, u32[]{:S(2)}) %collective-permute-start.6) | collective-permute-done | bytes 262176 | tf_op jit(solution)/shard_map/ppermute | solution.py:415
  42.4 7.8 %collective-permute-done.8.refs_0_ = bf16[256,1024]{1,0:T(8,128)(2,1)S(1)} collective-permute-done((bf16[256,1024]{1,0:T(8,128)(2,1)S(1)}, bf16[256,1024]{1,0:T(8,128)(2,1)S(1)}, u32[]{:S(2)}, u32[]{:S(2)}) %collective-permute-start.8) | collective-permute-done | bytes 524320 | tf_op jit(solution)/shard_map/ppermute | solution.py:431
  50.3 1.5 %project.4 = (bf16[256,256]{1,0:T(8,128)(2,1)S(1)}, bf16[256,256]{1,0:T(8,128)(2,1)}) custom-call(bf16[2,512,256]{2,1,0:T(8,128)(2,1)S(1)} %get-tuple-element.31.refs_0_.refs_4_, bf16[2,512,256]{2,1,0:T(8,128)(2,1)S(1)} %collective-permute-done.refs_2_.refs_1_.refs_5_, bf16[2,512,256]{2,1,0:T(8,128)(2,1)S(1)} %collective-permute-done.1.refs_3_.refs_2_.refs_6_, ...), custom_call_target="tpu_custom_call" | custom-call | tf_op jit(solution)/shard_map/project/pallas_call | solution.py:196
  51.8 1.5 %collective-permute-start.17 = (bf16[256,256]{1,0:T(8,128)(2,1)S(1)}, bf16[256,256]{1,0:T(8,128)(2,1)S(1)}, u32[]{:S(2)}, u32[]{:S(2)}) collective-permute-start(bf16[256,256]{1,0:T(8,128)(2,1)S(1)} %get-tuple-element.48), channel_id=1, source_target_pairs={{0,2},{2,0},{16,18},{18,16},{1,3},{3,1},{17,19},{19,17},{4,6},{6,4... | collective-permute-start | bytes 393224 | tf_op jit(solution)/shard_map/ppermute | solution.py:436
  53.3 1.8 %project.5 = (f32[256,256]{1,0:T(8,128)S(1)}, bf16[256,256]{1,0:T(8,128)(2,1)}, bf16[256,256]{1,0:T(8,128)(2,1)}) custom-call(bf16[2,512,256]{2,1,0:T(8,128)(2,1)S(1)} %get-tuple-element.31.refs_0_.refs_4_, bf16[2,512,256]{2,1,0:T(8,128)(2,1)S(1)} %collective-permute-done.refs_2_.refs_1_.refs_5_, ...), custom_call_target="tpu_custom_call" | custom-call | tf_op jit(solution)/shard_map/project/pallas_call | solution.py:196
  55.2 1.5 %collective-permute-start.15 = (bf16[256,256]{1,0:T(8,128)(2,1)}, bf16[256,256]{1,0:T(8,128)(2,1)}, u32[]{:S(2)}, u32[]{:S(2)}) collective-permute-start(bf16[256,256]{1,0:T(8,128)(2,1)} %get-tuple-element.46), channel_id=1, source_target_pairs={{0,18},{2,16},{16,2},{18,0},{1,19},{3,17},{17,3},{19,1},{4,22},{6,... | collective-permute-start | bytes 393224 | tf_op jit(solution)/shard_map/ppermute | solution.py:436
  57.2 1.5 %collective-permute-start.14 = (bf16[256,256]{1,0:T(8,128)(2,1)}, bf16[256,256]{1,0:T(8,128)(2,1)}, u32[]{:S(2)}, u32[]{:S(2)}) collective-permute-start(bf16[256,256]{1,0:T(8,128)(2,1)} %get-tuple-element.44), channel_id=1, source_target_pairs={{0,2},{2,0},{16,18},{18,16},{1,3},{3,1},{17,19},{19,17},{4,6},{6,4... | collective-permute-start | bytes 393224 | tf_op jit(solution)/shard_map/ppermute | solution.py:436
  58.7 1.8 %project.3 = (f32[256,256]{1,0:T(8,128)S(1)}, bf16[256,256]{1,0:T(8,128)(2,1)}, bf16[256,256]{1,0:T(8,128)(2,1)}) custom-call(bf16[2,512,256]{2,1,0:T(8,128)(2,1)S(1)} %get-tuple-element.31.refs_0_.refs_4_, bf16[2,512,256]{2,1,0:T(8,128)(2,1)S(1)} %collective-permute-done.refs_2_.refs_1_.refs_5_, ...), custom_call_target="tpu_custom_call" | custom-call | tf_op jit(solution)/shard_map/project/pallas_call | solution.py:196
  61.2 1.5 %collective-permute-start.11 = (bf16[256,256]{1,0:T(8,128)(2,1)}, bf16[256,256]{1,0:T(8,128)(2,1)}, u32[]{:S(2)}, u32[]{:S(2)}) collective-permute-start(bf16[256,256]{1,0:T(8,128)(2,1)} %get-tuple-element.42), channel_id=1, source_target_pairs={{0,18},{2,16},{16,2},{18,0},{1,19},{3,17},{17,3},{19,1},{4,22},{6,... | collective-permute-start | bytes 393224 | tf_op jit(solution)/shard_map/ppermute | solution.py:436
  63.8 1.5 %collective-permute-done.16.refs_2_ = bf16[256,256]{1,0:T(8,128)(2,1)} collective-permute-done((bf16[256,256]{1,0:T(8,128)(2,1)}, bf16[256,256]{1,0:T(8,128)(2,1)}, u32[]{:S(2)}, u32[]{:S(2)}) %collective-permute-start.16) | collective-permute-done | bytes 131104 | tf_op jit(solution)/shard_map/ppermute | solution.py:436
  67.8 3.1 %attend_own.3 = (f32[128,2048]{1,0:T(8,128)S(1)}, bf16[128,2048]{1,0:T(8,128)(2,1)S(1)}) custom-call(bf16[256,2048]{1,0:T(8,128)(2,1)S(1)} %bitcast.10, f32[256,256]{1,0:T(8,128)S(1)} %get-tuple-element.45.refs_0_, bf16[256,256]{1,0:T(8,128)(2,1)} %collective-permute-done.15.refs_1_, bf16[256,256]{1,0:T(8,128)(2,1)} %collective-permute-done.16.refs_2_, ...), custom_call_target="tpu_custom_call" | custom-call | tf_op jit(solution)/shard_map/attend_own/pallas_call | solution.py:318
  70.9 3.1 %attend_own.2 = (f32[128,2048]{1,0:T(8,128)S(1)}, bf16[128,2048]{1,0:T(8,128)(2,1)S(1)}) custom-call(bf16[256,2048]{1,0:T(8,128)(2,1)S(1)} %bitcast.11, f32[256,256]{1,0:T(8,128)S(1)} %get-tuple-element.45.refs_0_, bf16[256,256]{1,0:T(8,128)(2,1)} %collective-permute-done.15.refs_1_, bf16[256,256]{1,0:T(8,128)(2,1)} %collective-permute-done.16.refs_2_, ...), custom_call_target="tpu_custom_call" | custom-call | tf_op jit(solution)/shard_map/attend_own/pallas_call | solution.py:318
  74.1 2.4 %finish.1 = bf16[256,2048]{1,0:T(8,128)(2,1)} custom-call(s32[1]{0:T(128)} %bitcast.1.live_ref, f32[256,256]{1,0:T(8,128)S(1)} %copy-done.6, bf16[256,256]{1,0:T(8,128)(2,1)} %collective-permute-done.11.refs_1_, bf16[256,256]{1,0:T(8,128)(2,1)} %collective-permute-done.12.refs_2_, bf16[256,256]{1,0:T(8,128)(2,1)} %collective-permute-done.14.refs_3_, ...), custom_call_target="tpu_custom_call" | custom-call | tf_op jit(solution)/shard_map/finish/pallas_call | solution.py:350
  (40 shorter events, 7.0 us)
Async XLA Ops:
  1.4 26.1 %copy-start = (bf16[1,2,128,2048]{3,2,1,0:T(8,128)(2,1)S(1)}, bf16[1,2,128,2048]{3,2,1,0:T(8,128)(2,1)}, u32[]{:S(2)}) copy-start(bf16[1,2,128,2048]{3,2,1,0:T(8,128)(2,1)} %param.9) | copy-start | bytes 3145732
  1.4 16.5 %collective-permute-start = (bf16[2,512,256]{2,1,0:T(8,128)(2,1)S(1)}, bf16[2,512,256]{2,1,0:T(8,128)(2,1)S(1)}, u32[]{:S(2)}, u32[]{:S(2)}) collective-permute-start(bf16[2,512,256]{2,1,0:T(8,128)(2,1)S(1)} %get-tuple-element.31.refs_0_.refs_4_), channel_id=1, source_target_pairs={{0,8},{8,12},{12,4},{4,0},{1,9},{9,13},{13,5},{5,1},{2,10},{10,14}... | collective-permute-start | bytes 1572872 | tf_op jit(solution)/shard_map/ppermute | solution.py:405
  5.5 21.3 %collective-permute-start.5 = (bf16[2,512,256]{2,1,0:T(8,128)(2,1)S(1)}, bf16[2,512,256]{2,1,0:T(8,128)(2,1)S(1)}, u32[]{:S(2)}, u32[]{:S(2)}) collective-permute-start(bf16[2,512,256]{2,1,0:T(8,128)(2,1)S(1)} %get-tuple-element.35.refs_0_), channel_id=1, source_target_pairs={{0,2},{2,0},{1,3},{3,1},{4,6},{6,4},{5,7},{7,5},{8,10},{10,8},{9,1... | collective-permute-start | bytes 1572872 | tf_op jit(solution)/shard_map/ppermute | solution.py:400
  7.0 18.3 %collective-permute-start.2 = (bf16[512,256]{1,0:T(8,128)(2,1)S(1)}, bf16[512,256]{1,0:T(8,128)(2,1)S(1)}, u32[]{:S(2)}, u32[]{:S(2)}) collective-permute-start(bf16[512,256]{1,0:T(8,128)(2,1)S(1)} %get-tuple-element.32), channel_id=1, source_target_pairs={{8,0},{12,8},{4,12},{0,4},{9,1},{13,9},{5,13},{1,5},{10,2},{14,10}... | collective-permute-start | bytes 786440 | tf_op jit(solution)/shard_map/ppermute | solution.py:415
  8.6 26.0 %collective-permute-start.10 = (bf16[256,1024]{1,0:T(8,128)(2,1)S(1)}, bf16[256,1024]{1,0:T(8,128)(2,1)S(1)}, u32[]{:S(2)}, u32[]{:S(2)}) collective-permute-start(bf16[256,1024]{1,0:T(8,128)(2,1)S(1)} %get-tuple-element.40), channel_id=1, source_target_pairs={{0,2},{2,0},{16,18},{18,16},{1,3},{3,1},{17,19},{19,17},{4,6},{6,4... | collective-permute-start | bytes 1572872 | tf_op jit(solution)/shard_map/ppermute | solution.py:431
  9.2 33.2 %collective-permute-start.4 = (bf16[256,1024]{1,0:T(8,128)(2,1)S(1)}, bf16[256,1024]{1,0:T(8,128)(2,1)S(1)}, u32[]{:S(2)}, u32[]{:S(2)}) collective-permute-start(bf16[256,1024]{1,0:T(8,128)(2,1)S(1)} %get-tuple-element.34), channel_id=1, source_target_pairs={{0,18},{2,16},{16,2},{18,0},{1,19},{3,17},{17,3},{19,1},{4,22},{6,... | collective-permute-start | bytes 1572872 | tf_op jit(solution)/shard_map/ppermute | solution.py:431
  17.9 24.5 %collective-permute-start.1 = (bf16[2,512,256]{2,1,0:T(8,128)(2,1)S(1)}, bf16[2,512,256]{2,1,0:T(8,128)(2,1)S(1)}, u32[]{:S(2)}, u32[]{:S(2)}) collective-permute-start(bf16[2,512,256]{2,1,0:T(8,128)(2,1)S(1)} %collective-permute-done.refs_2_.refs_1_.refs_5_), channel_id=1, source_target_pairs={{0,8},{8,12},{12,4},{4,0},{1,9},{9,13},{13,5},{5,1},{2,10},{10,14}... | collective-permute-start | bytes 1572872 | tf_op jit(solution)/shard_map/ppermute | solution.py:405
  25.3 25.0 %collective-permute-start.8 = (bf16[256,1024]{1,0:T(8,128)(2,1)S(1)}, bf16[256,1024]{1,0:T(8,128)(2,1)S(1)}, u32[]{:S(2)}, u32[]{:S(2)}) collective-permute-start(bf16[256,1024]{1,0:T(8,128)(2,1)S(1)} %after.5), channel_id=1, source_target_pairs={{0,16},{2,18},{16,0},{18,2},{1,17},{3,19},{17,1},{19,3},{4,20},{6,... | collective-permute-start | bytes 1572872 | tf_op jit(solution)/shard_map/ppermute | solution.py:431
  26.8 14.2 %collective-permute-start.6 = (bf16[512,256]{1,0:T(8,128)(2,1)S(1)}, bf16[512,256]{1,0:T(8,128)(2,1)S(1)}, u32[]{:S(2)}, u32[]{:S(2)}) collective-permute-start(bf16[512,256]{1,0:T(8,128)(2,1)S(1)} %get-tuple-element.38), channel_id=1, source_target_pairs={{8,0},{12,8},{4,12},{0,4},{9,1},{13,9},{5,13},{1,5},{10,2},{14,10}... | collective-permute-start | bytes 786440 | tf_op jit(solution)/shard_map/ppermute | solution.py:415
  31.0 10.0 %copy-start.3 = (f32[128,2048]{1,0:T(8,128)}, f32[128,2048]{1,0:T(8,128)S(1)}, u32[]{:S(2)}) copy-start(f32[128,2048]{1,0:T(8,128)S(1)} %get-tuple-element.54.refs_6_) | copy-start | bytes 3145732
  31.0 11.4 %copy-start.1 = (f32[128,2048]{1,0:T(8,128)}, f32[128,2048]{1,0:T(8,128)S(1)}, u32[]{:S(2)}) copy-start(f32[128,2048]{1,0:T(8,128)S(1)} %get-tuple-element.53.refs_5_) | copy-start | bytes 3145732
  34.6 15.7 %collective-permute-start.13 = (bf16[256,1024]{1,0:T(8,128)(2,1)S(1)}, bf16[256,1024]{1,0:T(8,128)(2,1)S(1)}, u32[]{:S(2)}, u32[]{:S(2)}) collective-permute-start(bf16[256,1024]{1,0:T(8,128)(2,1)S(1)} %after.7.refs_10_.refs_8_), channel_id=1, source_target_pairs={{0,1},{1,0},{2,3},{3,2},{4,5},{5,4},{6,7},{7,6},{8,9},{9,8},{10,11... | collective-permute-start | bytes 1572872 | tf_op jit(solution)/shard_map/ppermute | solution.py:433
  41.0 12.3 %collective-permute-start.3 = (bf16[256,1024]{1,0:T(8,128)(2,1)S(1)}, bf16[256,1024]{1,0:T(8,128)(2,1)S(1)}, u32[]{:S(2)}, u32[]{:S(2)}) collective-permute-start(bf16[256,1024]{1,0:T(8,128)(2,1)S(1)} %get-tuple-element.33.refs_4_), channel_id=1, source_target_pairs={{0,1},{1,0},{2,3},{3,2},{4,5},{5,4},{6,7},{7,6},{8,9},{9,8},{10,11... | collective-permute-start | bytes 1572872 | tf_op jit(solution)/shard_map/ppermute | solution.py:433
  42.4 10.9 %collective-permute-start.7 = (bf16[256,1024]{1,0:T(8,128)(2,1)S(1)}, bf16[256,1024]{1,0:T(8,128)(2,1)S(1)}, u32[]{:S(2)}, u32[]{:S(2)}) collective-permute-start(bf16[256,1024]{1,0:T(8,128)(2,1)S(1)} %after.4.refs_6_), channel_id=1, source_target_pairs={{0,1},{1,0},{2,3},{3,2},{4,5},{5,4},{6,7},{7,6},{8,9},{9,8},{10,11... | collective-permute-start | bytes 1572872 | tf_op jit(solution)/shard_map/ppermute | solution.py:433
  50.3 3.1 %collective-permute-start.9 = (bf16[256,1024]{1,0:T(8,128)(2,1)S(1)}, bf16[256,1024]{1,0:T(8,128)(2,1)S(1)}, u32[]{:S(2)}, u32[]{:S(2)}) collective-permute-start(bf16[256,1024]{1,0:T(8,128)(2,1)S(1)} %after.6.refs_8_), channel_id=1, source_target_pairs={{0,1},{1,0},{2,3},{3,2},{4,5},{5,4},{6,7},{7,6},{8,9},{9,8},{10,11... | collective-permute-start | bytes 1572872 | tf_op jit(solution)/shard_map/ppermute | solution.py:433
  51.8 10.8 %collective-permute-start.17 = (bf16[256,256]{1,0:T(8,128)(2,1)S(1)}, bf16[256,256]{1,0:T(8,128)(2,1)S(1)}, u32[]{:S(2)}, u32[]{:S(2)}) collective-permute-start(bf16[256,256]{1,0:T(8,128)(2,1)S(1)} %get-tuple-element.48), channel_id=1, source_target_pairs={{0,2},{2,0},{16,18},{18,16},{1,3},{3,1},{17,19},{19,17},{4,6},{6,4... | collective-permute-start | bytes 393224 | tf_op jit(solution)/shard_map/ppermute | solution.py:436
  55.2 8.7 %collective-permute-start.15 = (bf16[256,256]{1,0:T(8,128)(2,1)}, bf16[256,256]{1,0:T(8,128)(2,1)}, u32[]{:S(2)}, u32[]{:S(2)}) collective-permute-start(bf16[256,256]{1,0:T(8,128)(2,1)} %get-tuple-element.46), channel_id=1, source_target_pairs={{0,18},{2,16},{16,2},{18,0},{1,19},{3,17},{17,3},{19,1},{4,22},{6,... | collective-permute-start | bytes 393224 | tf_op jit(solution)/shard_map/ppermute | solution.py:436
  56.7 8.7 %collective-permute-start.16 = (bf16[256,256]{1,0:T(8,128)(2,1)}, bf16[256,256]{1,0:T(8,128)(2,1)}, u32[]{:S(2)}, u32[]{:S(2)}) collective-permute-start(bf16[256,256]{1,0:T(8,128)(2,1)} %get-tuple-element.47), channel_id=1, source_target_pairs={{0,16},{2,18},{16,0},{18,2},{1,17},{3,19},{17,1},{19,3},{4,20},{6,... | collective-permute-start | bytes 393224 | tf_op jit(solution)/shard_map/ppermute | solution.py:436
  57.2 16.9 %collective-permute-start.14 = (bf16[256,256]{1,0:T(8,128)(2,1)}, bf16[256,256]{1,0:T(8,128)(2,1)}, u32[]{:S(2)}, u32[]{:S(2)}) collective-permute-start(bf16[256,256]{1,0:T(8,128)(2,1)} %get-tuple-element.44), channel_id=1, source_target_pairs={{0,2},{2,0},{16,18},{18,16},{1,3},{3,1},{17,19},{19,17},{4,6},{6,4... | collective-permute-start | bytes 393224 | tf_op jit(solution)/shard_map/ppermute | solution.py:436
  61.2 12.9 %collective-permute-start.11 = (bf16[256,256]{1,0:T(8,128)(2,1)}, bf16[256,256]{1,0:T(8,128)(2,1)}, u32[]{:S(2)}, u32[]{:S(2)}) collective-permute-start(bf16[256,256]{1,0:T(8,128)(2,1)} %get-tuple-element.42), channel_id=1, source_target_pairs={{0,18},{2,16},{16,2},{18,0},{1,19},{3,17},{17,3},{19,1},{4,22},{6,... | collective-permute-start | bytes 393224 | tf_op jit(solution)/shard_map/ppermute | solution.py:436
  62.7 11.4 %collective-permute-start.12 = (bf16[256,256]{1,0:T(8,128)(2,1)}, bf16[256,256]{1,0:T(8,128)(2,1)}, u32[]{:S(2)}, u32[]{:S(2)}) collective-permute-start(bf16[256,256]{1,0:T(8,128)(2,1)} %get-tuple-element.43), channel_id=1, source_target_pairs={{0,16},{2,18},{16,0},{18,2},{1,17},{3,19},{17,1},{19,3},{4,20},{6,... | collective-permute-start | bytes 393224 | tf_op jit(solution)/shard_map/ppermute | solution.py:436
  65.4 1.2 %copy-start.2 = (f32[128,2048]{1,0:T(8,128)S(1)}, f32[128,2048]{1,0:T(8,128)}, u32[]{:S(2)}) copy-start(f32[128,2048]{1,0:T(8,128)} %copy-done.1) | copy-start | bytes 3145732
  66.6 1.2 %copy-start.4 = (f32[128,2048]{1,0:T(8,128)S(1)}, f32[128,2048]{1,0:T(8,128)}, u32[]{:S(2)}) copy-start(f32[128,2048]{1,0:T(8,128)} %copy-done.3) | copy-start | bytes 3145732
  70.9 3.2 %copy-start.6 = (f32[256,256]{1,0:T(8,128)S(1)}, f32[256,256]{1,0:T(8,128)}, u32[]{:S(2)}) copy-start(f32[256,256]{1,0:T(8,128)} %copy-done.5) | copy-start | bytes 786436
  (1 other events, 0.7 us)

commit v7 on v6

v7 whole, which is shorter than its diff:
```python
import functools
import math

import jax
import jax.numpy as jnp
import numpy as np
from jax import lax
from jax.experimental import pallas as pl
from jax.experimental.pallas import tpu as pltpu
from jax.sharding import PartitionSpec as P

HD = 128
PLEN = 1024
FACTOR = HD**-0.5 * math.log2(math.e)
MIB = 1 << 20
ANYWHERE = pl.BlockSpec(memory_space=pl.ANY)
HBM = pl.BlockSpec(memory_space=pltpu.HBM)


def dot_nt(a, b):
    return lax.dot_general(a, b, (((1,), (1,)), ((), ())), preferred_element_type=jnp.float32)


def dot_nn(a, b):
    return lax.dot_general(a, b, (((1,), (0,)), ((), ())), preferred_element_type=jnp.float32)


def settings(limit):
    return {
        "compiler_params": pltpu.CompilerParams(vmem_limit_bytes=limit * MIB),
        "cost_estimate": pl.CostEstimate(flops=0, bytes_accessed=0, transcendentals=0),
    }


def after(value, *earlier):
    return pl.pallas_call(
        lambda *refs: None,
        in_specs=[ANYWHERE] * (1 + len(earlier)),
        out_specs=ANYWHERE,
        out_shape=jax.ShapeDtypeStruct(value.shape, value.dtype),
        input_output_aliases={0: 0},
        name="after",
        **settings(1),
    )(value, *earlier)


def run_copies(copies):
    for copy in copies:
        copy.start()
    for copy in copies:
        copy.wait()


def pack_rows(n_groups, key_weight, value_weight, prompt_keys, prompt_values):
    block, columns = key_weight.shape
    half = block // n_groups

    arguments = [
        pltpu.with_memory_space_constraint(x, pltpu.HBM)
        for x in (key_weight, value_weight, prompt_keys, prompt_values)
    ]

    def body(kw_ref, vw_ref, pk_ref, pv_ref, share_ref, cache_ref, sems):
        rows = pl.ds(pl.multiple_of(lax.axis_index("groups") * half, half), half)
        run_copies(
            [
                pltpu.make_async_copy(pk_ref, cache_ref.at[0], sems.at[0]),
                pltpu.make_async_copy(pv_ref, cache_ref.at[1], sems.at[1]),
                pltpu.make_async_copy(kw_ref.at[rows, :], share_ref.at[0], sems.at[2]),
                pltpu.make_async_copy(vw_ref.at[rows, :], share_ref.at[1], sems.at[3]),
            ]
        )

    return pl.pallas_call(
        body,
        in_specs=[HBM] * 4,
        out_specs=[ANYWHERE] * 2,
        out_shape=[
            jax.ShapeDtypeStruct((2, half, columns), key_weight.dtype),
            jax.ShapeDtypeStruct((2, *prompt_keys.shape), prompt_keys.dtype),
        ],
        scratch_shapes=[pltpu.SemaphoreType.DMA((4,))],
        name="pack_rows",
        **settings(1),
    )(*arguments)


def pack_features(sizes, block, sets, hidden):
    n_groups, n_fsdp, n_resp, n_tp = sizes
    rows, width = hidden.shape
    per_core = n_fsdp // n_tp
    half = block // n_groups

    def start_of(place, n):
        group = (lax.axis_index("groups") + place[0]) % n_groups
        resp = (lax.axis_index("resp") + place[1]) % n_resp
        return (n * n_resp + resp) * block + group * half

    if half % HD:
        return [
            jnp.concatenate(
                [
                    lax.dynamic_slice_in_dim(hidden, start_of(place, n), half, axis=1)
                    for n in range(per_core)
                ],
                axis=1,
            )
            for place in sets
        ]

    step = rows // 4

    def body(hidden_ref, *refs):
        outs, (held, sems) = refs[: len(sets)], refs[len(sets) :]
        copies = []
        for n in range(rows // step):
            part = pl.ds(n * step, step)
            copies.append(
                pltpu.make_async_copy(hidden_ref.at[part, :], held.at[part, :], sems.at[n])
            )
        for copy in copies:
            copy.start()
        for n, copy in enumerate(copies):
            copy.wait()
            part = slice(n * step, (n + 1) * step)
            for place, out in zip(sets, outs):
                for k in range(per_core):
                    first = pl.multiple_of(start_of(place, k), HD)
                    out[part, k * half : (k + 1) * half] = held[part, pl.ds(first, half)]

    shape = (rows, per_core * half)
    return pl.pallas_call(
        body,
        grid=(1,),
        in_specs=[HBM],
        out_specs=[pl.BlockSpec(shape, lambda _: (0, 0))] * len(sets),
        out_shape=[jax.ShapeDtypeStruct(shape, hidden.dtype)] * len(sets),
        scratch_shapes=[pltpu.VMEM((rows, width), hidden.dtype), pltpu.SemaphoreType.DMA((4,))],
        name="pack_features",
        **settings(12),
    )(pltpu.with_memory_space_constraint(hidden, pltpu.HBM))


def line_ring(size):
    return list(range(0, size, 2)) + list(range(1, size, 2))[::-1]


def owner_of(n_fsdp, hops):
    fsdp = lax.axis_index("fsdp")
    place = jnp.where(fsdp % 2 == 0, fsdp // 2, n_fsdp - (fsdp + 1) // 2)
    at = (place - hops + n_fsdp) % n_fsdp
    return jnp.where(at < n_fsdp // 2, 2 * at, 2 * n_fsdp - 1 - 2 * at)


def project(n_fsdp, pieces, pairs, types, waits=()):
    kinds, half, columns = pieces[0][0].shape
    rows, depth = pairs[0][0].shape
    dtype = pairs[0][0].dtype
    total, count = len(pieces), len(pairs)

    def body(*refs):
        piece_refs, refs = refs[:total], refs[total:]
        pair_refs, refs = refs[: 2 * count], refs[2 * count + len(waits) :]
        outs, weights = refs[:-1], refs[-1]
        core = lax.axis_index("tp")
        for ref, (_, hops) in zip(piece_refs, pieces):
            place = pl.ds(pl.multiple_of(owner_of(n_fsdp, hops) * half, half), half)
            for kind in range(kinds):
                weights[kind, place, :] = ref[kind]
        first = pl.ds(pl.multiple_of(core * depth, depth), depth)
        second = pl.ds(pl.multiple_of((1 - core) * depth, depth), depth)
        for n in range(count):
            near_ref, far_ref = pair_refs[2 * n : 2 * n + 2]
            for kind in range(kinds):
                sums = dot_nn(near_ref[...], weights[kind, first, :])
                sums = sums + dot_nn(far_ref[...], weights[kind, second, :])
                outs[n][kind] = sums.astype(outs[n].dtype)

    def whole(shape):
        return pl.BlockSpec(shape, lambda _: (0,) * len(shape))

    shape = (kinds, rows, columns)
    return pl.pallas_call(
        body,
        grid=(1,),
        in_specs=[whole((kinds, half, columns))] * total
        + [whole((rows, depth))] * (2 * count)
        + [ANYWHERE] * len(waits),
        out_specs=[whole(shape)] * count,
        out_shape=[jax.ShapeDtypeStruct(shape, t) for t in types],
        scratch_shapes=[pltpu.VMEM((kinds, n_fsdp * half, columns), dtype)],
        name="project",
        **settings(24),
    )(*[x for x, _ in pieces], *[x for pair in pairs for x in pair], *waits)


def take(ref, first, count):
    return jnp.concatenate(
        [ref[:, (first + n) * HD : (first + n + 1) * HD] for n in range(count)], axis=0
    )


def put(ref, first, count, value):
    tokens = ref.shape[0]
    value = jnp.broadcast_to(value, (count * tokens, HD)).astype(ref.dtype)
    for n in range(count):
        ref[:, (first + n) * HD : (first + n + 1) * HD] = value[n * tokens : (n + 1) * tokens]


def attend_cache(slots, group_size, queries, caches, waits):
    count = len(caches)
    tokens = queries.shape[0] // slots
    heads = queries.shape[1] // (group_size * HD)
    length = caches[0].shape[1]
    step = 2 if group_size % 2 == 0 else 1

    def body(q_ref, *refs):
        mixed_ref, level_ref, mark_ref = refs[-3:]
        mark_ref[...] = jnp.zeros(mark_ref.shape, mark_ref.dtype)
        keys = [ref[0] for ref in refs[:count]]
        values = [ref[1] for ref in refs[:count]]
        wide = [jnp.concatenate([v, jnp.ones(v.shape, v.dtype)], axis=1) for v in values]

        def scores_of(first):
            q = take(q_ref, first, step)
            return [dot_nt(q, k) for k in keys]

        coming = scores_of(0)
        for first in range(0, group_size, step):
            scores = coming
            if first + step < group_size:
                coming = scores_of(first + step)
            tops = [s[:, n * HD : (n + 1) * HD] for s in scores for n in range(length // HD)]
            top = jnp.max(functools.reduce(jnp.maximum, tops), axis=1, keepdims=True)
            out = None
            for s, v in zip(scores, wide):
                probs = jnp.exp2((s - top) * FACTOR).astype(jnp.bfloat16)
                part = dot_nn(probs, v)
                out = part if out is None else out + part
            total = out[:, HD:]
            put(mixed_ref, first, step, out[:, :HD] / total)
            put(level_ref, first, step, top * FACTOR + jnp.log2(total))

    spec_wide = pl.BlockSpec((tokens, group_size * HD), lambda head, slot: (slot, head))
    spec_c = pl.BlockSpec((2, length, HD), lambda head, slot: (0, 0, head))
    spec_mark = pl.BlockSpec((8, HD), lambda head, slot: (0, 0))
    return pl.pallas_call(
        body,
        grid=(heads, slots),
        in_specs=[spec_wide] + [spec_c] * count + [ANYWHERE] * len(waits),
        out_specs=[spec_wide] * 2 + [spec_mark],
        out_shape=[jax.ShapeDtypeStruct(queries.shape, jnp.float32)] * 2
        + [jax.ShapeDtypeStruct((8, HD), jnp.float32)],
        name="attend_cache",
        **settings(20),
    )(queries, *caches, *waits)


def attend_own(slots, group_size, live, queries, parts, table, state):
    count = len(parts)
    tokens = queries.shape[0] // slots
    heads = queries.shape[1] // (group_size * HD)

    def body(live_ref, q_ref, *refs):
        part_refs = refs[:count]
        table_ref, mixed_ref, level_ref, out_ref = refs[count:]
        slot = pl.program_id(0)

        def summed(kind):
            return functools.reduce(jnp.add, [ref[kind].astype(jnp.float32) for ref in part_refs])

        key = summed(0)
        key = key * table_ref[0] + pltpu.roll(key, HD // 2, 1) * table_ref[1]
        key = key.astype(jnp.bfloat16)
        value = summed(1).astype(jnp.bfloat16)
        wide = jnp.concatenate([value, jnp.ones((tokens, HD), jnp.bfloat16)], axis=1)
        row = lax.broadcasted_iota(jnp.int32, (tokens, tokens), 0)
        causal = row >= lax.broadcasted_iota(jnp.int32, (tokens, tokens), 1)
        causal = jnp.concatenate([causal] * group_size, axis=0)
        scores = dot_nt(take(q_ref, 0, group_size), key) * FACTOR
        scores = jnp.where(causal, scores, -1e30)
        level = take(level_ref, 0, group_size)
        top = jnp.max(jnp.maximum(level, scores), axis=1, keepdims=True)
        probs = jnp.exp2(scores - top).astype(jnp.bfloat16)
        kept = jnp.exp2(level - top)
        out = dot_nn(probs, wide)
        mixed = take(mixed_ref, 0, group_size) * kept + out[:, :HD]
        result = mixed / (kept + out[:, HD:])
        put(out_ref, 0, group_size, jnp.where(slot < live_ref[0], result, 0.0))

    spec_wide = pl.BlockSpec((tokens, group_size * HD), lambda slot, head: (slot, head))
    spec_part = pl.BlockSpec((2, tokens, HD), lambda slot, head: (0, slot, head))
    spec_table = pl.BlockSpec(table.shape, lambda slot, head: (0, 0, 0))
    kept_back = [pltpu.with_memory_space_constraint(x, pltpu.HBM) for x in (table, *state)]
    return pl.pallas_call(
        body,
        grid=(slots, heads),
        in_specs=[pl.BlockSpec(memory_space=pltpu.SMEM), spec_wide]
        + [spec_part] * count
        + [spec_table, spec_wide, spec_wide],
        out_specs=spec_wide,
        out_shape=jax.ShapeDtypeStruct(queries.shape, queries.dtype),
        name="attend_own",
        **settings(24),
    )(live, queries, *parts, *kept_back)


def rotation_tables(extent, offset):
    orders = np.arange(HD // 2, dtype=np.float64)
    inverse = np.exp(-(2.0 * orders / HD) * math.log(500000.0))
    angles = (offset + np.arange(extent))[:, None] * inverse[None, :]
    cosine, sine = np.cos(angles), np.sin(angles)
    halves = [np.concatenate([cosine, cosine], axis=1), np.concatenate([-sine, sine], axis=1)]
    return jnp.asarray(np.stack(halves), jnp.float32)


def on_device(sizes, hidden, queries, prompt_keys, prompt_values, key_weight, value_weight, counts):
    n_groups, n_fsdp, n_resp, n_tp = sizes
    _, slots, tokens, part_width = hidden.shape
    block, columns = key_weight.shape
    group_size = queries.shape[3] // columns
    rows = slots * tokens
    plane = ("groups", "resp")
    cores = [(n, (n + 1) % n_tp) for n in range(n_tp)]
    ring = line_ring(n_fsdp)
    rightward = [(ring[n], ring[(n + 1) % n_fsdp]) for n in range(n_fsdp)]
    leftward = [(b, a) for a, b in rightward]
    along = [(0, b) for b in range(1, n_resp)]
    across = [(a, b) for a in range(1, n_groups) for b in range(1, n_resp)]
    twins = [(a, 0) for a in range(1, n_groups)]
    sets = [(0, 0), *along, *twins, *across]

    def shift(a, b):
        return [
            (g * n_resp + r, (g + a) % n_groups * n_resp + (r + b) % n_resp)
            for g in range(n_groups)
            for r in range(n_resp)
        ]

    share, cache = pack_rows(n_groups, key_weight, value_weight, prompt_keys[0], prompt_values[0])

    caches = [cache]
    for b in range(1, n_resp):
        around = [(n, (n + b) % n_resp) for n in range(n_resp)]
        caches.append(lax.ppermute(cache, "resp", around))

    pieces = [(share, 0)]
    held = share
    for hop in range(1, n_fsdp // 2 + 1):
        held = lax.ppermute(held, "fsdp", rightward)
        pieces.append((held, hop))
    first_hop, ends = pieces[1][0], [held]
    held = share
    for hop in range(1, n_fsdp - n_fsdp // 2):
        held = lax.ppermute(held, "fsdp", leftward)
        pieces.append((held, -hop))
    ends.append(held)

    flat_queries = queries.reshape(rows, queries.shape[3])
    *state, mark = attend_cache(slots, group_size, flat_queries, caches, [first_hop])

    near = dict(zip(sets, pack_features(sizes, block, sets, hidden.reshape(rows, part_width))))
    for place in across:
        near[place] = after(near[place], first_hop)
    for place in sets[1:]:
        waits = ends if place in across else []
        moved = lax.ppermute(near[place], plane, shift(*place))
        near[place] = after(moved, mark, *waits)
    far = {place: lax.ppermute(near[place], "tp", cores) for place in sets}

    narrow, wide = jnp.bfloat16, jnp.float32
    parts = []
    for chosen, waits in (([*along, *twins, sets[0]], [near[p] for p in across]), (across, [])):
        types = [narrow if any(p) else wide for p in chosen]
        sums = project(n_fsdp, pieces, [(near[p], far[p]) for p in chosen], types, waits)
        for p, x in zip(chosen, sums):
            back = shift(n_groups - p[0], n_resp - p[1])
            parts.append(lax.ppermute(x, plane, back) if any(p) else x)

    table = rotation_tables(tokens, PLEN)
    live = (counts[0] - lax.axis_index("resp") * slots).astype(jnp.int32)[None]
    out = attend_own(slots, group_size, live, flat_queries, parts, table, state)
    return out.reshape(queries.shape)


def solution(mesh):
    placed = (
        P(("groups", "fsdp"), "resp", None, "tp"),
        P(("groups", "fsdp"), "resp", None, "tp"),
        P(("groups", "fsdp"), "resp", "tp"),
        P(("groups", "fsdp"), "resp", "tp"),
        P(("fsdp", "resp"), "tp"),
        P(("fsdp", "resp"), "tp"),
        P(("groups", "fsdp")),
    )
    sizes = tuple(mesh.shape[name] for name in ("groups", "fsdp", "resp", "tp"))
    return jax.shard_map(
        functools.partial(on_device, sizes),
        mesh=mesh,
        in_specs=placed,
        out_specs=P(("groups", "fsdp"), "resp", None, "tp"),
        check_vma=False,
    )
```

time: 76.9 us -> 65.6 us (0.85)
  Pallas kernels: 23.8 us -> 18.1 us
  starting transfers between devices: 21.3 us -> 17.7 us
  local copies, waits for them, and re-layouts: 3.17 us -> 0.01 us
  waiting for transfers between devices: 27.4 us -> 28.7 us
    ppermute x2, waiting for transfers between devices: 6.24 us -> 15.6 us  [on_device(): held = lax.ppermute(held, 'fsdp', rightward)]
    ppermute x3, waiting for transfers between devices: 9.24 us -> 2.68 us  [on_device(): moved = lax.ppermute(near[place], plane, shift(*place))]
    pallas_call x9 -> x5, Pallas kernels: 22.2 us -> 16.5 us  [the longest x1 6.9 us: attend_cache(): pl.pallas_call(body, grid=(heads, slots), in_specs=[spec_wide] + [spec_c]...]
    ppermute x8 -> x4, starting transfers between devices: 7.65 us -> 3.62 us  [the longest x3 3.62 us: on_device(): parts.append(lax.ppermute(x, plane, back) if any(p) else x)]
    unnamed x14 -> x6, local copies, waits for them, and re-layouts: 3.17 us -> 0.01 us
    ppermute x8 -> x4, waiting for transfers between devices: 11.9 us -> 10.4 us  [the longest x3 10.4 us: on_device(): parts.append(lax.ppermute(x, plane, back) if any(p) else x)]
  transfers between devices with their start and end apart: 18 -> 14, of which waited for: 6 -> 6; matrix products, arithmetic and copies ran while one was open for 0% -> 0% of each run, Pallas kernels for 26% -> 17%
where the time goes in v7:
time: 65.6 us; the launch traced here: 65.3 us
  waiting for transfers between devices  28.7 us (44%)
  Pallas kernels  18.1 us (28%)
  starting transfers between devices  17.7 us (27%)
  between operations  0.76 us (1%)
    ppermute x2, waiting for transfers between devices, on_device(): held = lax.ppermute(held, 'fsdp', rightward)  15.6 us
    ppermute x3, waiting for transfers between devices, on_device(): parts.append(lax.ppermute(x, plane, back) if any(p) else x)  10.4 us
    ppermute x2, starting transfers between devices, on_device(): held = lax.ppermute(held, 'fsdp', rightward)  7.47 us
    pallas_call x1, Pallas kernels, attend_cache(): pl.pallas_call(body, grid=(heads, slots), in_specs=[spec_wide] + [spec_c]...  6.9 us
    pallas_call x1, Pallas kernels, attend_own(): pl.pallas_call(body, grid=(slots, heads), in_specs=[pl.BlockSpec(memory_s...  5.58 us
    ppermute x3, starting transfers between devices, on_device(): moved = lax.ppermute(near[place], plane, shift(*place))  4.57 us
    ppermute x3, starting transfers between devices, on_device(): parts.append(lax.ppermute(x, plane, back) if any(p) else x)  3.62 us
    pallas_call x2, Pallas kernels, project(): pl.pallas_call(body, grid=(1,), in_specs=[whole((kinds, half, columns))]...  2.84 us
  transfers between devices with their start and end apart: 14, of which 6 were waited for; matrix products, arithmetic and copies ran while one was open for 0% of the time, Pallas kernels for 17%

profile of v7, /device:TPU:0, one launch (start us, length us, event | category | flops | bytes accessed | tf_op | source)
XLA Modules:
  0.0 65.3 jit_solution(9316165406752212882)
XLA Ops:
  0.0 1.2 %pack_rows.1 = (bf16[2,512,256]{2,1,0:T(8,128)(2,1)S(1)}, bf16[2,512,256]{2,1,0:T(8,128)(2,1)S(1)}) custom-call(bf16[1024,256]{1,0:T(8,128)(2,1)} %kw_ref.1, bf16[1024,256]{1,0:T(8,128)(2,1)} %vw_ref.1, bf16[512,256]{1,0:T(8,128)(2,1)} %bitcast.11, bf16[512,256]{1,0:T(8,128)(2,1)} %bitcast.12), custom_call_target="tpu_custom_call" | custom-call | tf_op jit(solution)/shard_map/pack_rows/pallas_call | solution.py:74
  1.2 0.0 copy-start
  1.2 4.1 %collective-permute-start = (bf16[2,512,256]{2,1,0:T(8,128)(2,1)S(1)}, bf16[2,512,256]{2,1,0:T(8,128)(2,1)S(1)}, u32[]{:S(2)}, u32[]{:S(2)}) collective-permute-start(bf16[2,512,256]{2,1,0:T(8,128)(2,1)S(1)} %get-tuple-element.17.refs_0_), channel_id=1, source_target_pairs={{0,8},{8,12},{12,4},{4,0},{1,9},{9,13},{13,5},{5,1},{2,10},{10,14}... | collective-permute-start | bytes 1572872 | tf_op jit(solution)/shard_map/ppermute | solution.py:350
  5.3 1.5 %collective-permute-start.4 = (bf16[2,512,256]{2,1,0:T(8,128)(2,1)S(1)}, bf16[2,512,256]{2,1,0:T(8,128)(2,1)S(1)}, u32[]{:S(2)}, u32[]{:S(2)}) collective-permute-start(bf16[2,512,256]{2,1,0:T(8,128)(2,1)S(1)} %get-tuple-element.19.refs_0_), channel_id=1, source_target_pairs={{0,2},{2,0},{1,3},{3,1},{4,6},{6,4},{5,7},{7,5},{8,10},{10,8},{9,1... | collective-permute-start | bytes 1572872 | tf_op jit(solution)/shard_map/ppermute | solution.py:345
  6.8 1.6 %pack_features.1 = (bf16[256,1024]{1,0:T(8,128)(2,1)S(1)}, bf16[256,1024]{1,0:T(8,128)(2,1)S(1)}, bf16[256,1024]{1,0:T(8,128)(2,1)S(1)}, bf16[256,1024]{1,0:T(8,128)(2,1)S(1)}) custom-call(bf16[256,4096]{1,0:T(8,128)(2,1)} %bitcast.10), custom_call_target="tpu_custom_call" | custom-call | tf_op jit(solution)/shard_map/pack_features/pallas_call | solution.py:132
  8.4 0.6 collective-permute-start.3
  9.0 1.5 %collective-permute-start.6 = (bf16[256,1024]{1,0:T(8,128)(2,1)S(1)}, bf16[256,1024]{1,0:T(8,128)(2,1)S(1)}, u32[]{:S(2)}, u32[]{:S(2)}) collective-permute-start(bf16[256,1024]{1,0:T(8,128)(2,1)S(1)} %get-tuple-element.21), channel_id=1, source_target_pairs={{0,16},{2,18},{16,0},{18,2},{1,17},{3,19},{17,1},{19,3},{4,20},{6,... | collective-permute-start | bytes 1572872 | tf_op jit(solution)/shard_map/ppermute | solution.py:367
  10.5 7.2 %collective-permute-done.refs_2_.refs_1_ = bf16[2,512,256]{2,1,0:T(8,128)(2,1)S(1)} collective-permute-done((bf16[2,512,256]{2,1,0:T(8,128)(2,1)S(1)}, bf16[2,512,256]{2,1,0:T(8,128)(2,1)S(1)}, u32[]{:S(2)}, u32[]{:S(2)}) %collective-permute-start) | collective-permute-done | bytes 524320 | tf_op jit(solution)/shard_map/ppermute | solution.py:350
  17.7 3.4 %collective-permute-start.1 = (bf16[2,512,256]{2,1,0:T(8,128)(2,1)S(1)}, bf16[2,512,256]{2,1,0:T(8,128)(2,1)S(1)}, u32[]{:S(2)}, u32[]{:S(2)}) collective-permute-start(bf16[2,512,256]{2,1,0:T(8,128)(2,1)S(1)} %collective-permute-done.refs_2_.refs_1_), channel_id=1, source_target_pairs={{0,8},{8,12},{12,4},{4,0},{1,9},{9,13},{13,5},{5,1},{2,10},{10,14}... | collective-permute-start | bytes 1572872 | tf_op jit(solution)/shard_map/ppermute | solution.py:350
  21.1 2.4 %collective-permute-start.9 = (bf16[256,1024]{1,0:T(8,128)(2,1)S(1)}, bf16[256,1024]{1,0:T(8,128)(2,1)S(1)}, u32[]{:S(2)}, u32[]{:S(2)}) collective-permute-start(bf16[256,1024]{1,0:T(8,128)(2,1)S(1)} %after.6), channel_id=1, source_target_pairs={{0,18},{2,16},{16,2},{18,0},{1,19},{3,17},{17,3},{19,1},{4,22},{6,... | collective-permute-start | bytes 1572872 | tf_op jit(solution)/shard_map/ppermute | solution.py:367
  23.5 6.9 %attend_cache.1 = (f32[256,2048]{1,0:T(8,128)S(1)}, f32[256,2048]{1,0:T(8,128)S(1)}, f32[8,128]{1,0:T(8,128)S(1)}) custom-call(bf16[256,2048]{1,0:T(8,128)(2,1)S(1)} %bitcast.8, bf16[2,512,256]{2,1,0:T(8,128)(2,1)S(1)} %get-tuple-element.19.refs_0_, bf16[2,512,256]{2,1,0:T(8,128)(2,1)S(1)} %collective-permute-done.4.refs_1_, ...), custom_call_target="tpu_custom_call" | custom-call | tf_op jit(solution)/shard_map/attend_cache/pallas_call | solution.py:247
  30.5 0.9 %collective-permute-done.3.refs_0_ = bf16[256,1024]{1,0:T(8,128)(2,1)S(1)} collective-permute-done((bf16[256,1024]{1,0:T(8,128)(2,1)S(1)}, bf16[256,1024]{1,0:T(8,128)(2,1)S(1)}, u32[]{:S(2)}, u32[]{:S(2)}) %collective-permute-start.3) | collective-permute-done | bytes 524320 | tf_op jit(solution)/shard_map/ppermute | solution.py:367
  31.4 0.5 collective-permute-start.5
  31.9 0.1 collective-permute-start.7
  32.0 8.4 %collective-permute-done.1.refs_2_ = bf16[2,512,256]{2,1,0:T(8,128)(2,1)S(1)} collective-permute-done((bf16[2,512,256]{2,1,0:T(8,128)(2,1)S(1)}, bf16[2,512,256]{2,1,0:T(8,128)(2,1)S(1)}, u32[]{:S(2)}, u32[]{:S(2)}) %collective-permute-start.1) | collective-permute-done | bytes 524320 | tf_op jit(solution)/shard_map/ppermute | solution.py:350
  40.4 1.7 %collective-permute-done.9.refs_0_ = bf16[256,1024]{1,0:T(8,128)(2,1)S(1)} collective-permute-done((bf16[256,1024]{1,0:T(8,128)(2,1)S(1)}, bf16[256,1024]{1,0:T(8,128)(2,1)S(1)}, u32[]{:S(2)}, u32[]{:S(2)}) %collective-permute-start.9) | collective-permute-done | bytes 524320 | tf_op jit(solution)/shard_map/ppermute | solution.py:367
  42.2 2.0 %project.2 = (bf16[2,256,256]{2,1,0:T(8,128)(2,1)S(1)}, bf16[2,256,256]{2,1,0:T(8,128)(2,1)S(1)}, f32[2,256,256]{2,1,0:T(8,128)S(1)}) custom-call(bf16[2,512,256]{2,1,0:T(8,128)(2,1)S(1)} %get-tuple-element.17.refs_0_, bf16[2,512,256]{2,1,0:T(8,128)(2,1)S(1)} %collective-permute-done.refs_2_.refs_1_, ...), custom_call_target="tpu_custom_call" | custom-call | tf_op jit(solution)/shard_map/project/pallas_call | solution.py:183
  44.2 1.6 %collective-permute-start.10 = (bf16[2,256,256]{2,1,0:T(8,128)(2,1)S(1)}, bf16[2,256,256]{2,1,0:T(8,128)(2,1)S(1)}, u32[]{:S(2)}, u32[]{:S(2)}) collective-permute-start(bf16[2,256,256]{2,1,0:T(8,128)(2,1)S(1)} %get-tuple-element.24), channel_id=1, source_target_pairs={{0,2},{2,0},{16,18},{18,16},{1,3},{3,1},{17,19},{19,17},{4,6},{6,4... | collective-permute-start | bytes 786440 | tf_op jit(solution)/shard_map/ppermute | solution.py:378
  45.7 0.5 collective-permute-start.11
  46.2 0.9 %project.3 = bf16[2,256,256]{2,1,0:T(8,128)(2,1)S(1)} custom-call(bf16[2,512,256]{2,1,0:T(8,128)(2,1)S(1)} %get-tuple-element.17.refs_0_, bf16[2,512,256]{2,1,0:T(8,128)(2,1)S(1)} %collective-permute-done.refs_2_.refs_1_, bf16[2,512,256]{2,1,0:T(8,128)(2,1)S(1)} %collective-permute-done.1.refs_2_, bf16[2,512,256]{2,1,0:T(8,128)(2,1)S(1)} %collective-permute-done.2.refs_3_, ...), custom_call_target="tpu_custom_call" | custom-call | tf_op jit(solution)/shard_map/project/pallas_call | solution.py:183
  47.1 1.6 %collective-permute-start.13 = (bf16[2,256,256]{2,1,0:T(8,128)(2,1)S(1)}, bf16[2,256,256]{2,1,0:T(8,128)(2,1)S(1)}, u32[]{:S(2)}, u32[]{:S(2)}) collective-permute-start(bf16[2,256,256]{2,1,0:T(8,128)(2,1)S(1)} %project.3), channel_id=1, source_target_pairs={{0,18},{2,16},{16,2},{18,0},{1,19},{3,17},{17,3},{19,1},{4,22},{6,... | collective-permute-start | bytes 786440 | tf_op jit(solution)/shard_map/ppermute | solution.py:378
  49.3 4.0 %collective-permute-done.10.refs_0_ = bf16[2,256,256]{2,1,0:T(8,128)(2,1)S(1)} collective-permute-done((bf16[2,256,256]{2,1,0:T(8,128)(2,1)S(1)}, bf16[2,256,256]{2,1,0:T(8,128)(2,1)S(1)}, u32[]{:S(2)}, u32[]{:S(2)}) %collective-permute-start.10) | collective-permute-done | bytes 262176 | tf_op jit(solution)/shard_map/ppermute | solution.py:378
  53.3 6.4 %collective-permute-done.11.refs_1_ = bf16[2,256,256]{2,1,0:T(8,128)(2,1)S(1)} collective-permute-done((bf16[2,256,256]{2,1,0:T(8,128)(2,1)S(1)}, bf16[2,256,256]{2,1,0:T(8,128)(2,1)S(1)}, u32[]{:S(2)}, u32[]{:S(2)}) %collective-permute-start.11) | collective-permute-done | bytes 262176 | tf_op jit(solution)/shard_map/ppermute | solution.py:378
  59.8 5.6 %attend_own.1 = bf16[256,2048]{1,0:T(8,128)(2,1)} custom-call(s32[1]{0:T(128)} %bitcast.1.live_ref, bf16[256,2048]{1,0:T(8,128)(2,1)S(1)} %bitcast.9, bf16[2,256,256]{2,1,0:T(8,128)(2,1)S(1)} %collective-permute-done.10.refs_0_, bf16[2,256,256]{2,1,0:T(8,128)(2,1)S(1)} %collective-permute-done.11.refs_1_, f32[2,256,256]{2,1,0:T(8,128)S(1)} %get-tuple-element.26.refs_2_, ...), custom_call_target="tpu_custom_call" | custom-call | tf_op jit(solution)/shard_map/attend_own/pallas_call | solution.py:295
  (20 shorter events, 0.0 us)
Async XLA Ops:
  1.2 22.3 %copy-start = (bf16[1,2,128,2048]{3,2,1,0:T(8,128)(2,1)S(1)}, bf16[1,2,128,2048]{3,2,1,0:T(8,128)(2,1)}, u32[]{:S(2)}) copy-start(bf16[1,2,128,2048]{3,2,1,0:T(8,128)(2,1)} %param.9) | copy-start | bytes 3145732
  1.2 16.5 %collective-permute-start = (bf16[2,512,256]{2,1,0:T(8,128)(2,1)S(1)}, bf16[2,512,256]{2,1,0:T(8,128)(2,1)S(1)}, u32[]{:S(2)}, u32[]{:S(2)}) collective-permute-start(bf16[2,512,256]{2,1,0:T(8,128)(2,1)S(1)} %get-tuple-element.17.refs_0_), channel_id=1, source_target_pairs={{0,8},{8,12},{12,4},{4,0},{1,9},{9,13},{13,5},{5,1},{2,10},{10,14}... | collective-permute-start | bytes 1572872 | tf_op jit(solution)/shard_map/ppermute | solution.py:350
  5.3 15.8 %collective-permute-start.4 = (bf16[2,512,256]{2,1,0:T(8,128)(2,1)S(1)}, bf16[2,512,256]{2,1,0:T(8,128)(2,1)S(1)}, u32[]{:S(2)}, u32[]{:S(2)}) collective-permute-start(bf16[2,512,256]{2,1,0:T(8,128)(2,1)S(1)} %get-tuple-element.19.refs_0_), channel_id=1, source_target_pairs={{0,2},{2,0},{1,3},{3,1},{4,6},{6,4},{5,7},{7,5},{8,10},{10,8},{9,1... | collective-permute-start | bytes 1572872 | tf_op jit(solution)/shard_map/ppermute | solution.py:345
  8.4 23.0 %collective-permute-start.3 = (bf16[256,1024]{1,0:T(8,128)(2,1)S(1)}, bf16[256,1024]{1,0:T(8,128)(2,1)S(1)}, u32[]{:S(2)}, u32[]{:S(2)}) collective-permute-start(bf16[256,1024]{1,0:T(8,128)(2,1)S(1)} %get-tuple-element.18), channel_id=1, source_target_pairs={{0,2},{2,0},{16,18},{18,16},{1,3},{3,1},{17,19},{19,17},{4,6},{6,4... | collective-permute-start | bytes 1572872 | tf_op jit(solution)/shard_map/ppermute | solution.py:367
  9.0 22.4 %collective-permute-start.6 = (bf16[256,1024]{1,0:T(8,128)(2,1)S(1)}, bf16[256,1024]{1,0:T(8,128)(2,1)S(1)}, u32[]{:S(2)}, u32[]{:S(2)}) collective-permute-start(bf16[256,1024]{1,0:T(8,128)(2,1)S(1)} %get-tuple-element.21), channel_id=1, source_target_pairs={{0,16},{2,18},{16,0},{18,2},{1,17},{3,19},{17,1},{19,3},{4,20},{6,... | collective-permute-start | bytes 1572872 | tf_op jit(solution)/shard_map/ppermute | solution.py:367
  10.5 21.4 %collective-permute-start.2 = (bf16[2,512,256]{2,1,0:T(8,128)(2,1)S(1)}, bf16[2,512,256]{2,1,0:T(8,128)(2,1)S(1)}, u32[]{:S(2)}, u32[]{:S(2)}) collective-permute-start(bf16[2,512,256]{2,1,0:T(8,128)(2,1)S(1)} %get-tuple-element.17.refs_0_), channel_id=1, source_target_pairs={{8,0},{12,8},{4,12},{0,4},{9,1},{13,9},{5,13},{1,5},{10,2},{14,10}... | collective-permute-start | bytes 1572872 | tf_op jit(solution)/shard_map/ppermute | solution.py:355
  17.7 22.7 %collective-permute-start.1 = (bf16[2,512,256]{2,1,0:T(8,128)(2,1)S(1)}, bf16[2,512,256]{2,1,0:T(8,128)(2,1)S(1)}, u32[]{:S(2)}, u32[]{:S(2)}) collective-permute-start(bf16[2,512,256]{2,1,0:T(8,128)(2,1)S(1)} %collective-permute-done.refs_2_.refs_1_), channel_id=1, source_target_pairs={{0,8},{8,12},{12,4},{4,0},{1,9},{9,13},{13,5},{5,1},{2,10},{10,14}... | collective-permute-start | bytes 1572872 | tf_op jit(solution)/shard_map/ppermute | solution.py:350
  21.1 21.1 %collective-permute-start.9 = (bf16[256,1024]{1,0:T(8,128)(2,1)S(1)}, bf16[256,1024]{1,0:T(8,128)(2,1)S(1)}, u32[]{:S(2)}, u32[]{:S(2)}) collective-permute-start(bf16[256,1024]{1,0:T(8,128)(2,1)S(1)} %after.6), channel_id=1, source_target_pairs={{0,18},{2,16},{16,2},{18,0},{1,19},{3,17},{17,3},{19,1},{4,22},{6,... | collective-permute-start | bytes 1572872 | tf_op jit(solution)/shard_map/ppermute | solution.py:367
  30.4 11.7 %copy-start.1 = (f32[256,2048]{1,0:T(8,128)}, f32[256,2048]{1,0:T(8,128)S(1)}, u32[]{:S(2)}) copy-start(f32[256,2048]{1,0:T(8,128)S(1)} %get-tuple-element.27.refs_5_) | copy-start | bytes 6291460
  30.5 11.7 %copy-start.2 = (f32[256,2048]{1,0:T(8,128)}, f32[256,2048]{1,0:T(8,128)S(1)}, u32[]{:S(2)}) copy-start(f32[256,2048]{1,0:T(8,128)S(1)} %get-tuple-element.28.refs_6_) | copy-start | bytes 6291460
  31.4 10.7 %collective-permute-start.8 = (bf16[256,1024]{1,0:T(8,128)(2,1)S(1)}, bf16[256,1024]{1,0:T(8,128)(2,1)S(1)}, u32[]{:S(2)}, u32[]{:S(2)}) collective-permute-start(bf16[256,1024]{1,0:T(8,128)(2,1)S(1)} %get-tuple-element.22.refs_8_), channel_id=1, source_target_pairs={{0,1},{1,0},{2,3},{3,2},{4,5},{5,4},{6,7},{7,6},{8,9},{9,8},{10,11... | collective-permute-start | bytes 1572872 | tf_op jit(solution)/shard_map/ppermute | solution.py:369
  31.4 10.7 %collective-permute-start.5 = (bf16[256,1024]{1,0:T(8,128)(2,1)S(1)}, bf16[256,1024]{1,0:T(8,128)(2,1)S(1)}, u32[]{:S(2)}, u32[]{:S(2)}) collective-permute-start(bf16[256,1024]{1,0:T(8,128)(2,1)S(1)} %after.4.refs_4_), channel_id=1, source_target_pairs={{0,1},{1,0},{2,3},{3,2},{4,5},{5,4},{6,7},{7,6},{8,9},{9,8},{10,11... | collective-permute-start | bytes 1572872 | tf_op jit(solution)/shard_map/ppermute | solution.py:369
  31.9 10.2 %collective-permute-start.7 = (bf16[256,1024]{1,0:T(8,128)(2,1)S(1)}, bf16[256,1024]{1,0:T(8,128)(2,1)S(1)}, u32[]{:S(2)}, u32[]{:S(2)}) collective-permute-start(bf16[256,1024]{1,0:T(8,128)(2,1)S(1)} %after.5.refs_6_), channel_id=1, source_target_pairs={{0,1},{1,0},{2,3},{3,2},{4,5},{5,4},{6,7},{7,6},{8,9},{9,8},{10,11... | collective-permute-start | bytes 1572872 | tf_op jit(solution)/shard_map/ppermute | solution.py:369
  42.1 4.1 %collective-permute-start.12 = (bf16[256,1024]{1,0:T(8,128)(2,1)S(1)}, bf16[256,1024]{1,0:T(8,128)(2,1)S(1)}, u32[]{:S(2)}, u32[]{:S(2)}) collective-permute-start(bf16[256,1024]{1,0:T(8,128)(2,1)S(1)} %after.7.refs_10_.refs_4_), channel_id=1, source_target_pairs={{0,1},{1,0},{2,3},{3,2},{4,5},{5,4},{6,7},{7,6},{8,9},{9,8},{10,11... | collective-permute-start | bytes 1572872 | tf_op jit(solution)/shard_map/ppermute | solution.py:369
  44.2 9.2 %collective-permute-start.10 = (bf16[2,256,256]{2,1,0:T(8,128)(2,1)S(1)}, bf16[2,256,256]{2,1,0:T(8,128)(2,1)S(1)}, u32[]{:S(2)}, u32[]{:S(2)}) collective-permute-start(bf16[2,256,256]{2,1,0:T(8,128)(2,1)S(1)} %get-tuple-element.24), channel_id=1, source_target_pairs={{0,2},{2,0},{16,18},{18,16},{1,3},{3,1},{17,19},{19,17},{4,6},{6,4... | collective-permute-start | bytes 786440 | tf_op jit(solution)/shard_map/ppermute | solution.py:378
  45.7 14.0 %collective-permute-start.11 = (bf16[2,256,256]{2,1,0:T(8,128)(2,1)S(1)}, bf16[2,256,256]{2,1,0:T(8,128)(2,1)S(1)}, u32[]{:S(2)}, u32[]{:S(2)}) collective-permute-start(bf16[2,256,256]{2,1,0:T(8,128)(2,1)S(1)} %get-tuple-element.25), channel_id=1, source_target_pairs={{0,16},{2,18},{16,0},{18,2},{1,17},{3,19},{17,1},{19,3},{4,20},{6,... | collective-permute-start | bytes 786440 | tf_op jit(solution)/shard_map/ppermute | solution.py:378
  47.1 12.6 %collective-permute-start.13 = (bf16[2,256,256]{2,1,0:T(8,128)(2,1)S(1)}, bf16[2,256,256]{2,1,0:T(8,128)(2,1)S(1)}, u32[]{:S(2)}, u32[]{:S(2)}) collective-permute-start(bf16[2,256,256]{2,1,0:T(8,128)(2,1)S(1)} %project.3), channel_id=1, source_target_pairs={{0,18},{2,16},{16,2},{18,0},{1,19},{3,17},{17,3},{19,1},{4,22},{6,... | collective-permute-start | bytes 786440 | tf_op jit(solution)/shard_map/ppermute | solution.py:378

commit v8 on v7

--- a/solution.py
+++ b/solution.py
@@ -13,6 +13,7 @@
 PLEN = 1024
 FACTOR = HD**-0.5 * math.log2(math.e)
 MIB = 1 << 20
+ATTEND_FLOPS = 1 << 31
 ANYWHERE = pl.BlockSpec(memory_space=pl.ANY)
 HBM = pl.BlockSpec(memory_space=pltpu.HBM)
 
@@ -25,10 +26,10 @@
     return lax.dot_general(a, b, (((1,), (0,)), ((), ())), preferred_element_type=jnp.float32)
 
 
-def settings(limit):
+def settings(limit, flops=0):
     return {
         "compiler_params": pltpu.CompilerParams(vmem_limit_bytes=limit * MIB),
-        "cost_estimate": pl.CostEstimate(flops=0, bytes_accessed=0, transcendentals=0),
+        "cost_estimate": pl.CostEstimate(flops=flops, bytes_accessed=0, transcendentals=0),
     }
 
 
@@ -83,6 +84,26 @@
         name="pack_rows",
         **settings(1),
     )(*arguments)
+
+
+def split_pair(pair):
+    def body(pair_ref, first_ref, second_ref, sems):
+        run_copies(
+            [
+                pltpu.make_async_copy(pair_ref.at[0], first_ref, sems.at[0]),
+                pltpu.make_async_copy(pair_ref.at[1], second_ref, sems.at[1]),
+            ]
+        )
+
+    return pl.pallas_call(
+        body,
+        in_specs=[ANYWHERE],
+        out_specs=[ANYWHERE] * 2,
+        out_shape=[jax.ShapeDtypeStruct(pair.shape[1:], pair.dtype)] * 2,
+        scratch_shapes=[pltpu.SemaphoreType.DMA((2,))],
+        name="split_pair",
+        **settings(1),
+    )(pair)
 
 
 def pack_features(sizes, block, sets, hidden):
@@ -153,7 +174,7 @@
 
 
 def project(n_fsdp, pieces, pairs, types, waits=()):
-    kinds, half, columns = pieces[0][0].shape
+    half, columns = pieces[0][0].shape[-2:]
     rows, depth = pairs[0][0].shape
     dtype = pairs[0][0].dtype
     total, count = len(pieces), len(pairs)
@@ -163,35 +184,37 @@
         pair_refs, refs = refs[: 2 * count], refs[2 * count + len(waits) :]
         outs, weights = refs[:-1], refs[-1]
         core = lax.axis_index("tp")
-        for ref, (_, hops) in zip(piece_refs, pieces):
+        for ref, (_, _, hops) in zip(piece_refs, pieces):
             place = pl.ds(pl.multiple_of(owner_of(n_fsdp, hops) * half, half), half)
-            for kind in range(kinds):
-                weights[kind, place, :] = ref[kind]
+            weights[place, :] = ref[0] if len(ref.shape) == 3 else ref[...]
         first = pl.ds(pl.multiple_of(core * depth, depth), depth)
         second = pl.ds(pl.multiple_of((1 - core) * depth, depth), depth)
         for n in range(count):
             near_ref, far_ref = pair_refs[2 * n : 2 * n + 2]
-            for kind in range(kinds):
-                sums = dot_nn(near_ref[...], weights[kind, first, :])
-                sums = sums + dot_nn(far_ref[...], weights[kind, second, :])
-                outs[n][kind] = sums.astype(outs[n].dtype)
+            sums = dot_nn(near_ref[...], weights[first, :])
+            sums = sums + dot_nn(far_ref[...], weights[second, :])
+            outs[n][...] = sums.astype(outs[n].dtype)
 
     def whole(shape):
         return pl.BlockSpec(shape, lambda _: (0,) * len(shape))
 
-    shape = (kinds, rows, columns)
+    def piece_spec(index):
+        if index is None:
+            return whole((half, columns))
+        return pl.BlockSpec((1, half, columns), lambda _: (index, 0, 0))
+
     return pl.pallas_call(
         body,
         grid=(1,),
-        in_specs=[whole((kinds, half, columns))] * total
+        in_specs=[piece_spec(index) for _, index, _ in pieces]
         + [whole((rows, depth))] * (2 * count)
         + [ANYWHERE] * len(waits),
-        out_specs=[whole(shape)] * count,
-        out_shape=[jax.ShapeDtypeStruct(shape, t) for t in types],
-        scratch_shapes=[pltpu.VMEM((kinds, n_fsdp * half, columns), dtype)],
+        out_specs=[whole((rows, columns))] * count,
+        out_shape=[jax.ShapeDtypeStruct((rows, columns), t) for t in types],
+        scratch_shapes=[pltpu.VMEM((n_fsdp * half, columns), dtype)],
         name="project",
         **settings(24),
-    )(*[x for x, _ in pieces], *[x for pair in pairs for x in pair], *waits)
+    )(*[x for x, _, _ in pieces], *[x for pair in pairs for x in pair], *waits)
 
 
 def take(ref, first, count):
@@ -207,102 +230,92 @@
         ref[:, (first + n) * HD : (first + n + 1) * HD] = value[n * tokens : (n + 1) * tokens]
 
 
-def attend_cache(slots, group_size, queries, caches, waits):
-    count = len(caches)
+def attend(slots, group_size, queries, caches, key_parts, table):
+    count, parts = len(caches), len(key_parts)
     tokens = queries.shape[0] // slots
     heads = queries.shape[1] // (group_size * HD)
     length = caches[0].shape[1]
     step = 2 if group_size % 2 == 0 else 1
 
     def body(q_ref, *refs):
-        mixed_ref, level_ref, mark_ref = refs[-3:]
-        mark_ref[...] = jnp.zeros(mark_ref.shape, mark_ref.dtype)
-        keys = [ref[0] for ref in refs[:count]]
-        values = [ref[1] for ref in refs[:count]]
-        wide = [jnp.concatenate([v, jnp.ones(v.shape, v.dtype)], axis=1) for v in values]
+        cache_refs, key_refs = refs[:count], refs[count : count + parts]
+        table_ref, mixed_ref, probs_ref = refs[count + parts :]
+        keys = [ref[0] for ref in cache_refs]
+        wide = [
+            jnp.concatenate([ref[1], jnp.ones((length, HD), ref.dtype)], axis=1)
+            for ref in cache_refs
+        ]
+        key = functools.reduce(jnp.add, [ref[...].astype(jnp.float32) for ref in key_refs])
+        key = key * table_ref[0] + pltpu.roll(key, HD // 2, 1) * table_ref[1]
+        key = key.astype(jnp.bfloat16)
+        ones = jnp.ones((tokens, HD), jnp.bfloat16)
+        row = lax.broadcasted_iota(jnp.int32, (tokens, tokens), 0)
+        causal = row >= lax.broadcasted_iota(jnp.int32, (tokens, tokens), 1)
+        causal = jnp.concatenate([causal] * step, axis=0)
 
         def scores_of(first):
             q = take(q_ref, first, step)
-            return [dot_nt(q, k) for k in keys]
+            return [dot_nt(q, k) for k in keys], jnp.where(causal, dot_nt(q, key), -1e30)
 
         coming = scores_of(0)
         for first in range(0, group_size, step):
-            scores = coming
+            scores, own = coming
             if first + step < group_size:
                 coming = scores_of(first + step)
             tops = [s[:, n * HD : (n + 1) * HD] for s in scores for n in range(length // HD)]
-            top = jnp.max(functools.reduce(jnp.maximum, tops), axis=1, keepdims=True)
+            top = jnp.max(functools.reduce(jnp.maximum, [own, *tops]), axis=1, keepdims=True)
+            probs = jnp.exp2((own - top) * FACTOR)
             out = None
             for s, v in zip(scores, wide):
-                probs = jnp.exp2((s - top) * FACTOR).astype(jnp.bfloat16)
-                part = dot_nn(probs, v)
+                weights = jnp.exp2((s - top) * FACTOR).astype(jnp.bfloat16)
+                part = dot_nn(weights, v)
                 out = part if out is None else out + part
-            total = out[:, HD:]
-            put(mixed_ref, first, step, out[:, :HD] / total)
-            put(level_ref, first, step, top * FACTOR + jnp.log2(total))
+            inverse = 1.0 / (out[:, HD:] + dot_nn(probs.astype(jnp.bfloat16), ones))
+            put(mixed_ref, first, step, out[:, :HD] * inverse)
+            put(probs_ref, first, step, probs * inverse)
 
     spec_wide = pl.BlockSpec((tokens, group_size * HD), lambda head, slot: (slot, head))
     spec_c = pl.BlockSpec((2, length, HD), lambda head, slot: (0, 0, head))
-    spec_mark = pl.BlockSpec((8, HD), lambda head, slot: (0, 0))
+    spec_key = pl.BlockSpec((tokens, HD), lambda head, slot: (slot, head))
+    spec_table = pl.BlockSpec(table.shape, lambda head, slot: (0, 0, 0))
     return pl.pallas_call(
         body,
         grid=(heads, slots),
-        in_specs=[spec_wide] + [spec_c] * count + [ANYWHERE] * len(waits),
-        out_specs=[spec_wide] * 2 + [spec_mark],
-        out_shape=[jax.ShapeDtypeStruct(queries.shape, jnp.float32)] * 2
-        + [jax.ShapeDtypeStruct((8, HD), jnp.float32)],
-        name="attend_cache",
+        in_specs=[spec_wide] + [spec_c] * count + [spec_key] * parts + [spec_table],
+        out_specs=[spec_wide] * 2,
+        out_shape=[
+            jax.ShapeDtypeStruct(queries.shape, jnp.float32),
+            jax.ShapeDtypeStruct(queries.shape, jnp.bfloat16),
+        ],
+        name="attend",
+        **settings(20, 4 * ATTEND_FLOPS),
+    )(queries, *caches, *key_parts, pltpu.with_memory_space_constraint(table, pltpu.HBM))
+
+
+def finish(slots, group_size, live, mixed, probs, value_parts):
+    parts = len(value_parts)
+    tokens = mixed.shape[0] // slots
+    heads = mixed.shape[1] // (group_size * HD)
+
+    def body(live_ref, mixed_ref, probs_ref, *refs):
+        value = functools.reduce(jnp.add, [ref[...].astype(jnp.float32) for ref in refs[:parts]])
+        value = value.astype(jnp.bfloat16)
+        out = take(mixed_ref, 0, group_size) + dot_nn(take(probs_ref, 0, group_size), value)
+        put(refs[-1], 0, group_size, jnp.where(pl.program_id(0) < live_ref[0], out, 0.0))
+
+    spec_wide = pl.BlockSpec((tokens, group_size * HD), lambda slot, head: (slot, head))
+    spec_value = pl.BlockSpec((tokens, HD), lambda slot, head: (slot, head))
+    return pl.pallas_call(
+        body,
+        grid=(slots, heads),
+        in_specs=[pl.BlockSpec(memory_space=pltpu.SMEM)]
+        + [spec_wide] * 2
+        + [spec_value] * parts,
+        out_specs=spec_wide,
+        out_shape=jax.ShapeDtypeStruct(mixed.shape, jnp.bfloat16),
+        name="finish",
         **settings(20),
-    )(queries, *caches, *waits)
-
-
-def attend_own(slots, group_size, live, queries, parts, table, state):
-    count = len(parts)
-    tokens = queries.shape[0] // slots
-    heads = queries.shape[1] // (group_size * HD)
-
-    def body(live_ref, q_ref, *refs):
-        part_refs = refs[:count]
-        table_ref, mixed_ref, level_ref, out_ref = refs[count:]
-        slot = pl.program_id(0)
-
-        def summed(kind):
-            return functools.reduce(jnp.add, [ref[kind].astype(jnp.float32) for ref in part_refs])
-
-        key = summed(0)
-        key = key * table_ref[0] + pltpu.roll(key, HD // 2, 1) * table_ref[1]
-        key = key.astype(jnp.bfloat16)
-        value = summed(1).astype(jnp.bfloat16)
-        wide = jnp.concatenate([value, jnp.ones((tokens, HD), jnp.bfloat16)], axis=1)
-        row = lax.broadcasted_iota(jnp.int32, (tokens, tokens), 0)
-        causal = row >= lax.broadcasted_iota(jnp.int32, (tokens, tokens), 1)
-        causal = jnp.concatenate([causal] * group_size, axis=0)
-        scores = dot_nt(take(q_ref, 0, group_size), key) * FACTOR
-        scores = jnp.where(causal, scores, -1e30)
-        level = take(level_ref, 0, group_size)
-        top = jnp.max(jnp.maximum(level, scores), axis=1, keepdims=True)
-        probs = jnp.exp2(scores - top).astype(jnp.bfloat16)
-        kept = jnp.exp2(level - top)
-        out = dot_nn(probs, wide)
-        mixed = take(mixed_ref, 0, group_size) * kept + out[:, :HD]
-        result = mixed / (kept + out[:, HD:])
-        put(out_ref, 0, group_size, jnp.where(slot < live_ref[0], result, 0.0))
-
-    spec_wide = pl.BlockSpec((tokens, group_size * HD), lambda slot, head: (slot, head))
-    spec_part = pl.BlockSpec((2, tokens, HD), lambda slot, head: (0, slot, head))
-    spec_table = pl.BlockSpec(table.shape, lambda slot, head: (0, 0, 0))
-    kept_back = [pltpu.with_memory_space_constraint(x, pltpu.HBM) for x in (table, *state)]
-    return pl.pallas_call(
-        body,
-        grid=(slots, heads),
-        in_specs=[pl.BlockSpec(memory_space=pltpu.SMEM), spec_wide]
-        + [spec_part] * count
-        + [spec_table, spec_wide, spec_wide],
-        out_specs=spec_wide,
-        out_shape=jax.ShapeDtypeStruct(queries.shape, queries.dtype),
-        name="attend_own",
-        **settings(24),
-    )(live, queries, *parts, *kept_back)
+    )(live, mixed, probs, *value_parts)
 
 
 def rotation_tables(extent, offset):
@@ -344,42 +357,40 @@
         around = [(n, (n + b) % n_resp) for n in range(n_resp)]
         caches.append(lax.ppermute(cache, "resp", around))
 
-    pieces = [(share, 0)]
+    pieces = [[(share, kind, 0)] for kind in range(2)]
     held = share
-    for hop in range(1, n_fsdp // 2 + 1):
+    for hop in range(1, n_fsdp // 2):
         held = lax.ppermute(held, "fsdp", rightward)
-        pieces.append((held, hop))
-    first_hop, ends = pieces[1][0], [held]
+        for kind in range(2):
+            pieces[kind].append((held, kind, hop))
+    first_hop = held
+    for kind, end in enumerate(split_pair(held)):
+        pieces[kind].append((lax.ppermute(end, "fsdp", rightward), None, n_fsdp // 2))
     held = share
     for hop in range(1, n_fsdp - n_fsdp // 2):
         held = lax.ppermute(held, "fsdp", leftward)
-        pieces.append((held, -hop))
-    ends.append(held)
+        for kind in range(2):
+            pieces[kind].append((held, kind, -hop))
+
+    near = dict(zip(sets, pack_features(sizes, block, sets, hidden.reshape(rows, part_width))))
+    for place in sets[1:]:
+        near[place] = lax.ppermute(near[place], plane, shift(*place))
+    far = {place: lax.ppermute(near[place], "tp", cores) for place in sets}
+
+    parts, done = [], []
+    order = [*across, *along, *twins, sets[0]]
+    types = [jnp.bfloat16 if any(p) else jnp.float32 for p in order]
+    for kind in range(2):
+        sums = project(n_fsdp, pieces[kind], [(near[p], far[p]) for p in order], types, done)
+        done = [sums[-1]]
+        back = [shift(n_groups - p[0], n_resp - p[1]) for p in order[:-1]]
+        parts.append([sums[-1], *[lax.ppermute(x, plane, b) for x, b in zip(sums, back)]])
 
     flat_queries = queries.reshape(rows, queries.shape[3])
-    *state, mark = attend_cache(slots, group_size, flat_queries, caches, [first_hop])
-
-    near = dict(zip(sets, pack_features(sizes, block, sets, hidden.reshape(rows, part_width))))
-    for place in across:
-        near[place] = after(near[place], first_hop)
-    for place in sets[1:]:
-        waits = ends if place in across else []
-        moved = lax.ppermute(near[place], plane, shift(*place))
-        near[place] = after(moved, mark, *waits)
-    far = {place: lax.ppermute(near[place], "tp", cores) for place in sets}
-
-    narrow, wide = jnp.bfloat16, jnp.float32
-    parts = []
-    for chosen, waits in (([*along, *twins, sets[0]], [near[p] for p in across]), (across, [])):
-        types = [narrow if any(p) else wide for p in chosen]
-        sums = project(n_fsdp, pieces, [(near[p], far[p]) for p in chosen], types, waits)
-        for p, x in zip(chosen, sums):
-            back = shift(n_groups - p[0], n_resp - p[1])
-            parts.append(lax.ppermute(x, plane, back) if any(p) else x)
-
     table = rotation_tables(tokens, PLEN)
+    state = attend(slots, group_size, flat_queries, caches, parts[0], table)
     live = (counts[0] - lax.axis_index("resp") * slots).astype(jnp.int32)[None]
-    out = attend_own(slots, group_size, live, flat_queries, parts, table, state)
+    out = finish(slots, group_size, live, *state, parts[1])
     return out.reshape(queries.shape)
 
 

time: 65.6 us -> 89.4 us (1.36)
  Pallas kernels: 18.1 us -> 34.8 us
  starting transfers between devices: 17.7 us -> 23.2 us
  local copies, waits for them, and re-layouts: 0.01 us -> 5.22 us
  waiting for transfers between devices: 28.7 us -> 24.9 us
    pallas_call x1, Pallas kernels: 1.22 us -> 17 us  [pack_rows(): pl.pallas_call(body, in_specs=[HBM] * 4, out_specs=[ANYWHERE] * 2, out_sh...]
    ppermute x2 -> x1, waiting for transfers between devices: 15.6 us -> 6.03 us  [on_device(): held = lax.ppermute(held, 'fsdp', rightward)]
    ppermute x6 -> x11, starting transfers between devices: 8.18 us -> 14.8 us  [the longest x6 7.11 us: on_device(): lax.ppermute(x, plane, b)]
    ppermute x6 -> x11, waiting for transfers between devices: 13.1 us -> 18.9 us  [the longest x3 13.7 us: on_device(): near[place] = lax.ppermute(near[place], plane, shift(*place))]
    unnamed x6 -> x22, local copies, waits for them, and re-layouts: 0.01 us -> 5.22 us
    ppermute x2 -> x1, starting transfers between devices: 7.47 us -> 4.09 us  [on_device(): held = lax.ppermute(held, 'fsdp', rightward)]
    ppermute x1, starting transfers between devices: 0.01 us -> 2.37 us  [on_device(): held = lax.ppermute(held, 'fsdp', leftward)]
    pallas_call x8 -> x5, Pallas kernels: 15.3 us -> 16.2 us  [the longest x1 8.69 us: attend(): pl.pallas_call(body, grid=(heads, slots), in_specs=[spec_wide] + [spec_c]...]
  transfers between devices with their start and end apart: 14 -> 18, of which waited for: 6 -> 4; matrix products, arithmetic and copies ran while one was open for 0% -> 0% of each run, Pallas kernels for 17% -> 17%
where the time goes in v8:
time: 89.4 us; the launch traced here: 89 us
  Pallas kernels  34.8 us (39%)
  waiting for transfers between devices  24.9 us (28%)
  starting transfers between devices  23.2 us (26%)
  local copies, waits for them, and re-layouts  5.22 us (6%)
    pallas_call x1, Pallas kernels, pack_rows(): pl.pallas_call(body, in_specs=[HBM] * 4, out_specs=[ANYWHERE] * 2, out_sh...  17 us
    ppermute x3, waiting for transfers between devices, on_device(): near[place] = lax.ppermute(near[place], plane, shift(*place))  13.7 us
    pallas_call x1, Pallas kernels, attend(): pl.pallas_call(body, grid=(heads, slots), in_specs=[spec_wide] + [spec_c]...  8.69 us
    ppermute x6, starting transfers between devices, on_device(): lax.ppermute(x, plane, b)  7.11 us
    ppermute x1, waiting for transfers between devices, on_device(): held = lax.ppermute(held, 'fsdp', rightward)  6.03 us
    unnamed x22, local copies, waits for them, and re-layouts  5.22 us
    ppermute x2, waiting for transfers between devices, on_device(): lax.ppermute(end, 'fsdp', rightward)  5.14 us
    pallas_call x2, Pallas kernels, project(): pl.pallas_call(body, grid=(1,), in_specs=[piece_spec(index) for _, index,...  4.37 us
  transfers between devices with their start and end apart: 18, of which 4 were waited for; matrix products, arithmetic and copies ran while one was open for 0% of the time, Pallas kernels for 17%

profile of v8, /device:TPU:0, one launch (start us, length us, event | category | flops | bytes accessed | tf_op | source)
XLA Modules:
  0.0 89.0 jit_solution(12017282163144064304)
XLA Ops:
  0.0 17.0 %pack_rows.1 = (bf16[2,512,256]{2,1,0:T(8,128)(2,1)S(1)}, bf16[2,512,256]{2,1,0:T(8,128)(2,1)}) custom-call(bf16[1024,256]{1,0:T(8,128)(2,1)} %kw_ref.1, bf16[1024,256]{1,0:T(8,128)(2,1)} %vw_ref.1, bf16[512,256]{1,0:T(8,128)(2,1)} %bitcast.10, bf16[512,256]{1,0:T(8,128)(2,1)} %bitcast.11), custom_call_target="tpu_custom_call" | custom-call | tf_op jit(solution)/shard_map/pack_rows/pallas_call | solution.py:75
  17.0 4.1 %collective-permute-start.1 = (bf16[2,512,256]{2,1,0:T(8,128)(2,1)S(1)}, bf16[2,512,256]{2,1,0:T(8,128)(2,1)S(1)}, u32[]{:S(2)}, u32[]{:S(2)}) collective-permute-start(bf16[2,512,256]{2,1,0:T(8,128)(2,1)S(1)} %get-tuple-element.24.refs_0_), channel_id=1, source_target_pairs={{0,8},{8,12},{12,4},{4,0},{1,9},{9,13},{13,5},{5,1},{2,10},{10,14}... | collective-permute-start | bytes 1572872 | tf_op jit(solution)/shard_map/ppermute | solution.py:363
  21.1 1.6 %pack_features.1 = (bf16[256,1024]{1,0:T(8,128)(2,1)S(1)}, bf16[256,1024]{1,0:T(8,128)(2,1)S(1)}, bf16[256,1024]{1,0:T(8,128)(2,1)S(1)}, bf16[256,1024]{1,0:T(8,128)(2,1)S(1)}) custom-call(bf16[256,4096]{1,0:T(8,128)(2,1)} %bitcast.9), custom_call_target="tpu_custom_call" | custom-call | tf_op jit(solution)/shard_map/pack_features/pallas_call | solution.py:153
  22.7 2.5 %collective-permute-start.4 = (bf16[256,1024]{1,0:T(8,128)(2,1)S(1)}, bf16[256,1024]{1,0:T(8,128)(2,1)S(1)}, u32[]{:S(2)}, u32[]{:S(2)}) collective-permute-start(bf16[256,1024]{1,0:T(8,128)(2,1)S(1)} %get-tuple-element.26), channel_id=1, source_target_pairs={{0,18},{2,16},{16,2},{18,0},{1,19},{3,17},{17,3},{19,1},{4,22},{6,... | collective-permute-start | bytes 1572872 | tf_op jit(solution)/shard_map/ppermute | solution.py:377
  26.3 6.0 %collective-permute-done.1.pair_ref.refs_1_ = bf16[2,512,256]{2,1,0:T(8,128)(2,1)S(1)} collective-permute-done((bf16[2,512,256]{2,1,0:T(8,128)(2,1)S(1)}, bf16[2,512,256]{2,1,0:T(8,128)(2,1)S(1)}, u32[]{:S(2)}, u32[]{:S(2)}) %collective-permute-start.1) | collective-permute-done | bytes 524320 | tf_op jit(solution)/shard_map/ppermute | solution.py:363
  32.3 2.4 %collective-permute-start.3 = (bf16[2,512,256]{2,1,0:T(8,128)(2,1)S(1)}, bf16[2,512,256]{2,1,0:T(8,128)(2,1)S(1)}, u32[]{:S(2)}, u32[]{:S(2)}) collective-permute-start(bf16[2,512,256]{2,1,0:T(8,128)(2,1)S(1)} %get-tuple-element.24.refs_0_), channel_id=1, source_target_pairs={{8,0},{12,8},{4,12},{0,4},{9,1},{13,9},{5,13},{1,5},{10,2},{14,10}... | collective-permute-start | bytes 1572872 | tf_op jit(solution)/shard_map/ppermute | solution.py:371
  34.7 3.9 %collective-permute-done.4.refs_4_ = bf16[256,1024]{1,0:T(8,128)(2,1)S(1)} collective-permute-done((bf16[256,1024]{1,0:T(8,128)(2,1)S(1)}, bf16[256,1024]{1,0:T(8,128)(2,1)S(1)}, u32[]{:S(2)}, u32[]{:S(2)}) %collective-permute-start.4) | collective-permute-done | bytes 524320 | tf_op jit(solution)/shard_map/ppermute | solution.py:377
  38.6 9.8 %collective-permute-done.6.refs_6_ = bf16[256,1024]{1,0:T(8,128)(2,1)S(1)} collective-permute-done((bf16[256,1024]{1,0:T(8,128)(2,1)S(1)}, bf16[256,1024]{1,0:T(8,128)(2,1)S(1)}, u32[]{:S(2)}, u32[]{:S(2)}) %collective-permute-start.6) | collective-permute-done | bytes 524320 | tf_op jit(solution)/shard_map/ppermute | solution.py:377
  48.9 0.7 split_pair.1
  49.7 1.6 %collective-permute-start.2 = (bf16[512,256]{1,0:T(8,128)(2,1)S(1)}, bf16[512,256]{1,0:T(8,128)(2,1)S(1)}, u32[]{:S(2)}, u32[]{:S(2)}) collective-permute-start(bf16[512,256]{1,0:T(8,128)(2,1)S(1)} %get-tuple-element.25), channel_id=1, source_target_pairs={{0,8},{8,12},{12,4},{4,0},{1,9},{9,13},{13,5},{5,1},{2,10},{10,14}... | collective-permute-start | bytes 786440 | tf_op jit(solution)/shard_map/ppermute | solution.py:368
  51.3 1.5 %collective-permute-start = (bf16[2,512,256]{2,1,0:T(8,128)(2,1)}, bf16[2,512,256]{2,1,0:T(8,128)(2,1)}, u32[]{:S(2)}, u32[]{:S(2)}) collective-permute-start(bf16[2,512,256]{2,1,0:T(8,128)(2,1)} %get-tuple-element.23.refs_0_), channel_id=1, source_target_pairs={{0,2},{2,0},{1,3},{3,1},{4,6},{6,4},{5,7},{7,5},{8,10},{10,8},{9,1... | collective-permute-start | bytes 1572872 | tf_op jit(solution)/shard_map/ppermute | solution.py:358
  52.8 5.1 %collective-permute-done.2.refs_2_ = bf16[512,256]{1,0:T(8,128)(2,1)S(1)} collective-permute-done((bf16[512,256]{1,0:T(8,128)(2,1)S(1)}, bf16[512,256]{1,0:T(8,128)(2,1)S(1)}, u32[]{:S(2)}, u32[]{:S(2)}) %collective-permute-start.2) | collective-permute-done | bytes 262176 | tf_op jit(solution)/shard_map/ppermute | solution.py:368
  57.9 2.5 %collective-permute-start.14 = (bf16[512,256]{1,0:T(8,128)(2,1)}, bf16[512,256]{1,0:T(8,128)(2,1)}, u32[]{:S(2)}, u32[]{:S(2)}) collective-permute-start(bf16[512,256]{1,0:T(8,128)(2,1)} %get-tuple-element.36), channel_id=1, source_target_pairs={{0,8},{8,12},{12,4},{4,0},{1,9},{9,13},{13,5},{5,1},{2,10},{10,14}... | collective-permute-start | bytes 786440 | tf_op jit(solution)/shard_map/ppermute | solution.py:368
  60.5 2.0 %project.2 = (bf16[256,256]{1,0:T(8,128)(2,1)}, bf16[256,256]{1,0:T(8,128)(2,1)}, bf16[256,256]{1,0:T(8,128)(2,1)}, f32[256,256]{1,0:T(8,128)S(1)}) custom-call(bf16[2,512,256]{2,1,0:T(8,128)(2,1)S(1)} %get-tuple-element.24.refs_0_, bf16[2,512,256]{2,1,0:T(8,128)(2,1)S(1)} %collective-permute-done.1.pair_ref.refs_1_, ...), custom_call_target="tpu_custom_call" | custom-call | tf_op jit(solution)/shard_map/project/pallas_call | solution.py:206
  62.5 2.4 %collective-permute-start.11 = (bf16[256,256]{1,0:T(8,128)(2,1)}, bf16[256,256]{1,0:T(8,128)(2,1)S(1)}, u32[]{:S(2)}, u32[]{:S(2)}) collective-permute-start(bf16[256,256]{1,0:T(8,128)(2,1)} %get-tuple-element.31), channel_id=1, source_target_pairs={{0,18},{2,16},{16,2},{18,0},{1,19},{3,17},{17,3},{19,1},{4,22},{6,... | collective-permute-start | bytes 393224 | tf_op jit(solution)/shard_map/ppermute | solution.py:387
  66.7 1.0 %copy-done.1 = bf16[256,1024]{1,0:T(8,128)(2,1)S(1)} copy-done((bf16[256,1024]{1,0:T(8,128)(2,1)S(1)}, bf16[256,1024]{1,0:T(8,128)(2,1)}, u32[]{:S(2)}) %copy-start.1) | copy-done | bytes 524312
  67.8 1.0 %copy-done.3 = bf16[2,512,256]{2,1,0:T(8,128)(2,1)S(1)} copy-done((bf16[2,512,256]{2,1,0:T(8,128)(2,1)S(1)}, bf16[2,512,256]{2,1,0:T(8,128)(2,1)}, u32[]{:S(2)}) %copy-start.3) | copy-done | bytes 524312
  68.8 1.0 %copy-done.5 = bf16[256,1024]{1,0:T(8,128)(2,1)S(1)} copy-done((bf16[256,1024]{1,0:T(8,128)(2,1)S(1)}, bf16[256,1024]{1,0:T(8,128)(2,1)}, u32[]{:S(2)}) %copy-start.5) | copy-done | bytes 524312
  69.9 1.0 %copy-done.7 = bf16[256,1024]{1,0:T(8,128)(2,1)S(1)} copy-done((bf16[256,1024]{1,0:T(8,128)(2,1)S(1)}, bf16[256,1024]{1,0:T(8,128)(2,1)}, u32[]{:S(2)}) %copy-start.7) | copy-done | bytes 524312
  70.9 1.0 %copy-done.9 = bf16[256,1024]{1,0:T(8,128)(2,1)S(1)} copy-done((bf16[256,1024]{1,0:T(8,128)(2,1)S(1)}, bf16[256,1024]{1,0:T(8,128)(2,1)}, u32[]{:S(2)}) %copy-start.9) | copy-done | bytes 524312
  71.9 2.4 %project.3 = (bf16[256,256]{1,0:T(8,128)(2,1)S(1)}, bf16[256,256]{1,0:T(8,128)(2,1)S(1)}, bf16[256,256]{1,0:T(8,128)(2,1)S(1)}, f32[256,256]{1,0:T(8,128)S(1)}) custom-call(bf16[2,512,256]{2,1,0:T(8,128)(2,1)S(1)} %get-tuple-element.24.refs_0_, bf16[2,512,256]{2,1,0:T(8,128)(2,1)S(1)} %collective-permute-done.1.pair_ref.refs_1_, ...), custom_call_target="tpu_custom_call" | custom-call | tf_op jit(solution)/shard_map/project/pallas_call | solution.py:206
  74.3 2.4 %collective-permute-start.15 = (bf16[256,256]{1,0:T(8,128)(2,1)S(1)}, bf16[256,256]{1,0:T(8,128)(2,1)S(1)}, u32[]{:S(2)}, u32[]{:S(2)}) collective-permute-start(bf16[256,256]{1,0:T(8,128)(2,1)S(1)} %get-tuple-element.38), channel_id=1, source_target_pairs={{0,18},{2,16},{16,2},{18,0},{1,19},{3,17},{17,3},{19,1},{4,22},{6,... | collective-permute-start | bytes 393224 | tf_op jit(solution)/shard_map/ppermute | solution.py:387
  77.9 8.7 %attend.1 = (f32[256,2048]{1,0:T(8,128)S(1)}, bf16[256,2048]{1,0:T(8,128)(2,1)S(1)}) custom-call(bf16[256,2048]{1,0:T(8,128)(2,1)S(1)} %bitcast.8, bf16[2,512,256]{2,1,0:T(8,128)(2,1)} %get-tuple-element.23.refs_0_, bf16[2,512,256]{2,1,0:T(8,128)(2,1)} %collective-permute-done.refs_1_, f32[256,256]{1,0:T(8,128)S(1)} %get-tuple-element.30.refs_2_.refs_12_, ...), custom_call_target="tpu_custom_call" | custom-call | flops 8589934592 | tf_op jit(solution)/shard_map/attend/pallas_call | solution.py:281
  86.6 2.4 %finish.1 = bf16[256,2048]{1,0:T(8,128)(2,1)} custom-call(s32[1]{0:T(128)} %bitcast.1.live_ref, f32[256,2048]{1,0:T(8,128)S(1)} %get-tuple-element.34.mixed_ref, bf16[256,2048]{1,0:T(8,128)(2,1)S(1)} %get-tuple-element.35.probs_ref, f32[256,256]{1,0:T(8,128)S(1)} %get-tuple-element.37.refs_0_, bf16[256,256]{1,0:T(8,128)(2,1)S(1)} %collective-permute-done.15.refs_1_, ...), custom_call_target="tpu_custom_call" | custom-call | tf_op jit(solution)/shard_map/finish/pallas_call | solution.py:308
  (41 shorter events, 3.9 us)
Async XLA Ops:
  17.0 15.3 %collective-permute-start.1 = (bf16[2,512,256]{2,1,0:T(8,128)(2,1)S(1)}, bf16[2,512,256]{2,1,0:T(8,128)(2,1)S(1)}, u32[]{:S(2)}, u32[]{:S(2)}) collective-permute-start(bf16[2,512,256]{2,1,0:T(8,128)(2,1)S(1)} %get-tuple-element.24.refs_0_), channel_id=1, source_target_pairs={{0,8},{8,12},{12,4},{4,0},{1,9},{9,13},{13,5},{5,1},{2,10},{10,14}... | collective-permute-start | bytes 1572872 | tf_op jit(solution)/shard_map/ppermute | solution.py:363
  22.7 15.9 %collective-permute-start.4 = (bf16[256,1024]{1,0:T(8,128)(2,1)S(1)}, bf16[256,1024]{1,0:T(8,128)(2,1)S(1)}, u32[]{:S(2)}, u32[]{:S(2)}) collective-permute-start(bf16[256,1024]{1,0:T(8,128)(2,1)S(1)} %get-tuple-element.26), channel_id=1, source_target_pairs={{0,18},{2,16},{16,2},{18,0},{1,19},{3,17},{17,3},{19,1},{4,22},{6,... | collective-permute-start | bytes 1572872 | tf_op jit(solution)/shard_map/ppermute | solution.py:377
  25.2 23.2 %collective-permute-start.6 = (bf16[256,1024]{1,0:T(8,128)(2,1)S(1)}, bf16[256,1024]{1,0:T(8,128)(2,1)S(1)}, u32[]{:S(2)}, u32[]{:S(2)}) collective-permute-start(bf16[256,1024]{1,0:T(8,128)(2,1)S(1)} %get-tuple-element.27), channel_id=1, source_target_pairs={{0,2},{2,0},{16,18},{18,16},{1,3},{3,1},{17,19},{19,17},{4,6},{6,4... | collective-permute-start | bytes 1572872 | tf_op jit(solution)/shard_map/ppermute | solution.py:377
  25.8 22.6 %collective-permute-start.8 = (bf16[256,1024]{1,0:T(8,128)(2,1)S(1)}, bf16[256,1024]{1,0:T(8,128)(2,1)S(1)}, u32[]{:S(2)}, u32[]{:S(2)}) collective-permute-start(bf16[256,1024]{1,0:T(8,128)(2,1)S(1)} %get-tuple-element.28), channel_id=1, source_target_pairs={{0,16},{2,18},{16,0},{18,2},{1,17},{3,19},{17,1},{19,3},{4,20},{6,... | collective-permute-start | bytes 1572872 | tf_op jit(solution)/shard_map/ppermute | solution.py:377
  26.3 23.4 %collective-permute-start.10 = (bf16[256,1024]{1,0:T(8,128)(2,1)S(1)}, bf16[256,1024]{1,0:T(8,128)(2,1)S(1)}, u32[]{:S(2)}, u32[]{:S(2)}) collective-permute-start(bf16[256,1024]{1,0:T(8,128)(2,1)S(1)} %get-tuple-element.29.refs_10_), channel_id=1, source_target_pairs={{0,1},{1,0},{2,3},{3,2},{4,5},{5,4},{6,7},{7,6},{8,9},{9,8},{10,11... | collective-permute-start | bytes 1572872 | tf_op jit(solution)/shard_map/ppermute | solution.py:378
  32.3 19.0 %collective-permute-start.3 = (bf16[2,512,256]{2,1,0:T(8,128)(2,1)S(1)}, bf16[2,512,256]{2,1,0:T(8,128)(2,1)S(1)}, u32[]{:S(2)}, u32[]{:S(2)}) collective-permute-start(bf16[2,512,256]{2,1,0:T(8,128)(2,1)S(1)} %get-tuple-element.24.refs_0_), channel_id=1, source_target_pairs={{8,0},{12,8},{4,12},{0,4},{9,1},{13,9},{5,13},{1,5},{10,2},{14,10}... | collective-permute-start | bytes 1572872 | tf_op jit(solution)/shard_map/ppermute | solution.py:371
  38.6 21.9 %collective-permute-start.5 = (bf16[256,1024]{1,0:T(8,128)(2,1)S(1)}, bf16[256,1024]{1,0:T(8,128)(2,1)S(1)}, u32[]{:S(2)}, u32[]{:S(2)}) collective-permute-start(bf16[256,1024]{1,0:T(8,128)(2,1)S(1)} %collective-permute-done.4.refs_4_), channel_id=1, source_target_pairs={{0,1},{1,0},{2,3},{3,2},{4,5},{5,4},{6,7},{7,6},{8,9},{9,8},{10,11... | collective-permute-start | bytes 1572872 | tf_op jit(solution)/shard_map/ppermute | solution.py:378
  48.4 12.0 %collective-permute-start.7 = (bf16[256,1024]{1,0:T(8,128)(2,1)S(1)}, bf16[256,1024]{1,0:T(8,128)(2,1)S(1)}, u32[]{:S(2)}, u32[]{:S(2)}) collective-permute-start(bf16[256,1024]{1,0:T(8,128)(2,1)S(1)} %collective-permute-done.6.refs_6_), channel_id=1, source_target_pairs={{0,1},{1,0},{2,3},{3,2},{4,5},{5,4},{6,7},{7,6},{8,9},{9,8},{10,11... | collective-permute-start | bytes 1572872 | tf_op jit(solution)/shard_map/ppermute | solution.py:378
  48.4 12.0 %collective-permute-start.9 = (bf16[256,1024]{1,0:T(8,128)(2,1)S(1)}, bf16[256,1024]{1,0:T(8,128)(2,1)S(1)}, u32[]{:S(2)}, u32[]{:S(2)}) collective-permute-start(bf16[256,1024]{1,0:T(8,128)(2,1)S(1)} %collective-permute-done.8.refs_8_), channel_id=1, source_target_pairs={{0,1},{1,0},{2,3},{3,2},{4,5},{5,4},{6,7},{7,6},{8,9},{9,8},{10,11... | collective-permute-start | bytes 1572872 | tf_op jit(solution)/shard_map/ppermute | solution.py:378
  49.7 12.8 %copy-start = (bf16[256,1024]{1,0:T(8,128)(2,1)}, bf16[256,1024]{1,0:T(8,128)(2,1)S(1)}, u32[]{:S(2)}) copy-start(bf16[256,1024]{1,0:T(8,128)(2,1)S(1)} %collective-permute-done.10.refs_11_) | copy-start | bytes 1572868
  49.7 8.3 %collective-permute-start.2 = (bf16[512,256]{1,0:T(8,128)(2,1)S(1)}, bf16[512,256]{1,0:T(8,128)(2,1)S(1)}, u32[]{:S(2)}, u32[]{:S(2)}) collective-permute-start(bf16[512,256]{1,0:T(8,128)(2,1)S(1)} %get-tuple-element.25), channel_id=1, source_target_pairs={{0,8},{8,12},{12,4},{4,0},{1,9},{9,13},{13,5},{5,1},{2,10},{10,14}... | collective-permute-start | bytes 786440 | tf_op jit(solution)/shard_map/ppermute | solution.py:368
  51.3 11.2 %copy-start.2 = (bf16[2,512,256]{2,1,0:T(8,128)(2,1)}, bf16[2,512,256]{2,1,0:T(8,128)(2,1)S(1)}, u32[]{:S(2)}) copy-start(bf16[2,512,256]{2,1,0:T(8,128)(2,1)S(1)} %collective-permute-done.3.refs_3_) | copy-start | bytes 1572868
  51.3 25.4 %collective-permute-start = (bf16[2,512,256]{2,1,0:T(8,128)(2,1)}, bf16[2,512,256]{2,1,0:T(8,128)(2,1)}, u32[]{:S(2)}, u32[]{:S(2)}) collective-permute-start(bf16[2,512,256]{2,1,0:T(8,128)(2,1)} %get-tuple-element.23.refs_0_), channel_id=1, source_target_pairs={{0,2},{2,0},{1,3},{3,1},{4,6},{6,4},{5,7},{7,5},{8,10},{10,8},{9,1... | collective-permute-start | bytes 1572872 | tf_op jit(solution)/shard_map/ppermute | solution.py:358
  57.9 8.8 %collective-permute-start.14 = (bf16[512,256]{1,0:T(8,128)(2,1)}, bf16[512,256]{1,0:T(8,128)(2,1)}, u32[]{:S(2)}, u32[]{:S(2)}) collective-permute-start(bf16[512,256]{1,0:T(8,128)(2,1)} %get-tuple-element.36), channel_id=1, source_target_pairs={{0,8},{8,12},{12,4},{4,0},{1,9},{9,13},{13,5},{5,1},{2,10},{10,14}... | collective-permute-start | bytes 786440 | tf_op jit(solution)/shard_map/ppermute | solution.py:368
  60.4 2.1 %copy-start.4 = (bf16[256,1024]{1,0:T(8,128)(2,1)}, bf16[256,1024]{1,0:T(8,128)(2,1)S(1)}, u32[]{:S(2)}) copy-start(bf16[256,1024]{1,0:T(8,128)(2,1)S(1)} %collective-permute-done.5.refs_5_) | copy-start | bytes 1572868
  60.4 2.1 %copy-start.6 = (bf16[256,1024]{1,0:T(8,128)(2,1)}, bf16[256,1024]{1,0:T(8,128)(2,1)S(1)}, u32[]{:S(2)}) copy-start(bf16[256,1024]{1,0:T(8,128)(2,1)S(1)} %collective-permute-done.7.refs_7_) | copy-start | bytes 1572868
  60.5 2.0 %copy-start.8 = (bf16[256,1024]{1,0:T(8,128)(2,1)}, bf16[256,1024]{1,0:T(8,128)(2,1)S(1)}, u32[]{:S(2)}) copy-start(bf16[256,1024]{1,0:T(8,128)(2,1)S(1)} %collective-permute-done.9.refs_9_) | copy-start | bytes 1572868
  62.5 14.8 %collective-permute-start.11 = (bf16[256,256]{1,0:T(8,128)(2,1)}, bf16[256,256]{1,0:T(8,128)(2,1)S(1)}, u32[]{:S(2)}, u32[]{:S(2)}) collective-permute-start(bf16[256,256]{1,0:T(8,128)(2,1)} %get-tuple-element.31), channel_id=1, source_target_pairs={{0,18},{2,16},{16,2},{18,0},{1,19},{3,17},{17,3},{19,1},{4,22},{6,... | collective-permute-start | bytes 393224 | tf_op jit(solution)/shard_map/ppermute | solution.py:387
  64.9 13.0 %collective-permute-start.12 = (bf16[256,256]{1,0:T(8,128)(2,1)}, bf16[256,256]{1,0:T(8,128)(2,1)}, u32[]{:S(2)}, u32[]{:S(2)}) collective-permute-start(bf16[256,256]{1,0:T(8,128)(2,1)} %get-tuple-element.32), channel_id=1, source_target_pairs={{0,2},{2,0},{16,18},{18,16},{1,3},{3,1},{17,19},{19,17},{4,6},{6,4... | collective-permute-start | bytes 393224 | tf_op jit(solution)/shard_map/ppermute | solution.py:387
  65.5 12.4 %collective-permute-start.13 = (bf16[256,256]{1,0:T(8,128)(2,1)}, bf16[256,256]{1,0:T(8,128)(2,1)}, u32[]{:S(2)}, u32[]{:S(2)}) collective-permute-start(bf16[256,256]{1,0:T(8,128)(2,1)} %get-tuple-element.33), channel_id=1, source_target_pairs={{0,16},{2,18},{16,0},{18,2},{1,17},{3,19},{17,1},{19,3},{4,20},{6,... | collective-permute-start | bytes 393224 | tf_op jit(solution)/shard_map/ppermute | solution.py:387
  71.9 5.9 %copy-start.10 = (bf16[1,2,128,2048]{3,2,1,0:T(8,128)(2,1)S(1)}, bf16[1,2,128,2048]{3,2,1,0:T(8,128)(2,1)}, u32[]{:S(2)}) copy-start(bf16[1,2,128,2048]{3,2,1,0:T(8,128)(2,1)} %param.9) | copy-start | bytes 3145732
  74.3 12.3 %collective-permute-start.15 = (bf16[256,256]{1,0:T(8,128)(2,1)S(1)}, bf16[256,256]{1,0:T(8,128)(2,1)S(1)}, u32[]{:S(2)}, u32[]{:S(2)}) collective-permute-start(bf16[256,256]{1,0:T(8,128)(2,1)S(1)} %get-tuple-element.38), channel_id=1, source_target_pairs={{0,18},{2,16},{16,2},{18,0},{1,19},{3,17},{17,3},{19,1},{4,22},{6,... | collective-permute-start | bytes 393224 | tf_op jit(solution)/shard_map/ppermute | solution.py:387
  76.7 9.9 %collective-permute-start.16 = (bf16[256,256]{1,0:T(8,128)(2,1)S(1)}, bf16[256,256]{1,0:T(8,128)(2,1)S(1)}, u32[]{:S(2)}, u32[]{:S(2)}) collective-permute-start(bf16[256,256]{1,0:T(8,128)(2,1)S(1)} %get-tuple-element.39), channel_id=1, source_target_pairs={{0,2},{2,0},{16,18},{18,16},{1,3},{3,1},{17,19},{19,17},{4,6},{6,4... | collective-permute-start | bytes 393224 | tf_op jit(solution)/shard_map/ppermute | solution.py:387
  77.3 9.3 %collective-permute-start.17 = (bf16[256,256]{1,0:T(8,128)(2,1)S(1)}, bf16[256,256]{1,0:T(8,128)(2,1)S(1)}, u32[]{:S(2)}, u32[]{:S(2)}) collective-permute-start(bf16[256,256]{1,0:T(8,128)(2,1)S(1)} %get-tuple-element.40), channel_id=1, source_target_pairs={{0,16},{2,18},{16,0},{18,2},{1,17},{3,19},{17,1},{19,3},{4,20},{6,... | collective-permute-start | bytes 393224 | tf_op jit(solution)/shard_map/ppermute | solution.py:387
  (5 other events, 5.2 us)

commit v9 on v7

--- a/solution.py
+++ b/solution.py
@@ -152,7 +152,7 @@
     return jnp.where(at < n_fsdp // 2, 2 * at, 2 * n_fsdp - 1 - 2 * at)
 
 
-def project(n_fsdp, pieces, pairs, types, waits=()):
+def project(n_fsdp, pieces, pairs, kind_of_sum, waits=(), apart=False):
     kinds, half, columns = pieces[0][0].shape
     rows, depth = pairs[0][0].shape
     dtype = pairs[0][0].dtype
@@ -174,20 +174,22 @@
             for kind in range(kinds):
                 sums = dot_nn(near_ref[...], weights[kind, first, :])
                 sums = sums + dot_nn(far_ref[...], weights[kind, second, :])
-                outs[n][kind] = sums.astype(outs[n].dtype)
+                out = outs[n * kinds + kind] if apart else outs[n].at[kind]
+                out[...] = sums.astype(out.dtype)
 
     def whole(shape):
         return pl.BlockSpec(shape, lambda _: (0,) * len(shape))
 
-    shape = (kinds, rows, columns)
+    shape = (rows, columns) if apart else (kinds, rows, columns)
+    number = count * kinds if apart else count
     return pl.pallas_call(
         body,
         grid=(1,),
         in_specs=[whole((kinds, half, columns))] * total
         + [whole((rows, depth))] * (2 * count)
         + [ANYWHERE] * len(waits),
-        out_specs=[whole(shape)] * count,
-        out_shape=[jax.ShapeDtypeStruct(shape, t) for t in types],
+        out_specs=[whole(shape)] * number,
+        out_shape=[jax.ShapeDtypeStruct(shape, kind_of_sum)] * number,
         scratch_shapes=[pltpu.VMEM((kinds, n_fsdp * half, columns), dtype)],
         name="project",
         **settings(24),
@@ -256,24 +258,27 @@
     )(queries, *caches, *waits)
 
 
-def attend_own(slots, group_size, live, queries, parts, table, state):
+def part_spec(part, kind, tokens):
+    if len(part.shape) == 3:
+        return pl.BlockSpec((None, tokens, HD), lambda slot, head: (kind, slot, head))
+    return pl.BlockSpec((tokens, HD), lambda slot, head: (slot, head))
+
+
+def sum_refs(refs):
+    return functools.reduce(jnp.add, [ref[...].astype(jnp.float32) for ref in refs])
+
+
+def attend_own(slots, group_size, queries, parts, table, state):
     count = len(parts)
     tokens = queries.shape[0] // slots
     heads = queries.shape[1] // (group_size * HD)
 
-    def body(live_ref, q_ref, *refs):
-        part_refs = refs[:count]
-        table_ref, mixed_ref, level_ref, out_ref = refs[count:]
-        slot = pl.program_id(0)
-
-        def summed(kind):
-            return functools.reduce(jnp.add, [ref[kind].astype(jnp.float32) for ref in part_refs])
-
-        key = summed(0)
+    def body(q_ref, *refs):
+        table_ref, mixed_ref, level_ref, out_ref, probs_ref = refs[count:]
+        key = sum_refs(refs[:count])
         key = key * table_ref[0] + pltpu.roll(key, HD // 2, 1) * table_ref[1]
         key = key.astype(jnp.bfloat16)
-        value = summed(1).astype(jnp.bfloat16)
-        wide = jnp.concatenate([value, jnp.ones((tokens, HD), jnp.bfloat16)], axis=1)
+        ones = jnp.ones((tokens, HD), jnp.bfloat16)
         row = lax.broadcasted_iota(jnp.int32, (tokens, tokens), 0)
         causal = row >= lax.broadcasted_iota(jnp.int32, (tokens, tokens), 1)
         causal = jnp.concatenate([causal] * group_size, axis=0)
@@ -281,28 +286,53 @@
         scores = jnp.where(causal, scores, -1e30)
         level = take(level_ref, 0, group_size)
         top = jnp.max(jnp.maximum(level, scores), axis=1, keepdims=True)
-        probs = jnp.exp2(scores - top).astype(jnp.bfloat16)
+        probs = jnp.exp2(scores - top)
         kept = jnp.exp2(level - top)
-        out = dot_nn(probs, wide)
-        mixed = take(mixed_ref, 0, group_size) * kept + out[:, :HD]
-        result = mixed / (kept + out[:, HD:])
-        put(out_ref, 0, group_size, jnp.where(slot < live_ref[0], result, 0.0))
+        inverse = 1.0 / (kept + dot_nn(probs.astype(jnp.bfloat16), ones))
+        put(out_ref, 0, group_size, take(mixed_ref, 0, group_size) * (kept * inverse))
+        put(probs_ref, 0, group_size, probs * inverse)
 
     spec_wide = pl.BlockSpec((tokens, group_size * HD), lambda slot, head: (slot, head))
-    spec_part = pl.BlockSpec((2, tokens, HD), lambda slot, head: (0, slot, head))
     spec_table = pl.BlockSpec(table.shape, lambda slot, head: (0, 0, 0))
     kept_back = [pltpu.with_memory_space_constraint(x, pltpu.HBM) for x in (table, *state)]
     return pl.pallas_call(
         body,
         grid=(slots, heads),
-        in_specs=[pl.BlockSpec(memory_space=pltpu.SMEM), spec_wide]
-        + [spec_part] * count
+        in_specs=[spec_wide]
+        + [part_spec(part, 0, tokens) for part in parts]
         + [spec_table, spec_wide, spec_wide],
-        out_specs=spec_wide,
-        out_shape=jax.ShapeDtypeStruct(queries.shape, queries.dtype),
+        out_specs=[spec_wide] * 2,
+        out_shape=[
+            jax.ShapeDtypeStruct(queries.shape, jnp.float32),
+            jax.ShapeDtypeStruct(queries.shape, queries.dtype),
+        ],
         name="attend_own",
         **settings(24),
-    )(live, queries, *parts, *kept_back)
+    )(queries, *parts, *kept_back)
+
+
+def finish(slots, group_size, live, mixed, probs, parts):
+    count = len(parts)
+    tokens = mixed.shape[0] // slots
+    heads = mixed.shape[1] // (group_size * HD)
+
+    def body(live_ref, mixed_ref, probs_ref, *refs):
+        value = sum_refs(refs[:count]).astype(jnp.bfloat16)
+        out = take(mixed_ref, 0, group_size) + dot_nn(take(probs_ref, 0, group_size), value)
+        put(refs[-1], 0, group_size, jnp.where(pl.program_id(0) < live_ref[0], out, 0.0))
+
+    spec_wide = pl.BlockSpec((tokens, group_size * HD), lambda slot, head: (slot, head))
+    return pl.pallas_call(
+        body,
+        grid=(slots, heads),
+        in_specs=[pl.BlockSpec(memory_space=pltpu.SMEM)]
+        + [spec_wide] * 2
+        + [part_spec(part, 1, tokens) for part in parts],
+        out_specs=spec_wide,
+        out_shape=jax.ShapeDtypeStruct(mixed.shape, jnp.bfloat16),
+        name="finish",
+        **settings(20),
+    )(live, mixed, probs, *parts)
 
 
 def rotation_tables(extent, offset):
@@ -368,18 +398,26 @@
         near[place] = after(moved, mark, *waits)
     far = {place: lax.ppermute(near[place], "tp", cores) for place in sets}
 
+    def send(p, x):
+        return lax.ppermute(x, plane, shift(n_groups - p[0], n_resp - p[1]))
+
     narrow, wide = jnp.bfloat16, jnp.float32
-    parts = []
-    for chosen, waits in (([*along, *twins, sets[0]], [near[p] for p in across]), (across, [])):
-        types = [narrow if any(p) else wide for p in chosen]
-        sums = project(n_fsdp, pieces, [(near[p], far[p]) for p in chosen], types, waits)
-        for p, x in zip(chosen, sums):
-            back = shift(n_groups - p[0], n_resp - p[1])
-            parts.append(lax.ppermute(x, plane, back) if any(p) else x)
+    pairs = {p: (near[p], far[p]) for p in sets}
+    sides = [*along, *twins]
+    sums = project(
+        n_fsdp, pieces, [pairs[p] for p in sides], narrow, waits=[near[p] for p in across]
+    )
+    both = [send(p, x) for p, x in zip(sides, sums)]
+    far_sums = project(n_fsdp, pieces, [pairs[p] for p in across], narrow, apart=True)
+    far_sums = [send(across[n // 2], x) for n, x in enumerate(far_sums)]
+    own = project(n_fsdp, pieces, [pairs[sets[0]]], wide, waits=[sums[0]])
+    key_parts = [*own, *both, *far_sums[0::2]]
+    value_parts = [*own, *both, *far_sums[1::2]]
 
     table = rotation_tables(tokens, PLEN)
+    state = attend_own(slots, group_size, flat_queries, key_parts, table, state)
     live = (counts[0] - lax.axis_index("resp") * slots).astype(jnp.int32)[None]
-    out = attend_own(slots, group_size, live, flat_queries, parts, table, state)
+    out = finish(slots, group_size, live, *state, value_parts)
     return out.reshape(queries.shape)
 
 

time: 65.6 us -> 69.1 us (1.053)
  Pallas kernels: 18.1 us -> 24.6 us
  waiting for transfers between devices: 28.7 us -> 24.1 us
  starting transfers between devices: 17.7 us -> 19.1 us
    ppermute x2, waiting for transfers between devices: 15.6 us -> 6.37 us  [on_device(): held = lax.ppermute(held, 'fsdp', rightward)]
    ppermute x3, waiting for transfers between devices: 2.68 us -> 11.6 us  [on_device(): moved = lax.ppermute(near[place], plane, shift(*place))]
    ppermute x3 -> x4, waiting for transfers between devices: 10.4 us -> 6.17 us  [send(): return lax.ppermute(x, plane, shift(n_groups - p[0], n_resp - p[1]))]
    pallas_call x2 -> x3, Pallas kernels: 2.84 us -> 5.79 us  [project(): pl.pallas_call(body, grid=(1,), in_specs=[whole((kinds, half, columns))]...]
    pallas_call x1 -> x2, Pallas kernels: 5.58 us -> 8.3 us  [the longest x1 4.76 us: attend_own(): pl.pallas_call(body, grid=(slots, heads), in_specs=[spec_wide] + [part_sp...]
    ppermute x3 -> x4, starting transfers between devices: 3.62 us -> 4.92 us  [send(): return lax.ppermute(x, plane, shift(n_groups - p[0], n_resp - p[1]))]
    pallas_call x1, Pallas kernels: 1.59 us -> 2.38 us  [pack_features(): pl.pallas_call(body, grid=(1,), in_specs=[HBM], out_specs=[pl.BlockSpec(s...]
  transfers between devices with their start and end apart: 14 -> 15, of which waited for: 6 -> 5; matrix products, arithmetic and copies ran while one was open for 0% -> 0% of each run, Pallas kernels for 17% -> 29%
where the time goes in v9:
time: 69.1 us; the launch traced here: 68.6 us
  Pallas kernels  24.6 us (36%)
  waiting for transfers between devices  24.1 us (35%)
  starting transfers between devices  19.1 us (28%)
  between operations  0.78 us (1%)
    ppermute x3, waiting for transfers between devices, on_device(): moved = lax.ppermute(near[place], plane, shift(*place))  11.6 us
    ppermute x2, starting transfers between devices, on_device(): held = lax.ppermute(held, 'fsdp', rightward)  7.45 us
    pallas_call x1, Pallas kernels, attend_cache(): pl.pallas_call(body, grid=(heads, slots), in_specs=[spec_wide] + [spec_c]...  6.9 us
    ppermute x2, waiting for transfers between devices, on_device(): held = lax.ppermute(held, 'fsdp', rightward)  6.37 us
    ppermute x4, waiting for transfers between devices, send(): return lax.ppermute(x, plane, shift(n_groups - p[0], n_resp - p[1]))  6.17 us
    pallas_call x3, Pallas kernels, project(): pl.pallas_call(body, grid=(1,), in_specs=[whole((kinds, half, columns))]...  5.79 us
    ppermute x4, starting transfers between devices, send(): return lax.ppermute(x, plane, shift(n_groups - p[0], n_resp - p[1]))  4.92 us
    pallas_call x1, Pallas kernels, attend_own(): pl.pallas_call(body, grid=(slots, heads), in_specs=[spec_wide] + [part_sp...  4.76 us
  transfers between devices with their start and end apart: 15, of which 5 were waited for; matrix products, arithmetic and copies ran while one was open for 0% of the time, Pallas kernels for 29%

profile of v9, /device:TPU:0, one launch (start us, length us, event | category | flops | bytes accessed | tf_op | source)
XLA Modules:
  0.0 68.6 jit_solution(4043303887095691891)
XLA Ops:
  0.0 1.2 %pack_rows.1 = (bf16[2,512,256]{2,1,0:T(8,128)(2,1)S(1)}, bf16[2,512,256]{2,1,0:T(8,128)(2,1)S(1)}) custom-call(bf16[1024,256]{1,0:T(8,128)(2,1)} %kw_ref.1, bf16[1024,256]{1,0:T(8,128)(2,1)} %vw_ref.1, bf16[512,256]{1,0:T(8,128)(2,1)} %bitcast.11, bf16[512,256]{1,0:T(8,128)(2,1)} %bitcast.12), custom_call_target="tpu_custom_call" | custom-call | tf_op jit(solution)/shard_map/pack_rows/pallas_call | solution.py:74
  1.2 4.1 %collective-permute-start = (bf16[2,512,256]{2,1,0:T(8,128)(2,1)S(1)}, bf16[2,512,256]{2,1,0:T(8,128)(2,1)S(1)}, u32[]{:S(2)}, u32[]{:S(2)}) collective-permute-start(bf16[2,512,256]{2,1,0:T(8,128)(2,1)S(1)} %get-tuple-element.20.refs_0_), channel_id=1, source_target_pairs={{0,8},{8,12},{12,4},{4,0},{1,9},{9,13},{13,5},{5,1},{2,10},{10,14}... | collective-permute-start | bytes 1572872 | tf_op jit(solution)/shard_map/ppermute | solution.py:380
  5.3 1.5 %collective-permute-start.5 = (bf16[2,512,256]{2,1,0:T(8,128)(2,1)S(1)}, bf16[2,512,256]{2,1,0:T(8,128)(2,1)S(1)}, u32[]{:S(2)}, u32[]{:S(2)}) collective-permute-start(bf16[2,512,256]{2,1,0:T(8,128)(2,1)S(1)} %get-tuple-element.23.refs_0_), channel_id=1, source_target_pairs={{0,2},{2,0},{1,3},{3,1},{4,6},{6,4},{5,7},{7,5},{8,10},{10,8},{9,1... | collective-permute-start | bytes 1572872 | tf_op jit(solution)/shard_map/ppermute | solution.py:375
  6.8 2.4 %pack_features.1 = (bf16[256,1024]{1,0:T(8,128)(2,1)}, bf16[256,1024]{1,0:T(8,128)(2,1)S(1)}, bf16[256,1024]{1,0:T(8,128)(2,1)S(1)}, bf16[256,1024]{1,0:T(8,128)(2,1)S(1)}) custom-call(bf16[256,4096]{1,0:T(8,128)(2,1)} %bitcast.10), custom_call_target="tpu_custom_call" | custom-call | tf_op jit(solution)/shard_map/pack_features/pallas_call | solution.py:132
  9.2 1.6 %collective-permute-start.7 = (bf16[256,1024]{1,0:T(8,128)(2,1)S(1)}, bf16[256,1024]{1,0:T(8,128)(2,1)S(1)}, u32[]{:S(2)}, u32[]{:S(2)}) collective-permute-start(bf16[256,1024]{1,0:T(8,128)(2,1)S(1)} %get-tuple-element.25), channel_id=1, source_target_pairs={{0,16},{2,18},{16,0},{18,2},{1,17},{3,19},{17,1},{19,3},{4,20},{6,... | collective-permute-start | bytes 1572872 | tf_op jit(solution)/shard_map/ppermute | solution.py:397
  10.8 0.5 collective-permute-start.4
  11.3 6.4 %collective-permute-done.refs_2_.refs_1_ = bf16[2,512,256]{2,1,0:T(8,128)(2,1)S(1)} collective-permute-done((bf16[2,512,256]{2,1,0:T(8,128)(2,1)S(1)}, bf16[2,512,256]{2,1,0:T(8,128)(2,1)S(1)}, u32[]{:S(2)}, u32[]{:S(2)}) %collective-permute-start) | collective-permute-done | bytes 524320 | tf_op jit(solution)/shard_map/ppermute | solution.py:380
  17.7 2.4 %collective-permute-start.9 = (bf16[256,1024]{1,0:T(8,128)(2,1)S(1)}, bf16[256,1024]{1,0:T(8,128)(2,1)S(1)}, u32[]{:S(2)}, u32[]{:S(2)}) collective-permute-start(bf16[256,1024]{1,0:T(8,128)(2,1)S(1)} %after.6), channel_id=1, source_target_pairs={{0,18},{2,16},{16,2},{18,0},{1,19},{3,17},{17,3},{19,1},{4,22},{6,... | collective-permute-start | bytes 1572872 | tf_op jit(solution)/shard_map/ppermute | solution.py:397
  20.2 3.4 %collective-permute-start.1 = (bf16[2,512,256]{2,1,0:T(8,128)(2,1)S(1)}, bf16[2,512,256]{2,1,0:T(8,128)(2,1)S(1)}, u32[]{:S(2)}, u32[]{:S(2)}) collective-permute-start(bf16[2,512,256]{2,1,0:T(8,128)(2,1)S(1)} %collective-permute-done.refs_2_.refs_1_), channel_id=1, source_target_pairs={{0,8},{8,12},{12,4},{4,0},{1,9},{9,13},{13,5},{5,1},{2,10},{10,14}... | collective-permute-start | bytes 1572872 | tf_op jit(solution)/shard_map/ppermute | solution.py:380
  23.5 6.9 %attend_cache.1 = (f32[256,2048]{1,0:T(8,128)S(1)}, f32[256,2048]{1,0:T(8,128)S(1)}, f32[8,128]{1,0:T(8,128)S(1)}) custom-call(bf16[256,2048]{1,0:T(8,128)(2,1)S(1)} %bitcast.8, bf16[2,512,256]{2,1,0:T(8,128)(2,1)S(1)} %get-tuple-element.23.refs_0_, bf16[2,512,256]{2,1,0:T(8,128)(2,1)S(1)} %collective-permute-done.5.refs_1_, ...), custom_call_target="tpu_custom_call" | custom-call | tf_op jit(solution)/shard_map/attend_cache/pallas_call | solution.py:249
  30.6 0.8 %collective-permute-done.4.refs_0_ = bf16[256,1024]{1,0:T(8,128)(2,1)S(1)} collective-permute-done((bf16[256,1024]{1,0:T(8,128)(2,1)S(1)}, bf16[256,1024]{1,0:T(8,128)(2,1)S(1)}, u32[]{:S(2)}, u32[]{:S(2)}) %collective-permute-start.4) | collective-permute-done | bytes 524320 | tf_op jit(solution)/shard_map/ppermute | solution.py:397
  31.4 10.7 %collective-permute-done.9.refs_0_ = bf16[256,1024]{1,0:T(8,128)(2,1)S(1)} collective-permute-done((bf16[256,1024]{1,0:T(8,128)(2,1)S(1)}, bf16[256,1024]{1,0:T(8,128)(2,1)S(1)}, u32[]{:S(2)}, u32[]{:S(2)}) %collective-permute-start.9) | collective-permute-done | bytes 524320 | tf_op jit(solution)/shard_map/ppermute | solution.py:397
  42.2 0.5 collective-permute-start.3
  42.7 2.1 %project.3 = (bf16[2,256,256]{2,1,0:T(8,128)(2,1)}, bf16[2,256,256]{2,1,0:T(8,128)(2,1)}) custom-call(bf16[2,512,256]{2,1,0:T(8,128)(2,1)S(1)} %get-tuple-element.20.refs_0_, bf16[2,512,256]{2,1,0:T(8,128)(2,1)S(1)} %collective-permute-done.refs_2_.refs_1_, bf16[2,512,256]{2,1,0:T(8,128)(2,1)S(1)} %collective-permute-done.1.refs_2_, ...), custom_call_target="tpu_custom_call" | custom-call | tf_op jit(solution)/shard_map/project/pallas_call | solution.py:185
  44.9 1.5 %collective-permute-start.10 = (bf16[2,256,256]{2,1,0:T(8,128)(2,1)}, bf16[2,256,256]{2,1,0:T(8,128)(2,1)S(1)}, u32[]{:S(2)}, u32[]{:S(2)}) collective-permute-start(bf16[2,256,256]{2,1,0:T(8,128)(2,1)} %get-tuple-element.27.refs_6_), channel_id=1, source_target_pairs={{0,2},{2,0},{16,18},{18,16},{1,3},{3,1},{17,19},{19,17},{4,6},{6,4... | collective-permute-start | bytes 786440 | tf_op jit(solution)/shard_map/ppermute | solution.py:402
  46.4 0.5 collective-permute-start.11
  46.9 1.6 %project.5 = (bf16[256,256]{1,0:T(8,128)(2,1)}, bf16[256,256]{1,0:T(8,128)(2,1)}) custom-call(bf16[2,512,256]{2,1,0:T(8,128)(2,1)S(1)} %get-tuple-element.20.refs_0_, bf16[2,512,256]{2,1,0:T(8,128)(2,1)S(1)} %collective-permute-done.refs_2_.refs_1_, bf16[2,512,256]{2,1,0:T(8,128)(2,1)S(1)} %collective-permute-done.1.refs_2_, ...), custom_call_target="tpu_custom_call" | custom-call | tf_op jit(solution)/shard_map/project/pallas_call | solution.py:185
  48.5 1.5 %collective-permute-start.13 = (bf16[256,256]{1,0:T(8,128)(2,1)}, bf16[256,256]{1,0:T(8,128)(2,1)}, u32[]{:S(2)}, u32[]{:S(2)}) collective-permute-start(bf16[256,256]{1,0:T(8,128)(2,1)} %get-tuple-element.29), channel_id=1, source_target_pairs={{0,18},{2,16},{16,2},{18,0},{1,19},{3,17},{17,3},{19,1},{4,22},{6,... | collective-permute-start | bytes 393224 | tf_op jit(solution)/shard_map/ppermute | solution.py:402
  50.0 1.4 %collective-permute-start.14 = (bf16[256,256]{1,0:T(8,128)(2,1)}, bf16[256,256]{1,0:T(8,128)(2,1)S(1)}, u32[]{:S(2)}, u32[]{:S(2)}) collective-permute-start(bf16[256,256]{1,0:T(8,128)(2,1)} %get-tuple-element.34), channel_id=1, source_target_pairs={{0,18},{2,16},{16,2},{18,0},{1,19},{3,17},{17,3},{19,1},{4,22},{6,... | collective-permute-start | bytes 393224 | tf_op jit(solution)/shard_map/ppermute | solution.py:402
  52.0 2.1 %project.4.refs_0_ = f32[2,256,256]{2,1,0:T(8,128)S(1)} custom-call(bf16[2,512,256]{2,1,0:T(8,128)(2,1)S(1)} %get-tuple-element.20.refs_0_, bf16[2,512,256]{2,1,0:T(8,128)(2,1)S(1)} %collective-permute-done.refs_2_.refs_1_, bf16[2,512,256]{2,1,0:T(8,128)(2,1)S(1)} %collective-permute-done.1.refs_2_, bf16[2,512,256]{2,1,0:T(8,128)(2,1)S(1)} %collective-permute-done.2.refs_3_, ...), custom_call_target="tpu_custom_call" | custom-call | tf_op jit(solution)/shard_map/project/pallas_call | solution.py:185
  54.1 0.1 collective-permute-done.10.refs_1_
  54.2 6.1 %collective-permute-done.11.refs_2_ = bf16[2,256,256]{2,1,0:T(8,128)(2,1)} collective-permute-done((bf16[2,256,256]{2,1,0:T(8,128)(2,1)}, bf16[2,256,256]{2,1,0:T(8,128)(2,1)}, u32[]{:S(2)}, u32[]{:S(2)}) %collective-permute-start.11) | collective-permute-done | bytes 262176 | tf_op jit(solution)/shard_map/ppermute | solution.py:402
  60.3 4.8 %attend_own.1 = (f32[256,2048]{1,0:T(8,128)S(1)}, bf16[256,2048]{1,0:T(8,128)(2,1)S(1)}) custom-call(bf16[256,2048]{1,0:T(8,128)(2,1)S(1)} %bitcast.9, f32[2,256,256]{2,1,0:T(8,128)S(1)} %project.4.refs_0_, bf16[2,256,256]{2,1,0:T(8,128)(2,1)S(1)} %collective-permute-done.10.refs_1_, bf16[2,256,256]{2,1,0:T(8,128)(2,1)} %collective-permute-done.11.refs_2_, ...), custom_call_target="tpu_custom_call" | custom-call | tf_op jit(solution)/shard_map/attend_own/pallas_call | solution.py:298
  65.1 3.5 %finish.1 = bf16[256,2048]{1,0:T(8,128)(2,1)} custom-call(s32[1]{0:T(128)} %bitcast.1.live_ref, f32[256,2048]{1,0:T(8,128)S(1)} %get-tuple-element.32.mixed_ref, bf16[256,2048]{1,0:T(8,128)(2,1)S(1)} %get-tuple-element.33.probs_ref, f32[2,256,256]{2,1,0:T(8,128)S(1)} %project.4.refs_0_, bf16[2,256,256]{2,1,0:T(8,128)(2,1)S(1)} %collective-permute-done.10.refs_1_, ...), custom_call_target="tpu_custom_call" | custom-call | tf_op jit(solution)/shard_map/finish/pallas_call | solution.py:325
  (24 shorter events, 0.2 us)
Async XLA Ops:
  1.2 22.3 %copy-start = (bf16[1,2,128,2048]{3,2,1,0:T(8,128)(2,1)S(1)}, bf16[1,2,128,2048]{3,2,1,0:T(8,128)(2,1)}, u32[]{:S(2)}) copy-start(bf16[1,2,128,2048]{3,2,1,0:T(8,128)(2,1)} %param.9) | copy-start | bytes 3145732
  1.2 16.5 %collective-permute-start = (bf16[2,512,256]{2,1,0:T(8,128)(2,1)S(1)}, bf16[2,512,256]{2,1,0:T(8,128)(2,1)S(1)}, u32[]{:S(2)}, u32[]{:S(2)}) collective-permute-start(bf16[2,512,256]{2,1,0:T(8,128)(2,1)S(1)} %get-tuple-element.20.refs_0_), channel_id=1, source_target_pairs={{0,8},{8,12},{12,4},{4,0},{1,9},{9,13},{13,5},{5,1},{2,10},{10,14}... | collective-permute-start | bytes 1572872 | tf_op jit(solution)/shard_map/ppermute | solution.py:380
  5.3 14.8 %collective-permute-start.5 = (bf16[2,512,256]{2,1,0:T(8,128)(2,1)S(1)}, bf16[2,512,256]{2,1,0:T(8,128)(2,1)S(1)}, u32[]{:S(2)}, u32[]{:S(2)}) collective-permute-start(bf16[2,512,256]{2,1,0:T(8,128)(2,1)S(1)} %get-tuple-element.23.refs_0_), channel_id=1, source_target_pairs={{0,2},{2,0},{1,3},{3,1},{4,6},{6,4},{5,7},{7,5},{8,10},{10,8},{9,1... | collective-permute-start | bytes 1572872 | tf_op jit(solution)/shard_map/ppermute | solution.py:375
  9.2 21.3 %collective-permute-start.7 = (bf16[256,1024]{1,0:T(8,128)(2,1)S(1)}, bf16[256,1024]{1,0:T(8,128)(2,1)S(1)}, u32[]{:S(2)}, u32[]{:S(2)}) collective-permute-start(bf16[256,1024]{1,0:T(8,128)(2,1)S(1)} %get-tuple-element.25), channel_id=1, source_target_pairs={{0,16},{2,18},{16,0},{18,2},{1,17},{3,19},{17,1},{19,3},{4,20},{6,... | collective-permute-start | bytes 1572872 | tf_op jit(solution)/shard_map/ppermute | solution.py:397
  10.8 20.6 %collective-permute-start.4 = (bf16[256,1024]{1,0:T(8,128)(2,1)S(1)}, bf16[256,1024]{1,0:T(8,128)(2,1)S(1)}, u32[]{:S(2)}, u32[]{:S(2)}) collective-permute-start(bf16[256,1024]{1,0:T(8,128)(2,1)S(1)} %get-tuple-element.22), channel_id=1, source_target_pairs={{0,2},{2,0},{16,18},{18,16},{1,3},{3,1},{17,19},{19,17},{4,6},{6,4... | collective-permute-start | bytes 1572872 | tf_op jit(solution)/shard_map/ppermute | solution.py:397
  11.3 20.1 %collective-permute-start.2 = (bf16[2,512,256]{2,1,0:T(8,128)(2,1)S(1)}, bf16[2,512,256]{2,1,0:T(8,128)(2,1)S(1)}, u32[]{:S(2)}, u32[]{:S(2)}) collective-permute-start(bf16[2,512,256]{2,1,0:T(8,128)(2,1)S(1)} %get-tuple-element.20.refs_0_), channel_id=1, source_target_pairs={{8,0},{12,8},{4,12},{0,4},{9,1},{13,9},{5,13},{1,5},{10,2},{14,10}... | collective-permute-start | bytes 1572872 | tf_op jit(solution)/shard_map/ppermute | solution.py:385
  17.7 24.4 %collective-permute-start.9 = (bf16[256,1024]{1,0:T(8,128)(2,1)S(1)}, bf16[256,1024]{1,0:T(8,128)(2,1)S(1)}, u32[]{:S(2)}, u32[]{:S(2)}) collective-permute-start(bf16[256,1024]{1,0:T(8,128)(2,1)S(1)} %after.6), channel_id=1, source_target_pairs={{0,18},{2,16},{16,2},{18,0},{1,19},{3,17},{17,3},{19,1},{4,22},{6,... | collective-permute-start | bytes 1572872 | tf_op jit(solution)/shard_map/ppermute | solution.py:397
  20.2 22.0 %collective-permute-start.1 = (bf16[2,512,256]{2,1,0:T(8,128)(2,1)S(1)}, bf16[2,512,256]{2,1,0:T(8,128)(2,1)S(1)}, u32[]{:S(2)}, u32[]{:S(2)}) collective-permute-start(bf16[2,512,256]{2,1,0:T(8,128)(2,1)S(1)} %collective-permute-done.refs_2_.refs_1_), channel_id=1, source_target_pairs={{0,8},{8,12},{12,4},{4,0},{1,9},{9,13},{13,5},{5,1},{2,10},{10,14}... | collective-permute-start | bytes 1572872 | tf_op jit(solution)/shard_map/ppermute | solution.py:380
  30.4 11.7 %copy-start.1 = (f32[256,2048]{1,0:T(8,128)}, f32[256,2048]{1,0:T(8,128)S(1)}, u32[]{:S(2)}) copy-start(f32[256,2048]{1,0:T(8,128)S(1)} %get-tuple-element.30.refs_5_) | copy-start | bytes 6291460
  30.5 11.7 %copy-start.2 = (f32[256,2048]{1,0:T(8,128)}, f32[256,2048]{1,0:T(8,128)S(1)}, u32[]{:S(2)}) copy-start(f32[256,2048]{1,0:T(8,128)S(1)} %get-tuple-element.31.refs_6_) | copy-start | bytes 6291460
  30.5 12.2 %collective-permute-start.8 = (bf16[256,1024]{1,0:T(8,128)(2,1)S(1)}, bf16[256,1024]{1,0:T(8,128)(2,1)S(1)}, u32[]{:S(2)}, u32[]{:S(2)}) collective-permute-start(bf16[256,1024]{1,0:T(8,128)(2,1)S(1)} %after.5.refs_6_), channel_id=1, source_target_pairs={{0,1},{1,0},{2,3},{3,2},{4,5},{5,4},{6,7},{7,6},{8,9},{9,8},{10,11... | collective-permute-start | bytes 1572872 | tf_op jit(solution)/shard_map/ppermute | solution.py:399
  31.4 11.3 %collective-permute-start.6 = (bf16[256,1024]{1,0:T(8,128)(2,1)S(1)}, bf16[256,1024]{1,0:T(8,128)(2,1)S(1)}, u32[]{:S(2)}, u32[]{:S(2)}) collective-permute-start(bf16[256,1024]{1,0:T(8,128)(2,1)S(1)} %after.4.refs_4_), channel_id=1, source_target_pairs={{0,1},{1,0},{2,3},{3,2},{4,5},{5,4},{6,7},{7,6},{8,9},{9,8},{10,11... | collective-permute-start | bytes 1572872 | tf_op jit(solution)/shard_map/ppermute | solution.py:399
  42.2 4.7 %collective-permute-start.12 = (bf16[256,1024]{1,0:T(8,128)(2,1)S(1)}, bf16[256,1024]{1,0:T(8,128)(2,1)S(1)}, u32[]{:S(2)}, u32[]{:S(2)}) collective-permute-start(bf16[256,1024]{1,0:T(8,128)(2,1)S(1)} %after.7.refs_8_.refs_4_), channel_id=1, source_target_pairs={{0,1},{1,0},{2,3},{3,2},{4,5},{5,4},{6,7},{7,6},{8,9},{9,8},{10,11... | collective-permute-start | bytes 1572872 | tf_op jit(solution)/shard_map/ppermute | solution.py:399
  42.2 9.8 %collective-permute-start.3 = (bf16[256,1024]{1,0:T(8,128)(2,1)}, bf16[256,1024]{1,0:T(8,128)(2,1)}, u32[]{:S(2)}, u32[]{:S(2)}) collective-permute-start(bf16[256,1024]{1,0:T(8,128)(2,1)} %get-tuple-element.21.refs_4_), channel_id=1, source_target_pairs={{0,1},{1,0},{2,3},{3,2},{4,5},{5,4},{6,7},{7,6},{8,9},{9,8},{10,11... | collective-permute-start | bytes 1572872 | tf_op jit(solution)/shard_map/ppermute | solution.py:399
  44.9 9.4 %collective-permute-start.10 = (bf16[2,256,256]{2,1,0:T(8,128)(2,1)}, bf16[2,256,256]{2,1,0:T(8,128)(2,1)S(1)}, u32[]{:S(2)}, u32[]{:S(2)}) collective-permute-start(bf16[2,256,256]{2,1,0:T(8,128)(2,1)} %get-tuple-element.27.refs_6_), channel_id=1, source_target_pairs={{0,2},{2,0},{16,18},{18,16},{1,3},{3,1},{17,19},{19,17},{4,6},{6,4... | collective-permute-start | bytes 786440 | tf_op jit(solution)/shard_map/ppermute | solution.py:402
  46.4 13.9 %collective-permute-start.11 = (bf16[2,256,256]{2,1,0:T(8,128)(2,1)}, bf16[2,256,256]{2,1,0:T(8,128)(2,1)}, u32[]{:S(2)}, u32[]{:S(2)}) collective-permute-start(bf16[2,256,256]{2,1,0:T(8,128)(2,1)} %get-tuple-element.28), channel_id=1, source_target_pairs={{0,16},{2,18},{16,0},{18,2},{1,17},{3,19},{17,1},{19,3},{4,20},{6,... | collective-permute-start | bytes 786440 | tf_op jit(solution)/shard_map/ppermute | solution.py:402
  48.5 11.8 %collective-permute-start.13 = (bf16[256,256]{1,0:T(8,128)(2,1)}, bf16[256,256]{1,0:T(8,128)(2,1)}, u32[]{:S(2)}, u32[]{:S(2)}) collective-permute-start(bf16[256,256]{1,0:T(8,128)(2,1)} %get-tuple-element.29), channel_id=1, source_target_pairs={{0,18},{2,16},{16,2},{18,0},{1,19},{3,17},{17,3},{19,1},{4,22},{6,... | collective-permute-start | bytes 393224 | tf_op jit(solution)/shard_map/ppermute | solution.py:402
  50.0 15.1 %collective-permute-start.14 = (bf16[256,256]{1,0:T(8,128)(2,1)}, bf16[256,256]{1,0:T(8,128)(2,1)S(1)}, u32[]{:S(2)}, u32[]{:S(2)}) collective-permute-start(bf16[256,256]{1,0:T(8,128)(2,1)} %get-tuple-element.34), channel_id=1, source_target_pairs={{0,18},{2,16},{16,2},{18,0},{1,19},{3,17},{17,3},{19,1},{4,22},{6,... | collective-permute-start | bytes 393224 | tf_op jit(solution)/shard_map/ppermute | solution.py:402

commit v10 on v7

--- a/solution.py
+++ b/solution.py
@@ -225,6 +225,8 @@
             q = take(q_ref, first, step)
             return [dot_nt(q, k) for k in keys]
 
+        lane = lax.broadcasted_iota(jnp.int32, (tokens, HD), 1)
+        levels = jnp.zeros((tokens, HD), jnp.float32)
         coming = scores_of(0)
         for first in range(0, group_size, step):
             scores = coming
@@ -239,18 +241,25 @@
                 out = part if out is None else out + part
             total = out[:, HD:]
             put(mixed_ref, first, step, out[:, :HD] / total)
-            put(level_ref, first, step, top * FACTOR + jnp.log2(total))
+            level = top * FACTOR + jnp.log2(total)
+            for n in range(step):
+                levels = jnp.where(lane == first + n, level[n * tokens : (n + 1) * tokens], levels)
+        level_ref[...] = levels
 
     spec_wide = pl.BlockSpec((tokens, group_size * HD), lambda head, slot: (slot, head))
     spec_c = pl.BlockSpec((2, length, HD), lambda head, slot: (0, 0, head))
+    spec_level = pl.BlockSpec((tokens, HD), lambda head, slot: (slot, head))
     spec_mark = pl.BlockSpec((8, HD), lambda head, slot: (0, 0))
     return pl.pallas_call(
         body,
         grid=(heads, slots),
         in_specs=[spec_wide] + [spec_c] * count + [ANYWHERE] * len(waits),
-        out_specs=[spec_wide] * 2 + [spec_mark],
-        out_shape=[jax.ShapeDtypeStruct(queries.shape, jnp.float32)] * 2
-        + [jax.ShapeDtypeStruct((8, HD), jnp.float32)],
+        out_specs=[spec_wide, spec_level, spec_mark],
+        out_shape=[
+            jax.ShapeDtypeStruct(queries.shape, queries.dtype),
+            jax.ShapeDtypeStruct((slots * tokens, heads * HD), jnp.float32),
+            jax.ShapeDtypeStruct((8, HD), jnp.float32),
+        ],
         name="attend_cache",
         **settings(20),
     )(queries, *caches, *waits)
@@ -279,17 +288,20 @@
         causal = jnp.concatenate([causal] * group_size, axis=0)
         scores = dot_nt(take(q_ref, 0, group_size), key) * FACTOR
         scores = jnp.where(causal, scores, -1e30)
-        level = take(level_ref, 0, group_size)
-        top = jnp.max(jnp.maximum(level, scores), axis=1, keepdims=True)
+        level = jnp.concatenate([level_ref[:, n : n + 1] for n in range(group_size)], axis=0)
+        top = jnp.maximum(level, jnp.max(scores, axis=1, keepdims=True))
         probs = jnp.exp2(scores - top).astype(jnp.bfloat16)
         kept = jnp.exp2(level - top)
         out = dot_nn(probs, wide)
-        mixed = take(mixed_ref, 0, group_size) * kept + out[:, :HD]
-        result = mixed / (kept + out[:, HD:])
+        mixed = take(mixed_ref, 0, group_size).astype(jnp.float32) * kept + out[:, :HD]
+        total = kept + out[:, HD:]
+        inverse = pl.reciprocal(total, approx=True)
+        result = mixed * (inverse * (2.0 - total * inverse))
         put(out_ref, 0, group_size, jnp.where(slot < live_ref[0], result, 0.0))
 
     spec_wide = pl.BlockSpec((tokens, group_size * HD), lambda slot, head: (slot, head))
     spec_part = pl.BlockSpec((2, tokens, HD), lambda slot, head: (0, slot, head))
+    spec_part_level = pl.BlockSpec((tokens, HD), lambda slot, head: (slot, head))
     spec_table = pl.BlockSpec(table.shape, lambda slot, head: (0, 0, 0))
     kept_back = [pltpu.with_memory_space_constraint(x, pltpu.HBM) for x in (table, *state)]
     return pl.pallas_call(
@@ -297,7 +309,7 @@
         grid=(slots, heads),
         in_specs=[pl.BlockSpec(memory_space=pltpu.SMEM), spec_wide]
         + [spec_part] * count
-        + [spec_table, spec_wide, spec_wide],
+        + [spec_table, spec_wide, spec_part_level],
         out_specs=spec_wide,
         out_shape=jax.ShapeDtypeStruct(queries.shape, queries.dtype),
         name="attend_own",

time: 65.6 us -> 66.9 us (1.020)
  Pallas kernels: 18.1 us -> 19.3 us
    pallas_call x1, Pallas kernels: 5.58 us -> 6.93 us  [attend_own(): pl.pallas_call(body, grid=(slots, heads), in_specs=[pl.BlockSpec(memory_s...]
where the time goes in v10:
time: 66.9 us; the launch traced here: 66.7 us
  waiting for transfers between devices  28.9 us (43%)
  Pallas kernels  19.3 us (29%)
  starting transfers between devices  17.7 us (26%)
  between operations  0.76 us (1%)
    ppermute x2, waiting for transfers between devices, on_device(): held = lax.ppermute(held, 'fsdp', rightward)  15.5 us
    ppermute x3, waiting for transfers between devices, on_device(): parts.append(lax.ppermute(x, plane, back) if any(p) else x)  10.4 us
    ppermute x2, starting transfers between devices, on_device(): held = lax.ppermute(held, 'fsdp', rightward)  7.47 us
    pallas_call x1, Pallas kernels, attend_own(): pl.pallas_call(body, grid=(slots, heads), in_specs=[pl.BlockSpec(memory_s...  6.93 us
    pallas_call x1, Pallas kernels, attend_cache(): pl.pallas_call(body, grid=(heads, slots), in_specs=[spec_wide] + [spec_c]...  6.7 us
    ppermute x3, starting transfers between devices, on_device(): moved = lax.ppermute(near[place], plane, shift(*place))  4.57 us
    ppermute x3, starting transfers between devices, on_device(): parts.append(lax.ppermute(x, plane, back) if any(p) else x)  3.62 us
    ppermute x3, waiting for transfers between devices, on_device(): moved = lax.ppermute(near[place], plane, shift(*place))  2.89 us
  transfers between devices with their start and end apart: 14, of which 6 were waited for; matrix products, arithmetic and copies ran while one was open for 0% of the time, Pallas kernels for 17%

profile of v10, /device:TPU:0, one launch (start us, length us, event | category | flops | bytes accessed | tf_op | source)
XLA Modules:
  0.0 66.7 jit_solution(16436495030502455715)
XLA Ops:
  0.0 1.2 %pack_rows.1 = (bf16[2,512,256]{2,1,0:T(8,128)(2,1)S(1)}, bf16[2,512,256]{2,1,0:T(8,128)(2,1)S(1)}) custom-call(bf16[1024,256]{1,0:T(8,128)(2,1)} %kw_ref.1, bf16[1024,256]{1,0:T(8,128)(2,1)} %vw_ref.1, bf16[512,256]{1,0:T(8,128)(2,1)} %bitcast.11, bf16[512,256]{1,0:T(8,128)(2,1)} %bitcast.12), custom_call_target="tpu_custom_call" | custom-call | tf_op jit(solution)/shard_map/pack_rows/pallas_call | solution.py:74
  1.2 0.0 copy-start
  1.2 4.1 %collective-permute-start = (bf16[2,512,256]{2,1,0:T(8,128)(2,1)S(1)}, bf16[2,512,256]{2,1,0:T(8,128)(2,1)S(1)}, u32[]{:S(2)}, u32[]{:S(2)}) collective-permute-start(bf16[2,512,256]{2,1,0:T(8,128)(2,1)S(1)} %get-tuple-element.17.refs_0_), channel_id=1, source_target_pairs={{0,8},{8,12},{12,4},{4,0},{1,9},{9,13},{13,5},{5,1},{2,10},{10,14}... | collective-permute-start | bytes 1572872 | tf_op jit(solution)/shard_map/ppermute | solution.py:362
  5.3 1.5 %collective-permute-start.4 = (bf16[2,512,256]{2,1,0:T(8,128)(2,1)S(1)}, bf16[2,512,256]{2,1,0:T(8,128)(2,1)S(1)}, u32[]{:S(2)}, u32[]{:S(2)}) collective-permute-start(bf16[2,512,256]{2,1,0:T(8,128)(2,1)S(1)} %get-tuple-element.19.refs_0_), channel_id=1, source_target_pairs={{0,2},{2,0},{1,3},{3,1},{4,6},{6,4},{5,7},{7,5},{8,10},{10,8},{9,1... | collective-permute-start | bytes 1572872 | tf_op jit(solution)/shard_map/ppermute | solution.py:357
  6.8 1.6 %pack_features.1 = (bf16[256,1024]{1,0:T(8,128)(2,1)S(1)}, bf16[256,1024]{1,0:T(8,128)(2,1)S(1)}, bf16[256,1024]{1,0:T(8,128)(2,1)S(1)}, bf16[256,1024]{1,0:T(8,128)(2,1)S(1)}) custom-call(bf16[256,4096]{1,0:T(8,128)(2,1)} %bitcast.10), custom_call_target="tpu_custom_call" | custom-call | tf_op jit(solution)/shard_map/pack_features/pallas_call | solution.py:132
  8.4 0.6 collective-permute-start.3
  9.0 1.5 %collective-permute-start.6 = (bf16[256,1024]{1,0:T(8,128)(2,1)S(1)}, bf16[256,1024]{1,0:T(8,128)(2,1)S(1)}, u32[]{:S(2)}, u32[]{:S(2)}) collective-permute-start(bf16[256,1024]{1,0:T(8,128)(2,1)S(1)} %get-tuple-element.21), channel_id=1, source_target_pairs={{0,16},{2,18},{16,0},{18,2},{1,17},{3,19},{17,1},{19,3},{4,20},{6,... | collective-permute-start | bytes 1572872 | tf_op jit(solution)/shard_map/ppermute | solution.py:379
  10.5 7.2 %collective-permute-done.refs_2_.refs_1_ = bf16[2,512,256]{2,1,0:T(8,128)(2,1)S(1)} collective-permute-done((bf16[2,512,256]{2,1,0:T(8,128)(2,1)S(1)}, bf16[2,512,256]{2,1,0:T(8,128)(2,1)S(1)}, u32[]{:S(2)}, u32[]{:S(2)}) %collective-permute-start) | collective-permute-done | bytes 524320 | tf_op jit(solution)/shard_map/ppermute | solution.py:362
  17.7 3.4 %collective-permute-start.1 = (bf16[2,512,256]{2,1,0:T(8,128)(2,1)S(1)}, bf16[2,512,256]{2,1,0:T(8,128)(2,1)S(1)}, u32[]{:S(2)}, u32[]{:S(2)}) collective-permute-start(bf16[2,512,256]{2,1,0:T(8,128)(2,1)S(1)} %collective-permute-done.refs_2_.refs_1_), channel_id=1, source_target_pairs={{0,8},{8,12},{12,4},{4,0},{1,9},{9,13},{13,5},{5,1},{2,10},{10,14}... | collective-permute-start | bytes 1572872 | tf_op jit(solution)/shard_map/ppermute | solution.py:362
  21.1 2.4 %collective-permute-start.9 = (bf16[256,1024]{1,0:T(8,128)(2,1)S(1)}, bf16[256,1024]{1,0:T(8,128)(2,1)S(1)}, u32[]{:S(2)}, u32[]{:S(2)}) collective-permute-start(bf16[256,1024]{1,0:T(8,128)(2,1)S(1)} %after.6), channel_id=1, source_target_pairs={{0,18},{2,16},{16,2},{18,0},{1,19},{3,17},{17,3},{19,1},{4,22},{6,... | collective-permute-start | bytes 1572872 | tf_op jit(solution)/shard_map/ppermute | solution.py:379
  23.5 6.7 %attend_cache.1 = (bf16[256,2048]{1,0:T(8,128)(2,1)S(1)}, f32[256,256]{1,0:T(8,128)S(1)}, f32[8,128]{1,0:T(8,128)S(1)}) custom-call(bf16[256,2048]{1,0:T(8,128)(2,1)S(1)} %bitcast.8, bf16[2,512,256]{2,1,0:T(8,128)(2,1)S(1)} %get-tuple-element.19.refs_0_, bf16[2,512,256]{2,1,0:T(8,128)(2,1)S(1)} %collective-permute-done.4.refs_1_, ...), custom_call_target="tpu_custom_call" | custom-call | tf_op jit(solution)/shard_map/attend_cache/pallas_call | solution.py:253
  30.3 1.1 %collective-permute-done.3.refs_0_ = bf16[256,1024]{1,0:T(8,128)(2,1)S(1)} collective-permute-done((bf16[256,1024]{1,0:T(8,128)(2,1)S(1)}, bf16[256,1024]{1,0:T(8,128)(2,1)S(1)}, u32[]{:S(2)}, u32[]{:S(2)}) %collective-permute-start.3) | collective-permute-done | bytes 524320 | tf_op jit(solution)/shard_map/ppermute | solution.py:379
  31.4 0.5 collective-permute-start.5
  31.9 0.1 collective-permute-start.7
  32.0 8.4 %collective-permute-done.1.refs_2_ = bf16[2,512,256]{2,1,0:T(8,128)(2,1)S(1)} collective-permute-done((bf16[2,512,256]{2,1,0:T(8,128)(2,1)S(1)}, bf16[2,512,256]{2,1,0:T(8,128)(2,1)S(1)}, u32[]{:S(2)}, u32[]{:S(2)}) %collective-permute-start.1) | collective-permute-done | bytes 524320 | tf_op jit(solution)/shard_map/ppermute | solution.py:362
  40.4 1.7 %collective-permute-done.9.refs_0_ = bf16[256,1024]{1,0:T(8,128)(2,1)S(1)} collective-permute-done((bf16[256,1024]{1,0:T(8,128)(2,1)S(1)}, bf16[256,1024]{1,0:T(8,128)(2,1)S(1)}, u32[]{:S(2)}, u32[]{:S(2)}) %collective-permute-start.9) | collective-permute-done | bytes 524320 | tf_op jit(solution)/shard_map/ppermute | solution.py:379
  42.2 2.0 %project.2 = (bf16[2,256,256]{2,1,0:T(8,128)(2,1)S(1)}, bf16[2,256,256]{2,1,0:T(8,128)(2,1)S(1)}, f32[2,256,256]{2,1,0:T(8,128)S(1)}) custom-call(bf16[2,512,256]{2,1,0:T(8,128)(2,1)S(1)} %get-tuple-element.17.refs_0_, bf16[2,512,256]{2,1,0:T(8,128)(2,1)S(1)} %collective-permute-done.refs_2_.refs_1_, ...), custom_call_target="tpu_custom_call" | custom-call | tf_op jit(solution)/shard_map/project/pallas_call | solution.py:183
  44.2 1.6 %collective-permute-start.10 = (bf16[2,256,256]{2,1,0:T(8,128)(2,1)S(1)}, bf16[2,256,256]{2,1,0:T(8,128)(2,1)S(1)}, u32[]{:S(2)}, u32[]{:S(2)}) collective-permute-start(bf16[2,256,256]{2,1,0:T(8,128)(2,1)S(1)} %get-tuple-element.24), channel_id=1, source_target_pairs={{0,2},{2,0},{16,18},{18,16},{1,3},{3,1},{17,19},{19,17},{4,6},{6,4... | collective-permute-start | bytes 786440 | tf_op jit(solution)/shard_map/ppermute | solution.py:390
  45.7 0.5 collective-permute-start.11
  46.2 0.9 %project.3 = bf16[2,256,256]{2,1,0:T(8,128)(2,1)S(1)} custom-call(bf16[2,512,256]{2,1,0:T(8,128)(2,1)S(1)} %get-tuple-element.17.refs_0_, bf16[2,512,256]{2,1,0:T(8,128)(2,1)S(1)} %collective-permute-done.refs_2_.refs_1_, bf16[2,512,256]{2,1,0:T(8,128)(2,1)S(1)} %collective-permute-done.1.refs_2_, bf16[2,512,256]{2,1,0:T(8,128)(2,1)S(1)} %collective-permute-done.2.refs_3_, ...), custom_call_target="tpu_custom_call" | custom-call | tf_op jit(solution)/shard_map/project/pallas_call | solution.py:183
  47.1 1.6 %collective-permute-start.13 = (bf16[2,256,256]{2,1,0:T(8,128)(2,1)S(1)}, bf16[2,256,256]{2,1,0:T(8,128)(2,1)S(1)}, u32[]{:S(2)}, u32[]{:S(2)}) collective-permute-start(bf16[2,256,256]{2,1,0:T(8,128)(2,1)S(1)} %project.3), channel_id=1, source_target_pairs={{0,18},{2,16},{16,2},{18,0},{1,19},{3,17},{17,3},{19,1},{4,22},{6,... | collective-permute-start | bytes 786440 | tf_op jit(solution)/shard_map/ppermute | solution.py:390
  49.3 4.0 %collective-permute-done.10.refs_0_ = bf16[2,256,256]{2,1,0:T(8,128)(2,1)S(1)} collective-permute-done((bf16[2,256,256]{2,1,0:T(8,128)(2,1)S(1)}, bf16[2,256,256]{2,1,0:T(8,128)(2,1)S(1)}, u32[]{:S(2)}, u32[]{:S(2)}) %collective-permute-start.10) | collective-permute-done | bytes 262176 | tf_op jit(solution)/shard_map/ppermute | solution.py:390
  53.3 6.4 %collective-permute-done.11.refs_1_ = bf16[2,256,256]{2,1,0:T(8,128)(2,1)S(1)} collective-permute-done((bf16[2,256,256]{2,1,0:T(8,128)(2,1)S(1)}, bf16[2,256,256]{2,1,0:T(8,128)(2,1)S(1)}, u32[]{:S(2)}, u32[]{:S(2)}) %collective-permute-start.11) | collective-permute-done | bytes 262176 | tf_op jit(solution)/shard_map/ppermute | solution.py:390
  59.7 6.9 %attend_own.1 = bf16[256,2048]{1,0:T(8,128)(2,1)} custom-call(s32[1]{0:T(128)} %bitcast.1.live_ref, bf16[256,2048]{1,0:T(8,128)(2,1)S(1)} %bitcast.9, bf16[2,256,256]{2,1,0:T(8,128)(2,1)S(1)} %collective-permute-done.10.refs_0_, bf16[2,256,256]{2,1,0:T(8,128)(2,1)S(1)} %collective-permute-done.11.refs_1_, f32[2,256,256]{2,1,0:T(8,128)S(1)} %get-tuple-element.26.refs_2_, ...), custom_call_target="tpu_custom_call" | custom-call | tf_op jit(solution)/shard_map/attend_own/pallas_call | solution.py:307
  (20 shorter events, 0.0 us)
Async XLA Ops:
  1.2 22.3 %copy-start = (bf16[1,2,128,2048]{3,2,1,0:T(8,128)(2,1)S(1)}, bf16[1,2,128,2048]{3,2,1,0:T(8,128)(2,1)}, u32[]{:S(2)}) copy-start(bf16[1,2,128,2048]{3,2,1,0:T(8,128)(2,1)} %param.9) | copy-start | bytes 3145732
  1.2 16.5 %collective-permute-start = (bf16[2,512,256]{2,1,0:T(8,128)(2,1)S(1)}, bf16[2,512,256]{2,1,0:T(8,128)(2,1)S(1)}, u32[]{:S(2)}, u32[]{:S(2)}) collective-permute-start(bf16[2,512,256]{2,1,0:T(8,128)(2,1)S(1)} %get-tuple-element.17.refs_0_), channel_id=1, source_target_pairs={{0,8},{8,12},{12,4},{4,0},{1,9},{9,13},{13,5},{5,1},{2,10},{10,14}... | collective-permute-start | bytes 1572872 | tf_op jit(solution)/shard_map/ppermute | solution.py:362
  5.3 15.8 %collective-permute-start.4 = (bf16[2,512,256]{2,1,0:T(8,128)(2,1)S(1)}, bf16[2,512,256]{2,1,0:T(8,128)(2,1)S(1)}, u32[]{:S(2)}, u32[]{:S(2)}) collective-permute-start(bf16[2,512,256]{2,1,0:T(8,128)(2,1)S(1)} %get-tuple-element.19.refs_0_), channel_id=1, source_target_pairs={{0,2},{2,0},{1,3},{3,1},{4,6},{6,4},{5,7},{7,5},{8,10},{10,8},{9,1... | collective-permute-start | bytes 1572872 | tf_op jit(solution)/shard_map/ppermute | solution.py:357
  8.4 23.0 %collective-permute-start.3 = (bf16[256,1024]{1,0:T(8,128)(2,1)S(1)}, bf16[256,1024]{1,0:T(8,128)(2,1)S(1)}, u32[]{:S(2)}, u32[]{:S(2)}) collective-permute-start(bf16[256,1024]{1,0:T(8,128)(2,1)S(1)} %get-tuple-element.18), channel_id=1, source_target_pairs={{0,2},{2,0},{16,18},{18,16},{1,3},{3,1},{17,19},{19,17},{4,6},{6,4... | collective-permute-start | bytes 1572872 | tf_op jit(solution)/shard_map/ppermute | solution.py:379
  9.0 22.4 %collective-permute-start.6 = (bf16[256,1024]{1,0:T(8,128)(2,1)S(1)}, bf16[256,1024]{1,0:T(8,128)(2,1)S(1)}, u32[]{:S(2)}, u32[]{:S(2)}) collective-permute-start(bf16[256,1024]{1,0:T(8,128)(2,1)S(1)} %get-tuple-element.21), channel_id=1, source_target_pairs={{0,16},{2,18},{16,0},{18,2},{1,17},{3,19},{17,1},{19,3},{4,20},{6,... | collective-permute-start | bytes 1572872 | tf_op jit(solution)/shard_map/ppermute | solution.py:379
  10.5 21.4 %collective-permute-start.2 = (bf16[2,512,256]{2,1,0:T(8,128)(2,1)S(1)}, bf16[2,512,256]{2,1,0:T(8,128)(2,1)S(1)}, u32[]{:S(2)}, u32[]{:S(2)}) collective-permute-start(bf16[2,512,256]{2,1,0:T(8,128)(2,1)S(1)} %get-tuple-element.17.refs_0_), channel_id=1, source_target_pairs={{8,0},{12,8},{4,12},{0,4},{9,1},{13,9},{5,13},{1,5},{10,2},{14,10}... | collective-permute-start | bytes 1572872 | tf_op jit(solution)/shard_map/ppermute | solution.py:367
  17.7 22.7 %collective-permute-start.1 = (bf16[2,512,256]{2,1,0:T(8,128)(2,1)S(1)}, bf16[2,512,256]{2,1,0:T(8,128)(2,1)S(1)}, u32[]{:S(2)}, u32[]{:S(2)}) collective-permute-start(bf16[2,512,256]{2,1,0:T(8,128)(2,1)S(1)} %collective-permute-done.refs_2_.refs_1_), channel_id=1, source_target_pairs={{0,8},{8,12},{12,4},{4,0},{1,9},{9,13},{13,5},{5,1},{2,10},{10,14}... | collective-permute-start | bytes 1572872 | tf_op jit(solution)/shard_map/ppermute | solution.py:362
  21.1 21.1 %collective-permute-start.9 = (bf16[256,1024]{1,0:T(8,128)(2,1)S(1)}, bf16[256,1024]{1,0:T(8,128)(2,1)S(1)}, u32[]{:S(2)}, u32[]{:S(2)}) collective-permute-start(bf16[256,1024]{1,0:T(8,128)(2,1)S(1)} %after.6), channel_id=1, source_target_pairs={{0,18},{2,16},{16,2},{18,0},{1,19},{3,17},{17,3},{19,1},{4,22},{6,... | collective-permute-start | bytes 1572872 | tf_op jit(solution)/shard_map/ppermute | solution.py:379
  30.2 11.9 %copy-start.2 = (f32[256,256]{1,0:T(8,128)}, f32[256,256]{1,0:T(8,128)S(1)}, u32[]{:S(2)}) copy-start(f32[256,256]{1,0:T(8,128)S(1)} %get-tuple-element.28.refs_6_) | copy-start | bytes 786436
  30.3 11.9 %copy-start.1 = (bf16[256,2048]{1,0:T(8,128)(2,1)}, bf16[256,2048]{1,0:T(8,128)(2,1)S(1)}, u32[]{:S(2)}) copy-start(bf16[256,2048]{1,0:T(8,128)(2,1)S(1)} %get-tuple-element.27.refs_5_) | copy-start | bytes 3145732
  31.4 10.7 %collective-permute-start.8 = (bf16[256,1024]{1,0:T(8,128)(2,1)S(1)}, bf16[256,1024]{1,0:T(8,128)(2,1)S(1)}, u32[]{:S(2)}, u32[]{:S(2)}) collective-permute-start(bf16[256,1024]{1,0:T(8,128)(2,1)S(1)} %get-tuple-element.22.refs_8_), channel_id=1, source_target_pairs={{0,1},{1,0},{2,3},{3,2},{4,5},{5,4},{6,7},{7,6},{8,9},{9,8},{10,11... | collective-permute-start | bytes 1572872 | tf_op jit(solution)/shard_map/ppermute | solution.py:381
  31.4 10.7 %collective-permute-start.5 = (bf16[256,1024]{1,0:T(8,128)(2,1)S(1)}, bf16[256,1024]{1,0:T(8,128)(2,1)S(1)}, u32[]{:S(2)}, u32[]{:S(2)}) collective-permute-start(bf16[256,1024]{1,0:T(8,128)(2,1)S(1)} %after.4.refs_4_), channel_id=1, source_target_pairs={{0,1},{1,0},{2,3},{3,2},{4,5},{5,4},{6,7},{7,6},{8,9},{9,8},{10,11... | collective-permute-start | bytes 1572872 | tf_op jit(solution)/shard_map/ppermute | solution.py:381
  31.9 10.2 %collective-permute-start.7 = (bf16[256,1024]{1,0:T(8,128)(2,1)S(1)}, bf16[256,1024]{1,0:T(8,128)(2,1)S(1)}, u32[]{:S(2)}, u32[]{:S(2)}) collective-permute-start(bf16[256,1024]{1,0:T(8,128)(2,1)S(1)} %after.5.refs_6_), channel_id=1, source_target_pairs={{0,1},{1,0},{2,3},{3,2},{4,5},{5,4},{6,7},{7,6},{8,9},{9,8},{10,11... | collective-permute-start | bytes 1572872 | tf_op jit(solution)/shard_map/ppermute | solution.py:381
  42.1 4.1 %collective-permute-start.12 = (bf16[256,1024]{1,0:T(8,128)(2,1)S(1)}, bf16[256,1024]{1,0:T(8,128)(2,1)S(1)}, u32[]{:S(2)}, u32[]{:S(2)}) collective-permute-start(bf16[256,1024]{1,0:T(8,128)(2,1)S(1)} %after.7.refs_10_.refs_4_), channel_id=1, source_target_pairs={{0,1},{1,0},{2,3},{3,2},{4,5},{5,4},{6,7},{7,6},{8,9},{9,8},{10,11... | collective-permute-start | bytes 1572872 | tf_op jit(solution)/shard_map/ppermute | solution.py:381
  44.2 9.2 %collective-permute-start.10 = (bf16[2,256,256]{2,1,0:T(8,128)(2,1)S(1)}, bf16[2,256,256]{2,1,0:T(8,128)(2,1)S(1)}, u32[]{:S(2)}, u32[]{:S(2)}) collective-permute-start(bf16[2,256,256]{2,1,0:T(8,128)(2,1)S(1)} %get-tuple-element.24), channel_id=1, source_target_pairs={{0,2},{2,0},{16,18},{18,16},{1,3},{3,1},{17,19},{19,17},{4,6},{6,4... | collective-permute-start | bytes 786440 | tf_op jit(solution)/shard_map/ppermute | solution.py:390
  45.7 14.0 %collective-permute-start.11 = (bf16[2,256,256]{2,1,0:T(8,128)(2,1)S(1)}, bf16[2,256,256]{2,1,0:T(8,128)(2,1)S(1)}, u32[]{:S(2)}, u32[]{:S(2)}) collective-permute-start(bf16[2,256,256]{2,1,0:T(8,128)(2,1)S(1)} %get-tuple-element.25), channel_id=1, source_target_pairs={{0,16},{2,18},{16,0},{18,2},{1,17},{3,19},{17,1},{19,3},{4,20},{6,... | collective-permute-start | bytes 786440 | tf_op jit(solution)/shard_map/ppermute | solution.py:390
  47.1 12.6 %collective-permute-start.13 = (bf16[2,256,256]{2,1,0:T(8,128)(2,1)S(1)}, bf16[2,256,256]{2,1,0:T(8,128)(2,1)S(1)}, u32[]{:S(2)}, u32[]{:S(2)}) collective-permute-start(bf16[2,256,256]{2,1,0:T(8,128)(2,1)S(1)} %project.3), channel_id=1, source_target_pairs={{0,18},{2,16},{16,2},{18,0},{1,19},{3,17},{17,3},{19,1},{4,22},{6,... | collective-permute-start | bytes 786440 | tf_op jit(solution)/shard_map/ppermute | solution.py:390

commit v11 on v7

--- a/solution.py
+++ b/solution.py
@@ -285,7 +285,9 @@
         kept = jnp.exp2(level - top)
         out = dot_nn(probs, wide)
         mixed = take(mixed_ref, 0, group_size) * kept + out[:, :HD]
-        result = mixed / (kept + out[:, HD:])
+        total = kept + out[:, HD:]
+        inverse = pl.reciprocal(total, approx=True)
+        result = mixed * (inverse * (2.0 - total * inverse))
         put(out_ref, 0, group_size, jnp.where(slot < live_ref[0], result, 0.0))
 
     spec_wide = pl.BlockSpec((tokens, group_size * HD), lambda slot, head: (slot, head))
@@ -328,7 +330,7 @@
     along = [(0, b) for b in range(1, n_resp)]
     across = [(a, b) for a in range(1, n_groups) for b in range(1, n_resp)]
     twins = [(a, 0) for a in range(1, n_groups)]
-    sets = [(0, 0), *along, *twins, *across]
+    sets = [(0, 0), *across, *twins, *along]
 
     def shift(a, b):
         return [
@@ -360,17 +362,17 @@
     *state, mark = attend_cache(slots, group_size, flat_queries, caches, [first_hop])
 
     near = dict(zip(sets, pack_features(sizes, block, sets, hidden.reshape(rows, part_width))))
-    for place in across:
+    for place in along:
         near[place] = after(near[place], first_hop)
     for place in sets[1:]:
-        waits = ends if place in across else []
+        waits = ends if place in along else []
         moved = lax.ppermute(near[place], plane, shift(*place))
         near[place] = after(moved, mark, *waits)
     far = {place: lax.ppermute(near[place], "tp", cores) for place in sets}
 
     narrow, wide = jnp.bfloat16, jnp.float32
     parts = []
-    for chosen, waits in (([*along, *twins, sets[0]], [near[p] for p in across]), (across, [])):
+    for chosen, waits in (([*across, *twins, sets[0]], [near[p] for p in along]), (along, [])):
         types = [narrow if any(p) else wide for p in chosen]
         sums = project(n_fsdp, pieces, [(near[p], far[p]) for p in chosen], types, waits)
         for p, x in zip(chosen, sums):

time: 65.6 us -> 64.5 us (0.983)
  starting transfers between devices: 17.7 us -> 16.7 us
    ppermute x3, waiting for transfers between devices: 2.68 us -> 5.35 us  [on_device(): moved = lax.ppermute(near[place], plane, shift(*place))]
    ppermute x2, waiting for transfers between devices: 15.6 us -> 13.1 us  [on_device(): held = lax.ppermute(held, 'fsdp', rightward)]
    ppermute x3, starting transfers between devices: 4.57 us -> 3.55 us  [on_device(): moved = lax.ppermute(near[place], plane, shift(*place))]
  transfers between devices with their start and end apart: 14 -> 14, of which waited for: 6 -> 8; matrix products, arithmetic and copies ran while one was open for 0% -> 0% of each run, Pallas kernels for 17% -> 18%
where the time goes in v11:
time: 64.5 us; the launch traced here: 64.2 us
  waiting for transfers between devices  28.6 us (44%)
  Pallas kernels  18.2 us (28%)
  starting transfers between devices  16.7 us (26%)
  between operations  0.76 us (1%)
    ppermute x2, waiting for transfers between devices, on_device(): held = lax.ppermute(held, 'fsdp', rightward)  13.1 us
    ppermute x3, waiting for transfers between devices, on_device(): parts.append(lax.ppermute(x, plane, back) if any(p) else x)  10.2 us
    ppermute x2, starting transfers between devices, on_device(): held = lax.ppermute(held, 'fsdp', rightward)  7.47 us
    pallas_call x1, Pallas kernels, attend_cache(): pl.pallas_call(body, grid=(heads, slots), in_specs=[spec_wide] + [spec_c]...  6.9 us
    pallas_call x1, Pallas kernels, attend_own(): pl.pallas_call(body, grid=(slots, heads), in_specs=[pl.BlockSpec(memory_s...  5.62 us
    ppermute x3, waiting for transfers between devices, on_device(): moved = lax.ppermute(near[place], plane, shift(*place))  5.35 us
    ppermute x3, starting transfers between devices, on_device(): parts.append(lax.ppermute(x, plane, back) if any(p) else x)  3.62 us
    ppermute x3, starting transfers between devices, on_device(): moved = lax.ppermute(near[place], plane, shift(*place))  3.55 us
  transfers between devices with their start and end apart: 14, of which 8 were waited for; matrix products, arithmetic and copies ran while one was open for 0% of the time, Pallas kernels for 18%

profile of v11, /device:TPU:0, one launch (start us, length us, event | category | flops | bytes accessed | tf_op | source)
XLA Modules:
  0.0 64.2 jit_solution(3693539419901517934)
XLA Ops:
  0.0 1.2 %pack_rows.1 = (bf16[2,512,256]{2,1,0:T(8,128)(2,1)S(1)}, bf16[2,512,256]{2,1,0:T(8,128)(2,1)S(1)}) custom-call(bf16[1024,256]{1,0:T(8,128)(2,1)} %kw_ref.1, bf16[1024,256]{1,0:T(8,128)(2,1)} %vw_ref.1, bf16[512,256]{1,0:T(8,128)(2,1)} %bitcast.11, bf16[512,256]{1,0:T(8,128)(2,1)} %bitcast.12), custom_call_target="tpu_custom_call" | custom-call | tf_op jit(solution)/shard_map/pack_rows/pallas_call | solution.py:74
  1.2 4.1 %collective-permute-start = (bf16[2,512,256]{2,1,0:T(8,128)(2,1)S(1)}, bf16[2,512,256]{2,1,0:T(8,128)(2,1)S(1)}, u32[]{:S(2)}, u32[]{:S(2)}) collective-permute-start(bf16[2,512,256]{2,1,0:T(8,128)(2,1)S(1)} %get-tuple-element.17.refs_0_), channel_id=1, source_target_pairs={{0,8},{8,12},{12,4},{4,0},{1,9},{9,13},{13,5},{5,1},{2,10},{10,14}... | collective-permute-start | bytes 1572872 | tf_op jit(solution)/shard_map/ppermute | solution.py:352
  5.3 1.5 %collective-permute-start.4 = (bf16[2,512,256]{2,1,0:T(8,128)(2,1)S(1)}, bf16[2,512,256]{2,1,0:T(8,128)(2,1)S(1)}, u32[]{:S(2)}, u32[]{:S(2)}) collective-permute-start(bf16[2,512,256]{2,1,0:T(8,128)(2,1)S(1)} %get-tuple-element.19.refs_0_), channel_id=1, source_target_pairs={{0,2},{2,0},{1,3},{3,1},{4,6},{6,4},{5,7},{7,5},{8,10},{10,8},{9,1... | collective-permute-start | bytes 1572872 | tf_op jit(solution)/shard_map/ppermute | solution.py:347
  6.8 1.6 %pack_features.1 = (bf16[256,1024]{1,0:T(8,128)(2,1)S(1)}, bf16[256,1024]{1,0:T(8,128)(2,1)S(1)}, bf16[256,1024]{1,0:T(8,128)(2,1)S(1)}, bf16[256,1024]{1,0:T(8,128)(2,1)S(1)}) custom-call(bf16[256,4096]{1,0:T(8,128)(2,1)} %bitcast.10), custom_call_target="tpu_custom_call" | custom-call | tf_op jit(solution)/shard_map/pack_features/pallas_call | solution.py:132
  8.4 1.6 %collective-permute-start.3 = (bf16[256,1024]{1,0:T(8,128)(2,1)S(1)}, bf16[256,1024]{1,0:T(8,128)(2,1)S(1)}, u32[]{:S(2)}, u32[]{:S(2)}) collective-permute-start(bf16[256,1024]{1,0:T(8,128)(2,1)S(1)} %get-tuple-element.18), channel_id=1, source_target_pairs={{0,18},{2,16},{16,2},{18,0},{1,19},{3,17},{17,3},{19,1},{4,22},{6,... | collective-permute-start | bytes 1572872 | tf_op jit(solution)/shard_map/ppermute | solution.py:369
  10.0 0.5 collective-permute-start.6
  10.5 7.2 %collective-permute-done.refs_2_.refs_1_ = bf16[2,512,256]{2,1,0:T(8,128)(2,1)S(1)} collective-permute-done((bf16[2,512,256]{2,1,0:T(8,128)(2,1)S(1)}, bf16[2,512,256]{2,1,0:T(8,128)(2,1)S(1)}, u32[]{:S(2)}, u32[]{:S(2)}) %collective-permute-start) | collective-permute-done | bytes 524320 | tf_op jit(solution)/shard_map/ppermute | solution.py:352
  17.7 3.4 %collective-permute-start.1 = (bf16[2,512,256]{2,1,0:T(8,128)(2,1)S(1)}, bf16[2,512,256]{2,1,0:T(8,128)(2,1)S(1)}, u32[]{:S(2)}, u32[]{:S(2)}) collective-permute-start(bf16[2,512,256]{2,1,0:T(8,128)(2,1)S(1)} %collective-permute-done.refs_2_.refs_1_), channel_id=1, source_target_pairs={{0,8},{8,12},{12,4},{4,0},{1,9},{9,13},{13,5},{5,1},{2,10},{10,14}... | collective-permute-start | bytes 1572872 | tf_op jit(solution)/shard_map/ppermute | solution.py:352
  21.1 1.5 %collective-permute-start.9 = (bf16[256,1024]{1,0:T(8,128)(2,1)S(1)}, bf16[256,1024]{1,0:T(8,128)(2,1)S(1)}, u32[]{:S(2)}, u32[]{:S(2)}) collective-permute-start(bf16[256,1024]{1,0:T(8,128)(2,1)S(1)} %after.6), channel_id=1, source_target_pairs={{0,2},{2,0},{16,18},{18,16},{1,3},{3,1},{17,19},{19,17},{4,6},{6,4... | collective-permute-start | bytes 1572872 | tf_op jit(solution)/shard_map/ppermute | solution.py:369
  22.6 6.9 %attend_cache.1 = (f32[256,2048]{1,0:T(8,128)S(1)}, f32[256,2048]{1,0:T(8,128)S(1)}, f32[8,128]{1,0:T(8,128)S(1)}) custom-call(bf16[256,2048]{1,0:T(8,128)(2,1)S(1)} %bitcast.8, bf16[2,512,256]{2,1,0:T(8,128)(2,1)S(1)} %get-tuple-element.19.refs_0_, bf16[2,512,256]{2,1,0:T(8,128)(2,1)S(1)} %collective-permute-done.4.refs_1_, ...), custom_call_target="tpu_custom_call" | custom-call | tf_op jit(solution)/shard_map/attend_cache/pallas_call | solution.py:247
  29.5 2.9 %collective-permute-done.3.refs_0_ = bf16[256,1024]{1,0:T(8,128)(2,1)S(1)} collective-permute-done((bf16[256,1024]{1,0:T(8,128)(2,1)S(1)}, bf16[256,1024]{1,0:T(8,128)(2,1)S(1)}, u32[]{:S(2)}, u32[]{:S(2)}) %collective-permute-start.3) | collective-permute-done | bytes 524320 | tf_op jit(solution)/shard_map/ppermute | solution.py:369
  32.4 1.6 %collective-permute-done.6.refs_0_ = bf16[256,1024]{1,0:T(8,128)(2,1)S(1)} collective-permute-done((bf16[256,1024]{1,0:T(8,128)(2,1)S(1)}, bf16[256,1024]{1,0:T(8,128)(2,1)S(1)}, u32[]{:S(2)}, u32[]{:S(2)}) %collective-permute-start.6) | collective-permute-done | bytes 524320 | tf_op jit(solution)/shard_map/ppermute | solution.py:369
  34.0 0.5 collective-permute-start.7
  34.5 5.9 %collective-permute-done.1.refs_2_ = bf16[2,512,256]{2,1,0:T(8,128)(2,1)S(1)} collective-permute-done((bf16[2,512,256]{2,1,0:T(8,128)(2,1)S(1)}, bf16[2,512,256]{2,1,0:T(8,128)(2,1)S(1)}, u32[]{:S(2)}, u32[]{:S(2)}) %collective-permute-start.1) | collective-permute-done | bytes 524320 | tf_op jit(solution)/shard_map/ppermute | solution.py:352
  40.4 0.8 %collective-permute-done.9.refs_0_ = bf16[256,1024]{1,0:T(8,128)(2,1)S(1)} collective-permute-done((bf16[256,1024]{1,0:T(8,128)(2,1)S(1)}, bf16[256,1024]{1,0:T(8,128)(2,1)S(1)}, u32[]{:S(2)}, u32[]{:S(2)}) %collective-permute-start.9) | collective-permute-done | bytes 524320 | tf_op jit(solution)/shard_map/ppermute | solution.py:369
  41.3 2.0 %project.2 = (bf16[2,256,256]{2,1,0:T(8,128)(2,1)S(1)}, bf16[2,256,256]{2,1,0:T(8,128)(2,1)S(1)}, f32[2,256,256]{2,1,0:T(8,128)S(1)}) custom-call(bf16[2,512,256]{2,1,0:T(8,128)(2,1)S(1)} %get-tuple-element.17.refs_0_, bf16[2,512,256]{2,1,0:T(8,128)(2,1)S(1)} %collective-permute-done.refs_2_.refs_1_, ...), custom_call_target="tpu_custom_call" | custom-call | tf_op jit(solution)/shard_map/project/pallas_call | solution.py:183
  43.3 2.5 %collective-permute-start.10 = (bf16[2,256,256]{2,1,0:T(8,128)(2,1)S(1)}, bf16[2,256,256]{2,1,0:T(8,128)(2,1)S(1)}, u32[]{:S(2)}, u32[]{:S(2)}) collective-permute-start(bf16[2,256,256]{2,1,0:T(8,128)(2,1)S(1)} %get-tuple-element.24), channel_id=1, source_target_pairs={{0,18},{2,16},{16,2},{18,0},{1,19},{3,17},{17,3},{19,1},{4,22},{6,... | collective-permute-start | bytes 786440 | tf_op jit(solution)/shard_map/ppermute | solution.py:380
  45.8 0.5 collective-permute-start.11
  46.3 0.9 %project.3 = bf16[2,256,256]{2,1,0:T(8,128)(2,1)S(1)} custom-call(bf16[2,512,256]{2,1,0:T(8,128)(2,1)S(1)} %get-tuple-element.17.refs_0_, bf16[2,512,256]{2,1,0:T(8,128)(2,1)S(1)} %collective-permute-done.refs_2_.refs_1_, bf16[2,512,256]{2,1,0:T(8,128)(2,1)S(1)} %collective-permute-done.1.refs_2_, bf16[2,512,256]{2,1,0:T(8,128)(2,1)S(1)} %collective-permute-done.2.refs_3_, ...), custom_call_target="tpu_custom_call" | custom-call | tf_op jit(solution)/shard_map/project/pallas_call | solution.py:183
  47.2 0.6 collective-permute-start.13
  48.4 5.0 %collective-permute-done.10.refs_0_ = bf16[2,256,256]{2,1,0:T(8,128)(2,1)S(1)} collective-permute-done((bf16[2,256,256]{2,1,0:T(8,128)(2,1)S(1)}, bf16[2,256,256]{2,1,0:T(8,128)(2,1)S(1)}, u32[]{:S(2)}, u32[]{:S(2)}) %collective-permute-start.10) | collective-permute-done | bytes 262176 | tf_op jit(solution)/shard_map/ppermute | solution.py:380
  53.4 5.2 %collective-permute-done.11.refs_1_ = bf16[2,256,256]{2,1,0:T(8,128)(2,1)S(1)} collective-permute-done((bf16[2,256,256]{2,1,0:T(8,128)(2,1)S(1)}, bf16[2,256,256]{2,1,0:T(8,128)(2,1)S(1)}, u32[]{:S(2)}, u32[]{:S(2)}) %collective-permute-start.11) | collective-permute-done | bytes 262176 | tf_op jit(solution)/shard_map/ppermute | solution.py:380
  58.5 0.1 collective-permute-done.13.refs_3_
  58.6 5.6 %attend_own.1 = bf16[256,2048]{1,0:T(8,128)(2,1)} custom-call(s32[1]{0:T(128)} %bitcast.1.live_ref, bf16[256,2048]{1,0:T(8,128)(2,1)S(1)} %bitcast.9, bf16[2,256,256]{2,1,0:T(8,128)(2,1)S(1)} %collective-permute-done.10.refs_0_, bf16[2,256,256]{2,1,0:T(8,128)(2,1)S(1)} %collective-permute-done.11.refs_1_, f32[2,256,256]{2,1,0:T(8,128)S(1)} %get-tuple-element.26.refs_2_, ...), custom_call_target="tpu_custom_call" | custom-call | tf_op jit(solution)/shard_map/attend_own/pallas_call | solution.py:297
  (20 shorter events, 0.0 us)
Async XLA Ops:
  1.2 21.4 %copy-start = (bf16[1,2,128,2048]{3,2,1,0:T(8,128)(2,1)S(1)}, bf16[1,2,128,2048]{3,2,1,0:T(8,128)(2,1)}, u32[]{:S(2)}) copy-start(bf16[1,2,128,2048]{3,2,1,0:T(8,128)(2,1)} %param.9) | copy-start | bytes 3145732
  1.2 16.5 %collective-permute-start = (bf16[2,512,256]{2,1,0:T(8,128)(2,1)S(1)}, bf16[2,512,256]{2,1,0:T(8,128)(2,1)S(1)}, u32[]{:S(2)}, u32[]{:S(2)}) collective-permute-start(bf16[2,512,256]{2,1,0:T(8,128)(2,1)S(1)} %get-tuple-element.17.refs_0_), channel_id=1, source_target_pairs={{0,8},{8,12},{12,4},{4,0},{1,9},{9,13},{13,5},{5,1},{2,10},{10,14}... | collective-permute-start | bytes 1572872 | tf_op jit(solution)/shard_map/ppermute | solution.py:352
  5.3 15.8 %collective-permute-start.4 = (bf16[2,512,256]{2,1,0:T(8,128)(2,1)S(1)}, bf16[2,512,256]{2,1,0:T(8,128)(2,1)S(1)}, u32[]{:S(2)}, u32[]{:S(2)}) collective-permute-start(bf16[2,512,256]{2,1,0:T(8,128)(2,1)S(1)} %get-tuple-element.19.refs_0_), channel_id=1, source_target_pairs={{0,2},{2,0},{1,3},{3,1},{4,6},{6,4},{5,7},{7,5},{8,10},{10,8},{9,1... | collective-permute-start | bytes 1572872 | tf_op jit(solution)/shard_map/ppermute | solution.py:347
  8.4 24.0 %collective-permute-start.3 = (bf16[256,1024]{1,0:T(8,128)(2,1)S(1)}, bf16[256,1024]{1,0:T(8,128)(2,1)S(1)}, u32[]{:S(2)}, u32[]{:S(2)}) collective-permute-start(bf16[256,1024]{1,0:T(8,128)(2,1)S(1)} %get-tuple-element.18), channel_id=1, source_target_pairs={{0,18},{2,16},{16,2},{18,0},{1,19},{3,17},{17,3},{19,1},{4,22},{6,... | collective-permute-start | bytes 1572872 | tf_op jit(solution)/shard_map/ppermute | solution.py:369
  10.0 24.1 %collective-permute-start.6 = (bf16[256,1024]{1,0:T(8,128)(2,1)S(1)}, bf16[256,1024]{1,0:T(8,128)(2,1)S(1)}, u32[]{:S(2)}, u32[]{:S(2)}) collective-permute-start(bf16[256,1024]{1,0:T(8,128)(2,1)S(1)} %get-tuple-element.21), channel_id=1, source_target_pairs={{0,16},{2,18},{16,0},{18,2},{1,17},{3,19},{17,1},{19,3},{4,20},{6,... | collective-permute-start | bytes 1572872 | tf_op jit(solution)/shard_map/ppermute | solution.py:369
  10.5 23.6 %collective-permute-start.2 = (bf16[2,512,256]{2,1,0:T(8,128)(2,1)S(1)}, bf16[2,512,256]{2,1,0:T(8,128)(2,1)S(1)}, u32[]{:S(2)}, u32[]{:S(2)}) collective-permute-start(bf16[2,512,256]{2,1,0:T(8,128)(2,1)S(1)} %get-tuple-element.17.refs_0_), channel_id=1, source_target_pairs={{8,0},{12,8},{4,12},{0,4},{9,1},{13,9},{5,13},{1,5},{10,2},{14,10}... | collective-permute-start | bytes 1572872 | tf_op jit(solution)/shard_map/ppermute | solution.py:357
  17.7 22.7 %collective-permute-start.1 = (bf16[2,512,256]{2,1,0:T(8,128)(2,1)S(1)}, bf16[2,512,256]{2,1,0:T(8,128)(2,1)S(1)}, u32[]{:S(2)}, u32[]{:S(2)}) collective-permute-start(bf16[2,512,256]{2,1,0:T(8,128)(2,1)S(1)} %collective-permute-done.refs_2_.refs_1_), channel_id=1, source_target_pairs={{0,8},{8,12},{12,4},{4,0},{1,9},{9,13},{13,5},{5,1},{2,10},{10,14}... | collective-permute-start | bytes 1572872 | tf_op jit(solution)/shard_map/ppermute | solution.py:352
  21.1 20.1 %collective-permute-start.9 = (bf16[256,1024]{1,0:T(8,128)(2,1)S(1)}, bf16[256,1024]{1,0:T(8,128)(2,1)S(1)}, u32[]{:S(2)}, u32[]{:S(2)}) collective-permute-start(bf16[256,1024]{1,0:T(8,128)(2,1)S(1)} %after.6), channel_id=1, source_target_pairs={{0,2},{2,0},{16,18},{18,16},{1,3},{3,1},{17,19},{19,17},{4,6},{6,4... | collective-permute-start | bytes 1572872 | tf_op jit(solution)/shard_map/ppermute | solution.py:369
  29.5 11.7 %copy-start.1 = (f32[256,2048]{1,0:T(8,128)}, f32[256,2048]{1,0:T(8,128)S(1)}, u32[]{:S(2)}) copy-start(f32[256,2048]{1,0:T(8,128)S(1)} %get-tuple-element.27.refs_5_) | copy-start | bytes 6291460
  29.5 11.7 %copy-start.2 = (f32[256,2048]{1,0:T(8,128)}, f32[256,2048]{1,0:T(8,128)S(1)}, u32[]{:S(2)}) copy-start(f32[256,2048]{1,0:T(8,128)S(1)} %get-tuple-element.28.refs_6_) | copy-start | bytes 6291460
  32.4 8.8 %collective-permute-start.8 = (bf16[256,1024]{1,0:T(8,128)(2,1)S(1)}, bf16[256,1024]{1,0:T(8,128)(2,1)S(1)}, u32[]{:S(2)}, u32[]{:S(2)}) collective-permute-start(bf16[256,1024]{1,0:T(8,128)(2,1)S(1)} %get-tuple-element.22.refs_8_), channel_id=1, source_target_pairs={{0,1},{1,0},{2,3},{3,2},{4,5},{5,4},{6,7},{7,6},{8,9},{9,8},{10,11... | collective-permute-start | bytes 1572872 | tf_op jit(solution)/shard_map/ppermute | solution.py:371
  34.0 7.2 %collective-permute-start.5 = (bf16[256,1024]{1,0:T(8,128)(2,1)S(1)}, bf16[256,1024]{1,0:T(8,128)(2,1)S(1)}, u32[]{:S(2)}, u32[]{:S(2)}) collective-permute-start(bf16[256,1024]{1,0:T(8,128)(2,1)S(1)} %after.4.refs_4_), channel_id=1, source_target_pairs={{0,1},{1,0},{2,3},{3,2},{4,5},{5,4},{6,7},{7,6},{8,9},{9,8},{10,11... | collective-permute-start | bytes 1572872 | tf_op jit(solution)/shard_map/ppermute | solution.py:371
  34.0 7.2 %collective-permute-start.7 = (bf16[256,1024]{1,0:T(8,128)(2,1)S(1)}, bf16[256,1024]{1,0:T(8,128)(2,1)S(1)}, u32[]{:S(2)}, u32[]{:S(2)}) collective-permute-start(bf16[256,1024]{1,0:T(8,128)(2,1)S(1)} %after.5.refs_6_), channel_id=1, source_target_pairs={{0,1},{1,0},{2,3},{3,2},{4,5},{5,4},{6,7},{7,6},{8,9},{9,8},{10,11... | collective-permute-start | bytes 1572872 | tf_op jit(solution)/shard_map/ppermute | solution.py:371
  41.2 5.0 %collective-permute-start.12 = (bf16[256,1024]{1,0:T(8,128)(2,1)S(1)}, bf16[256,1024]{1,0:T(8,128)(2,1)S(1)}, u32[]{:S(2)}, u32[]{:S(2)}) collective-permute-start(bf16[256,1024]{1,0:T(8,128)(2,1)S(1)} %after.7.refs_10_.refs_4_), channel_id=1, source_target_pairs={{0,1},{1,0},{2,3},{3,2},{4,5},{5,4},{6,7},{7,6},{8,9},{9,8},{10,11... | collective-permute-start | bytes 1572872 | tf_op jit(solution)/shard_map/ppermute | solution.py:371
  43.3 10.1 %collective-permute-start.10 = (bf16[2,256,256]{2,1,0:T(8,128)(2,1)S(1)}, bf16[2,256,256]{2,1,0:T(8,128)(2,1)S(1)}, u32[]{:S(2)}, u32[]{:S(2)}) collective-permute-start(bf16[2,256,256]{2,1,0:T(8,128)(2,1)S(1)} %get-tuple-element.24), channel_id=1, source_target_pairs={{0,18},{2,16},{16,2},{18,0},{1,19},{3,17},{17,3},{19,1},{4,22},{6,... | collective-permute-start | bytes 786440 | tf_op jit(solution)/shard_map/ppermute | solution.py:380
  45.8 12.8 %collective-permute-start.11 = (bf16[2,256,256]{2,1,0:T(8,128)(2,1)S(1)}, bf16[2,256,256]{2,1,0:T(8,128)(2,1)S(1)}, u32[]{:S(2)}, u32[]{:S(2)}) collective-permute-start(bf16[2,256,256]{2,1,0:T(8,128)(2,1)S(1)} %get-tuple-element.25), channel_id=1, source_target_pairs={{0,16},{2,18},{16,0},{18,2},{1,17},{3,19},{17,1},{19,3},{4,20},{6,... | collective-permute-start | bytes 786440 | tf_op jit(solution)/shard_map/ppermute | solution.py:380
  47.2 11.5 %collective-permute-start.13 = (bf16[2,256,256]{2,1,0:T(8,128)(2,1)S(1)}, bf16[2,256,256]{2,1,0:T(8,128)(2,1)S(1)}, u32[]{:S(2)}, u32[]{:S(2)}) collective-permute-start(bf16[2,256,256]{2,1,0:T(8,128)(2,1)S(1)} %project.3), channel_id=1, source_target_pairs={{0,2},{2,0},{16,18},{18,16},{1,3},{3,1},{17,19},{19,17},{4,6},{6,4... | collective-permute-start | bytes 786440 | tf_op jit(solution)/shard_map/ppermute | solution.py:380

commit v12 on v11

--- a/solution.py
+++ b/solution.py
@@ -370,11 +370,12 @@
         near[place] = after(moved, mark, *waits)
     far = {place: lax.ppermute(near[place], "tp", cores) for place in sets}
 
-    narrow, wide = jnp.bfloat16, jnp.float32
-    parts = []
-    for chosen, waits in (([*across, *twins, sets[0]], [near[p] for p in along]), (along, [])):
-        types = [narrow if any(p) else wide for p in chosen]
-        sums = project(n_fsdp, pieces, [(near[p], far[p]) for p in chosen], types, waits)
+    parts, waits = [], [*(near[p] for p in along), far[sets[0]]]
+    for chosen in (across, twins, along, sets[:1]):
+        kind = jnp.bfloat16 if any(chosen[0]) else jnp.float32
+        pairs = [(near[p], far[p]) for p in chosen]
+        sums = project(n_fsdp, pieces, pairs, [kind] * len(chosen), waits)
+        waits = [sums[0]]
         for p, x in zip(chosen, sums):
             back = shift(n_groups - p[0], n_resp - p[1])
             parts.append(lax.ppermute(x, plane, back) if any(p) else x)

time: 64.5 us -> 64.6 us (level)
  waiting for transfers between devices: 28.6 us -> 23.1 us
  local copies, waits for them, and re-layouts: 0.01 us -> 3.38 us
  Pallas kernels: 18.2 us -> 20.3 us
    ppermute x3, waiting for transfers between devices: 10.2 us -> 6 us  [on_device(): parts.append(lax.ppermute(x, plane, back) if any(p) else x)]
    unnamed x6 -> x14, local copies, waits for them, and re-layouts: 0.01 us -> 3.38 us
    pallas_call x2 -> x4, Pallas kernels: 2.84 us -> 4.9 us  [project(): pl.pallas_call(body, grid=(1,), in_specs=[whole((kinds, half, columns))]...]
    ppermute x3, waiting for transfers between devices: 5.35 us -> 4.08 us  [on_device(): moved = lax.ppermute(near[place], plane, shift(*place))]
  transfers between devices with their start and end apart: 14 -> 14, of which waited for: 8 -> 7; matrix products, arithmetic and copies ran while one was open for 0% -> 0% of each run, Pallas kernels for 18% -> 21%
where the time goes in v12:
time: 64.6 us; the launch traced here: 64.2 us
  waiting for transfers between devices  23.1 us (36%)
  Pallas kernels  20.3 us (31%)
  starting transfers between devices  16.6 us (26%)
  local copies, waits for them, and re-layouts  3.38 us (5%)
  between operations  0.77 us (1%)
    ppermute x2, waiting for transfers between devices, on_device(): held = lax.ppermute(held, 'fsdp', rightward)  13 us
    ppermute x2, starting transfers between devices, on_device(): held = lax.ppermute(held, 'fsdp', rightward)  7.47 us
    pallas_call x1, Pallas kernels, attend_cache(): pl.pallas_call(body, grid=(heads, slots), in_specs=[spec_wide] + [spec_c]...  6.9 us
    ppermute x3, waiting for transfers between devices, on_device(): parts.append(lax.ppermute(x, plane, back) if any(p) else x)  6 us
    pallas_call x1, Pallas kernels, attend_own(): pl.pallas_call(body, grid=(slots, heads), in_specs=[pl.BlockSpec(memory_s...  5.73 us
    pallas_call x4, Pallas kernels, project(): pl.pallas_call(body, grid=(1,), in_specs=[whole((kinds, half, columns))]...  4.9 us
    ppermute x3, waiting for transfers between devices, on_device(): moved = lax.ppermute(near[place], plane, shift(*place))  4.08 us
    ppermute x3, starting transfers between devices, on_device(): moved = lax.ppermute(near[place], plane, shift(*place))  3.55 us
  transfers between devices with their start and end apart: 14, of which 7 were waited for; matrix products, arithmetic and copies ran while one was open for 0% of the time, Pallas kernels for 21%

profile of v12, /device:TPU:0, one launch (start us, length us, event | category | flops | bytes accessed | tf_op | source)
XLA Modules:
  0.0 64.2 jit_solution(13915864814466092591)
XLA Ops:
  0.0 1.2 %pack_rows.1 = (bf16[2,512,256]{2,1,0:T(8,128)(2,1)S(1)}, bf16[2,512,256]{2,1,0:T(8,128)(2,1)S(1)}) custom-call(bf16[1024,256]{1,0:T(8,128)(2,1)} %kw_ref.1, bf16[1024,256]{1,0:T(8,128)(2,1)} %vw_ref.1, bf16[512,256]{1,0:T(8,128)(2,1)} %bitcast.11, bf16[512,256]{1,0:T(8,128)(2,1)} %bitcast.12), custom_call_target="tpu_custom_call" | custom-call | tf_op jit(solution)/shard_map/pack_rows/pallas_call | solution.py:74
  1.2 4.1 %collective-permute-start = (bf16[2,512,256]{2,1,0:T(8,128)(2,1)S(1)}, bf16[2,512,256]{2,1,0:T(8,128)(2,1)S(1)}, u32[]{:S(2)}, u32[]{:S(2)}) collective-permute-start(bf16[2,512,256]{2,1,0:T(8,128)(2,1)S(1)} %get-tuple-element.14.refs_0_), channel_id=1, source_target_pairs={{0,8},{8,12},{12,4},{4,0},{1,9},{9,13},{13,5},{5,1},{2,10},{10,14}... | collective-permute-start | bytes 1572872 | tf_op jit(solution)/shard_map/ppermute | solution.py:352
  5.3 1.5 %collective-permute-start.4 = (bf16[2,512,256]{2,1,0:T(8,128)(2,1)S(1)}, bf16[2,512,256]{2,1,0:T(8,128)(2,1)S(1)}, u32[]{:S(2)}, u32[]{:S(2)}) collective-permute-start(bf16[2,512,256]{2,1,0:T(8,128)(2,1)S(1)} %get-tuple-element.16.refs_0_), channel_id=1, source_target_pairs={{0,2},{2,0},{1,3},{3,1},{4,6},{6,4},{5,7},{7,5},{8,10},{10,8},{9,1... | collective-permute-start | bytes 1572872 | tf_op jit(solution)/shard_map/ppermute | solution.py:347
  6.8 1.6 %pack_features.1 = (bf16[256,1024]{1,0:T(8,128)(2,1)S(1)}, bf16[256,1024]{1,0:T(8,128)(2,1)S(1)}, bf16[256,1024]{1,0:T(8,128)(2,1)S(1)}, bf16[256,1024]{1,0:T(8,128)(2,1)S(1)}) custom-call(bf16[256,4096]{1,0:T(8,128)(2,1)} %bitcast.10), custom_call_target="tpu_custom_call" | custom-call | tf_op jit(solution)/shard_map/pack_features/pallas_call | solution.py:132
  8.4 1.6 %collective-permute-start.3 = (bf16[256,1024]{1,0:T(8,128)(2,1)S(1)}, bf16[256,1024]{1,0:T(8,128)(2,1)S(1)}, u32[]{:S(2)}, u32[]{:S(2)}) collective-permute-start(bf16[256,1024]{1,0:T(8,128)(2,1)S(1)} %get-tuple-element.15), channel_id=1, source_target_pairs={{0,18},{2,16},{16,2},{18,0},{1,19},{3,17},{17,3},{19,1},{4,22},{6,... | collective-permute-start | bytes 1572872 | tf_op jit(solution)/shard_map/ppermute | solution.py:369
  10.5 7.2 %collective-permute-done.refs_2_.refs_1_ = bf16[2,512,256]{2,1,0:T(8,128)(2,1)S(1)} collective-permute-done((bf16[2,512,256]{2,1,0:T(8,128)(2,1)S(1)}, bf16[2,512,256]{2,1,0:T(8,128)(2,1)S(1)}, u32[]{:S(2)}, u32[]{:S(2)}) %collective-permute-start) | collective-permute-done | bytes 524320 | tf_op jit(solution)/shard_map/ppermute | solution.py:352
  17.7 3.4 %collective-permute-start.1 = (bf16[2,512,256]{2,1,0:T(8,128)(2,1)S(1)}, bf16[2,512,256]{2,1,0:T(8,128)(2,1)S(1)}, u32[]{:S(2)}, u32[]{:S(2)}) collective-permute-start(bf16[2,512,256]{2,1,0:T(8,128)(2,1)S(1)} %collective-permute-done.refs_2_.refs_1_), channel_id=1, source_target_pairs={{0,8},{8,12},{12,4},{4,0},{1,9},{9,13},{13,5},{5,1},{2,10},{10,14}... | collective-permute-start | bytes 1572872 | tf_op jit(solution)/shard_map/ppermute | solution.py:352
  21.1 1.5 %collective-permute-start.6 = (bf16[256,1024]{1,0:T(8,128)(2,1)S(1)}, bf16[256,1024]{1,0:T(8,128)(2,1)S(1)}, u32[]{:S(2)}, u32[]{:S(2)}) collective-permute-start(bf16[256,1024]{1,0:T(8,128)(2,1)S(1)} %after.5), channel_id=1, source_target_pairs={{0,2},{2,0},{16,18},{18,16},{1,3},{3,1},{17,19},{19,17},{4,6},{6,4... | collective-permute-start | bytes 1572872 | tf_op jit(solution)/shard_map/ppermute | solution.py:369
  22.6 6.9 %attend_cache.1 = (f32[256,2048]{1,0:T(8,128)S(1)}, f32[256,2048]{1,0:T(8,128)S(1)}, f32[8,128]{1,0:T(8,128)S(1)}) custom-call(bf16[256,2048]{1,0:T(8,128)(2,1)S(1)} %bitcast.8, bf16[2,512,256]{2,1,0:T(8,128)(2,1)S(1)} %get-tuple-element.16.refs_0_, bf16[2,512,256]{2,1,0:T(8,128)(2,1)S(1)} %collective-permute-done.4.refs_1_, ...), custom_call_target="tpu_custom_call" | custom-call | tf_op jit(solution)/shard_map/attend_cache/pallas_call | solution.py:247
  29.5 1.3 %copy-done.4 = f32[256,2048]{1,0:T(8,128)} copy-done((f32[256,2048]{1,0:T(8,128)}, f32[256,2048]{1,0:T(8,128)S(1)}, u32[]{:S(2)}) %copy-start.4) | copy-done | bytes 2097176
  30.8 1.6 %collective-permute-done.3.refs_0_ = bf16[256,1024]{1,0:T(8,128)(2,1)S(1)} collective-permute-done((bf16[256,1024]{1,0:T(8,128)(2,1)S(1)}, bf16[256,1024]{1,0:T(8,128)(2,1)S(1)}, u32[]{:S(2)}, u32[]{:S(2)}) %collective-permute-start.3) | collective-permute-done | bytes 524320 | tf_op jit(solution)/shard_map/ppermute | solution.py:369
  32.4 1.6 %collective-permute-done.9.refs_0_ = bf16[256,1024]{1,0:T(8,128)(2,1)S(1)} collective-permute-done((bf16[256,1024]{1,0:T(8,128)(2,1)S(1)}, bf16[256,1024]{1,0:T(8,128)(2,1)S(1)}, u32[]{:S(2)}, u32[]{:S(2)}) %collective-permute-start.9) | collective-permute-done | bytes 524320 | tf_op jit(solution)/shard_map/ppermute | solution.py:369
  34.6 5.8 %collective-permute-done.1.refs_2_ = bf16[2,512,256]{2,1,0:T(8,128)(2,1)S(1)} collective-permute-done((bf16[2,512,256]{2,1,0:T(8,128)(2,1)S(1)}, bf16[2,512,256]{2,1,0:T(8,128)(2,1)S(1)}, u32[]{:S(2)}, u32[]{:S(2)}) %collective-permute-start.1) | collective-permute-done | bytes 524320 | tf_op jit(solution)/shard_map/ppermute | solution.py:352
  40.4 0.8 %collective-permute-done.6.refs_0_ = bf16[256,1024]{1,0:T(8,128)(2,1)S(1)} collective-permute-done((bf16[256,1024]{1,0:T(8,128)(2,1)S(1)}, bf16[256,1024]{1,0:T(8,128)(2,1)S(1)}, u32[]{:S(2)}, u32[]{:S(2)}) %collective-permute-start.6) | collective-permute-done | bytes 524320 | tf_op jit(solution)/shard_map/ppermute | solution.py:369
  41.3 1.6 %project.4.refs_6_ = bf16[2,256,256]{2,1,0:T(8,128)(2,1)} custom-call(bf16[2,512,256]{2,1,0:T(8,128)(2,1)S(1)} %get-tuple-element.14.refs_0_, bf16[2,512,256]{2,1,0:T(8,128)(2,1)S(1)} %collective-permute-done.refs_2_.refs_1_, bf16[2,512,256]{2,1,0:T(8,128)(2,1)S(1)} %collective-permute-done.1.refs_2_, ...), custom_call_target="tpu_custom_call" | custom-call | tf_op jit(solution)/shard_map/project/pallas_call | solution.py:183
  42.8 2.4 %collective-permute-start.8 = (bf16[2,256,256]{2,1,0:T(8,128)(2,1)}, bf16[2,256,256]{2,1,0:T(8,128)(2,1)}, u32[]{:S(2)}, u32[]{:S(2)}) collective-permute-start(bf16[2,256,256]{2,1,0:T(8,128)(2,1)} %project.4.refs_6_), channel_id=1, source_target_pairs={{0,18},{2,16},{16,2},{18,0},{1,19},{3,17},{17,3},{19,1},{4,22},{6,... | collective-permute-start | bytes 786440 | tf_op jit(solution)/shard_map/ppermute | solution.py:381
  45.3 0.9 %project.5.refs_6_ = bf16[2,256,256]{2,1,0:T(8,128)(2,1)S(1)} custom-call(bf16[2,512,256]{2,1,0:T(8,128)(2,1)S(1)} %get-tuple-element.14.refs_0_, bf16[2,512,256]{2,1,0:T(8,128)(2,1)S(1)} %collective-permute-done.refs_2_.refs_1_, bf16[2,512,256]{2,1,0:T(8,128)(2,1)S(1)} %collective-permute-done.1.refs_2_, ...), custom_call_target="tpu_custom_call" | custom-call | tf_op jit(solution)/shard_map/project/pallas_call | solution.py:183
  46.2 0.6 collective-permute-start.11
  46.8 1.6 %project.6.refs_6_ = bf16[2,256,256]{2,1,0:T(8,128)(2,1)} custom-call(bf16[2,512,256]{2,1,0:T(8,128)(2,1)S(1)} %get-tuple-element.14.refs_0_, bf16[2,512,256]{2,1,0:T(8,128)(2,1)S(1)} %collective-permute-done.refs_2_.refs_1_, bf16[2,512,256]{2,1,0:T(8,128)(2,1)S(1)} %collective-permute-done.1.refs_2_, ...), custom_call_target="tpu_custom_call" | custom-call | tf_op jit(solution)/shard_map/project/pallas_call | solution.py:183
  49.5 1.0 %copy-done.2 = bf16[256,1024]{1,0:T(8,128)(2,1)S(1)} copy-done((bf16[256,1024]{1,0:T(8,128)(2,1)S(1)}, bf16[256,1024]{1,0:T(8,128)(2,1)}, u32[]{:S(2)}) %copy-start.2) | copy-done | bytes 524312
  50.6 1.0 %copy-done.6 = bf16[256,1024]{1,0:T(8,128)(2,1)S(1)} copy-done((bf16[256,1024]{1,0:T(8,128)(2,1)S(1)}, bf16[256,1024]{1,0:T(8,128)(2,1)}, u32[]{:S(2)}) %copy-start.6) | copy-done | bytes 524312
  51.6 0.9 %project.7.refs_3_ = f32[2,256,256]{2,1,0:T(8,128)S(1)} custom-call(bf16[2,512,256]{2,1,0:T(8,128)(2,1)S(1)} %get-tuple-element.14.refs_0_, bf16[2,512,256]{2,1,0:T(8,128)(2,1)S(1)} %collective-permute-done.refs_2_.refs_1_, bf16[2,512,256]{2,1,0:T(8,128)(2,1)S(1)} %collective-permute-done.1.refs_2_, bf16[2,512,256]{2,1,0:T(8,128)(2,1)S(1)} %collective-permute-done.2.refs_3_, ...), custom_call_target="tpu_custom_call" | custom-call | tf_op jit(solution)/shard_map/project/pallas_call | solution.py:183
  52.5 5.9 %collective-permute-done.11.refs_1_ = bf16[2,256,256]{2,1,0:T(8,128)(2,1)} collective-permute-done((bf16[2,256,256]{2,1,0:T(8,128)(2,1)S(1)}, bf16[2,256,256]{2,1,0:T(8,128)(2,1)}, u32[]{:S(2)}, u32[]{:S(2)}) %collective-permute-start.11) | collective-permute-done | bytes 262176 | tf_op jit(solution)/shard_map/ppermute | solution.py:381
  58.5 5.7 %attend_own.1 = bf16[256,2048]{1,0:T(8,128)(2,1)} custom-call(s32[1]{0:T(128)} %bitcast.1.live_ref, bf16[256,2048]{1,0:T(8,128)(2,1)S(1)} %bitcast.9, bf16[2,256,256]{2,1,0:T(8,128)(2,1)} %collective-permute-done.8.refs_0_, bf16[2,256,256]{2,1,0:T(8,128)(2,1)} %collective-permute-done.11.refs_1_, bf16[2,256,256]{2,1,0:T(8,128)(2,1)} %collective-permute-done.13.refs_2_, ...), custom_call_target="tpu_custom_call" | custom-call | tf_op jit(solution)/shard_map/attend_own/pallas_call | solution.py:297
  (30 shorter events, 1.7 us)
Async XLA Ops:
  1.2 21.4 %copy-start = (bf16[1,2,128,2048]{3,2,1,0:T(8,128)(2,1)S(1)}, bf16[1,2,128,2048]{3,2,1,0:T(8,128)(2,1)}, u32[]{:S(2)}) copy-start(bf16[1,2,128,2048]{3,2,1,0:T(8,128)(2,1)} %param.9) | copy-start | bytes 3145732
  1.2 16.5 %collective-permute-start = (bf16[2,512,256]{2,1,0:T(8,128)(2,1)S(1)}, bf16[2,512,256]{2,1,0:T(8,128)(2,1)S(1)}, u32[]{:S(2)}, u32[]{:S(2)}) collective-permute-start(bf16[2,512,256]{2,1,0:T(8,128)(2,1)S(1)} %get-tuple-element.14.refs_0_), channel_id=1, source_target_pairs={{0,8},{8,12},{12,4},{4,0},{1,9},{9,13},{13,5},{5,1},{2,10},{10,14}... | collective-permute-start | bytes 1572872 | tf_op jit(solution)/shard_map/ppermute | solution.py:352
  5.3 15.8 %collective-permute-start.4 = (bf16[2,512,256]{2,1,0:T(8,128)(2,1)S(1)}, bf16[2,512,256]{2,1,0:T(8,128)(2,1)S(1)}, u32[]{:S(2)}, u32[]{:S(2)}) collective-permute-start(bf16[2,512,256]{2,1,0:T(8,128)(2,1)S(1)} %get-tuple-element.16.refs_0_), channel_id=1, source_target_pairs={{0,2},{2,0},{1,3},{3,1},{4,6},{6,4},{5,7},{7,5},{8,10},{10,8},{9,1... | collective-permute-start | bytes 1572872 | tf_op jit(solution)/shard_map/ppermute | solution.py:347
  8.4 24.0 %copy-start.5 = (bf16[256,1024]{1,0:T(8,128)(2,1)}, bf16[256,1024]{1,0:T(8,128)(2,1)S(1)}, u32[]{:S(2)}) copy-start(bf16[256,1024]{1,0:T(8,128)(2,1)S(1)} %get-tuple-element.19.refs_4_) | copy-start | bytes 1572868
  8.4 24.0 %collective-permute-start.3 = (bf16[256,1024]{1,0:T(8,128)(2,1)S(1)}, bf16[256,1024]{1,0:T(8,128)(2,1)S(1)}, u32[]{:S(2)}, u32[]{:S(2)}) collective-permute-start(bf16[256,1024]{1,0:T(8,128)(2,1)S(1)} %get-tuple-element.15), channel_id=1, source_target_pairs={{0,18},{2,16},{16,2},{18,0},{1,19},{3,17},{17,3},{19,1},{4,22},{6,... | collective-permute-start | bytes 1572872 | tf_op jit(solution)/shard_map/ppermute | solution.py:369
  10.0 24.1 %collective-permute-start.2 = (bf16[2,512,256]{2,1,0:T(8,128)(2,1)S(1)}, bf16[2,512,256]{2,1,0:T(8,128)(2,1)S(1)}, u32[]{:S(2)}, u32[]{:S(2)}) collective-permute-start(bf16[2,512,256]{2,1,0:T(8,128)(2,1)S(1)} %get-tuple-element.14.refs_0_), channel_id=1, source_target_pairs={{8,0},{12,8},{4,12},{0,4},{9,1},{13,9},{5,13},{1,5},{10,2},{14,10}... | collective-permute-start | bytes 1572872 | tf_op jit(solution)/shard_map/ppermute | solution.py:357
  10.0 24.1 %collective-permute-start.9 = (bf16[256,1024]{1,0:T(8,128)(2,1)S(1)}, bf16[256,1024]{1,0:T(8,128)(2,1)S(1)}, u32[]{:S(2)}, u32[]{:S(2)}) collective-permute-start(bf16[256,1024]{1,0:T(8,128)(2,1)S(1)} %get-tuple-element.20), channel_id=1, source_target_pairs={{0,16},{2,18},{16,0},{18,2},{1,17},{3,19},{17,1},{19,3},{4,20},{6,... | collective-permute-start | bytes 1572872 | tf_op jit(solution)/shard_map/ppermute | solution.py:369
  17.7 22.7 %collective-permute-start.1 = (bf16[2,512,256]{2,1,0:T(8,128)(2,1)S(1)}, bf16[2,512,256]{2,1,0:T(8,128)(2,1)S(1)}, u32[]{:S(2)}, u32[]{:S(2)}) collective-permute-start(bf16[2,512,256]{2,1,0:T(8,128)(2,1)S(1)} %collective-permute-done.refs_2_.refs_1_), channel_id=1, source_target_pairs={{0,8},{8,12},{12,4},{4,0},{1,9},{9,13},{13,5},{5,1},{2,10},{10,14}... | collective-permute-start | bytes 1572872 | tf_op jit(solution)/shard_map/ppermute | solution.py:352
  21.1 20.1 %collective-permute-start.6 = (bf16[256,1024]{1,0:T(8,128)(2,1)S(1)}, bf16[256,1024]{1,0:T(8,128)(2,1)S(1)}, u32[]{:S(2)}, u32[]{:S(2)}) collective-permute-start(bf16[256,1024]{1,0:T(8,128)(2,1)S(1)} %after.5), channel_id=1, source_target_pairs={{0,2},{2,0},{16,18},{18,16},{1,3},{3,1},{17,19},{19,17},{4,6},{6,4... | collective-permute-start | bytes 1572872 | tf_op jit(solution)/shard_map/ppermute | solution.py:369
  29.5 1.3 %copy-start.4 = (f32[256,2048]{1,0:T(8,128)}, f32[256,2048]{1,0:T(8,128)S(1)}, u32[]{:S(2)}) copy-start(f32[256,2048]{1,0:T(8,128)S(1)} %get-tuple-element.22.refs_6_) | copy-start | bytes 6291460
  30.8 10.4 %copy-start.3 = (f32[256,2048]{1,0:T(8,128)}, f32[256,2048]{1,0:T(8,128)S(1)}, u32[]{:S(2)}) copy-start(f32[256,2048]{1,0:T(8,128)S(1)} %get-tuple-element.21.refs_5_) | copy-start | bytes 6291460
  32.4 8.8 %collective-permute-start.7 = (bf16[256,1024]{1,0:T(8,128)(2,1)S(1)}, bf16[256,1024]{1,0:T(8,128)(2,1)S(1)}, u32[]{:S(2)}, u32[]{:S(2)}) collective-permute-start(bf16[256,1024]{1,0:T(8,128)(2,1)S(1)} %get-tuple-element.19.refs_4_), channel_id=1, source_target_pairs={{0,1},{1,0},{2,3},{3,2},{4,5},{5,4},{6,7},{7,6},{8,9},{9,8},{10,11... | collective-permute-start | bytes 1572872 | tf_op jit(solution)/shard_map/ppermute | solution.py:371
  34.0 7.2 %collective-permute-start.5 = (bf16[256,1024]{1,0:T(8,128)(2,1)S(1)}, bf16[256,1024]{1,0:T(8,128)(2,1)S(1)}, u32[]{:S(2)}, u32[]{:S(2)}) collective-permute-start(bf16[256,1024]{1,0:T(8,128)(2,1)S(1)} %after.4.refs_4_), channel_id=1, source_target_pairs={{0,1},{1,0},{2,3},{3,2},{4,5},{5,4},{6,7},{7,6},{8,9},{9,8},{10,11... | collective-permute-start | bytes 1572872 | tf_op jit(solution)/shard_map/ppermute | solution.py:371
  34.1 11.2 %collective-permute-start.10 = (bf16[256,1024]{1,0:T(8,128)(2,1)S(1)}, bf16[256,1024]{1,0:T(8,128)(2,1)S(1)}, u32[]{:S(2)}, u32[]{:S(2)}) collective-permute-start(bf16[256,1024]{1,0:T(8,128)(2,1)S(1)} %after.7.refs_4_), channel_id=1, source_target_pairs={{0,1},{1,0},{2,3},{3,2},{4,5},{5,4},{6,7},{7,6},{8,9},{9,8},{10,11... | collective-permute-start | bytes 1572872 | tf_op jit(solution)/shard_map/ppermute | solution.py:371
  41.2 5.5 %collective-permute-start.12 = (bf16[256,1024]{1,0:T(8,128)(2,1)S(1)}, bf16[256,1024]{1,0:T(8,128)(2,1)S(1)}, u32[]{:S(2)}, u32[]{:S(2)}) collective-permute-start(bf16[256,1024]{1,0:T(8,128)(2,1)S(1)} %after.6.refs_6_.refs_4_), channel_id=1, source_target_pairs={{0,1},{1,0},{2,3},{3,2},{4,5},{5,4},{6,7},{7,6},{8,9},{9,8},{10,11... | collective-permute-start | bytes 1572872 | tf_op jit(solution)/shard_map/ppermute | solution.py:371
  41.2 1.6 %copy-start.1 = (bf16[256,1024]{1,0:T(8,128)(2,1)}, bf16[256,1024]{1,0:T(8,128)(2,1)S(1)}, u32[]{:S(2)}) copy-start(bf16[256,1024]{1,0:T(8,128)(2,1)S(1)} %collective-permute-done.7.refs_7_.refs_5_) | copy-start | bytes 1572868
  42.8 15.5 %collective-permute-start.8 = (bf16[2,256,256]{2,1,0:T(8,128)(2,1)}, bf16[2,256,256]{2,1,0:T(8,128)(2,1)}, u32[]{:S(2)}, u32[]{:S(2)}) collective-permute-start(bf16[2,256,256]{2,1,0:T(8,128)(2,1)} %project.4.refs_6_), channel_id=1, source_target_pairs={{0,18},{2,16},{16,2},{18,0},{1,19},{3,17},{17,3},{19,1},{4,22},{6,... | collective-permute-start | bytes 786440 | tf_op jit(solution)/shard_map/ppermute | solution.py:381
  46.2 12.2 %collective-permute-start.11 = (bf16[2,256,256]{2,1,0:T(8,128)(2,1)S(1)}, bf16[2,256,256]{2,1,0:T(8,128)(2,1)}, u32[]{:S(2)}, u32[]{:S(2)}) collective-permute-start(bf16[2,256,256]{2,1,0:T(8,128)(2,1)S(1)} %project.5.refs_6_), channel_id=1, source_target_pairs={{0,16},{2,18},{16,0},{18,2},{1,17},{3,19},{17,1},{19,3},{4,20},{6,... | collective-permute-start | bytes 786440 | tf_op jit(solution)/shard_map/ppermute | solution.py:381
  48.3 10.2 %collective-permute-start.13 = (bf16[2,256,256]{2,1,0:T(8,128)(2,1)}, bf16[2,256,256]{2,1,0:T(8,128)(2,1)}, u32[]{:S(2)}, u32[]{:S(2)}) collective-permute-start(bf16[2,256,256]{2,1,0:T(8,128)(2,1)} %project.6.refs_6_), channel_id=1, source_target_pairs={{0,2},{2,0},{16,18},{18,16},{1,3},{3,1},{17,19},{19,17},{4,6},{6,4... | collective-permute-start | bytes 786440 | tf_op jit(solution)/shard_map/ppermute | solution.py:381
  49.5 1.0 %copy-start.2 = (bf16[256,1024]{1,0:T(8,128)(2,1)S(1)}, bf16[256,1024]{1,0:T(8,128)(2,1)}, u32[]{:S(2)}) copy-start(bf16[256,1024]{1,0:T(8,128)(2,1)} %copy-done.1) | copy-start | bytes 1572868
  50.6 1.0 %copy-start.6 = (bf16[256,1024]{1,0:T(8,128)(2,1)S(1)}, bf16[256,1024]{1,0:T(8,128)(2,1)}, u32[]{:S(2)}) copy-start(bf16[256,1024]{1,0:T(8,128)(2,1)} %copy-done.5) | copy-start | bytes 1572868

commit v13 on v11

--- a/solution.py
+++ b/solution.py
@@ -276,9 +276,9 @@
         wide = jnp.concatenate([value, jnp.ones((tokens, HD), jnp.bfloat16)], axis=1)
         row = lax.broadcasted_iota(jnp.int32, (tokens, tokens), 0)
         causal = row >= lax.broadcasted_iota(jnp.int32, (tokens, tokens), 1)
-        causal = jnp.concatenate([causal] * group_size, axis=0)
-        scores = dot_nt(take(q_ref, 0, group_size), key) * FACTOR
-        scores = jnp.where(causal, scores, -1e30)
+        hidden_later = jnp.where(causal, 0.0, -1e30)
+        hidden_later = jnp.concatenate([hidden_later] * group_size, axis=0)
+        scores = dot_nt(take(q_ref, 0, group_size), key) * FACTOR + hidden_later
         level = take(level_ref, 0, group_size)
         top = jnp.max(jnp.maximum(level, scores), axis=1, keepdims=True)
         probs = jnp.exp2(scores - top).astype(jnp.bfloat16)

time: 64.5 us -> 64.5 us (level)
  no operation moved by 1% of the time
where the time goes in v13:
time: 64.5 us; the launch traced here: 64.2 us
  waiting for transfers between devices  28.6 us (44%)
  Pallas kernels  18.1 us (28%)
  starting transfers between devices  16.7 us (26%)
  between operations  0.76 us (1%)
    ppermute x2, waiting for transfers between devices, on_device(): held = lax.ppermute(held, 'fsdp', rightward)  13.1 us
    ppermute x3, waiting for transfers between devices, on_device(): parts.append(lax.ppermute(x, plane, back) if any(p) else x)  10.2 us
    ppermute x2, starting transfers between devices, on_device(): held = lax.ppermute(held, 'fsdp', rightward)  7.47 us
    pallas_call x1, Pallas kernels, attend_cache(): pl.pallas_call(body, grid=(heads, slots), in_specs=[spec_wide] + [spec_c]...  6.9 us
    pallas_call x1, Pallas kernels, attend_own(): pl.pallas_call(body, grid=(slots, heads), in_specs=[pl.BlockSpec(memory_s...  5.59 us
    ppermute x3, waiting for transfers between devices, on_device(): moved = lax.ppermute(near[place], plane, shift(*place))  5.35 us
    ppermute x3, starting transfers between devices, on_device(): parts.append(lax.ppermute(x, plane, back) if any(p) else x)  3.62 us
    ppermute x3, starting transfers between devices, on_device(): moved = lax.ppermute(near[place], plane, shift(*place))  3.55 us
  transfers between devices with their start and end apart: 14, of which 8 were waited for; matrix products, arithmetic and copies ran while one was open for 0% of the time, Pallas kernels for 18%

profile of v13, /device:TPU:0, one launch (start us, length us, event | category | flops | bytes accessed | tf_op | source)
XLA Modules:
  0.0 64.2 jit_solution(16552702367621236971)
XLA Ops:
  0.0 1.2 %pack_rows.1 = (bf16[2,512,256]{2,1,0:T(8,128)(2,1)S(1)}, bf16[2,512,256]{2,1,0:T(8,128)(2,1)S(1)}) custom-call(bf16[1024,256]{1,0:T(8,128)(2,1)} %kw_ref.1, bf16[1024,256]{1,0:T(8,128)(2,1)} %vw_ref.1, bf16[512,256]{1,0:T(8,128)(2,1)} %bitcast.11, bf16[512,256]{1,0:T(8,128)(2,1)} %bitcast.12), custom_call_target="tpu_custom_call" | custom-call | tf_op jit(solution)/shard_map/pack_rows/pallas_call | solution.py:74
  1.2 4.1 %collective-permute-start = (bf16[2,512,256]{2,1,0:T(8,128)(2,1)S(1)}, bf16[2,512,256]{2,1,0:T(8,128)(2,1)S(1)}, u32[]{:S(2)}, u32[]{:S(2)}) collective-permute-start(bf16[2,512,256]{2,1,0:T(8,128)(2,1)S(1)} %get-tuple-element.17.refs_0_), channel_id=1, source_target_pairs={{0,8},{8,12},{12,4},{4,0},{1,9},{9,13},{13,5},{5,1},{2,10},{10,14}... | collective-permute-start | bytes 1572872 | tf_op jit(solution)/shard_map/ppermute | solution.py:352
  5.3 1.5 %collective-permute-start.4 = (bf16[2,512,256]{2,1,0:T(8,128)(2,1)S(1)}, bf16[2,512,256]{2,1,0:T(8,128)(2,1)S(1)}, u32[]{:S(2)}, u32[]{:S(2)}) collective-permute-start(bf16[2,512,256]{2,1,0:T(8,128)(2,1)S(1)} %get-tuple-element.19.refs_0_), channel_id=1, source_target_pairs={{0,2},{2,0},{1,3},{3,1},{4,6},{6,4},{5,7},{7,5},{8,10},{10,8},{9,1... | collective-permute-start | bytes 1572872 | tf_op jit(solution)/shard_map/ppermute | solution.py:347
  6.8 1.6 %pack_features.1 = (bf16[256,1024]{1,0:T(8,128)(2,1)S(1)}, bf16[256,1024]{1,0:T(8,128)(2,1)S(1)}, bf16[256,1024]{1,0:T(8,128)(2,1)S(1)}, bf16[256,1024]{1,0:T(8,128)(2,1)S(1)}) custom-call(bf16[256,4096]{1,0:T(8,128)(2,1)} %bitcast.10), custom_call_target="tpu_custom_call" | custom-call | tf_op jit(solution)/shard_map/pack_features/pallas_call | solution.py:132
  8.4 1.6 %collective-permute-start.3 = (bf16[256,1024]{1,0:T(8,128)(2,1)S(1)}, bf16[256,1024]{1,0:T(8,128)(2,1)S(1)}, u32[]{:S(2)}, u32[]{:S(2)}) collective-permute-start(bf16[256,1024]{1,0:T(8,128)(2,1)S(1)} %get-tuple-element.18), channel_id=1, source_target_pairs={{0,18},{2,16},{16,2},{18,0},{1,19},{3,17},{17,3},{19,1},{4,22},{6,... | collective-permute-start | bytes 1572872 | tf_op jit(solution)/shard_map/ppermute | solution.py:369
  10.0 0.5 collective-permute-start.6
  10.5 7.2 %collective-permute-done.refs_2_.refs_1_ = bf16[2,512,256]{2,1,0:T(8,128)(2,1)S(1)} collective-permute-done((bf16[2,512,256]{2,1,0:T(8,128)(2,1)S(1)}, bf16[2,512,256]{2,1,0:T(8,128)(2,1)S(1)}, u32[]{:S(2)}, u32[]{:S(2)}) %collective-permute-start) | collective-permute-done | bytes 524320 | tf_op jit(solution)/shard_map/ppermute | solution.py:352
  17.7 3.4 %collective-permute-start.1 = (bf16[2,512,256]{2,1,0:T(8,128)(2,1)S(1)}, bf16[2,512,256]{2,1,0:T(8,128)(2,1)S(1)}, u32[]{:S(2)}, u32[]{:S(2)}) collective-permute-start(bf16[2,512,256]{2,1,0:T(8,128)(2,1)S(1)} %collective-permute-done.refs_2_.refs_1_), channel_id=1, source_target_pairs={{0,8},{8,12},{12,4},{4,0},{1,9},{9,13},{13,5},{5,1},{2,10},{10,14}... | collective-permute-start | bytes 1572872 | tf_op jit(solution)/shard_map/ppermute | solution.py:352
  21.1 1.5 %collective-permute-start.9 = (bf16[256,1024]{1,0:T(8,128)(2,1)S(1)}, bf16[256,1024]{1,0:T(8,128)(2,1)S(1)}, u32[]{:S(2)}, u32[]{:S(2)}) collective-permute-start(bf16[256,1024]{1,0:T(8,128)(2,1)S(1)} %after.6), channel_id=1, source_target_pairs={{0,2},{2,0},{16,18},{18,16},{1,3},{3,1},{17,19},{19,17},{4,6},{6,4... | collective-permute-start | bytes 1572872 | tf_op jit(solution)/shard_map/ppermute | solution.py:369
  22.6 6.9 %attend_cache.1 = (f32[256,2048]{1,0:T(8,128)S(1)}, f32[256,2048]{1,0:T(8,128)S(1)}, f32[8,128]{1,0:T(8,128)S(1)}) custom-call(bf16[256,2048]{1,0:T(8,128)(2,1)S(1)} %bitcast.8, bf16[2,512,256]{2,1,0:T(8,128)(2,1)S(1)} %get-tuple-element.19.refs_0_, bf16[2,512,256]{2,1,0:T(8,128)(2,1)S(1)} %collective-permute-done.4.refs_1_, ...), custom_call_target="tpu_custom_call" | custom-call | tf_op jit(solution)/shard_map/attend_cache/pallas_call | solution.py:247
  29.5 2.9 %collective-permute-done.3.refs_0_ = bf16[256,1024]{1,0:T(8,128)(2,1)S(1)} collective-permute-done((bf16[256,1024]{1,0:T(8,128)(2,1)S(1)}, bf16[256,1024]{1,0:T(8,128)(2,1)S(1)}, u32[]{:S(2)}, u32[]{:S(2)}) %collective-permute-start.3) | collective-permute-done | bytes 524320 | tf_op jit(solution)/shard_map/ppermute | solution.py:369
  32.4 1.6 %collective-permute-done.6.refs_0_ = bf16[256,1024]{1,0:T(8,128)(2,1)S(1)} collective-permute-done((bf16[256,1024]{1,0:T(8,128)(2,1)S(1)}, bf16[256,1024]{1,0:T(8,128)(2,1)S(1)}, u32[]{:S(2)}, u32[]{:S(2)}) %collective-permute-start.6) | collective-permute-done | bytes 524320 | tf_op jit(solution)/shard_map/ppermute | solution.py:369
  34.0 0.5 collective-permute-start.7
  34.5 5.9 %collective-permute-done.1.refs_2_ = bf16[2,512,256]{2,1,0:T(8,128)(2,1)S(1)} collective-permute-done((bf16[2,512,256]{2,1,0:T(8,128)(2,1)S(1)}, bf16[2,512,256]{2,1,0:T(8,128)(2,1)S(1)}, u32[]{:S(2)}, u32[]{:S(2)}) %collective-permute-start.1) | collective-permute-done | bytes 524320 | tf_op jit(solution)/shard_map/ppermute | solution.py:352
  40.4 0.8 %collective-permute-done.9.refs_0_ = bf16[256,1024]{1,0:T(8,128)(2,1)S(1)} collective-permute-done((bf16[256,1024]{1,0:T(8,128)(2,1)S(1)}, bf16[256,1024]{1,0:T(8,128)(2,1)S(1)}, u32[]{:S(2)}, u32[]{:S(2)}) %collective-permute-start.9) | collective-permute-done | bytes 524320 | tf_op jit(solution)/shard_map/ppermute | solution.py:369
  41.3 2.0 %project.2 = (bf16[2,256,256]{2,1,0:T(8,128)(2,1)S(1)}, bf16[2,256,256]{2,1,0:T(8,128)(2,1)S(1)}, f32[2,256,256]{2,1,0:T(8,128)S(1)}) custom-call(bf16[2,512,256]{2,1,0:T(8,128)(2,1)S(1)} %get-tuple-element.17.refs_0_, bf16[2,512,256]{2,1,0:T(8,128)(2,1)S(1)} %collective-permute-done.refs_2_.refs_1_, ...), custom_call_target="tpu_custom_call" | custom-call | tf_op jit(solution)/shard_map/project/pallas_call | solution.py:183
  43.3 2.5 %collective-permute-start.10 = (bf16[2,256,256]{2,1,0:T(8,128)(2,1)S(1)}, bf16[2,256,256]{2,1,0:T(8,128)(2,1)S(1)}, u32[]{:S(2)}, u32[]{:S(2)}) collective-permute-start(bf16[2,256,256]{2,1,0:T(8,128)(2,1)S(1)} %get-tuple-element.24), channel_id=1, source_target_pairs={{0,18},{2,16},{16,2},{18,0},{1,19},{3,17},{17,3},{19,1},{4,22},{6,... | collective-permute-start | bytes 786440 | tf_op jit(solution)/shard_map/ppermute | solution.py:380
  45.8 0.5 collective-permute-start.11
  46.3 0.9 %project.3 = bf16[2,256,256]{2,1,0:T(8,128)(2,1)S(1)} custom-call(bf16[2,512,256]{2,1,0:T(8,128)(2,1)S(1)} %get-tuple-element.17.refs_0_, bf16[2,512,256]{2,1,0:T(8,128)(2,1)S(1)} %collective-permute-done.refs_2_.refs_1_, bf16[2,512,256]{2,1,0:T(8,128)(2,1)S(1)} %collective-permute-done.1.refs_2_, bf16[2,512,256]{2,1,0:T(8,128)(2,1)S(1)} %collective-permute-done.2.refs_3_, ...), custom_call_target="tpu_custom_call" | custom-call | tf_op jit(solution)/shard_map/project/pallas_call | solution.py:183
  47.2 0.6 collective-permute-start.13
  48.4 5.0 %collective-permute-done.10.refs_0_ = bf16[2,256,256]{2,1,0:T(8,128)(2,1)S(1)} collective-permute-done((bf16[2,256,256]{2,1,0:T(8,128)(2,1)S(1)}, bf16[2,256,256]{2,1,0:T(8,128)(2,1)S(1)}, u32[]{:S(2)}, u32[]{:S(2)}) %collective-permute-start.10) | collective-permute-done | bytes 262176 | tf_op jit(solution)/shard_map/ppermute | solution.py:380
  53.4 5.2 %collective-permute-done.11.refs_1_ = bf16[2,256,256]{2,1,0:T(8,128)(2,1)S(1)} collective-permute-done((bf16[2,256,256]{2,1,0:T(8,128)(2,1)S(1)}, bf16[2,256,256]{2,1,0:T(8,128)(2,1)S(1)}, u32[]{:S(2)}, u32[]{:S(2)}) %collective-permute-start.11) | collective-permute-done | bytes 262176 | tf_op jit(solution)/shard_map/ppermute | solution.py:380
  58.5 0.1 collective-permute-done.13.refs_3_
  58.6 5.6 %attend_own.1 = bf16[256,2048]{1,0:T(8,128)(2,1)} custom-call(s32[1]{0:T(128)} %bitcast.1.live_ref, bf16[256,2048]{1,0:T(8,128)(2,1)S(1)} %bitcast.9, bf16[2,256,256]{2,1,0:T(8,128)(2,1)S(1)} %collective-permute-done.10.refs_0_, bf16[2,256,256]{2,1,0:T(8,128)(2,1)S(1)} %collective-permute-done.11.refs_1_, f32[2,256,256]{2,1,0:T(8,128)S(1)} %get-tuple-element.26.refs_2_, ...), custom_call_target="tpu_custom_call" | custom-call | tf_op jit(solution)/shard_map/attend_own/pallas_call | solution.py:297
  (20 shorter events, 0.0 us)
Async XLA Ops:
  1.2 21.4 %copy-start = (bf16[1,2,128,2048]{3,2,1,0:T(8,128)(2,1)S(1)}, bf16[1,2,128,2048]{3,2,1,0:T(8,128)(2,1)}, u32[]{:S(2)}) copy-start(bf16[1,2,128,2048]{3,2,1,0:T(8,128)(2,1)} %param.9) | copy-start | bytes 3145732
  1.2 16.5 %collective-permute-start = (bf16[2,512,256]{2,1,0:T(8,128)(2,1)S(1)}, bf16[2,512,256]{2,1,0:T(8,128)(2,1)S(1)}, u32[]{:S(2)}, u32[]{:S(2)}) collective-permute-start(bf16[2,512,256]{2,1,0:T(8,128)(2,1)S(1)} %get-tuple-element.17.refs_0_), channel_id=1, source_target_pairs={{0,8},{8,12},{12,4},{4,0},{1,9},{9,13},{13,5},{5,1},{2,10},{10,14}... | collective-permute-start | bytes 1572872 | tf_op jit(solution)/shard_map/ppermute | solution.py:352
  5.3 15.8 %collective-permute-start.4 = (bf16[2,512,256]{2,1,0:T(8,128)(2,1)S(1)}, bf16[2,512,256]{2,1,0:T(8,128)(2,1)S(1)}, u32[]{:S(2)}, u32[]{:S(2)}) collective-permute-start(bf16[2,512,256]{2,1,0:T(8,128)(2,1)S(1)} %get-tuple-element.19.refs_0_), channel_id=1, source_target_pairs={{0,2},{2,0},{1,3},{3,1},{4,6},{6,4},{5,7},{7,5},{8,10},{10,8},{9,1... | collective-permute-start | bytes 1572872 | tf_op jit(solution)/shard_map/ppermute | solution.py:347
  8.4 24.0 %collective-permute-start.3 = (bf16[256,1024]{1,0:T(8,128)(2,1)S(1)}, bf16[256,1024]{1,0:T(8,128)(2,1)S(1)}, u32[]{:S(2)}, u32[]{:S(2)}) collective-permute-start(bf16[256,1024]{1,0:T(8,128)(2,1)S(1)} %get-tuple-element.18), channel_id=1, source_target_pairs={{0,18},{2,16},{16,2},{18,0},{1,19},{3,17},{17,3},{19,1},{4,22},{6,... | collective-permute-start | bytes 1572872 | tf_op jit(solution)/shard_map/ppermute | solution.py:369
  10.0 24.1 %collective-permute-start.6 = (bf16[256,1024]{1,0:T(8,128)(2,1)S(1)}, bf16[256,1024]{1,0:T(8,128)(2,1)S(1)}, u32[]{:S(2)}, u32[]{:S(2)}) collective-permute-start(bf16[256,1024]{1,0:T(8,128)(2,1)S(1)} %get-tuple-element.21), channel_id=1, source_target_pairs={{0,16},{2,18},{16,0},{18,2},{1,17},{3,19},{17,1},{19,3},{4,20},{6,... | collective-permute-start | bytes 1572872 | tf_op jit(solution)/shard_map/ppermute | solution.py:369
  10.5 23.6 %collective-permute-start.2 = (bf16[2,512,256]{2,1,0:T(8,128)(2,1)S(1)}, bf16[2,512,256]{2,1,0:T(8,128)(2,1)S(1)}, u32[]{:S(2)}, u32[]{:S(2)}) collective-permute-start(bf16[2,512,256]{2,1,0:T(8,128)(2,1)S(1)} %get-tuple-element.17.refs_0_), channel_id=1, source_target_pairs={{8,0},{12,8},{4,12},{0,4},{9,1},{13,9},{5,13},{1,5},{10,2},{14,10}... | collective-permute-start | bytes 1572872 | tf_op jit(solution)/shard_map/ppermute | solution.py:357
  17.7 22.7 %collective-permute-start.1 = (bf16[2,512,256]{2,1,0:T(8,128)(2,1)S(1)}, bf16[2,512,256]{2,1,0:T(8,128)(2,1)S(1)}, u32[]{:S(2)}, u32[]{:S(2)}) collective-permute-start(bf16[2,512,256]{2,1,0:T(8,128)(2,1)S(1)} %collective-permute-done.refs_2_.refs_1_), channel_id=1, source_target_pairs={{0,8},{8,12},{12,4},{4,0},{1,9},{9,13},{13,5},{5,1},{2,10},{10,14}... | collective-permute-start | bytes 1572872 | tf_op jit(solution)/shard_map/ppermute | solution.py:352
  21.1 20.1 %collective-permute-start.9 = (bf16[256,1024]{1,0:T(8,128)(2,1)S(1)}, bf16[256,1024]{1,0:T(8,128)(2,1)S(1)}, u32[]{:S(2)}, u32[]{:S(2)}) collective-permute-start(bf16[256,1024]{1,0:T(8,128)(2,1)S(1)} %after.6), channel_id=1, source_target_pairs={{0,2},{2,0},{16,18},{18,16},{1,3},{3,1},{17,19},{19,17},{4,6},{6,4... | collective-permute-start | bytes 1572872 | tf_op jit(solution)/shard_map/ppermute | solution.py:369
  29.5 11.7 %copy-start.1 = (f32[256,2048]{1,0:T(8,128)}, f32[256,2048]{1,0:T(8,128)S(1)}, u32[]{:S(2)}) copy-start(f32[256,2048]{1,0:T(8,128)S(1)} %get-tuple-element.27.refs_5_) | copy-start | bytes 6291460
  29.5 11.7 %copy-start.2 = (f32[256,2048]{1,0:T(8,128)}, f32[256,2048]{1,0:T(8,128)S(1)}, u32[]{:S(2)}) copy-start(f32[256,2048]{1,0:T(8,128)S(1)} %get-tuple-element.28.refs_6_) | copy-start | bytes 6291460
  32.4 8.8 %collective-permute-start.8 = (bf16[256,1024]{1,0:T(8,128)(2,1)S(1)}, bf16[256,1024]{1,0:T(8,128)(2,1)S(1)}, u32[]{:S(2)}, u32[]{:S(2)}) collective-permute-start(bf16[256,1024]{1,0:T(8,128)(2,1)S(1)} %get-tuple-element.22.refs_8_), channel_id=1, source_target_pairs={{0,1},{1,0},{2,3},{3,2},{4,5},{5,4},{6,7},{7,6},{8,9},{9,8},{10,11... | collective-permute-start | bytes 1572872 | tf_op jit(solution)/shard_map/ppermute | solution.py:371
  34.0 7.2 %collective-permute-start.5 = (bf16[256,1024]{1,0:T(8,128)(2,1)S(1)}, bf16[256,1024]{1,0:T(8,128)(2,1)S(1)}, u32[]{:S(2)}, u32[]{:S(2)}) collective-permute-start(bf16[256,1024]{1,0:T(8,128)(2,1)S(1)} %after.4.refs_4_), channel_id=1, source_target_pairs={{0,1},{1,0},{2,3},{3,2},{4,5},{5,4},{6,7},{7,6},{8,9},{9,8},{10,11... | collective-permute-start | bytes 1572872 | tf_op jit(solution)/shard_map/ppermute | solution.py:371
  34.0 7.2 %collective-permute-start.7 = (bf16[256,1024]{1,0:T(8,128)(2,1)S(1)}, bf16[256,1024]{1,0:T(8,128)(2,1)S(1)}, u32[]{:S(2)}, u32[]{:S(2)}) collective-permute-start(bf16[256,1024]{1,0:T(8,128)(2,1)S(1)} %after.5.refs_6_), channel_id=1, source_target_pairs={{0,1},{1,0},{2,3},{3,2},{4,5},{5,4},{6,7},{7,6},{8,9},{9,8},{10,11... | collective-permute-start | bytes 1572872 | tf_op jit(solution)/shard_map/ppermute | solution.py:371
  41.2 5.0 %collective-permute-start.12 = (bf16[256,1024]{1,0:T(8,128)(2,1)S(1)}, bf16[256,1024]{1,0:T(8,128)(2,1)S(1)}, u32[]{:S(2)}, u32[]{:S(2)}) collective-permute-start(bf16[256,1024]{1,0:T(8,128)(2,1)S(1)} %after.7.refs_10_.refs_4_), channel_id=1, source_target_pairs={{0,1},{1,0},{2,3},{3,2},{4,5},{5,4},{6,7},{7,6},{8,9},{9,8},{10,11... | collective-permute-start | bytes 1572872 | tf_op jit(solution)/shard_map/ppermute | solution.py:371
  43.3 10.1 %collective-permute-start.10 = (bf16[2,256,256]{2,1,0:T(8,128)(2,1)S(1)}, bf16[2,256,256]{2,1,0:T(8,128)(2,1)S(1)}, u32[]{:S(2)}, u32[]{:S(2)}) collective-permute-start(bf16[2,256,256]{2,1,0:T(8,128)(2,1)S(1)} %get-tuple-element.24), channel_id=1, source_target_pairs={{0,18},{2,16},{16,2},{18,0},{1,19},{3,17},{17,3},{19,1},{4,22},{6,... | collective-permute-start | bytes 786440 | tf_op jit(solution)/shard_map/ppermute | solution.py:380
  45.8 12.8 %collective-permute-start.11 = (bf16[2,256,256]{2,1,0:T(8,128)(2,1)S(1)}, bf16[2,256,256]{2,1,0:T(8,128)(2,1)S(1)}, u32[]{:S(2)}, u32[]{:S(2)}) collective-permute-start(bf16[2,256,256]{2,1,0:T(8,128)(2,1)S(1)} %get-tuple-element.25), channel_id=1, source_target_pairs={{0,16},{2,18},{16,0},{18,2},{1,17},{3,19},{17,1},{19,3},{4,20},{6,... | collective-permute-start | bytes 786440 | tf_op jit(solution)/shard_map/ppermute | solution.py:380
  47.2 11.5 %collective-permute-start.13 = (bf16[2,256,256]{2,1,0:T(8,128)(2,1)S(1)}, bf16[2,256,256]{2,1,0:T(8,128)(2,1)S(1)}, u32[]{:S(2)}, u32[]{:S(2)}) collective-permute-start(bf16[2,256,256]{2,1,0:T(8,128)(2,1)S(1)} %project.3), channel_id=1, source_target_pairs={{0,2},{2,0},{16,18},{18,16},{1,3},{3,1},{17,19},{19,17},{4,6},{6,4... | collective-permute-start | bytes 786440 | tf_op jit(solution)/shard_map/ppermute | solution.py:380
